TPU v7x, 32 devices: a whole 2x2x4 slice. The times are simulated.
32 devices in a mesh: dp: 8 (over y, x, core), seq: 4 (over z).
Axes of the slice: x: 2, y: 2, z: 4, core: 2. Of those that a mesh axis runs over, the one named last changes fastest.
Arguments:
- tokens: bfloat16 [16, 1024, 1024], P('dp', 'seq'), may hold values from -6 to 6
- source: bfloat16 [16, 1024, 1024], P('dp', 'seq'), may hold values from -6 to 6
- target_lengths: int32 [16, 4], P('dp'), may hold values from 1 to 896, 1024 in all within a row
- source_lengths: int32 [16], P('dp'), may hold values from 896 to 1024, as said below
- step_index: int32 [1], replicated, may hold values from 0 to 4
- self_query: bfloat16 [1024, 1024], P('dp'), may hold values from -0.1875 to 0.1875
- self_key: bfloat16 [1024, 1024], P('dp'), may hold values from -0.1875 to 0.1875
- self_value: bfloat16 [1024, 1024], P('dp'), may hold values from -0.1875 to 0.1875
- self_out: bfloat16 [1024, 1024], P('dp'), may hold values from -0.75 to 0.75
- cross_query: bfloat16 [1024, 1024], P('dp'), may hold values from -0.1875 to 0.1875
- cross_key: bfloat16 [1024, 1024], P('dp'), may hold values from -0.1875 to 0.1875
- cross_value: bfloat16 [1024, 1024], P('dp'), may hold values from -0.1875 to 0.1875
- cross_out: bfloat16 [1024, 1024], P('dp'), may hold values from -0.75 to 0.75
- ffn_expand: bfloat16 [1024, 4096], P('dp'), may hold values from -0.1875 to 0.1875
- ffn_contract: bfloat16 [4096, 1024], P('dp'), may hold values from -0.09375 to 0.09375
- adapter_down: bfloat16 [1024, 512], replicated, may hold values from -0.1875 to 0.1875
- adapter_up: bfloat16 [512, 1024], replicated, may hold values from -0.25 to 0.25
- grad_output: bfloat16 [16, 1024, 1024], P('dp', 'seq'), may hold values from -6 to 6
Outputs:
- output: bfloat16 [16, 1024, 1024], P('dp', 'seq')
- grad_tokens: bfloat16 [16, 1024, 1024], P('dp', 'seq')
- grad_source: bfloat16 [16, 1024, 1024], P('dp', 'seq')
- grad_down: float32 [1024, 512], replicated
- grad_up: float32 [512, 1024], replicated
Inputs may be any that keep to these rules, and one draw needn't show every extreme that they name: `target_lengths`: each row's lengths sum to 1024; the largest of each row is exactly 896. `source_lengths`: some row has exactly 1024, some row exactly 896.
All inputs are finite; a program needn't handle non-finite values.
Results may differ from a plain program's by a relative error of at most 0.02.
Values may be sent and summed in bfloat16 or wider, within the bound.
No kernel may reach another device: no remote copies, remote signals or barrier semaphores. Data moves between devices by JAX's collectives and lax.ppermute only.
A program may use at most 320 MiB of HBM per device.

v0:
```python
import jax
import jax.numpy as jnp
from jax import lax
from jax.sharding import PartitionSpec as P

HEADS = 16


def product(left, right):
    return jnp.dot(left, right, preferred_element_type=jnp.float32)


def normalize(values):
    centered = values - jnp.mean(values, axis=-1, keepdims=True)
    spread = jnp.mean(centered * centered, axis=-1, keepdims=True)
    return centered * lax.rsqrt(spread + 1e-05)


def smooth(values):
    return jax.nn.gelu(values, approximate=False)


def normalize_back(values, grads):
    return jax.vjp(normalize, values)[1](grads)[0]


def smooth_back(values, grads):
    return jax.vjp(smooth, values)[1](grads)[0]


def split_heads(values):
    return values.reshape(values.shape[0], values.shape[1], HEADS, values.shape[2] // HEADS)


def attend_forward(query, keys, values, allowed):
    scores = jnp.einsum(
        "rqhd,rkhd->rhqk", query, split_heads(keys), preferred_element_type=jnp.float32
    )
    scores = jnp.where(allowed, scores, -1e30)
    largest = jnp.max(scores, axis=-1, keepdims=True)
    shifted = jnp.exp(scores - largest)
    totals = jnp.sum(shifted, axis=-1, keepdims=True)
    probs = (shifted / totals).astype(jnp.bfloat16)
    attended = jnp.einsum(
        "rhqk,rkhd->rqhd", probs, split_heads(values), preferred_element_type=jnp.float32
    )
    shape = attended.shape
    merged = attended.reshape(shape[0], shape[1], shape[2] * shape[3]).astype(jnp.bfloat16)
    return (merged, largest + jnp.log(totals))


def attend_backward(query, keys, values, allowed, logsum, grad_attended):
    key_heads = split_heads(keys)
    grad_heads = split_heads(grad_attended)
    scores = jnp.einsum("rqhd,rkhd->rhqk", query, key_heads, preferred_element_type=jnp.float32)
    scores = jnp.where(allowed, scores, -1e30)
    probs = jnp.exp(scores - logsum)
    grad_probs = jnp.einsum(
        "rqhd,rkhd->rhqk", grad_heads, split_heads(values), preferred_element_type=jnp.float32
    )
    row_dot = jnp.sum(probs * grad_probs, axis=-1, keepdims=True)
    grad_scores = (probs * (grad_probs - row_dot)).astype(jnp.bfloat16)
    grad_query = jnp.einsum(
        "rhqk,rkhd->rqhd", grad_scores, key_heads, preferred_element_type=jnp.float32
    )
    grad_keys = jnp.einsum(
        "rhqk,rqhd->rkhd", grad_scores, query, preferred_element_type=jnp.float32
    )
    grad_values = jnp.einsum(
        "rhqk,rqhd->rkhd",
        probs.astype(jnp.bfloat16),
        grad_heads,
        preferred_element_type=jnp.float32,
    )
    shape = grad_keys.shape
    return (
        grad_query,
        grad_keys.reshape(shape[0], shape[1], shape[2] * shape[3]),
        grad_values.reshape(shape[0], shape[1], shape[2] * shape[3]),
    )


def local(
    tokens,
    source,
    target_lengths,
    source_lengths,
    step_index,
    self_query,
    self_key,
    self_value,
    self_out,
    cross_query,
    cross_key,
    cross_value,
    cross_out,
    ffn_expand,
    ffn_contract,
    adapter_down,
    adapter_up,
    grad_output,
):
    shards = (
        self_query,
        self_key,
        self_value,
        self_out,
        cross_query,
        cross_key,
        cross_value,
        cross_out,
        ffn_expand,
        ffn_contract,
    )
    w_query, w_key, w_value, w_out, c_query, c_key, c_value, c_out, w_expand, w_contract = (
        lax.all_gather(shards[0], "dp", axis=0, tiled=True),
        lax.all_gather(shards[1], "dp", axis=0, tiled=True),
        lax.all_gather(shards[2], "dp", axis=0, tiled=True),
        lax.all_gather(shards[3], "dp", axis=0, tiled=True),
        lax.all_gather(shards[4], "dp", axis=0, tiled=True),
        lax.all_gather(shards[5], "dp", axis=0, tiled=True),
        lax.all_gather(shards[6], "dp", axis=0, tiled=True),
        lax.all_gather(shards[7], "dp", axis=0, tiled=True),
        lax.all_gather(shards[8], "dp", axis=0, tiled=True),
        lax.all_gather(shards[9], "dp", axis=0, tiled=True),
    )
    row_count, own_len, features = tokens.shape
    src_own = source.shape[1]
    group = lax.axis_size("seq")
    full_len = own_len * group
    full_src = src_own * group
    branch_scale = (step_index[0] + 1).astype(jnp.float32) / 5.0
    offset = lax.axis_index("seq") * own_len
    query_pos = offset + jnp.arange(own_len, dtype=jnp.int32)
    key_pos = jnp.arange(full_len, dtype=jnp.int32)
    doc_ends = jnp.cumsum(target_lengths, axis=1)[:, :-1]
    query_doc = jnp.sum(
        (query_pos[None, :, None] >= doc_ends[:, None, :]).astype(jnp.int32), axis=-1
    )
    key_doc = jnp.sum((key_pos[None, :, None] >= doc_ends[:, None, :]).astype(jnp.int32), axis=-1)
    self_allowed = (
        (key_pos[None, None, :] <= query_pos[None, :, None])
        & (query_doc[:, :, None] == key_doc[:, None, :])
    )[:, None]
    src_pos = jnp.arange(full_src, dtype=jnp.int32)
    source_allowed = (src_pos[None, :] < source_lengths[:, None])[:, None, None, :]
    token_rows = tokens.reshape(row_count * own_len, features)
    source_rows = source.reshape(row_count * src_own, features)
    query = (
        (product(token_rows, w_query) * 0.125)
        .astype(jnp.bfloat16)
        .reshape(row_count, own_len, HEADS, features // HEADS)
    )
    own_keys = product(token_rows, w_key).astype(jnp.bfloat16).reshape(row_count, own_len, features)
    own_values = (
        product(token_rows, w_value).astype(jnp.bfloat16).reshape(row_count, own_len, features)
    )
    own_src_keys = (
        product(source_rows, c_key).astype(jnp.bfloat16).reshape(row_count, src_own, features)
    )
    own_src_values = (
        product(source_rows, c_value).astype(jnp.bfloat16).reshape(row_count, src_own, features)
    )
    all_keys, all_values = (
        lax.all_gather(own_keys, "seq", axis=1, tiled=True),
        lax.all_gather(own_values, "seq", axis=1, tiled=True),
    )
    src_keys, src_values = (
        lax.all_gather(own_src_keys, "seq", axis=1, tiled=True),
        lax.all_gather(own_src_values, "seq", axis=1, tiled=True),
    )
    attended, self_logsum = attend_forward(query, all_keys, all_values, self_allowed)
    first_sum = token_rows.astype(jnp.float32) + product(attended.reshape(-1, features), w_out)
    first_norm = normalize(first_sum)
    cross_q = (
        (product(first_norm.astype(jnp.bfloat16), c_query) * 0.125)
        .astype(jnp.bfloat16)
        .reshape(row_count, own_len, HEADS, features // HEADS)
    )
    cross_attended, cross_logsum = attend_forward(cross_q, src_keys, src_values, source_allowed)
    second_sum = first_norm + product(cross_attended.reshape(-1, features), c_out)
    second_norm = normalize(second_sum)
    second_low = second_norm.astype(jnp.bfloat16)
    hidden_pre = product(second_low, w_expand)
    hidden = smooth(hidden_pre).astype(jnp.bfloat16)
    narrow = product(second_low, adapter_down)
    squeezed = smooth(narrow).astype(jnp.bfloat16)
    third_sum = (
        second_norm + product(hidden, w_contract) + branch_scale * product(squeezed, adapter_up)
    )
    output = normalize(third_sum).astype(jnp.bfloat16).reshape(row_count, own_len, features)
    grad_third = normalize_back(third_sum, grad_output.reshape(-1, features).astype(jnp.float32))
    grad_ffn = grad_third.astype(jnp.bfloat16)
    grad_adapt = (branch_scale * grad_third).astype(jnp.bfloat16)
    grad_hidden = smooth_back(hidden_pre, product(grad_ffn, w_contract.T)).astype(jnp.bfloat16)
    grad_up = product(squeezed.T, grad_adapt)
    grad_narrow = smooth_back(narrow, product(grad_adapt, adapter_up.T)).astype(jnp.bfloat16)
    grad_down = product(second_low.T, grad_narrow)
    grad_second = (
        grad_third + product(grad_hidden, w_expand.T) + product(grad_narrow, adapter_down.T)
    )
    grad_second_sum = normalize_back(second_sum, grad_second)
    grad_cross = (
        product(grad_second_sum.astype(jnp.bfloat16), c_out.T)
        .astype(jnp.bfloat16)
        .reshape(row_count, own_len, features)
    )
    gq_cross, gk_cross, gv_cross = attend_backward(
        cross_q, src_keys, src_values, source_allowed, cross_logsum, grad_cross
    )
    grad_first = grad_second_sum + 0.125 * product(
        gq_cross.astype(jnp.bfloat16).reshape(-1, features), c_query.T
    )
    own_gk_cross, own_gv_cross = (
        lax.psum_scatter(
            gk_cross.astype(jnp.bfloat16), "seq", scatter_dimension=1, tiled=True
        ).astype(jnp.float32),
        lax.psum_scatter(
            gv_cross.astype(jnp.bfloat16), "seq", scatter_dimension=1, tiled=True
        ).astype(jnp.float32),
    )
    grad_source = product(
        own_gk_cross.astype(jnp.bfloat16).reshape(-1, features), c_key.T
    ) + product(own_gv_cross.astype(jnp.bfloat16).reshape(-1, features), c_value.T)
    grad_source = grad_source.astype(jnp.bfloat16).reshape(row_count, src_own, features)
    grad_first_sum = normalize_back(first_sum, grad_first)
    grad_self = (
        product(grad_first_sum.astype(jnp.bfloat16), w_out.T)
        .astype(jnp.bfloat16)
        .reshape(row_count, own_len, features)
    )
    gq_self, gk_self, gv_self = attend_backward(
        query, all_keys, all_values, self_allowed, self_logsum, grad_self
    )
    own_gk_self, own_gv_self = (
        lax.psum_scatter(
            gk_self.astype(jnp.bfloat16), "seq", scatter_dimension=1, tiled=True
        ).astype(jnp.float32),
        lax.psum_scatter(
            gv_self.astype(jnp.bfloat16), "seq", scatter_dimension=1, tiled=True
        ).astype(jnp.float32),
    )
    grad_tokens = grad_first_sum + 0.125 * product(
        gq_self.astype(jnp.bfloat16).reshape(-1, features), w_query.T
    )
    grad_tokens = grad_tokens + product(
        own_gk_self.astype(jnp.bfloat16).reshape(-1, features), w_key.T
    )
    grad_tokens = grad_tokens + product(
        own_gv_self.astype(jnp.bfloat16).reshape(-1, features), w_value.T
    )
    grad_tokens = grad_tokens.astype(jnp.bfloat16).reshape(row_count, own_len, features)
    grad_down, grad_up = lax.psum((grad_down, grad_up), ("dp", "seq"))
    return (output, grad_tokens, grad_source, grad_down, grad_up)


def solution(mesh):
    return jax.shard_map(
        local,
        mesh=mesh,
        in_specs=(
            P("dp", "seq", None),
            P("dp", "seq", None),
            P("dp", None),
            P("dp"),
            P(),
            P("dp", None),
            P("dp", None),
            P("dp", None),
            P("dp", None),
            P("dp", None),
            P("dp", None),
            P("dp", None),
            P("dp", None),
            P("dp", None),
            P("dp", None),
            P(),
            P(),
            P("dp", "seq", None),
        ),
        out_specs=(P("dp", "seq", None), P("dp", "seq", None), P("dp", "seq", None), P(), P()),
        check_vma=False,
    )
```

profile of v0, /device:TPU:1, one launch (start us, length us, event | category | flops | bytes accessed | tf_op | source)
XLA Modules:
  0.0 1276.8 jit_solution(12669673854961467209)
XLA Ops:
  10.6 29.7 %all-gather.21.cloned.1.call-done = bf16[1024,1024]{1,0:T(8,128)(2,1)} async-done(((bf16[128,1024]{1,0:T(8,128)(2,1)}), bf16[1024,1024]{1,0:T(8,128)(2,1)}) %all-gather.21.cloned.1.call-update) | async-done | bytes 2097168 | tf_op jit(solution)/shard_map/all_gather | solution.py:117
  40.3 4.1 convolution_convert_fusion.8
  44.6 25.6 %all-gather.15.cloned.1.call-done = bf16[1024,1024]{1,0:T(8,128)(2,1)} async-done(((bf16[128,1024]{1,0:T(8,128)(2,1)}), bf16[1024,1024]{1,0:T(8,128)(2,1)}) %all-gather.15.cloned.1.call-update) | async-done | bytes 2097168 | tf_op jit(solution)/shard_map/all_gather | solution.py:118
  75.5 24.4 %all-gather.33.cloned.1.call-done = bf16[1024,1024]{1,0:T(8,128)(2,1)} async-done(((bf16[128,1024]{1,0:T(8,128)(2,1)}), bf16[1024,1024]{1,0:T(8,128)(2,1)}) %all-gather.33.cloned.1.call-update) | async-done | bytes 2097168 | tf_op jit(solution)/shard_map/all_gather | solution.py:121
  103.9 25.7 %all-gather.27.cloned.1.call-done = bf16[1024,1024]{1,0:T(8,128)(2,1)} async-done(((bf16[128,1024]{1,0:T(8,128)(2,1)}), bf16[1024,1024]{1,0:T(8,128)(2,1)}) %all-gather.27.cloned.1.call-update) | async-done | bytes 2097168 | tf_op jit(solution)/shard_map/all_gather | solution.py:122
  137.3 22.0 %all-gather.19.cloned.1.call-done = bf16[1024,1024]{1,0:T(8,128)(2,1)} async-done(((bf16[128,1024]{1,0:T(8,128)(2,1)}), bf16[1024,1024]{1,0:T(8,128)(2,1)}) %all-gather.19.cloned.1.call-update) | async-done | bytes 2097168 | tf_op jit(solution)/shard_map/all_gather | solution.py:116
  167.5 74.2 %all-gather.23.cloned.1.call-done = bf16[2,1024,1024]{2,1,0:T(8,128)(2,1)} async-done(((bf16[2,256,1024]{2,1,0:T(8,128)(2,1)}), bf16[2,1024,1024]{2,1,0:T(8,128)(2,1)}) %all-gather.23.cloned.1.call-update) | async-done | bytes 4194320 | tf_op jit(solution)/shard_map/all_gather | solution.py:165
  241.7 6.2 copy.63
  247.9 16.0 %select_reduce_fusion.1 = (f32[2,16,256]{2,1,0:T(8,128)S(1)}, f32[2,16,256,1024]{3,2,1,0:T(8,128)}) fusion(pred[2,256,1024]{2,1,0:T(8,128)(4,1)S(1)} %compare_and_fusion, bf16[2,256,16,64]{1,3,2,0:T(8,128)(2,1)S(1)} %copy.64, bf16[2,1024,16,64]{1,3,2,0:T(8,128)(2,1)} %bitcast.136), kind=kOutput, calls=%fused_computation.13 | convolution fusion | flops 1090510848 | bytes 39354368 | tf_op jit(solution)/shard_map/rqhd,rkhd->rhqk/dot_general | solution.py:36
  263.9 14.6 %fusion = f32[2,16,256]{2,1,0:T(8,128)S(1)} fusion(f32[2,16,256,1024]{3,2,1,0:T(8,128)} %get-tuple-element.21, f32[2,16,256]{2,1,0:T(8,128)S(1)} %get-tuple-element.20, pred[2,256,1024]{2,1,0:T(8,128)(4,1)S(1)} %compare_and_fusion), kind=kLoop, calls=%fused_computation.10 | loop fusion | flops 25157632 | bytes 34144256 | tf_op jit(solution)/shard_map/reduce_sum | solution.py:42
  278.6 44.6 %all-gather.17.cloned.1.call-done = bf16[2,1024,1024]{2,1,0:T(8,128)(2,1)} async-done(((bf16[2,256,1024]{2,1,0:T(8,128)(2,1)}), bf16[2,1024,1024]{2,1,0:T(8,128)(2,1)}) %all-gather.17.cloned.1.call-update) | async-done | bytes 4194320 | tf_op jit(solution)/shard_map/all_gather | solution.py:166
  323.2 6.2 copy.59
  329.4 15.3 %fusion.37 = bf16[2,256,16,64]{1,3,2,0:T(8,128)(2,1)S(1)} fusion(bf16[2,1024,16,64]{1,3,2,0:T(8,128)(2,1)} %bitcast.138, f32[2,16,256,1024]{3,2,1,0:T(8,128)} %get-tuple-element.21, f32[2,16,256]{2,1,0:T(8,128)S(1)} %fusion, f32[2,16,256]{2,1,0:T(8,128)S(1)} %get-tuple-element.20, pred[2,256,1024]{2,1,0:T(8,128)(4,1)S(1)} %compare_and_fusion), kind=kOutput, calls=%fused_computation.92 | convolution fusion | flops 1107820544 | bytes 39387136 | tf_op jit(solution)/shard_map/rhqk,rkhd->rqhd/dot_general | solution.py:44
  347.0 5.0 all-gather.25.cloned.1.call-done
  355.9 25.9 %all-gather.31.cloned.1.call-done = bf16[1024,1024]{1,0:T(8,128)(2,1)} async-done(((bf16[128,1024]{1,0:T(8,128)(2,1)}), bf16[1024,1024]{1,0:T(8,128)(2,1)}) %all-gather.31.cloned.1.call-update) | async-done | bytes 2097168 | tf_op jit(solution)/shard_map/all_gather | solution.py:120
  390.2 73.3 %all-gather.35.cloned.1.call-done = bf16[2,1024,1024]{2,1,0:T(8,128)(2,1)} async-done(((bf16[2,256,1024]{2,1,0:T(8,128)(2,1)}), bf16[2,1024,1024]{2,1,0:T(8,128)(2,1)}) %all-gather.35.cloned.1.call-update) | async-done | bytes 4194320 | tf_op jit(solution)/shard_map/all_gather | solution.py:169
  463.5 6.2 copy.68
  469.7 15.9 %select_reduce_fusion = (f32[2,16,256]{2,1,0:T(8,128)S(1)}, f32[2,16,256,1024]{3,2,1,0:T(8,128)}) fusion(pred[2,1024]{1,0:T(4,128)(4,1)S(1)} %iota_compare_fusion.1, bf16[2,256,16,64]{1,3,2,0:T(8,128)(2,1)S(1)} %copy.69, bf16[2,1024,16,64]{1,3,2,0:T(8,128)(2,1)} %bitcast.134), kind=kOutput, calls=%fused_computation.12 | convolution fusion | flops 1090510848 | bytes 38832128 | tf_op jit(solution)/shard_map/rqhd,rkhd->rhqk/dot_general | solution.py:36
  485.6 14.3 %fusion.1 = f32[2,16,256]{2,1,0:T(8,128)S(1)} fusion(f32[2,16,256,1024]{3,2,1,0:T(8,128)} %get-tuple-element.25, f32[2,16,256]{2,1,0:T(8,128)S(1)} %get-tuple-element.24, pred[2,1024]{1,0:T(4,128)(4,1)S(1)} %iota_compare_fusion.1), kind=kLoop, calls=%fused_computation.11 | loop fusion | flops 25157632 | bytes 33622016 | tf_op jit(solution)/shard_map/reduce_sum | solution.py:42
  499.9 45.1 %all-gather.29.cloned.1.call-done = bf16[2,1024,1024]{2,1,0:T(8,128)(2,1)} async-done(((bf16[2,256,1024]{2,1,0:T(8,128)(2,1)}), bf16[2,1024,1024]{2,1,0:T(8,128)(2,1)}) %all-gather.29.cloned.1.call-update) | async-done | bytes 4194320 | tf_op jit(solution)/shard_map/all_gather | solution.py:170
  545.0 6.2 copy.66
  551.2 15.8 %fusion.36 = bf16[2,256,16,64]{1,3,2,0:T(8,128)(2,1)S(1)} fusion(bf16[2,1024,16,64]{1,3,2,0:T(8,128)(2,1)} %bitcast.140, f32[2,16,256,1024]{3,2,1,0:T(8,128)} %get-tuple-element.25, f32[2,16,256]{2,1,0:T(8,128)S(1)} %fusion.1, f32[2,16,256]{2,1,0:T(8,128)S(1)} %get-tuple-element.24, pred[2,1024]{1,0:T(4,128)(4,1)S(1)} %iota_compare_fusion.1), kind=kOutput, calls=%fused_computation.91 | convolution fusion | flops 1107820544 | bytes 38864896 | tf_op jit(solution)/shard_map/rhqk,rkhd->rqhd/dot_general | solution.py:44
  569.4 4.2 all-gather.37.cloned.1.call-done
  582.7 47.2 %all-gather.39.cloned.1.call-done = bf16[1024,4096]{1,0:T(8,128)(2,1)} async-done(((bf16[128,4096]{1,0:T(8,128)(2,1)}), bf16[1024,4096]{1,0:T(8,128)(2,1)}) %all-gather.39.cloned.1.call-update) | async-done | bytes 8388624 | tf_op jit(solution)/shard_map/all_gather | solution.py:124
  629.9 24.7 %fusion.16 = (f32[512,4096]{1,0:T(8,128)}, f32[512,4096]{1,0:T(8,128)}) fusion(bf16[512,1024]{1,0:T(8,128)(2,1)S(1)} %multiply_convert_fusion.8, bf16[1024,4096]{1,0:T(8,128)(2,1)} %all-gather.39.cloned.1.call-done), kind=kOutput, calls=%fused_computation.27 | convolution fusion | flops 4424990720 | bytes 26214400 | tf_op jit(solution)/shard_map/dot_general | solution.py:10
  654.6 31.5 %all-gather.41.cloned.1.call-done = bf16[4096,1024]{1,0:T(8,128)(2,1)} async-done(((bf16[512,1024]{1,0:T(8,128)(2,1)}), bf16[4096,1024]{1,0:T(8,128)(2,1)}) %all-gather.41.cloned.1.call-update) | async-done | bytes 8388624 | tf_op jit(solution)/shard_map/all_gather | solution.py:125
  686.1 10.9 fusion.22
  703.0 18.8 %fusion.24 = f32[512,1024]{1,0:T(8,128)} fusion(bf16[1024,4096]{1,0:T(8,128)(2,1)} %all-gather.39.cloned.1.call-done, f32[512,4096]{1,0:T(8,128)} %get-tuple-element.28, f32[512,4096]{1,0:T(8,128)} %get-tuple-element.29, bf16[4096,1024]{1,0:T(8,128)(2,1)} %all-gather.41.cloned.1.call-done, f32[512,1024]{1,0:T(8,128)} %copy-done.4, ...), kind=kOutput, calls=%fused_computation.45 | convolution fusion | flops 8620343296 | bytes 37750784 | tf_op jit(solution)/shard_map/dot_general | solution.py:10
  733.7 25.3 %multiply_reduce_fusion.1 = (f32[2,16,256]{2,1,0:T(8,128)S(1)}, f32[2,16,256,1024]{3,2,1,0:T(8,128)}) fusion(f32[2,16,256,1024]{3,2,1,0:T(8,128)} %get-tuple-element.25, f32[2,16,256]{2,1,0:T(8,128)S(1)} %log_add_fusion.1, pred[2,1024]{1,0:T(4,128)(4,1)S(1)} %iota_compare_fusion.1, bf16[2,256,16,64]{1,3,2,0:T(8,128)(2,1)S(1)} %copy.72, ...), kind=kOutput, calls=%fused_computation.4 | convolution fusion | flops 1107288064 | bytes 72419328 | tf_op jit(solution)/shard_map/rqhd,rkhd->rhqk/dot_general | solution.py:58
  759.0 28.0 %multiply_convert_fusion.1 = bf16[2,16,256,1024]{3,2,1,0:T(8,128)(2,1)} fusion(f32[2,16,256,1024]{3,2,1,0:T(8,128)} %get-tuple-element.36, f32[2,16,256,1024]{3,2,1,0:T(8,128)} %get-tuple-element.25, f32[2,16,256]{2,1,0:T(8,128)S(1)} %get-tuple-element.35, f32[2,16,256]{2,1,0:T(8,128)S(1)} %log_add_fusion.1, pred[2,1024]{1,0:T(4,128)(4,1)S(1)} %iota_compare_fusion.1), kind=kLoop, calls=%fused_computation.3 | loop fusion | flops 41943040 | bytes 83953664 | tf_op jit(solution)/shard_map/convert_element_type | solution.py:62
  787.0 10.8 convolution_convert_fusion
  797.7 6.2 copy.82
  804.8 13.0 %fusion.34 = bf16[2,256,16,64]{1,3,2,0:T(8,128)(2,1)S(1)} fusion(bf16[2,1024,16,64]{1,3,2,0:T(8,128)(2,1)} %bitcast.135, bf16[2,16,256,1024]{3,2,1,0:T(8,128)(2,1)} %multiply_convert_fusion.1), kind=kOutput, calls=%fused_computation.89 | convolution fusion | flops 1074266112 | bytes 22020096 | tf_op jit(solution)/shard_map/rhqk,rkhd->rqhd/dot_general | solution.py:63
  832.2 16.1 %fusion.28 = bf16[2,16,64,1024]{3,2,1,0:T(8,128)(2,1)} fusion(bf16[2,256,16,64]{1,3,2,0:T(8,128)(2,1)S(1)} %copy.75, f32[2,16,256,1024]{3,2,1,0:T(8,128)} %get-tuple-element.21, f32[2,16,256]{2,1,0:T(8,128)S(1)} %log_add_fusion, pred[2,256,1024]{2,1,0:T(8,128)(4,1)S(1)} %copy-done.3), kind=kOutput, calls=%fused_computation.52 | convolution fusion | flops 1101004800 | bytes 39354368 | tf_op jit(solution)/shard_map/rhqk,rqhd->rkhd/dot_general | solution.py:69
  848.3 6.2 copy.80
  854.6 25.9 %multiply_reduce_fusion = (f32[2,16,256]{2,1,0:T(8,128)S(1)}, f32[2,16,256,1024]{3,2,1,0:T(8,128)}) fusion(f32[2,16,256,1024]{3,2,1,0:T(8,128)} %get-tuple-element.21, f32[2,16,256]{2,1,0:T(8,128)S(1)} %log_add_fusion, pred[2,256,1024]{2,1,0:T(8,128)(4,1)S(1)} %copy-done.3, bf16[2,256,16,64]{1,3,2,0:T(8,128)(2,1)S(1)} %copy.75, ...), kind=kOutput, calls=%fused_computation.1 | convolution fusion | flops 1107288064 | bytes 72941568 | tf_op jit(solution)/shard_map/rqhd,rkhd->rhqk/dot_general | solution.py:58
  880.5 28.7 %multiply_convert_fusion = bf16[2,16,256,1024]{3,2,1,0:T(8,128)(2,1)} fusion(f32[2,16,256,1024]{3,2,1,0:T(8,128)} %get-tuple-element.40, f32[2,16,256,1024]{3,2,1,0:T(8,128)} %get-tuple-element.21, f32[2,16,256]{2,1,0:T(8,128)S(1)} %get-tuple-element.39, f32[2,16,256]{2,1,0:T(8,128)S(1)} %log_add_fusion, pred[2,256,1024]{2,1,0:T(8,128)(4,1)S(1)} %copy-done.3), kind=kLoop, calls=%fused_computation | loop fusion | flops 41943040 | bytes 84475904 | tf_op jit(solution)/shard_map/convert_element_type | solution.py:62
  909.2 10.8 convolution_convert_fusion.1
  920.0 6.2 copy.78
  926.3 16.0 %fusion.25 = bf16[2,16,64,1024]{3,2,1,0:T(8,128)(2,1)} fusion(bf16[2,256,16,64]{1,3,2,0:T(8,128)(2,1)S(1)} %copy.72, f32[2,16,256,1024]{3,2,1,0:T(8,128)} %get-tuple-element.25, f32[2,16,256]{2,1,0:T(8,128)S(1)} %log_add_fusion.1, pred[2,1024]{1,0:T(4,128)(4,1)S(1)} %iota_compare_fusion.1), kind=kOutput, calls=%fused_computation.51 | convolution fusion | flops 1101004800 | bytes 38832128 | tf_op jit(solution)/shard_map/rhqk,rqhd->rkhd/dot_general | solution.py:69
  942.2 6.2 copy.84
  949.0 12.3 fusion.35
  972.1 4.7 fusion.73
  976.8 62.7 %reduce-scatter.5.cloned.1.call-done = bf16[2,256,1024]{2,1,0:T(8,128)(2,1)} async-done(((bf16[2,1024,1024]{2,1,0:T(8,128)(2,1)}), bf16[2,256,1024]{2,1,0:T(8,128)(2,1)}) %reduce-scatter.5.cloned.1.call-update) | async-done | bytes 1048592 | tf_op jit(solution)/shard_map/reduce_scatter | solution.py:236
  1043.4 75.7 %reduce-scatter.11.cloned.1.call-done = bf16[2,256,1024]{2,1,0:T(8,128)(2,1)} async-done(((bf16[2,1024,1024]{2,1,0:T(8,128)(2,1)}), bf16[2,256,1024]{2,1,0:T(8,128)(2,1)}) %reduce-scatter.11.cloned.1.call-update) | async-done | bytes 1048592 | tf_op jit(solution)/shard_map/reduce_scatter | solution.py:218
  1119.1 4.9 add_convert_fusion.2
  1124.0 4.2 add_convert_fusion.3
  1128.2 137.4 %all-reduce.3.cloned.1.call-done = (f32[1024,512]{1,0:T(8,128)}, f32[512,1024]{1,0:T(8,128)}) async-done(((f32[1024,512]{1,0:T(8,128)}, f32[512,1024]{1,0:T(8,128)}), (f32[1024,512]{1,0:T(8,128)}, f32[512,1024]{1,0:T(8,128)})) %all-reduce.3.cloned.1.call-update) | async-done | bytes 4194320 | tf_op jit(solution)/shard_map/psum | solution.py:253
  (204 shorter events, 106.2 us)
Async XLA Ops:
  7.2 92.8 %copy-start = (bf16[2,256,1024]{2,1,0:T(8,128)(2,1)S(1)}, bf16[2,256,1024]{2,1,0:T(8,128)(2,1)}, u32[]{:S(2)}) copy-start(bf16[2,256,1024]{2,1,0:T(8,128)(2,1)} %param.19) | copy-start | bytes 3145732
  7.2 33.2 %all-gather.21.cloned.1.call-start = ((), (), s32[]{:S(2)}) async-start(), calls=%async_computation.7 | async-start | bytes 2359296 | tf_op jit(solution)/shard_map/all_gather | solution.py:117
  7.9 62.2 %all-gather.15.cloned.1.call-start = ((), (), s32[]{:S(2)}) async-start(), calls=%async_computation.4 | async-start | bytes 2359296 | tf_op jit(solution)/shard_map/all_gather | solution.py:118
  8.7 91.3 %all-gather.33.cloned.1.call-start = ((), (), s32[]{:S(2)}) async-start(), calls=%async_computation.13 | async-start | bytes 2359296 | tf_op jit(solution)/shard_map/all_gather | solution.py:121
  9.4 120.3 %all-gather.27.cloned.1.call-start = ((), (), s32[]{:S(2)}) async-start(), calls=%async_computation.10 | async-start | bytes 2359296 | tf_op jit(solution)/shard_map/all_gather | solution.py:122
  10.0 60.2 %copy-start.28 = (bf16[2,256,1024]{2,1,0:T(8,128)(2,1)S(1)}, bf16[2,256,1024]{2,1,0:T(8,128)(2,1)}, u32[]{:S(2)}) copy-start(bf16[2,256,1024]{2,1,0:T(8,128)(2,1)} %param.18) | copy-start | bytes 3145732
  10.0 149.3 %all-gather.19.cloned.1.call-start = ((), (), s32[]{:S(2)}) async-start(), calls=%async_computation.6 | async-start | bytes 2359296 | tf_op jit(solution)/shard_map/all_gather | solution.py:116
  10.6 231.1 %all-gather.23.cloned.1.call-start = ((), (), s32[]{:S(2)}) async-start(), calls=%async_computation.8 | async-start | bytes 5242880 | tf_op jit(solution)/shard_map/all_gather | solution.py:165
  44.5 278.7 %all-gather.17.cloned.1.call-start = ((), (), s32[]{:S(2)}) async-start(), calls=%async_computation.5 | async-start | bytes 5242880 | tf_op jit(solution)/shard_map/all_gather | solution.py:166
  74.0 277.9 %all-gather.25.cloned.1.call-start = ((), (), s32[]{:S(2)}) async-start(), calls=%async_computation.9 | async-start | bytes 2359296 | tf_op jit(solution)/shard_map/all_gather | solution.py:119
  74.8 307.0 %all-gather.31.cloned.1.call-start = ((), (), s32[]{:S(2)}) async-start(), calls=%async_computation.12 | async-start | bytes 2359296 | tf_op jit(solution)/shard_map/all_gather | solution.py:120
  75.5 388.1 %all-gather.35.cloned.1.call-start = ((), (), s32[]{:S(2)}) async-start(), calls=%async_computation.14 | async-start | bytes 5242880 | tf_op jit(solution)/shard_map/all_gather | solution.py:169
  103.8 31.6 %copy-start.41 = (s32[2,4]{1,0:T(2,128)S(1)}, s32[2,4]{1,0:T(2,128)}, u32[]{:S(2)}) copy-start(s32[2,4]{1,0:T(2,128)} %param.20) | copy-start | bytes 100
  103.9 32.9 %copy-start.42 = (s32[2]{0:T(128)S(1)}, s32[2]{0:T(128)}, u32[]{:S(2)}) copy-start(s32[2]{0:T(128)} %param.21) | copy-start | bytes 28
  103.9 441.2 %all-gather.29.cloned.1.call-start = ((), (), s32[]{:S(2)}) async-start(), calls=%async_computation.11 | async-start | bytes 5242880 | tf_op jit(solution)/shard_map/all_gather | solution.py:170
  133.5 440.2 %all-gather.37.cloned.1.call-start = ((), (), s32[]{:S(2)}) async-start(), calls=%async_computation.15 | async-start | bytes 2359296 | tf_op jit(solution)/shard_map/all_gather | solution.py:123
  134.1 495.9 %all-gather.39.cloned.1.call-start = ((), (), s32[]{:S(2)}) async-start(), calls=%async_computation.16 | async-start | bytes 9437184 | tf_op jit(solution)/shard_map/all_gather | solution.py:124
  134.8 551.3 %all-gather.41.cloned.1.call-start = ((), (), s32[]{:S(2)}) async-start(), calls=%async_computation.17 | async-start | bytes 9437184 | tf_op jit(solution)/shard_map/all_gather | solution.py:125
  135.4 832.7 %reduce-scatter.9.cloned.1.call-start = ((), (), s32[]{:S(2)}) async-start(), calls=%async_computation.20 | async-start | bytes 5242880 | tf_op jit(solution)/shard_map/reduce_scatter | solution.py:215
  137.3 192.1 %copy-start.2 = (pred[2,256,1024]{2,1,0:T(8,128)(4,1)}, pred[2,256,1024]{2,1,0:T(8,128)(4,1)S(1)}, u32[]{:S(2)}) copy-start(pred[2,256,1024]{2,1,0:T(8,128)(4,1)S(1)} %compare_and_fusion) | copy-start | bytes 1572868
  167.5 80.4 %copy-start.8 = (bf16[2,256,16,64]{1,3,2,0:T(8,128)(2,1)}, bf16[2,256,16,64]{1,3,2,0:T(8,128)(2,1)S(1)}, u32[]{:S(2)}) copy-start(bf16[2,256,16,64]{1,3,2,0:T(8,128)(2,1)S(1)} %copy.64) | copy-start | bytes 3145732
  263.9 65.4 %copy-start.29 = (f32[2,16,256]{2,1,0:T(8,128)}, f32[2,16,256]{2,1,0:T(8,128)S(1)}, u32[]{:S(2)}) copy-start(f32[2,16,256]{2,1,0:T(8,128)S(1)} %get-tuple-element.20) | copy-start | bytes 98308
  278.6 50.8 %copy-start.31 = (f32[2,16,256]{2,1,0:T(8,128)}, f32[2,16,256]{2,1,0:T(8,128)S(1)}, u32[]{:S(2)}) copy-start(f32[2,16,256]{2,1,0:T(8,128)S(1)} %fusion) | copy-start | bytes 98308
  355.4 29.2 %copy-start.6 = (f32[512,1024]{1,0:T(8,128)}, f32[512,1024]{1,0:T(8,128)S(1)}, u32[]{:S(2)}) copy-start(f32[512,1024]{1,0:T(8,128)S(1)} %get-tuple-element.23) | copy-start | bytes 6291460
  355.5 218.2 %copy-start.35 = (f32[512]{0:T(512)}, f32[512]{0:T(512)S(1)}, u32[]{:S(2)}) copy-start(f32[512]{0:T(512)S(1)} %broadcast_multiply_fusion.2) | copy-start | bytes 6148
  355.8 28.8 %copy-start.37 = (f32[512]{0:T(512)}, f32[512]{0:T(512)S(1)}, u32[]{:S(2)}) copy-start(f32[512]{0:T(512)S(1)} %multiply_reduce_fusion.6) | copy-start | bytes 6148
  355.8 217.8 %copy-start.39 = (f32[512]{0:T(512)}, f32[512]{0:T(512)S(1)}, u32[]{:S(2)}) copy-start(f32[512]{0:T(512)S(1)} %fusion.52) | copy-start | bytes 6148
  390.2 79.5 %copy-start.10 = (bf16[2,256,16,64]{1,3,2,0:T(8,128)(2,1)}, bf16[2,256,16,64]{1,3,2,0:T(8,128)(2,1)S(1)}, u32[]{:S(2)}) copy-start(bf16[2,256,16,64]{1,3,2,0:T(8,128)(2,1)S(1)} %copy.69) | copy-start | bytes 3145732
  578.8 51.2 %copy-start.12 = (bf16[512,1024]{1,0:T(8,128)(2,1)}, bf16[512,1024]{1,0:T(8,128)(2,1)S(1)}, u32[]{:S(2)}) copy-start(bf16[512,1024]{1,0:T(8,128)(2,1)S(1)} %multiply_convert_fusion.8) | copy-start | bytes 3145732
  686.1 10.9 copy-start.15
  686.1 10.9 copy-start.25
  700.6 21.2 %copy-start.33 = (f32[512]{0:T(512)}, f32[512]{0:T(512)S(1)}, u32[]{:S(2)}) copy-start(f32[512]{0:T(512)S(1)} %negate_multiply_fusion.4) | copy-start | bytes 6148
  702.9 18.8 %copy-start.17 = (bf16[512,512]{1,0:T(8,128)(2,1)}, bf16[512,512]{1,0:T(8,128)(2,1)S(1)}, u32[]{:S(2)}) copy-start(bf16[512,512]{1,0:T(8,128)(2,1)S(1)} %add_convert_fusion.10) | copy-start | bytes 1572868
  759.0 28.0 %copy-start.11 = (bf16[2,256,16,64]{1,3,2,0:T(8,128)(2,1)S(1)}, bf16[2,256,16,64]{1,3,2,0:T(8,128)(2,1)}, u32[]{:S(2)}) copy-start(bf16[2,256,16,64]{1,3,2,0:T(8,128)(2,1)} %copy-done.10) | copy-start | bytes 3145732
  804.0 168.1 %reduce-scatter.7.cloned.1.call-start = ((), (), s32[]{:S(2)}) async-start(), calls=%async_computation.19 | async-start | bytes 5242880 | tf_op jit(solution)/shard_map/reduce_scatter | solution.py:239
  826.8 5.4 copy-start.3
  854.5 185.0 %reduce-scatter.5.cloned.1.call-start = ((), (), s32[]{:S(2)}) async-start(), calls=%async_computation.18 | async-start | bytes 5242880 | tf_op jit(solution)/shard_map/reduce_scatter | solution.py:236
  880.5 28.7 %copy-start.9 = (bf16[2,256,16,64]{1,3,2,0:T(8,128)(2,1)S(1)}, bf16[2,256,16,64]{1,3,2,0:T(8,128)(2,1)}, u32[]{:S(2)}) copy-start(bf16[2,256,16,64]{1,3,2,0:T(8,128)(2,1)} %copy-done.8) | copy-start | bytes 3145732
  926.2 192.8 %reduce-scatter.11.cloned.1.call-start = ((), (), s32[]{:S(2)}) async-start(), calls=%async_computation.21 | async-start | bytes 5242880 | tf_op jit(solution)/shard_map/reduce_scatter | solution.py:218
  948.5 317.0 %all-reduce.3.cloned.1.call-start = ((), (), s32[]{:S(2)}) async-start(), calls=%async_computation.22 | async-start | bytes 8388608 | tf_op jit(solution)/shard_map/psum | solution.py:253
  961.3 4.5 copy-start.5
  961.3 4.5 copy-start.16
  972.1 67.4 %copy-start.43 = (bf16[1024,1024]{1,0:T(8,128)(2,1)S(1)}, bf16[1024,1024]{1,0:T(8,128)(2,1)}, u32[]{:S(2)}) copy-start(bf16[1024,1024]{1,0:T(8,128)(2,1)} %all-gather.21.cloned.1.call-done) | copy-start | bytes 6291460
  1043.3 80.7 %copy-start.21 = (f32[512,1024]{1,0:T(8,128)S(1)}, f32[512,1024]{1,0:T(8,128)}, u32[]{:S(2)}) copy-start(f32[512,1024]{1,0:T(8,128)} %copy-done.20) | copy-start | bytes 6291460
  1043.3 80.7 %copy-start.27 = (bf16[128,8,2,256]{3,1,2,0:T(8,128)(2,1)S(1)}, bf16[128,8,2,256]{3,1,2,0:T(8,128)(2,1)}, u32[]{:S(2)}) copy-start(bf16[128,8,2,256]{3,1,2,0:T(8,128)(2,1)} %copy.96) | copy-start | bytes 3145732
  1119.1 5.0 copy-start.44
  1119.1 5.0 copy-start.47
  1265.6 4.6 copy-start.1
  (21 other events, 47.0 us)
Sparse Core Ops, SparseCore 0:
  9.9 30.3 all-gather.20
  42.2 27.8 all-gather.14
  72.1 27.8 all-gather.32
  101.7 27.8 all-gather.26
  131.4 27.8 all-gather.18
  161.3 80.3 all-gather.22
  243.8 79.2 all-gather.16
  325.0 26.8 all-gather.24
  353.8 27.8 all-gather.30
  383.2 80.3 all-gather.34
  465.7 79.2 all-gather.28
  546.8 26.8 all-gather.36
  575.5 54.3 all-gather.38
  631.7 54.3 all-gather.40
  804.1 76.3 reduce-scatter.8
  882.8 77.2 reduce-scatter.6
  962.2 77.2 reduce-scatter.4
  1041.8 77.2 reduce-scatter.10
  1124.8 140.7 all-reduce.2
where the time goes:
time: 1290 us; the launch traced here: 1280 us
  waiting for transfers between devices  761 us (59%)
  matrix products  318 us (25%)
  other arithmetic  91.3 us (7%)
  local copies, waits for them, and re-layouts  90.2 us (7%)
  between operations  15.4 us (1%)
    psum x1, waiting for transfers between devices, local(): grad_down, grad_up = lax.psum((grad_down, grad_up), ('dp', 'seq'))  137 us
    dot_general x25, matrix products, product(): return jnp.dot(left, right, preferred_element_type=jnp.float32)  125 us
    reduce_scatter x1, waiting for transfers between devices, local(): lax.psum_scatter(gv_cross.astype(jnp.bfloat16), 'seq', scatter_dimension=...  75.7 us
    all_gather x1, waiting for transfers between devices, local(): lax.all_gather(own_keys, 'seq', axis=1, tiled=True)  74.2 us
    all_gather x1, waiting for transfers between devices, local(): lax.all_gather(own_src_keys, 'seq', axis=1, tiled=True)  73.3 us
    reduce_scatter x1, waiting for transfers between devices, local(): lax.psum_scatter(gk_self.astype(jnp.bfloat16), 'seq', scatter_dimension=1...  62.7 us
    convert_element_type x2, other arithmetic, attend_backward(): grad_scores = (probs * (grad_probs - row_dot)).astype(jnp.bfloat16)  56.6 us
    dot_general x2, matrix products, attend_backward(): jnp.einsum('rqhd,rkhd->rhqk', grad_heads, split_heads(values), preferred_...  51.2 us
  transfers between devices with their start and end apart: 19, of which 17 were waited for; matrix products, arithmetic and copies ran while one was open for 29% of the time, Pallas kernels for 0%

commit v1 on v0

v1 whole, which is shorter than its diff:
```python
import functools
import jax
import jax.numpy as jnp
from jax.sharding import PartitionSpec as P
from jax import lax
from jax.experimental import pallas as pl
from jax.experimental.pallas import tpu as pltpu
BF=jnp.bfloat16; F32=jnp.float32
NEG=-1e30
LOG2E=1.4426950408889634
VM=56*1024*1024

SELF_PLANS=(((((0,True),)), ((0,False),(2,False),(3,False),(1,True))),
            (((2,False),(0,True)), ((2,False),(0,False),(1,True))))
CROSS_PLANS=((((0,False),(1,False),(2,False),(3,False)),)*2,)

def nt(a,b): return lax.dot_general(a,b,(((1,),(1,)),((),())),preferred_element_type=F32)
def nn(a,b): return lax.dot_general(a,b,(((1,),(0,)),((),())),preferred_element_type=F32)

def half_mask(shape, h):
    l=lax.broadcasted_iota(jnp.int32, shape, 1)
    return (l<64) if h==0 else (l>=64)

def fwd_body(plan, C, q, ks, vs, qa, kas, o_ref, p_ref):
    n=0
    kaug=[[jnp.where(half_mask(k.shape,h),k,a) for k,a in zip(ks,kas)] for h in range(2)]
    vts=[v.T for v in vs]
    for slot,blocks in enumerate(plan):
        halves=[]
        for h in range(2):
            qs=q[slot*C:(slot+1)*C]; qas=qa[slot*C:(slot+1)*C]
            qh=jnp.where(half_mask(qs.shape,h),qs,qas)
            ss=[]
            for (kb,diag) in blocks:
                s=nt(kaug[h][kb],qh)
                if diag:
                    ki=lax.broadcasted_iota(jnp.int32,s.shape,0); qi=lax.broadcasted_iota(jnp.int32,s.shape,1)
                    s=jnp.where(ki<=qi,s,NEG)
                ss.append(s)
            m=functools.reduce(jnp.maximum,[jnp.max(s,axis=0,keepdims=True) for s in ss])
            ps=[jnp.exp2(s-m) for s in ss]
            l=functools.reduce(jnp.add,[jnp.sum(p,axis=0,keepdims=True) for p in ps])
            inv=1.0/l
            acc=None
            for i,((kb,_),p) in enumerate(zip(blocks,ps)):
                pb=(p*inv).astype(BF)
                p_ref[0,h,n+i]=pb
                t=nn(vts[kb][64*h:64*h+64],pb)
                acc=t if acc is None else acc+t
            halves.append(acc)
        n+=len(blocks)
        ot=jnp.concatenate(halves,axis=0)
        o_ref[slot*C:(slot+1)*C]=ot.T.astype(BF)

def fwd_kernel(plans, C, info, q_ref, ko, kp, vo, vp, qa, kao, kap, o_ref, p_ref):
    def run(plan):
        ks=[ko[0:C],ko[C:2*C],kp[0:C],kp[C:2*C]]
        vs=[vo[0:C],vo[C:2*C],vp[0:C],vp[C:2*C]]
        kas=[kao[0:C],kao[C:2*C],kap[0:C],kap[C:2*C]]
        fwd_body(plan,C,q_ref[...],ks,vs,qa[...],kas,o_ref,p_ref)
    if len(plans)==1: run(plans[0])
    else:
        for v,plan in enumerate(plans):
            pl.when(info[0]==v)(functools.partial(run,plan))

def attend(plans, info, q, ko, kp, vo, vp, qa, kao, kap):
    T,D=q.shape; C=T//2; pairs=D//128
    nb=sum(len(b) for b in plans[0])
    col=pl.BlockSpec((T,128),lambda h,*_:(0,h))
    fix=pl.BlockSpec((T,128),lambda h,*_:(0,0))
    return pl.pallas_call(
        functools.partial(fwd_kernel,plans,C),
        grid_spec=pltpu.PrefetchScalarGridSpec(num_scalar_prefetch=1,grid=(pairs,),
            in_specs=[col]*5+[fix]*3,
            out_specs=[col,pl.BlockSpec((1,2,nb,C,C),lambda h,*_:(h,0,0,0,0))]),
        out_shape=[jax.ShapeDtypeStruct((T,D),BF),jax.ShapeDtypeStruct((pairs,2,nb,C,C),BF)],
        compiler_params=pltpu.CompilerParams(vmem_limit_bytes=VM),
        cost_estimate=pl.CostEstimate(flops=2*2*nb*C*C*64*2*pairs*4,bytes_accessed=pairs*2*nb*C*C*2,transcendentals=0),
        name="attend")(info,q,ko,kp,vo,vp,qa,kao,kap)

def bwd_body(plan, C, q, ks, vs, do, o, p_ref, gq_ref, gko, gvo, gkp, gvp):
    lane=lax.broadcasted_iota(jnp.int32,(C,128),1)
    l64=lax.rem(lane,64)
    ones=jnp.where(l64<2,1.0,0.0).astype(BF)
    vaug=[[jnp.where(half_mask(v.shape,h),v,ones) for v in vs] for h in range(2)]
    kts=[k.T for k in ks]
    gk=[None]*4; gv=[None]*4
    n=0
    zero=jnp.zeros((C,128),BF)
    for slot,blocks in enumerate(plan):
        halves=[]
        for h in range(2):
            hm=lane<64 if h==0 else lane>=64
            dos=do[slot*C:(slot+1)*C]; os=o[slot*C:(slot+1)*C]; qs=q[slot*C:(slot+1)*C]
            prod=jnp.where(hm,dos.astype(F32)*os.astype(F32),0.0)
            d=-jnp.sum(prod,axis=1,keepdims=True)
            hi=d.astype(BF); lo=(d-hi.astype(F32)).astype(BF)
            doa=jnp.where(hm,dos,jnp.where(l64==0,jnp.broadcast_to(hi,(C,128)),jnp.where(l64==1,jnp.broadcast_to(lo,(C,128)),zero)))
            dom=jnp.where(hm,dos,zero)
            qm=jnp.where(hm,qs,zero)
            acc=None
            for i,(kb,_) in enumerate(blocks):
                pb=p_ref[0,h,n+i]
                dp=nt(vaug[h][kb],doa)
                ds=(pb.astype(F32)*dp).astype(BF)
                a=nn(pb,dom); gv[kb]=a if gv[kb] is None else gv[kb]+a
                b=nn(ds,qm); gk[kb]=b if gk[kb] is None else gk[kb]+b
                t=nn(kts[kb][64*h:64*h+64],ds)
                acc=t if acc is None else acc+t
            halves.append(acc)
        n+=len(blocks)
        gq_ref[slot*C:(slot+1)*C]=jnp.concatenate(halves,axis=0).T.astype(BF)
    for kb in range(4):
        rk,rv=(gko,gvo) if kb<2 else (gkp,gvp)
        sl=slice((kb%2)*C,(kb%2)*C+C)
        z=jnp.zeros((C,128),F32)
        rk[sl]=((gk[kb] if gk[kb] is not None else z)*(1.0/LOG2E)).astype(rk.dtype)
        rv[sl]=(gv[kb] if gv[kb] is not None else z).astype(rv.dtype)

def bwd_kernel(plans, C, info, q_ref, ko, kp, vo, vp, do, o, p_ref, gq, gko, gvo, gkp, gvp):
    def run(plan):
        ks=[ko[0:C],ko[C:2*C],kp[0:C],kp[C:2*C]]
        vs=[vo[0:C],vo[C:2*C],vp[0:C],vp[C:2*C]]
        bwd_body(plan,C,q_ref[...],ks,vs,do[...],o[...],p_ref,gq,gko,gvo,gkp,gvp)
    if len(plans)==1: run(plans[0])
    else:
        for v,plan in enumerate(plans):
            pl.when(info[0]==v)(functools.partial(run,plan))

def attend_back(plans, info, q, ko, kp, vo, vp, do, o, p):
    T,D=q.shape; C=T//2; pairs=D//128
    nb=p.shape[2]
    col=pl.BlockSpec((T,128),lambda h,*_:(0,h))
    return pl.pallas_call(
        functools.partial(bwd_kernel,plans,C),
        grid_spec=pltpu.PrefetchScalarGridSpec(num_scalar_prefetch=1,grid=(pairs,),
            in_specs=[col]*7+[pl.BlockSpec((1,2,nb,C,C),lambda h,*_:(h,0,0,0,0))],
            out_specs=[col]*5),
        out_shape=[jax.ShapeDtypeStruct((T,D),BF),jax.ShapeDtypeStruct((T,D),F32),jax.ShapeDtypeStruct((T,D),F32),
                   jax.ShapeDtypeStruct((T,D),BF),jax.ShapeDtypeStruct((T,D),BF)],
        compiler_params=pltpu.CompilerParams(vmem_limit_bytes=VM),
        cost_estimate=pl.CostEstimate(flops=2*4*nb*C*C*64*2*pairs*4,bytes_accessed=pairs*2*nb*C*C*2,transcendentals=0),
        name="attend_back")(info,q,ko,kp,vo,vp,do,o,p)


def product(left, right):
    return jnp.dot(left, right, preferred_element_type=F32)


def normalize(values):
    centered = values - jnp.mean(values, axis=-1, keepdims=True)
    spread = jnp.mean(centered * centered, axis=-1, keepdims=True)
    return centered * lax.rsqrt(spread + 1e-05)


def smooth(values):
    return jax.nn.gelu(values, approximate=False)


def normalize_back(values, grads):
    return jax.vjp(normalize, values)[1](grads)[0]


def smooth_back(values, grads):
    return jax.vjp(smooth, values)[1](grads)[0]


def move(value, target):
    dp, seq = lax.axis_size("dp"), lax.axis_size("seq")
    pairs = []
    for d in range(dp):
        for s in range(seq):
            a, b = target(d, s)
            pairs.append((d * seq + s, a * seq + b))
    return lax.ppermute(value, ("dp", "seq"), pairs)


def flip(value, bit):
    return move(value, lambda d, s: (d ^ bit, s))


def core_of(chunk):
    return (0, 1, 1, 0)[chunk]


def pick(flag, first, second):
    return jnp.where(flag, first, second)


def reshard_in(value, d, s):
    got = []
    for k in range(2):
        piece = lax.dynamic_index_in_dim(value, (s + k) % 2, 0, keepdims=False)
        got.append(
            move(piece, lambda a, q: (2 * (a // 2) + core_of(q), 2 * (a % 2) + (q + k) % 2))
        )
    even = (s + d) % 2 == 0
    return jnp.concatenate([pick(even, got[0], got[1]), pick(even, got[1], got[0])], axis=0)


def reshard_out(value, d, s):
    C = value.shape[0] // 2
    dp, seq = lax.axis_size("dp"), lax.axis_size("seq")
    got = []
    for k in range(2):
        slot = (s + k + d) % 2
        piece = lax.dynamic_slice_in_dim(value, slot * C, C, 0)
        back = {}
        for a in range(dp):
            for q in range(seq):
                back[(2 * (a // 2) + core_of(q), 2 * (a % 2) + (q + k) % 2)] = (a, q)
        got.append(move(piece, lambda a, b: back[(a, b)]))
    even = s % 2 == 0
    return jnp.stack([pick(even, got[0], got[1]), pick(even, got[1], got[0])])


def spread_pieces(shard, low, order):
    b1, b2 = order
    pieces = {0: shard}
    pieces[b1] = flip(shard, b1 * low)
    for m in (0, b1):
        pieces[m ^ b2] = flip(pieces[m], b2 * low)
    for m in (0, b1, b2, b1 ^ b2):
        pieces[m ^ 1] = flip(pieces[m], low)
    return [pieces[m] for m in range(8)]


def assemble_kernel(parts, n_in, info, *refs):
    ins, rest = refs[:n_in], refs[n_in:]
    outs, sem = rest[:-1], rest[-1]
    copies = []
    for which, src, rows, out, stride, base in parts:
        for m in range(8):
            owner = info[1] ^ m
            at = pl.multiple_of(owner * stride + base, 16)
            copies.append(
                pltpu.make_async_copy(
                    ins[which * 8 + m].at[pl.ds(src, rows)],
                    outs[out].at[pl.ds(at, rows)],
                    sem.at[len(copies)],
                )
            )
    for c in copies:
        c.start()
    for c in copies:
        c.wait()


def assemble(info, sets, parts, shapes):
    flat = [p for s in sets for p in s]
    return pl.pallas_call(
        functools.partial(assemble_kernel, parts, len(flat)),
        grid_spec=pltpu.PrefetchScalarGridSpec(
            num_scalar_prefetch=1,
            grid=(1,),
            in_specs=[pl.BlockSpec(memory_space=pl.ANY)] * len(flat),
            out_specs=[pl.BlockSpec(memory_space=pl.ANY)] * len(shapes),
            scratch_shapes=[pltpu.SemaphoreType.DMA((len(parts) * 8,))],
        ),
        out_shape=[jax.ShapeDtypeStruct(s, BF) for s in shapes],
        name="assemble",
    )(info, *flat)


def reduce_all(value, d, s, steps):
    def other(v, step):
        axis, bit = step
        if axis == "dp":
            return move(v, lambda a, b: (a ^ bit, b))
        return move(v, lambda a, b: (a, b ^ bit))

    def high(step):
        axis, bit = step
        return ((d if axis == "dp" else s) // bit) % 2 == 1

    for step in steps:
        half = value.shape[0] // 2
        up = high(step)
        lo, hi = value[:half], value[half:]
        sent = pick(up, lo, hi).astype(BF)
        kept = pick(up, hi, lo)
        value = kept.astype(F32) + other(sent, step).astype(F32)
    value = value.astype(BF)
    for step in reversed(steps):
        up = high(step)
        got = other(value, step)
        value = jnp.concatenate([pick(up, got, value), pick(up, value, got)], axis=0)
    return value.astype(F32)


def local(tokens, source, target_lengths, source_lengths, step_index, self_query, self_key, self_value,
          self_out, cross_query, cross_key, cross_value, cross_out, ffn_expand, ffn_contract, adapter_down,
          adapter_up, grad_output):
    rows, C, D = tokens.shape
    dp, seq = lax.axis_size("dp"), lax.axis_size("seq")
    assert rows == 2 and seq == 4 and dp % 8 == 0
    low = dp // 8
    d, s = lax.axis_index("dp"), lax.axis_index("seq")
    core = d % 2
    info = jnp.stack([core, d // low]).astype(jnp.int32)

    x = reshard_in(tokens, d, s)

    def widen(shard):
        if low == 1:
            return shard
        groups = [[g * low + i for i in range(low)] for g in range(8)]
        return lax.all_gather(shard, "dp", axis=0, tiled=True, axis_index_groups=groups)

    def two(a, b):
        return jnp.concatenate([a, b], axis=0)

    wide = [widen(w) for w in (self_query, self_key, self_value, self_out, cross_query, cross_key,
                               cross_value, cross_out, ffn_expand, ffn_contract)]
    sq, sk, sv, so, cq_, ck_, cv_, co_, ex, con = wide
    n = sq.shape[0]
    f = con.shape[0]
    XY, YX = (2, 4), (4, 2)
    a1 = spread_pieces(two(sq, sv), low, XY)
    b1 = spread_pieces(two(sk, ck_), low, YX)
    a2 = spread_pieces(two(so, cv_), low, XY)
    b2 = spread_pieces(two(cq_, co_), low, YX)
    a3 = spread_pieces(ex[: n // 2], low, XY)
    b3 = spread_pieces(ex[n // 2 :], low, YX)
    a4 = spread_pieces(con[: f // 2], low, XY)
    b4 = spread_pieces(con[f // 2 :], low, YX)
    four = ((0, 0, n, 0, n, 0), (0, n, n, 1, n, 0), (1, 0, n, 2, n, 0), (1, n, n, 3, n, 0))
    w_query, w_value, w_key, c_key = assemble(info, [a1, b1], four, [(D, D)] * 4)
    w_out, c_value, c_query, c_out = assemble(info, [a2, b2], four, [(D, D)] * 4)
    FF = ex.shape[1]
    (w_expand,) = assemble(info, [a3, b3], ((0, 0, n // 2, 0, n, 0), (1, 0, n // 2, 0, n, n // 2)), [(D, FF)])
    (w_contract,) = assemble(info, [a4, b4], ((0, 0, f // 2, 0, f, 0), (1, 0, f // 2, 0, f, f // 2)), [(FF, D)])
    src = reshard_in(source, d, s)
    g_out = reshard_in(grad_output, d, s)

    mine = jnp.concatenate([target_lengths, source_lengths[:, None]], axis=1)
    other = flip(mine, 1)
    table = jnp.concatenate([pick(core == 0, mine, other), pick(core == 0, other, mine)], axis=0)
    row = lax.dynamic_index_in_dim(table, s, 0, keepdims=False)
    lens, src_len = row[:-1], row[-1]
    docs = lens.shape[0]
    ends = jnp.cumsum(lens)[:-1]
    i = jnp.arange(2 * C, dtype=jnp.int32)
    slot = i // C

    def place(which):
        chunk = pick(which == 0, slot * 3, slot + 1)
        return chunk * C + i % C

    lanes = jnp.arange(128, dtype=jnp.int32) % 64

    def doc_hot(pos):
        doc = jnp.sum((pos[:, None] >= ends[None, :]).astype(jnp.int32), axis=-1)
        return doc[:, None] == lanes[None, :]

    own_pos, peer_pos = place(core), place(1 - core)
    k_aug = [doc_hot(own_pos).astype(BF), doc_hot(peer_pos).astype(BF)]
    q_aug = jnp.where(doc_hot(own_pos) | (lanes >= docs)[None, :], 0.0, NEG).astype(BF)
    ck_aug = [((pos[:, None] >= src_len) & (lanes == 0)[None, :]).astype(BF) for pos in (own_pos, peer_pos)]
    cq_aug = jnp.broadcast_to(jnp.where(lanes == 0, NEG, 0.0).astype(BF)[None, :], (2 * C, 128))

    scale = 0.125 * LOG2E
    branch_scale = (step_index[0] + 1).astype(F32) / 5.0
    q = (product(x, w_query) * scale).astype(BF)
    k = product(x, w_key).astype(BF)
    v = product(x, w_value).astype(BF)
    k_peer, v_peer = flip(k, 1), flip(v, 1)
    ck = product(src, c_key).astype(BF)
    cv = product(src, c_value).astype(BF)
    ck_peer, cv_peer = flip(ck, 1), flip(cv, 1)
    attended, p_self = attend(SELF_PLANS, info, q, k, k_peer, v, v_peer, q_aug, *k_aug)
    first_sum = x.astype(F32) + product(attended, w_out)
    first_norm = normalize(first_sum)
    cq = (product(first_norm.astype(BF), c_query) * scale).astype(BF)
    cross_attended, p_cross = attend(CROSS_PLANS, info, cq, ck, ck_peer, cv, cv_peer, cq_aug, *ck_aug)
    second_sum = first_norm + product(cross_attended, c_out)
    second_norm = normalize(second_sum)
    second_low = second_norm.astype(BF)
    hidden_pre = product(second_low, w_expand)
    hidden = smooth(hidden_pre).astype(BF)
    narrow = product(second_low, adapter_down)
    squeezed = smooth(narrow).astype(BF)
    third_sum = second_norm + product(hidden, w_contract) + branch_scale * product(squeezed, adapter_up)
    output = normalize(third_sum).astype(BF)
    output = reshard_out(output, d, s)
    grad_third = normalize_back(third_sum, g_out.astype(F32))
    grad_ffn = grad_third.astype(BF)
    grad_adapt = (branch_scale * grad_third).astype(BF)
    grad_up = product(squeezed.T, grad_adapt)
    grad_narrow = smooth_back(narrow, product(grad_adapt, adapter_up.T)).astype(BF)
    grad_down = product(second_low.T, grad_narrow)
    last = [("seq", 2), ("seq", 1)] + [("dp", 1 << j) for j in range(low.bit_length() - 1)]
    grad_up = reduce_all(grad_up, d, s, [("dp", low), ("dp", 2 * low), ("dp", 4 * low)] + last)
    grad_down = reduce_all(grad_down, d, s, [("dp", low), ("dp", 4 * low), ("dp", 2 * low)] + last)
    grad_hidden = smooth_back(hidden_pre, product(grad_ffn, w_contract.T)).astype(BF)
    grad_second = grad_third + product(grad_hidden, w_expand.T) + product(grad_narrow, adapter_down.T)
    grad_second_sum = normalize_back(second_sum, grad_second)
    grad_cross = product(grad_second_sum.astype(BF), c_out.T).astype(BF)
    gq, gk, gv, gk_peer, gv_peer = attend_back(
        CROSS_PLANS, info, cq, ck, ck_peer, cv, cv_peer, grad_cross, cross_attended, p_cross
    )
    gk = (gk + flip(gk_peer, 1).astype(F32)).astype(BF)
    gv = (gv + flip(gv_peer, 1).astype(F32)).astype(BF)
    grad_source = (product(gk, c_key.T) + product(gv, c_value.T)).astype(BF)
    grad_source = reshard_out(grad_source, d, s)
    grad_first = grad_second_sum + 0.125 * product(gq, c_query.T)
    grad_first_sum = normalize_back(first_sum, grad_first)
    grad_self = product(grad_first_sum.astype(BF), w_out.T).astype(BF)
    gq, gk, gv, gk_peer, gv_peer = attend_back(
        SELF_PLANS, info, q, k, k_peer, v, v_peer, grad_self, attended, p_self
    )
    gk = (gk + flip(gk_peer, 1).astype(F32)).astype(BF)
    gv = (gv + flip(gv_peer, 1).astype(F32)).astype(BF)
    grad_tokens = grad_first_sum + 0.125 * product(gq, w_query.T) + product(gk, w_key.T) + product(gv, w_value.T)
    grad_tokens = reshard_out(grad_tokens.astype(BF), d, s)
    return (output, grad_tokens, grad_source, grad_down, grad_up)


def solution(mesh):
    rows = P("dp", "seq", None)
    weight = P("dp", None)
    return jax.shard_map(
        local,
        mesh=mesh,
        in_specs=(rows, rows, weight, P("dp"), P()) + (weight,) * 10 + (P(), P(), rows),
        out_specs=(rows, rows, rows, P(), P()),
        check_vma=False,
    )
```

time: 1290 us -> 1580 us (1.22)
  Pallas kernels: 0 us -> 1120 us
  waiting for transfers between devices: 761 us -> 148 us
  matrix products: 318 us -> 119 us
  starting transfers between devices: 1.33 us -> 133 us
  local copies, waits for them, and re-layouts: 90.2 us -> 22.7 us
  other arithmetic: 91.3 us -> 27.3 us
    pallas_call x0 -> x8, Pallas kernels: none -> 1120 us  [the longest x4 1020 us: assemble(): pl.pallas_call(functools.partial(assemble_kernel, parts, len(flat)), grid...]
    all_gather x14 -> x0, waiting for transfers between devices: 479 us -> none  [the longest x1 74.2 us: local(): lax.all_gather(own_keys, 'seq', axis=1, tiled=True)]
    dot_general x37 -> x25, matrix products: 318 us -> 119 us  [product(): return jnp.dot(left, right, preferred_element_type=F32)]
    ppermute x0 -> x97, waiting for transfers between devices: none -> 148 us  [move(): return lax.ppermute(value, ('dp', 'seq'), pairs)]
    reduce_scatter x4 -> x0, waiting for transfers between devices: 138 us -> none  [the longest x1 75.7 us: local(): lax.psum_scatter(gv_cross.astype(jnp.bfloat16), 'seq', scatter_dimension=...]
    psum x1 -> x0, waiting for transfers between devices: 137 us -> none  [local(): grad_down, grad_up = lax.psum((grad_down, grad_up), ('dp', 'seq'))]
    ppermute x0 -> x97, starting transfers between devices: none -> 133 us  [move(): return lax.ppermute(value, ('dp', 'seq'), pairs)]
    convert_element_type x3 -> x19, other arithmetic: 56.9 us -> 7.33 us  [the longest x2 3.18 us: reduce_all(): return value.astype(F32)]
  transfers between devices with their start and end apart: 19 -> 97, of which waited for: 17 -> 33; matrix products, arithmetic and copies ran while one was open for 29% -> 7% of each run, Pallas kernels for 0% -> 70%
where the time goes in v1:
time: 1580 us; the launch traced here: 1570 us
  Pallas kernels  1120 us (71%)
  waiting for transfers between devices  148 us (9%)
  starting transfers between devices  133 us (8%)
  matrix products  119 us (8%)
  other arithmetic  27.3 us (2%)
  local copies, waits for them, and re-layouts  22.7 us (1%)
    pallas_call x4, Pallas kernels, assemble(): pl.pallas_call(functools.partial(assemble_kernel, parts, len(flat)), grid...  1020 us
    ppermute x97, waiting for transfers between devices, move(): return lax.ppermute(value, ('dp', 'seq'), pairs)  148 us
    ppermute x97, starting transfers between devices, move(): return lax.ppermute(value, ('dp', 'seq'), pairs)  133 us
    dot_general x25, matrix products, product(): return jnp.dot(left, right, preferred_element_type=F32)  119 us
    pallas_call x2, Pallas kernels, attend_back(): pl.pallas_call(functools.partial(bwd_kernel, plans, C), grid_spec=pltpu.P...  46.7 us
    pallas_call x2, Pallas kernels, attend(): pl.pallas_call(functools.partial(fwd_kernel, plans, C), grid_spec=pltpu.P...  44.8 us
  transfers between devices with their start and end apart: 97, of which 33 were waited for; matrix products, arithmetic and copies ran while one was open for 7% of the time, Pallas kernels for 70%

profile of v1, /device:TPU:1, one launch (start us, length us, event | category | flops | bytes accessed | tf_op | source)
XLA Modules:
  0.0 1569.1 jit_solution(14472739463762303357)
XLA Ops:
  10.9 5.7 collective-permute-done.29.refs_12_
  23.5 4.4 collective-permute-done.22.refs_4_
  35.7 3.4 collective-permute-done.12.refs_12_
  41.2 6.2 collective-permute-start
  50.4 5.5 collective-permute-start.33
  59.5 3.0 collective-permute-start.68
  62.5 7.8 collective-permute-done.1
  70.5 10.7 collective-permute-done.33
  82.4 4.4 collective-permute-done.34
  86.8 2.8 collective-permute-start.44
  89.6 20.8 %collective-permute-done.67 = bf16[256,1024]{1,0:T(8,128)(2,1)S(1)} collective-permute-done((bf16[256,1024]{1,0:T(8,128)(2,1)S(1)}, bf16[256,1024]{1,0:T(8,128)(2,1)S(1)}, u32[]{:S(2)}, u32[]{:S(2)}) %collective-permute-start.67) | collective-permute-done | bytes 524320 | tf_op jit(solution)/shard_map/ppermute | solution.py:175
  114.9 6.0 collective-permute-done.40.refs_4_
  125.5 6.7 collective-permute-done.61.refs_12_
  134.7 6.6 collective-permute-done.54.refs_4_
  146.2 6.7 collective-permute-done.31.refs_14_
  161.5 4.8 collective-permute-done.14.refs_14_
  170.3 2.9 collective-permute-done.7.refs_6_
  175.6 5.9 collective-permute-done.49.refs_14_
  191.4 256.2 %assemble.4 = (bf16[1024,1024]{1,0:T(8,128)(2,1)}, bf16[1024,1024]{1,0:T(8,128)(2,1)}, bf16[1024,1024]{1,0:T(8,128)(2,1)}, bf16[1024,1024]{1,0:T(8,128)(2,1)}) custom-call(s32[2]{0:T(128)} %pad_add_fusion.2.info, bf16[256,1024]{1,0:T(8,128)(2,1)} %copy-done.15, bf16[256,1024]{1,0:T(8,128)(2,1)} %copy-done.37, ...), custom_call_target="tpu_custom_call" | custom-call | tf_op jit(solution)/shard_map/assemble/pallas_call | solution.py:251
  448.2 4.3 convolution_convert_fusion.5.ko
  458.4 256.2 %assemble.5 = (bf16[1024,1024]{1,0:T(8,128)(2,1)}, bf16[1024,1024]{1,0:T(8,128)(2,1)}, bf16[1024,1024]{1,0:T(8,128)(2,1)}, bf16[1024,1024]{1,0:T(8,128)(2,1)}) custom-call(s32[2]{0:T(128)} %pad_add_fusion.2.info, bf16[256,1024]{1,0:T(8,128)(2,1)} %copy-done.17, bf16[256,1024]{1,0:T(8,128)(2,1)} %copy-done.26, bf16[256,1024]{1,0:T(8,128)(2,1)} %copy-done.25, ...), custom_call_target="tpu_custom_call" | custom-call | tf_op jit(solution)/shard_map/assemble/pallas_call | solution.py:251
  714.5 256.0 %assemble.6 = bf16[1024,4096]{1,0:T(8,128)(2,1)} custom-call(s32[2]{0:T(128)} %pad_add_fusion.2.info, bf16[64,4096]{1,0:T(8,128)(2,1)} %copy-done.12, bf16[64,4096]{1,0:T(8,128)(2,1)} %copy-done.39, bf16[64,4096]{1,0:T(8,128)(2,1)} %copy-done.38, bf16[64,4096]{1,0:T(8,128)(2,1)} %collective-permute-done.39.refs_3_, bf16[64,4096]{1,0:T(8,128)(2,1)} %copy-done.36, ...), custom_call_target="tpu_custom_call" | custom-call | tf_op jit(solution)/shard_map/assemble/pallas_call | solution.py:251
  971.5 4.3 convolution_convert_fusion.2.vo
  978.9 256.0 %assemble.7 = bf16[4096,1024]{1,0:T(8,128)(2,1)} custom-call(s32[2]{0:T(128)} %pad_add_fusion.2.info, bf16[256,1024]{1,0:T(8,128)(2,1)} %copy-done.14, bf16[256,1024]{1,0:T(8,128)(2,1)} %copy-done.46, bf16[256,1024]{1,0:T(8,128)(2,1)} %copy-done.33, bf16[256,1024]{1,0:T(8,128)(2,1)} %copy-done.55, bf16[256,1024]{1,0:T(8,128)(2,1)} %collective-permute-done.54.refs_4_, ...), custom_call_target="tpu_custom_call" | custom-call | tf_op jit(solution)/shard_map/assemble/pallas_call | solution.py:251
  1234.9 3.8 multiply_convert_fusion.5.q_ref
  1238.8 19.7 %attend.2 = (bf16[512,1024]{1,0:T(8,128)(2,1)}, bf16[8,2,5,256,256]{4,3,2,1,0:T(8,128)(2,1)}) custom-call(s32[2]{0:T(128)} %pad_add_fusion.2.info, bf16[512,1024]{1,0:T(8,128)(2,1)} %multiply_convert_fusion.5.q_ref, bf16[512,1024]{1,0:T(8,128)(2,1)} %convolution_convert_fusion.5.ko, bf16[512,1024]{1,0:T(8,128)(2,1)} %collective-permute-done.16.kp, ...), custom_call_target="tpu_custom_call" | custom-call | flops 5368709120 | bytes 10485760 | tf_op jit(solution)/shard_map/attend/pallas_call | solution.py:71
  1266.5 25.1 %attend.3 = (bf16[512,1024]{1,0:T(8,128)(2,1)}, bf16[8,2,8,256,256]{4,3,2,1,0:T(8,128)(2,1)}) custom-call(s32[2]{0:T(128)} %pad_add_fusion.2.info, bf16[512,1024]{1,0:T(8,128)(2,1)} %multiply_convert_fusion.4.q_ref, bf16[512,1024]{1,0:T(8,128)(2,1)} %convolution_convert_fusion.3.ko, bf16[512,1024]{1,0:T(8,128)(2,1)} %collective-permute-done.35.kp, ...), custom_call_target="tpu_custom_call" | custom-call | flops 8589934592 | bytes 16777216 | tf_op jit(solution)/shard_map/attend/pallas_call | solution.py:71
  1291.6 2.6 fusion.54
  1295.5 5.5 multiply_convert_fusion.11
  1301.0 7.1 fusion.56
  1308.8 24.2 %fusion.55 = (f32[512]{0:T(512)S(1)}, f32[512,1024]{1,0:T(8,128)S(1)}) fusion(f32[512,1024]{1,0:T(8,128)S(1)} %fusion.57, f32[]{:T(128)} %bitcast.10, bf16[4096,1024]{1,0:T(8,128)(2,1)S(1)} %bitcast.75, f32[512,4096]{1,0:T(8,128)} %fusion.56, f32[512]{0:T(512)S(1)} %fusion.35, f32[512,1024]{1,0:T(8,128)S(1)} %get-tuple-element.121, ...), kind=kOutput, calls=%fused_computation.238 | convolution fusion | flops 4434427392 | bytes 23074820 | tf_op jit(solution)/shard_map/dot_general | solution.py:147
  1341.9 12.0 collective-permute-start.65
  1354.8 37.7 %multiply_reduce_fusion.1 = (f32[512]{0:T(512)S(1)}, f32[512,1024]{1,0:T(8,128)}) fusion(f32[512,1024]{1,0:T(8,128)S(1)} %get-tuple-element.121, f32[512]{0:T(512)S(1)} %broadcast_multiply_fusion.1, f32[512,1024]{1,0:T(8,128)} %fusion.58, bf16[1024,4096]{1,0:T(8,128)(2,1)} %assemble.6, f32[512,4096]{1,0:T(8,128)} %fusion.56, f32[512,1024]{1,0:T(8,128)} %copy-done.8, ...), kind=kOutput, calls=%fused_computation.34 | convolution fusion | flops 8745123840 | bytes 33560576 | tf_op jit(solution)/shard_map/dot_general | solution.py:147
  1397.3 27.1 %attend_back.2 = (bf16[512,1024]{1,0:T(8,128)(2,1)}, f32[512,1024]{1,0:T(8,128)}, f32[512,1024]{1,0:T(8,128)}, bf16[512,1024]{1,0:T(8,128)(2,1)}, bf16[512,1024]{1,0:T(8,128)(2,1)}) custom-call(s32[2]{0:T(128)} %pad_add_fusion.2.info, bf16[512,1024]{1,0:T(8,128)(2,1)} %multiply_convert_fusion.4.q_ref, bf16[512,1024]{1,0:T(8,128)(2,1)} %convolution_convert_fusion.3.ko, ...), custom_call_target="tpu_custom_call" | custom-call | flops 17179869184 | bytes 16777216 | tf_op jit(solution)/shard_map/attend_back/pallas_call | solution.py:134
  1424.4 2.8 multiply_reduce_fusion
  1431.2 19.6 %attend_back.3 = (bf16[512,1024]{1,0:T(8,128)(2,1)}, f32[512,1024]{1,0:T(8,128)}, f32[512,1024]{1,0:T(8,128)}, bf16[512,1024]{1,0:T(8,128)(2,1)}, bf16[512,1024]{1,0:T(8,128)(2,1)}) custom-call(s32[2]{0:T(128)} %pad_add_fusion.2.info, bf16[512,1024]{1,0:T(8,128)(2,1)} %multiply_convert_fusion.5.q_ref, bf16[512,1024]{1,0:T(8,128)(2,1)} %convolution_convert_fusion.5.ko, ...), custom_call_target="tpu_custom_call" | custom-call | flops 10737418240 | bytes 10485760 | tf_op jit(solution)/shard_map/attend_back/pallas_call | solution.py:134
  1459.4 4.3 collective-permute-done.78
  1465.1 5.2 collective-permute-done.88
  1475.0 3.0 collective-permute-done.89
  1477.9 3.5 collective-permute-start.80
  1499.6 2.9 collective-permute-start.83
  1508.4 15.3 collective-permute-start.71
  1534.9 4.0 collective-permute-done.84
  1539.7 3.5 collective-permute-done.94
  1544.0 5.4 collective-permute-done.85
  1550.7 4.2 collective-permute-done.95
  1554.9 3.4 collective-permute-start.86
  1559.7 4.4 collective-permute-done.75
  (471 shorter events, 172.7 us)
Async XLA Ops:
  9.3 18.6 %collective-permute-start.22 = (bf16[256,1024]{1,0:T(8,128)(2,1)S(1)}, bf16[256,1024]{1,0:T(8,128)(2,1)}, u32[]{:S(2)}, u32[]{:S(2)}) collective-permute-start(bf16[256,1024]{1,0:T(8,128)(2,1)S(1)} %constant_dynamic-update-slice_fusion.4.refs_0_), channel_id=1, source_target_pairs={{0,16},{1,17},{2,18},{3,19},{4,20},{5,21},{6,22},{7,23},{8,24},{9,... | collective-permute-start | bytes 1572872 | tf_op jit(solution)/shard_map/ppermute | solution.py:175
  10.9 20.0 %collective-permute-start.20 = (bf16[256,1024]{1,0:T(8,128)(2,1)S(1)}, bf16[256,1024]{1,0:T(8,128)(2,1)S(1)}, u32[]{:S(2)}, u32[]{:S(2)}) collective-permute-start(bf16[256,1024]{1,0:T(8,128)(2,1)S(1)} %constant_dynamic-update-slice_fusion.4.refs_0_), channel_id=1, source_target_pairs={{0,8},{1,9},{2,10},{3,11},{4,12},{5,13},{6,14},{7,15},{8,0},{9,1},... | collective-permute-start | bytes 1572872 | tf_op jit(solution)/shard_map/ppermute | solution.py:175
  20.4 18.7 %collective-permute-start.12 = (bf16[256,1024]{1,0:T(8,128)(2,1)S(1)}, bf16[256,1024]{1,0:T(8,128)(2,1)}, u32[]{:S(2)}, u32[]{:S(2)}) collective-permute-start(bf16[256,1024]{1,0:T(8,128)(2,1)S(1)} %constant_dynamic-update-slice_fusion.2.refs_8_), channel_id=1, source_target_pairs={{0,16},{1,17},{2,18},{3,19},{4,20},{5,21},{6,22},{7,23},{8,24},{9,... | collective-permute-start | bytes 1572872 | tf_op jit(solution)/shard_map/ppermute | solution.py:175
  22.3 18.9 %collective-permute-start.10 = (bf16[256,1024]{1,0:T(8,128)(2,1)S(1)}, bf16[256,1024]{1,0:T(8,128)(2,1)}, u32[]{:S(2)}, u32[]{:S(2)}) collective-permute-start(bf16[256,1024]{1,0:T(8,128)(2,1)S(1)} %constant_dynamic-update-slice_fusion.2.refs_8_), channel_id=1, source_target_pairs={{0,8},{1,9},{2,10},{3,11},{4,12},{5,13},{6,14},{7,15},{8,0},{9,1},... | collective-permute-start | bytes 1572872 | tf_op jit(solution)/shard_map/ppermute | solution.py:175
  27.9 19.5 %collective-permute-start.9 = (bf16[256,1024]{1,0:T(8,128)(2,1)S(1)}, bf16[256,1024]{1,0:T(8,128)(2,1)}, u32[]{:S(2)}, u32[]{:S(2)}) collective-permute-start(bf16[256,1024]{1,0:T(8,128)(2,1)S(1)} %constant_dynamic-update-slice_fusion.2.refs_8_), channel_id=1, source_target_pairs={{0,4},{1,5},{2,6},{3,7},{4,0},{5,1},{6,2},{7,3},{8,12},{9,13},{10,... | collective-permute-start | bytes 1572872 | tf_op jit(solution)/shard_map/ppermute | solution.py:175
  30.9 19.4 %collective-permute-start.5 = (bf16[256,1024]{1,0:T(8,128)(2,1)S(1)}, bf16[256,1024]{1,0:T(8,128)(2,1)}, u32[]{:S(2)}, u32[]{:S(2)}) collective-permute-start(bf16[256,1024]{1,0:T(8,128)(2,1)S(1)} %constant_dynamic-update-slice_fusion.refs_0_), channel_id=1, source_target_pairs={{0,16},{1,17},{2,18},{3,19},{4,20},{5,21},{6,22},{7,23},{8,24},{9,... | collective-permute-start | bytes 1572872 | tf_op jit(solution)/shard_map/ppermute | solution.py:175
  32.8 23.1 %collective-permute-start.3 = (bf16[256,1024]{1,0:T(8,128)(2,1)S(1)}, bf16[256,1024]{1,0:T(8,128)(2,1)}, u32[]{:S(2)}, u32[]{:S(2)}) collective-permute-start(bf16[256,1024]{1,0:T(8,128)(2,1)S(1)} %constant_dynamic-update-slice_fusion.refs_0_), channel_id=1, source_target_pairs={{0,8},{1,9},{2,10},{3,11},{4,12},{5,13},{6,14},{7,15},{8,0},{9,1},... | collective-permute-start | bytes 1572872 | tf_op jit(solution)/shard_map/ppermute | solution.py:175
  39.1 18.4 %collective-permute-start.2 = (bf16[256,1024]{1,0:T(8,128)(2,1)S(1)}, bf16[256,1024]{1,0:T(8,128)(2,1)S(1)}, u32[]{:S(2)}, u32[]{:S(2)}) collective-permute-start(bf16[256,1024]{1,0:T(8,128)(2,1)S(1)} %constant_dynamic-update-slice_fusion.refs_0_), channel_id=1, source_target_pairs={{0,4},{1,5},{2,6},{3,7},{4,0},{5,1},{6,2},{7,3},{8,12},{9,13},{10,... | collective-permute-start | bytes 1572872 | tf_op jit(solution)/shard_map/ppermute | solution.py:175
  41.2 18.3 %collective-permute-start = (bf16[256,1024]{1,0:T(8,128)(2,1)S(1)}, bf16[256,1024]{1,0:T(8,128)(2,1)S(1)}, u32[]{:S(2)}, u32[]{:S(2)}) collective-permute-start(bf16[256,1024]{1,0:T(8,128)(2,1)S(1)} %get-tuple-element.92), channel_id=1, source_target_pairs={{0,0},{1,5},{2,4},{3,1},{4,2},{5,7},{6,6},{7,3},{8,8},{9,13},{10,1... | collective-permute-start | bytes 1572872 | tf_op jit(solution)/shard_map/ppermute | solution.py:175
  47.4 22.9 %collective-permute-start.1 = (bf16[256,1024]{1,0:T(8,128)(2,1)S(1)}, bf16[256,1024]{1,0:T(8,128)(2,1)S(1)}, u32[]{:S(2)}, u32[]{:S(2)}) collective-permute-start(bf16[256,1024]{1,0:T(8,128)(2,1)S(1)} %get-tuple-element.93), channel_id=1, source_target_pairs={{0,1},{1,4},{2,5},{3,0},{4,3},{5,6},{6,7},{7,2},{8,9},{9,12},{10,1... | collective-permute-start | bytes 1572872 | tf_op jit(solution)/shard_map/ppermute | solution.py:175
  50.4 30.9 %collective-permute-start.33 = (bf16[256,1024]{1,0:T(8,128)(2,1)S(1)}, bf16[256,1024]{1,0:T(8,128)(2,1)S(1)}, u32[]{:S(2)}, u32[]{:S(2)}) collective-permute-start(bf16[256,1024]{1,0:T(8,128)(2,1)S(1)} %get-tuple-element.88), channel_id=1, source_target_pairs={{0,0},{1,5},{2,4},{3,1},{4,2},{5,7},{6,6},{7,3},{8,8},{9,13},{10,1... | collective-permute-start | bytes 1572872 | tf_op jit(solution)/shard_map/ppermute | solution.py:175
  55.9 30.9 %collective-permute-start.34 = (bf16[256,1024]{1,0:T(8,128)(2,1)S(1)}, bf16[256,1024]{1,0:T(8,128)(2,1)S(1)}, u32[]{:S(2)}, u32[]{:S(2)}) collective-permute-start(bf16[256,1024]{1,0:T(8,128)(2,1)S(1)} %get-tuple-element.89), channel_id=1, source_target_pairs={{0,1},{1,4},{2,5},{3,0},{4,3},{5,6},{6,7},{7,2},{8,9},{9,12},{10,1... | collective-permute-start | bytes 1572872 | tf_op jit(solution)/shard_map/ppermute | solution.py:175
  57.6 52.9 %collective-permute-start.67 = (bf16[256,1024]{1,0:T(8,128)(2,1)S(1)}, bf16[256,1024]{1,0:T(8,128)(2,1)S(1)}, u32[]{:S(2)}, u32[]{:S(2)}) collective-permute-start(bf16[256,1024]{1,0:T(8,128)(2,1)S(1)} %get-tuple-element.80), channel_id=1, source_target_pairs={{0,0},{1,5},{2,4},{3,1},{4,2},{5,7},{6,6},{7,3},{8,8},{9,13},{10,1... | collective-permute-start | bytes 1572872 | tf_op jit(solution)/shard_map/ppermute | solution.py:175
  59.5 51.2 %collective-permute-start.68 = (bf16[256,1024]{1,0:T(8,128)(2,1)S(1)}, bf16[256,1024]{1,0:T(8,128)(2,1)S(1)}, u32[]{:S(2)}, u32[]{:S(2)}) collective-permute-start(bf16[256,1024]{1,0:T(8,128)(2,1)S(1)} %get-tuple-element.81), channel_id=1, source_target_pairs={{0,1},{1,4},{2,5},{3,0},{4,3},{5,6},{6,7},{7,2},{8,9},{9,12},{10,1... | collective-permute-start | bytes 1572872 | tf_op jit(solution)/shard_map/ppermute | solution.py:175
  70.3 41.6 %collective-permute-start.47 = (bf16[64,4096]{1,0:T(8,128)(2,1)S(1)}, bf16[64,4096]{1,0:T(8,128)(2,1)S(1)}, u32[]{:S(2)}, u32[]{:S(2)}) collective-permute-start(bf16[64,4096]{1,0:T(8,128)(2,1)S(1)} %get-tuple-element.82.refs_8_), channel_id=1, source_target_pairs={{0,16},{1,17},{2,18},{3,19},{4,20},{5,21},{6,22},{7,23},{8,24},{9,... | collective-permute-start | bytes 1572872 | tf_op jit(solution)/shard_map/ppermute | solution.py:175
  81.2 31.7 %collective-permute-start.45 = (bf16[64,4096]{1,0:T(8,128)(2,1)S(1)}, bf16[64,4096]{1,0:T(8,128)(2,1)S(1)}, u32[]{:S(2)}, u32[]{:S(2)}) collective-permute-start(bf16[64,4096]{1,0:T(8,128)(2,1)S(1)} %get-tuple-element.82.refs_8_), channel_id=1, source_target_pairs={{0,8},{1,9},{2,10},{3,11},{4,12},{5,13},{6,14},{7,15},{8,0},{9,1},... | collective-permute-start | bytes 1572872 | tf_op jit(solution)/shard_map/ppermute | solution.py:175
  86.8 27.4 %collective-permute-start.44 = (bf16[64,4096]{1,0:T(8,128)(2,1)S(1)}, bf16[64,4096]{1,0:T(8,128)(2,1)S(1)}, u32[]{:S(2)}, u32[]{:S(2)}) collective-permute-start(bf16[64,4096]{1,0:T(8,128)(2,1)S(1)} %get-tuple-element.82.refs_8_), channel_id=1, source_target_pairs={{0,4},{1,5},{2,6},{3,7},{4,0},{5,1},{6,2},{7,3},{8,12},{9,13},{10,... | collective-permute-start | bytes 1572872 | tf_op jit(solution)/shard_map/ppermute | solution.py:175
  112.9 19.2 %collective-permute-start.61 = (bf16[256,1024]{1,0:T(8,128)(2,1)S(1)}, bf16[256,1024]{1,0:T(8,128)(2,1)}, u32[]{:S(2)}, u32[]{:S(2)}) collective-permute-start(bf16[256,1024]{1,0:T(8,128)(2,1)S(1)} %get-tuple-element.84.refs_8_), channel_id=1, source_target_pairs={{0,16},{1,17},{2,18},{3,19},{4,20},{5,21},{6,22},{7,23},{8,24},{9,... | collective-permute-start | bytes 1572872 | tf_op jit(solution)/shard_map/ppermute | solution.py:175
  120.9 20.4 %collective-permute-start.54 = (bf16[256,1024]{1,0:T(8,128)(2,1)S(1)}, bf16[256,1024]{1,0:T(8,128)(2,1)}, u32[]{:S(2)}, u32[]{:S(2)}) collective-permute-start(bf16[256,1024]{1,0:T(8,128)(2,1)S(1)} %get-tuple-element.85.refs_0_), channel_id=1, source_target_pairs={{0,16},{1,17},{2,18},{3,19},{4,20},{5,21},{6,22},{7,23},{8,24},{9,... | collective-permute-start | bytes 1572872 | tf_op jit(solution)/shard_map/ppermute | solution.py:175
  123.1 19.3 %collective-permute-start.52 = (bf16[256,1024]{1,0:T(8,128)(2,1)S(1)}, bf16[256,1024]{1,0:T(8,128)(2,1)S(1)}, u32[]{:S(2)}, u32[]{:S(2)}) collective-permute-start(bf16[256,1024]{1,0:T(8,128)(2,1)S(1)} %get-tuple-element.85.refs_0_), channel_id=1, source_target_pairs={{0,8},{1,9},{2,10},{3,11},{4,12},{5,13},{6,14},{7,15},{8,0},{9,1},... | collective-permute-start | bytes 1572872 | tf_op jit(solution)/shard_map/ppermute | solution.py:175
  132.2 20.7 %collective-permute-start.31 = (bf16[256,1024]{1,0:T(8,128)(2,1)}, bf16[256,1024]{1,0:T(8,128)(2,1)}, u32[]{:S(2)}, u32[]{:S(2)}) collective-permute-start(bf16[256,1024]{1,0:T(8,128)(2,1)} %copy-done.24), channel_id=1, source_target_pairs={{0,8},{1,9},{2,10},{3,11},{4,12},{5,13},{6,14},{7,15},{8,0},{9,1},... | collective-permute-start | bytes 1572872 | tf_op jit(solution)/shard_map/ppermute | solution.py:175
  133.9 19.0 %collective-permute-start.30 = (bf16[256,1024]{1,0:T(8,128)(2,1)}, bf16[256,1024]{1,0:T(8,128)(2,1)}, u32[]{:S(2)}, u32[]{:S(2)}) collective-permute-start(bf16[256,1024]{1,0:T(8,128)(2,1)} %copy-done.24), channel_id=1, source_target_pairs={{0,4},{1,5},{2,6},{3,7},{4,0},{5,1},{6,2},{7,3},{8,12},{9,13},{10,... | collective-permute-start | bytes 1572872 | tf_op jit(solution)/shard_map/ppermute | solution.py:175
  184.1 263.5 %collective-permute-start.39 = (bf16[64,4096]{1,0:T(8,128)(2,1)}, bf16[64,4096]{1,0:T(8,128)(2,1)}, u32[]{:S(2)}, u32[]{:S(2)}) collective-permute-start(bf16[64,4096]{1,0:T(8,128)(2,1)} %copy-done.38), channel_id=1, source_target_pairs={{0,4},{1,5},{2,6},{3,7},{4,0},{5,1},{6,2},{7,3},{8,12},{9,13},{10,... | collective-permute-start | bytes 1572872 | tf_op jit(solution)/shard_map/ppermute | solution.py:175
  184.5 263.2 %collective-permute-start.63 = (bf16[256,1024]{1,0:T(8,128)(2,1)}, bf16[256,1024]{1,0:T(8,128)(2,1)}, u32[]{:S(2)}, u32[]{:S(2)}) collective-permute-start(bf16[256,1024]{1,0:T(8,128)(2,1)} %collective-permute-done.61.refs_12_), channel_id=1, source_target_pairs={{0,8},{1,9},{2,10},{3,11},{4,12},{5,13},{6,14},{7,15},{8,0},{9,1},... | collective-permute-start | bytes 1572872 | tf_op jit(solution)/shard_map/ppermute | solution.py:175
  188.0 264.5 %collective-permute-start.62 = (bf16[256,1024]{1,0:T(8,128)(2,1)}, bf16[256,1024]{1,0:T(8,128)(2,1)}, u32[]{:S(2)}, u32[]{:S(2)}) collective-permute-start(bf16[256,1024]{1,0:T(8,128)(2,1)} %collective-permute-done.61.refs_12_), channel_id=1, source_target_pairs={{0,4},{1,5},{2,6},{3,7},{4,0},{5,1},{6,2},{7,3},{8,12},{9,13},{10,... | collective-permute-start | bytes 1572872 | tf_op jit(solution)/shard_map/ppermute | solution.py:175
  188.8 263.8 %collective-permute-start.32 = (bf16[256,1024]{1,0:T(8,128)(2,1)}, bf16[256,1024]{1,0:T(8,128)(2,1)}, u32[]{:S(2)}, u32[]{:S(2)}) collective-permute-start(bf16[256,1024]{1,0:T(8,128)(2,1)} %collective-permute-done.31.refs_14_), channel_id=1, source_target_pairs={{0,4},{1,5},{2,6},{3,7},{4,0},{5,1},{6,2},{7,3},{8,12},{9,13},{10,... | collective-permute-start | bytes 1572872 | tf_op jit(solution)/shard_map/ppermute | solution.py:175
  189.6 263.4 %collective-permute-start.25 = (bf16[256,1024]{1,0:T(8,128)(2,1)}, bf16[256,1024]{1,0:T(8,128)(2,1)}, u32[]{:S(2)}, u32[]{:S(2)}) collective-permute-start(bf16[256,1024]{1,0:T(8,128)(2,1)} %collective-permute-done.24.refs_6_), channel_id=1, source_target_pairs={{0,4},{1,5},{2,6},{3,7},{4,0},{5,1},{6,2},{7,3},{8,12},{9,13},{10,... | collective-permute-start | bytes 1572872 | tf_op jit(solution)/shard_map/ppermute | solution.py:175
  452.5 518.1 %collective-permute-start.60 = (bf16[256,1024]{1,0:T(8,128)(2,1)S(1)}, bf16[256,1024]{1,0:T(8,128)(2,1)}, u32[]{:S(2)}, u32[]{:S(2)}) collective-permute-start(bf16[256,1024]{1,0:T(8,128)(2,1)S(1)} %collective-permute-done.59.refs_10_), channel_id=1, source_target_pairs={{0,4},{1,5},{2,6},{3,7},{4,0},{5,1},{6,2},{7,3},{8,12},{9,13},{10,... | collective-permute-start | bytes 1572872 | tf_op jit(solution)/shard_map/ppermute | solution.py:175
  452.6 518.4 %collective-permute-start.55 = (bf16[256,1024]{1,0:T(8,128)(2,1)}, bf16[256,1024]{1,0:T(8,128)(2,1)}, u32[]{:S(2)}, u32[]{:S(2)}) collective-permute-start(bf16[256,1024]{1,0:T(8,128)(2,1)} %collective-permute-done.54.refs_4_), channel_id=1, source_target_pairs={{0,4},{1,5},{2,6},{3,7},{4,0},{5,1},{6,2},{7,3},{8,12},{9,13},{10,... | collective-permute-start | bytes 1572872 | tf_op jit(solution)/shard_map/ppermute | solution.py:175
  453.0 518.2 %collective-permute-start.56 = (bf16[256,1024]{1,0:T(8,128)(2,1)S(1)}, bf16[256,1024]{1,0:T(8,128)(2,1)}, u32[]{:S(2)}, u32[]{:S(2)}) collective-permute-start(bf16[256,1024]{1,0:T(8,128)(2,1)S(1)} %collective-permute-done.52.refs_2_), channel_id=1, source_target_pairs={{0,16},{1,17},{2,18},{3,19},{4,20},{5,21},{6,22},{7,23},{8,24},{9,... | collective-permute-start | bytes 1572872 | tf_op jit(solution)/shard_map/ppermute | solution.py:175
  456.8 782.0 %collective-permute-start.17 = (bf16[512,1024]{1,0:T(8,128)(2,1)}, bf16[512,1024]{1,0:T(8,128)(2,1)}, u32[]{:S(2)}, u32[]{:S(2)}) collective-permute-start(bf16[512,1024]{1,0:T(8,128)(2,1)} %convolution_convert_fusion.4.vo), channel_id=1, source_target_pairs={{0,4},{1,5},{2,6},{3,7},{4,0},{5,1},{6,2},{7,3},{8,12},{9,13},{10,... | collective-permute-start | bytes 3145736 | tf_op jit(solution)/shard_map/ppermute | solution.py:175
  457.1 781.6 %collective-permute-start.16 = (bf16[512,1024]{1,0:T(8,128)(2,1)}, bf16[512,1024]{1,0:T(8,128)(2,1)}, u32[]{:S(2)}, u32[]{:S(2)}) collective-permute-start(bf16[512,1024]{1,0:T(8,128)(2,1)} %convolution_convert_fusion.5.ko), channel_id=1, source_target_pairs={{0,4},{1,5},{2,6},{3,7},{4,0},{5,1},{6,2},{7,3},{8,12},{9,13},{10,... | collective-permute-start | bytes 3145736 | tf_op jit(solution)/shard_map/ppermute | solution.py:175
  978.1 287.7 %collective-permute-start.35 = (bf16[512,1024]{1,0:T(8,128)(2,1)}, bf16[512,1024]{1,0:T(8,128)(2,1)}, u32[]{:S(2)}, u32[]{:S(2)}) collective-permute-start(bf16[512,1024]{1,0:T(8,128)(2,1)} %convolution_convert_fusion.3.ko), channel_id=1, source_target_pairs={{0,4},{1,5},{2,6},{3,7},{4,0},{5,1},{6,2},{7,3},{8,12},{9,13},{10,... | collective-permute-start | bytes 3145736 | tf_op jit(solution)/shard_map/ppermute | solution.py:175
  978.3 287.5 %collective-permute-start.36 = (bf16[512,1024]{1,0:T(8,128)(2,1)}, bf16[512,1024]{1,0:T(8,128)(2,1)}, u32[]{:S(2)}, u32[]{:S(2)}) collective-permute-start(bf16[512,1024]{1,0:T(8,128)(2,1)} %convolution_convert_fusion.2.vo), channel_id=1, source_target_pairs={{0,4},{1,5},{2,6},{3,7},{4,0},{5,1},{6,2},{7,3},{8,12},{9,13},{10,... | collective-permute-start | bytes 3145736 | tf_op jit(solution)/shard_map/ppermute | solution.py:175
  1339.8 111.8 %collective-permute-start.77 = (bf16[512,512]{1,0:T(8,128)(2,1)S(1)}, bf16[512,512]{1,0:T(8,128)(2,1)S(1)}, u32[]{:S(2)}, u32[]{:S(2)}) collective-permute-start(bf16[512,512]{1,0:T(8,128)(2,1)S(1)} %select_convert_fusion.1), channel_id=1, source_target_pairs={{0,4},{1,5},{2,6},{3,7},{4,0},{5,1},{6,2},{7,3},{8,12},{9,13},{10,... | collective-permute-start | bytes 1572872 | tf_op jit(solution)/shard_map/ppermute | solution.py:175
  1341.9 114.1 %collective-permute-start.65 = (bf16[256,1024]{1,0:T(8,128)(2,1)}, bf16[256,1024]{1,0:T(8,128)(2,1)}, u32[]{:S(2)}, u32[]{:S(2)}) collective-permute-start(bf16[256,1024]{1,0:T(8,128)(2,1)} %get-tuple-element.76), channel_id=1, source_target_pairs={{0,0},{1,3},{2,4},{3,7},{4,2},{5,1},{6,6},{7,5},{8,8},{9,11},{10,1... | collective-permute-start | bytes 1572872 | tf_op jit(solution)/shard_map/ppermute | solution.py:175
  1353.8 102.4 %collective-permute-start.66 = (bf16[256,1024]{1,0:T(8,128)(2,1)}, bf16[256,1024]{1,0:T(8,128)(2,1)}, u32[]{:S(2)}, u32[]{:S(2)}) collective-permute-start(bf16[256,1024]{1,0:T(8,128)(2,1)} %get-tuple-element.77), channel_id=1, source_target_pairs={{0,3},{1,0},{2,7},{3,4},{4,1},{5,2},{6,5},{7,6},{8,11},{9,8},{10,1... | collective-permute-start | bytes 1572872 | tf_op jit(solution)/shard_map/ppermute | solution.py:175
  1354.8 99.1 %collective-permute-start.87 = (bf16[256,1024]{1,0:T(8,128)(2,1)}, bf16[256,1024]{1,0:T(8,128)(2,1)}, u32[]{:S(2)}, u32[]{:S(2)}) collective-permute-start(bf16[256,1024]{1,0:T(8,128)(2,1)} %select_convert_fusion), channel_id=1, source_target_pairs={{0,4},{1,5},{2,6},{3,7},{4,0},{5,1},{6,2},{7,3},{8,12},{9,13},{10,... | collective-permute-start | bytes 1572872 | tf_op jit(solution)/shard_map/ppermute | solution.py:175
  1450.8 51.8 %collective-permute-start.69 = (bf16[512,1024]{1,0:T(8,128)(2,1)}, bf16[512,1024]{1,0:T(8,128)(2,1)S(1)}, u32[]{:S(2)}, u32[]{:S(2)}) collective-permute-start(bf16[512,1024]{1,0:T(8,128)(2,1)} %get-tuple-element.42), channel_id=1, source_target_pairs={{0,4},{1,5},{2,6},{3,7},{4,0},{5,1},{6,2},{7,3},{8,12},{9,13},{10,... | collective-permute-start | bytes 3145736 | tf_op jit(solution)/shard_map/ppermute | solution.py:175
  1452.4 51.6 %collective-permute-start.70 = (bf16[512,1024]{1,0:T(8,128)(2,1)}, bf16[512,1024]{1,0:T(8,128)(2,1)S(1)}, u32[]{:S(2)}, u32[]{:S(2)}) collective-permute-start(bf16[512,1024]{1,0:T(8,128)(2,1)} %get-tuple-element.44), channel_id=1, source_target_pairs={{0,4},{1,5},{2,6},{3,7},{4,0},{5,1},{6,2},{7,3},{8,12},{9,13},{10,... | collective-permute-start | bytes 3145736 | tf_op jit(solution)/shard_map/ppermute | solution.py:175
  1454.0 73.2 %collective-permute-start.73 = (bf16[512,1024]{1,0:T(8,128)(2,1)S(1)}, bf16[512,1024]{1,0:T(8,128)(2,1)S(1)}, u32[]{:S(2)}, u32[]{:S(2)}) collective-permute-start(bf16[512,1024]{1,0:T(8,128)(2,1)S(1)} %copy-done.81), channel_id=1, source_target_pairs={{0,4},{1,5},{2,6},{3,7},{4,0},{5,1},{6,2},{7,3},{8,12},{9,13},{10,... | collective-permute-start | bytes 3145736 | tf_op jit(solution)/shard_map/ppermute | solution.py:175
  1456.0 67.7 %collective-permute-start.74 = (bf16[512,1024]{1,0:T(8,128)(2,1)S(1)}, bf16[512,1024]{1,0:T(8,128)(2,1)S(1)}, u32[]{:S(2)}, u32[]{:S(2)}) collective-permute-start(bf16[512,1024]{1,0:T(8,128)(2,1)S(1)} %copy-done.82), channel_id=1, source_target_pairs={{0,4},{1,5},{2,6},{3,7},{4,0},{5,1},{6,2},{7,3},{8,12},{9,13},{10,... | collective-permute-start | bytes 3145736 | tf_op jit(solution)/shard_map/ppermute | solution.py:175
  1499.6 31.7 %collective-permute-start.83 = (bf16[64,512]{1,0:T(8,128)(2,1)S(1)}, bf16[64,512]{1,0:T(8,128)(2,1)S(1)}, u32[]{:S(2)}, u32[]{:S(2)}) collective-permute-start(bf16[64,512]{1,0:T(8,128)(2,1)S(1)} %pad_maximum_fusion.14), channel_id=1, source_target_pairs={{0,2},{1,3},{2,0},{3,1},{4,6},{5,7},{6,4},{7,5},{8,10},{9,11},{10,... | collective-permute-start | bytes 196616 | tf_op jit(solution)/shard_map/ppermute | solution.py:175
  1502.5 31.0 %collective-permute-start.93 = (bf16[32,1024]{1,0:T(8,128)(2,1)S(1)}, bf16[32,1024]{1,0:T(8,128)(2,1)S(1)}, u32[]{:S(2)}, u32[]{:S(2)}) collective-permute-start(bf16[32,1024]{1,0:T(8,128)(2,1)S(1)} %pad_maximum_fusion.15), channel_id=1, source_target_pairs={{0,2},{1,3},{2,0},{3,1},{4,6},{5,7},{6,4},{7,5},{8,10},{9,11},{10,... | collective-permute-start | bytes 196616 | tf_op jit(solution)/shard_map/ppermute | solution.py:175
  1508.4 50.0 %collective-permute-start.71 = (bf16[256,1024]{1,0:T(8,128)(2,1)S(1)}, bf16[256,1024]{1,0:T(8,128)(2,1)S(1)}, u32[]{:S(2)}, u32[]{:S(2)}) collective-permute-start(bf16[256,1024]{1,0:T(8,128)(2,1)S(1)} %get-tuple-element.72), channel_id=1, source_target_pairs={{0,0},{1,3},{2,4},{3,7},{4,2},{5,1},{6,6},{7,5},{8,8},{9,11},{10,1... | collective-permute-start | bytes 1572872 | tf_op jit(solution)/shard_map/ppermute | solution.py:175
  1523.7 34.8 %collective-permute-start.72 = (bf16[256,1024]{1,0:T(8,128)(2,1)S(1)}, bf16[256,1024]{1,0:T(8,128)(2,1)S(1)}, u32[]{:S(2)}, u32[]{:S(2)}) collective-permute-start(bf16[256,1024]{1,0:T(8,128)(2,1)S(1)} %get-tuple-element.73), channel_id=1, source_target_pairs={{0,3},{1,0},{2,7},{3,4},{4,1},{5,2},{6,5},{7,6},{8,11},{9,8},{10,1... | collective-permute-start | bytes 1572872 | tf_op jit(solution)/shard_map/ppermute | solution.py:175
  1529.4 34.7 %collective-permute-start.75 = (bf16[256,1024]{1,0:T(8,128)(2,1)S(1)}, bf16[256,1024]{1,0:T(8,128)(2,1)S(1)}, u32[]{:S(2)}, u32[]{:S(2)}) collective-permute-start(bf16[256,1024]{1,0:T(8,128)(2,1)S(1)} %get-tuple-element.68), channel_id=1, source_target_pairs={{0,0},{1,3},{2,4},{3,7},{4,2},{5,1},{6,6},{7,5},{8,8},{9,11},{10,1... | collective-permute-start | bytes 1572872 | tf_op jit(solution)/shard_map/ppermute | solution.py:175
  1531.4 32.7 %collective-permute-start.76 = (bf16[256,1024]{1,0:T(8,128)(2,1)S(1)}, bf16[256,1024]{1,0:T(8,128)(2,1)S(1)}, u32[]{:S(2)}, u32[]{:S(2)}) collective-permute-start(bf16[256,1024]{1,0:T(8,128)(2,1)S(1)} %get-tuple-element.69), channel_id=1, source_target_pairs={{0,3},{1,0},{2,7},{3,4},{4,1},{5,2},{6,5},{7,6},{8,11},{9,8},{10,1... | collective-permute-start | bytes 1572872 | tf_op jit(solution)/shard_map/ppermute | solution.py:175
  (142 other events, 4334.7 us)

commit v2 on v1

--- a/solution.py
+++ b/solution.py
@@ -143,26 +143,321 @@
         name="attend_back")(info,q,ko,kp,vo,vp,do,o,p)
 
 
-def product(left, right):
-    return jnp.dot(left, right, preferred_element_type=F32)
-
-
-def normalize(values):
-    centered = values - jnp.mean(values, axis=-1, keepdims=True)
-    spread = jnp.mean(centered * centered, axis=-1, keepdims=True)
-    return centered * lax.rsqrt(spread + 1e-05)
-
-
-def smooth(values):
-    return jax.nn.gelu(values, approximate=False)
-
-
-def normalize_back(values, grads):
-    return jax.vjp(normalize, values)[1](grads)[0]
-
-
-def smooth_back(values, grads):
-    return jax.vjp(smooth, values)[1](grads)[0]
+def vmem(mib):
+    return pltpu.CompilerParams(vmem_limit_bytes=mib * 1024 * 1024)
+
+
+class Piece:
+    def __init__(self, parts, at, rows):
+        self.parts, self.at, self.rows = parts, at, rows
+
+
+def fused(name, info, body, loads, outs, mib=48, flops=0):
+    flat, plan, scratch = [], [], []
+    seen = {}
+
+    def arg(a):
+        if id(a) not in seen:
+            seen[id(a)] = len(flat)
+            flat.append(a)
+        return seen[id(a)]
+
+    count = 0
+    for load in loads:
+        if isinstance(load, Piece):
+            plan.append((count, load.at, load.rows, [arg(p) for p in load.parts]))
+            scratch.append(pltpu.VMEM((8 * load.rows, load.parts[0].shape[1]), load.parts[0].dtype))
+            count += 8
+        else:
+            plan.append((count, None, None, [arg(load)]))
+            scratch.append(pltpu.VMEM(load.shape, load.dtype))
+            count += 1
+    nout = len(outs)
+
+    def kernel(info_ref, *refs):
+        ins, out_refs = refs[: len(flat)], refs[len(flat) : len(flat) + nout]
+        bufs, sem = refs[len(flat) + nout : -1], refs[-1]
+        started = []
+        for (first, at, rows, args), buf in zip(plan, bufs):
+            copies = []
+            if at is None:
+                copies.append(pltpu.make_async_copy(ins[args[0]], buf, sem.at[first]))
+            else:
+                for m in range(8):
+                    owner = info_ref[1] ^ m
+                    to = pl.multiple_of(owner * rows, 16)
+                    copies.append(
+                        pltpu.make_async_copy(
+                            ins[args[m]].at[pl.ds(at, rows)], buf.at[pl.ds(to, rows)], sem.at[first + m]
+                        )
+                    )
+            for c in copies:
+                c.start()
+            started.append(copies)
+        ready = set()
+
+        def get(i):
+            if i not in ready:
+                for c in started[i]:
+                    c.wait()
+                ready.add(i)
+            return bufs[i]
+
+        body(info_ref, get, *out_refs)
+
+    return pl.pallas_call(
+        kernel,
+        grid_spec=pltpu.PrefetchScalarGridSpec(
+            num_scalar_prefetch=1,
+            grid=(1,),
+            in_specs=[pl.BlockSpec(memory_space=pl.ANY)] * len(flat),
+            out_specs=[pl.BlockSpec(o.shape, lambda i, *_: (0, 0)) for o in outs],
+            scratch_shapes=scratch + [pltpu.SemaphoreType.DMA((count,))],
+        ),
+        out_shape=list(outs),
+        compiler_params=vmem(mib),
+        cost_estimate=pl.CostEstimate(flops=flops, bytes_accessed=sum(a.size * a.dtype.itemsize for a in flat), transcendentals=0),
+        name=name,
+    )(info, *flat)
+
+
+def gather_pieces(info, piece):
+    def body(info_ref, get, out):
+        out[...] = get(0)[...]
+
+    rows = 8 * piece.rows
+    return fused("whole", info, body, [piece], [shape(rows, piece.parts[0].shape[1], piece.parts[0].dtype)])[0]
+
+
+def shape(rows, cols, dtype):
+    return jax.ShapeDtypeStruct((rows, cols), dtype)
+
+
+def norm_parts(v):
+    mean = jnp.mean(v, axis=-1, keepdims=True)
+    c = v - mean
+    inv = lax.rsqrt(jnp.mean(c * c, axis=-1, keepdims=True) + 1e-05)
+    return c * inv, inv
+
+
+def norm_back(y, inv, g):
+    return inv * (g - jnp.mean(g, axis=-1, keepdims=True) - y * jnp.mean(g * y, axis=-1, keepdims=True))
+
+
+def gelu_pair(v):
+    phi = 0.5 + 0.5 * lax.erf(v * 0.7071067811865476)
+    pdf = jnp.exp(v * v * -0.5) * 0.3989422804014327
+    return v * phi, phi + v * pdf
+
+
+def tn(a, b):
+    return lax.dot_general(a, b, (((0,), (0,)), ((), ())), preferred_element_type=F32)
+
+
+GMAC = 512 * 1024 * 1024 * 2
+
+
+def project_qkv(info, x, a1, b1, n):
+    T, D = x.shape
+
+    def body(info_ref, get, q, k, v):
+        xv = get(0)[...]
+        q[...] = (nn(xv, get(1)[...]) * (0.125 * LOG2E)).astype(BF)
+        k[...] = nn(xv, get(2)[...]).astype(BF)
+        v[...] = nn(xv, get(3)[...]).astype(BF)
+
+    return fused("qkv", info, body, [x, Piece(a1, 0, n), Piece(b1, 0, n), Piece(b1, n, n)],
+                 [shape(T, D, BF)] * 3, flops=3 * GMAC)
+
+
+def project_source(info, x, key, value):
+    T, D = x.shape
+
+    def body(info_ref, get, k, v):
+        xv = get(0)[...]
+        k[...] = nn(xv, get(1)[...]).astype(BF)
+        v[...] = nn(xv, get(2)[...]).astype(BF)
+
+    return fused("source_kv", info, body, [x, key, value], [shape(T, D, BF)] * 2, flops=2 * GMAC)
+
+
+def after_self(info, x, att, w_out, c_query):
+    T, D = x.shape
+
+    def body(info_ref, get, y_ref, inv_ref, cq_ref):
+        y, inv = norm_parts(get(0)[...].astype(F32) + nn(get(1)[...], get(2)[...]))
+        y_ref[...] = y
+        inv_ref[...] = jnp.broadcast_to(inv, inv_ref.shape)
+        cq_ref[...] = (nn(y.astype(BF), get(3)[...]) * (0.125 * LOG2E)).astype(BF)
+
+    return fused("after_self", info, body, [x, att, w_out, c_query],
+                 [shape(T, D, F32), shape(T, 128, F32), shape(T, D, BF)], flops=2 * GMAC)
+
+
+def after_cross(info, y1, att, c_out, down, up, scale):
+    T, D = y1.shape
+    A = down.shape[1]
+
+    def body(info_ref, get, y_ref, inv_ref, low_ref, sq_ref, gn_ref, base_ref):
+        y, inv = norm_parts(get(0)[...] + nn(get(1)[...], get(2)[...]))
+        y_ref[...] = y
+        inv_ref[...] = jnp.broadcast_to(inv, inv_ref.shape)
+        low = y.astype(BF)
+        low_ref[...] = low
+        h, g = gelu_pair(nn(low, get(3)[...]))
+        hb = h.astype(BF)
+        sq_ref[...] = hb
+        gn_ref[...] = g.astype(BF)
+        base_ref[...] = y + get(5)[0:1, 0:1] * nn(hb, get(4)[...])
+
+    return fused("after_cross", info, body, [y1, att, c_out, down, up, scale],
+                 [shape(T, D, F32), shape(T, 128, F32), shape(T, D, BF), shape(T, A, BF), shape(T, A, BF),
+                  shape(T, D, F32)], flops=2 * GMAC)
+
+
+def expand_kernel(x, e, h_ref, g_ref):
+    h, g = gelu_pair(nn(x[...], e[...]))
+    h_ref[...] = h.astype(BF)
+    g_ref[...] = g.astype(BF)
+
+
+def expand(x, e, block=1024):
+    T, D = x.shape
+    F = e.shape[1]
+    out = pl.BlockSpec((T, block), lambda i: (0, i))
+    return pl.pallas_call(
+        expand_kernel,
+        grid=(F // block,),
+        in_specs=[pl.BlockSpec((T, D), lambda i: (0, 0)), pl.BlockSpec((D, block), lambda i: (0, i))],
+        out_specs=[out, out],
+        out_shape=[shape(T, F, BF)] * 2,
+        compiler_params=vmem(40),
+        cost_estimate=pl.CostEstimate(flops=4 * GMAC, bytes_accessed=D * F * 2, transcendentals=0),
+        name="expand",
+    )(x, e)
+
+
+def contract_kernel(h, c, base, low, sq, gn, up, g_out, scale, out_ref, g3_ref, gup_ref, gdown_ref, gnar_ref, acc):
+    i = pl.program_id(0)
+
+    @pl.when(i == 0)
+    def _():
+        acc[...] = base[...]
+
+    acc[...] += nn(h[...], c[...])
+
+    @pl.when(i == pl.num_programs(0) - 1)
+    def _():
+        y, inv = norm_parts(acc[...])
+        out_ref[...] = y.astype(BF)
+        g3 = norm_back(y, inv, g_out[...].astype(F32))
+        g3_ref[...] = g3
+        ga = (scale[0:1, 0:1] * g3).astype(BF)
+        gup_ref[...] = tn(sq[...], ga)
+        gnar = (gn[...].astype(F32) * nt(ga, up[...])).astype(BF)
+        gnar_ref[...] = gnar
+        gdown_ref[...] = tn(low[...], gnar)
+
+
+def contract(h, c, base, low, sq, gn, up, g_out, scale, block=1024):
+    T, D = base.shape
+    F = c.shape[0]
+    A = sq.shape[1]
+
+    def whole(a):
+        return pl.BlockSpec(a.shape, lambda i: (0, 0), pipeline_mode=pl.Buffered(1))
+
+    outs = [shape(T, D, BF), shape(T, D, F32), shape(A, D, F32), shape(D, A, F32), shape(T, A, BF)]
+    return pl.pallas_call(
+        contract_kernel,
+        grid=(F // block,),
+        in_specs=[pl.BlockSpec((T, block), lambda i: (0, i)), pl.BlockSpec((block, D), lambda i: (i, 0))]
+        + [whole(a) for a in (base, low, sq, gn, up, g_out, scale)],
+        out_specs=[pl.BlockSpec(o.shape, lambda i: (0, 0)) for o in outs],
+        out_shape=outs,
+        scratch_shapes=[pltpu.VMEM((T, D), F32)],
+        compiler_params=vmem(48),
+        cost_estimate=pl.CostEstimate(flops=6 * GMAC, bytes_accessed=D * F * 2, transcendentals=0),
+        name="contract",
+    )(h, c, base, low, sq, gn, up, g_out, scale)
+
+
+def ffn_back_kernel(g3, c, e, gp, gnar, down, y2, inv2, co, g2_ref, ga_ref, acc):
+    i = pl.program_id(0)
+
+    @pl.when(i == 0)
+    def _():
+        acc[...] = g3[...] + nt(gnar[...], down[...])
+
+    gh = (nt(g3[...].astype(BF), c[...]) * gp[...].astype(F32)).astype(BF)
+    acc[...] += nt(gh, e[...])
+
+    @pl.when(i == pl.num_programs(0) - 1)
+    def _():
+        g2 = norm_back(y2[...], inv2[:, 0:1], acc[...])
+        g2_ref[...] = g2
+        ga_ref[...] = nt(g2.astype(BF), co[...]).astype(BF)
+
+
+def ffn_back(g3, c, e, gp, gnar, down, y2, inv2, co, block=1024):
+    T, D = g3.shape
+    F = c.shape[0]
+
+    def whole(a):
+        return pl.BlockSpec(a.shape, lambda i: (0, 0), pipeline_mode=pl.Buffered(1))
+
+    outs = [shape(T, D, F32), shape(T, D, BF)]
+    return pl.pallas_call(
+        ffn_back_kernel,
+        grid=(F // block,),
+        in_specs=[whole(g3), pl.BlockSpec((block, D), lambda i: (i, 0)), pl.BlockSpec((D, block), lambda i: (0, i)),
+                  pl.BlockSpec((T, block), lambda i: (0, i))] + [whole(a) for a in (gnar, down, y2, inv2, co)],
+        out_specs=[pl.BlockSpec(o.shape, lambda i: (0, 0)) for o in outs],
+        out_shape=outs,
+        scratch_shapes=[pltpu.VMEM((T, D), F32)],
+        compiler_params=vmem(52),
+        cost_estimate=pl.CostEstimate(flops=9 * GMAC, bytes_accessed=2 * D * F * 2, transcendentals=0),
+        name="ffn_back",
+    )(g3, c, e, gp, gnar, down, y2, inv2, co)
+
+
+def before_self(info, g2, gq, y1, inv1, c_query, w_out):
+    T, D = g2.shape
+
+    def body(info_ref, get, g1_ref, ga_ref):
+        g = get(0)[...] + 0.125 * nt(get(1)[...], get(2)[...])
+        g1 = norm_back(get(3)[...], get(4)[:, 0:1], g)
+        g1_ref[...] = g1
+        ga_ref[...] = nt(g1.astype(BF), get(5)[...]).astype(BF)
+
+    return fused("before_self", info, body, [g2, gq, c_query, y1, inv1, w_out],
+                 [shape(T, D, F32), shape(T, D, BF)], flops=2 * GMAC)
+
+
+def source_grad(info, gk, gk_got, gv, gv_got, key, value):
+    T, D = gk.shape
+
+    def body(info_ref, get, out):
+        k = (get(0)[...] + get(1)[...].astype(F32)).astype(BF)
+        v = (get(3)[...] + get(4)[...].astype(F32)).astype(BF)
+        out[...] = (nt(k, get(2)[...]) + nt(v, get(5)[...])).astype(BF)
+
+    return fused("source_grad", info, body, [gk, gk_got, key, gv, gv_got, value], [shape(T, D, BF)], flops=2 * GMAC)[0]
+
+
+def token_grad(info, g1, gq, gk, gk_got, gv, gv_got, a1, b1, n):
+    T, D = g1.shape
+
+    def body(info_ref, get, out):
+        acc = get(0)[...] + 0.125 * nt(get(1)[...], get(2)[...])
+        k = (get(3)[...] + get(4)[...].astype(F32)).astype(BF)
+        acc += nt(k, get(5)[...])
+        v = (get(6)[...] + get(7)[...].astype(F32)).astype(BF)
+        out[...] = (acc + nt(v, get(8)[...])).astype(BF)
+
+    return fused("token_grad", info, body,
+                 [g1, gq, Piece(a1, 0, n), gk, gk_got, Piece(b1, 0, n), gv, gv_got, Piece(b1, n, n)],
+                 [shape(T, D, BF)], flops=3 * GMAC)[0]
 
 
 def move(value, target):
@@ -225,43 +520,6 @@
     return [pieces[m] for m in range(8)]
 
 
-def assemble_kernel(parts, n_in, info, *refs):
-    ins, rest = refs[:n_in], refs[n_in:]
-    outs, sem = rest[:-1], rest[-1]
-    copies = []
-    for which, src, rows, out, stride, base in parts:
-        for m in range(8):
-            owner = info[1] ^ m
-            at = pl.multiple_of(owner * stride + base, 16)
-            copies.append(
-                pltpu.make_async_copy(
-                    ins[which * 8 + m].at[pl.ds(src, rows)],
-                    outs[out].at[pl.ds(at, rows)],
-                    sem.at[len(copies)],
-                )
-            )
-    for c in copies:
-        c.start()
-    for c in copies:
-        c.wait()
-
-
-def assemble(info, sets, parts, shapes):
-    flat = [p for s in sets for p in s]
-    return pl.pallas_call(
-        functools.partial(assemble_kernel, parts, len(flat)),
-        grid_spec=pltpu.PrefetchScalarGridSpec(
-            num_scalar_prefetch=1,
-            grid=(1,),
-            in_specs=[pl.BlockSpec(memory_space=pl.ANY)] * len(flat),
-            out_specs=[pl.BlockSpec(memory_space=pl.ANY)] * len(shapes),
-            scratch_shapes=[pltpu.SemaphoreType.DMA((len(parts) * 8,))],
-        ),
-        out_shape=[jax.ShapeDtypeStruct(s, BF) for s in shapes],
-        name="assemble",
-    )(info, *flat)
-
-
 def reduce_all(value, d, s, steps):
     def other(v, step):
         axis, bit = step
@@ -311,25 +569,16 @@
         return jnp.concatenate([a, b], axis=0)
 
     wide = [widen(w) for w in (self_query, self_key, self_value, self_out, cross_query, cross_key,
-                               cross_value, cross_out, ffn_expand, ffn_contract)]
-    sq, sk, sv, so, cq_, ck_, cv_, co_, ex, con = wide
+                               cross_value, cross_out)]
+    sq, sk, sv, so, cq_, ck_, cv_, co_ = wide
     n = sq.shape[0]
-    f = con.shape[0]
     XY, YX = (2, 4), (4, 2)
-    a1 = spread_pieces(two(sq, sv), low, XY)
-    b1 = spread_pieces(two(sk, ck_), low, YX)
+    a1 = spread_pieces(two(sq, ck_), low, XY)
+    b1 = spread_pieces(two(sk, sv), low, YX)
     a2 = spread_pieces(two(so, cv_), low, XY)
     b2 = spread_pieces(two(cq_, co_), low, YX)
-    a3 = spread_pieces(ex[: n // 2], low, XY)
-    b3 = spread_pieces(ex[n // 2 :], low, YX)
-    a4 = spread_pieces(con[: f // 2], low, XY)
-    b4 = spread_pieces(con[f // 2 :], low, YX)
-    four = ((0, 0, n, 0, n, 0), (0, n, n, 1, n, 0), (1, 0, n, 2, n, 0), (1, n, n, 3, n, 0))
-    w_query, w_value, w_key, c_key = assemble(info, [a1, b1], four, [(D, D)] * 4)
-    w_out, c_value, c_query, c_out = assemble(info, [a2, b2], four, [(D, D)] * 4)
-    FF = ex.shape[1]
-    (w_expand,) = assemble(info, [a3, b3], ((0, 0, n // 2, 0, n, 0), (1, 0, n // 2, 0, n, n // 2)), [(D, FF)])
-    (w_contract,) = assemble(info, [a4, b4], ((0, 0, f // 2, 0, f, 0), (1, 0, f // 2, 0, f, f // 2)), [(FF, D)])
+    w_expand = lax.all_gather(ffn_expand, "dp", axis=0, tiled=True)
+    w_contract = lax.all_gather(ffn_contract, "dp", axis=0, tiled=True)
     src = reshard_in(source, d, s)
     g_out = reshard_in(grad_output, d, s)
 
@@ -359,60 +608,40 @@
     ck_aug = [((pos[:, None] >= src_len) & (lanes == 0)[None, :]).astype(BF) for pos in (own_pos, peer_pos)]
     cq_aug = jnp.broadcast_to(jnp.where(lanes == 0, NEG, 0.0).astype(BF)[None, :], (2 * C, 128))
 
-    scale = 0.125 * LOG2E
-    branch_scale = (step_index[0] + 1).astype(F32) / 5.0
-    q = (product(x, w_query) * scale).astype(BF)
-    k = product(x, w_key).astype(BF)
-    v = product(x, w_value).astype(BF)
+    scale = jnp.full((8, 128), (step_index[0] + 1).astype(F32) / 5.0, F32)
+    q, k, v = project_qkv(info, x, a1, b1, n)
     k_peer, v_peer = flip(k, 1), flip(v, 1)
-    ck = product(src, c_key).astype(BF)
-    cv = product(src, c_value).astype(BF)
+    attended, p_self = attend(SELF_PLANS, info, q, k, k_peer, v, v_peer, q_aug, *k_aug)
+    ck, cv = project_source(info, src, Piece(a1, n, n), Piece(a2, n, n))
     ck_peer, cv_peer = flip(ck, 1), flip(cv, 1)
-    attended, p_self = attend(SELF_PLANS, info, q, k, k_peer, v, v_peer, q_aug, *k_aug)
-    first_sum = x.astype(F32) + product(attended, w_out)
-    first_norm = normalize(first_sum)
-    cq = (product(first_norm.astype(BF), c_query) * scale).astype(BF)
+    y1, inv1, cq = after_self(info, x, attended, Piece(a2, 0, n), Piece(b2, 0, n))
     cross_attended, p_cross = attend(CROSS_PLANS, info, cq, ck, ck_peer, cv, cv_peer, cq_aug, *ck_aug)
-    second_sum = first_norm + product(cross_attended, c_out)
-    second_norm = normalize(second_sum)
-    second_low = second_norm.astype(BF)
-    hidden_pre = product(second_low, w_expand)
-    hidden = smooth(hidden_pre).astype(BF)
-    narrow = product(second_low, adapter_down)
-    squeezed = smooth(narrow).astype(BF)
-    third_sum = second_norm + product(hidden, w_contract) + branch_scale * product(squeezed, adapter_up)
-    output = normalize(third_sum).astype(BF)
+    y2, inv2, second_low, squeezed, gn, base = after_cross(
+        info, y1, cross_attended, Piece(b2, n, n), adapter_down, adapter_up, scale
+    )
+    hidden, gp = expand(second_low, w_expand)
+    output, g3, grad_up, grad_down, gnar = contract(
+        hidden, w_contract, base, second_low, squeezed, gn, adapter_up, g_out, scale
+    )
     output = reshard_out(output, d, s)
-    grad_third = normalize_back(third_sum, g_out.astype(F32))
-    grad_ffn = grad_third.astype(BF)
-    grad_adapt = (branch_scale * grad_third).astype(BF)
-    grad_up = product(squeezed.T, grad_adapt)
-    grad_narrow = smooth_back(narrow, product(grad_adapt, adapter_up.T)).astype(BF)
-    grad_down = product(second_low.T, grad_narrow)
     last = [("seq", 2), ("seq", 1)] + [("dp", 1 << j) for j in range(low.bit_length() - 1)]
     grad_up = reduce_all(grad_up, d, s, [("dp", low), ("dp", 2 * low), ("dp", 4 * low)] + last)
     grad_down = reduce_all(grad_down, d, s, [("dp", low), ("dp", 4 * low), ("dp", 2 * low)] + last)
-    grad_hidden = smooth_back(hidden_pre, product(grad_ffn, w_contract.T)).astype(BF)
-    grad_second = grad_third + product(grad_hidden, w_expand.T) + product(grad_narrow, adapter_down.T)
-    grad_second_sum = normalize_back(second_sum, grad_second)
-    grad_cross = product(grad_second_sum.astype(BF), c_out.T).astype(BF)
+    c_out = gather_pieces(info, Piece(b2, n, n))
+    g2, grad_cross = ffn_back(g3, w_contract, w_expand, gp, gnar, adapter_down, y2, inv2, c_out)
     gq, gk, gv, gk_peer, gv_peer = attend_back(
         CROSS_PLANS, info, cq, ck, ck_peer, cv, cv_peer, grad_cross, cross_attended, p_cross
     )
-    gk = (gk + flip(gk_peer, 1).astype(F32)).astype(BF)
-    gv = (gv + flip(gv_peer, 1).astype(F32)).astype(BF)
-    grad_source = (product(gk, c_key.T) + product(gv, c_value.T)).astype(BF)
+    gk_got, gv_got = flip(gk_peer, 1), flip(gv_peer, 1)
+    g1, grad_self = before_self(info, g2, gq, y1, inv1, Piece(b2, 0, n), Piece(a2, 0, n))
+    grad_source = source_grad(info, gk, gk_got, gv, gv_got, Piece(a1, n, n), Piece(a2, n, n))
     grad_source = reshard_out(grad_source, d, s)
-    grad_first = grad_second_sum + 0.125 * product(gq, c_query.T)
-    grad_first_sum = normalize_back(first_sum, grad_first)
-    grad_self = product(grad_first_sum.astype(BF), w_out.T).astype(BF)
     gq, gk, gv, gk_peer, gv_peer = attend_back(
         SELF_PLANS, info, q, k, k_peer, v, v_peer, grad_self, attended, p_self
     )
-    gk = (gk + flip(gk_peer, 1).astype(F32)).astype(BF)
-    gv = (gv + flip(gv_peer, 1).astype(F32)).astype(BF)
-    grad_tokens = grad_first_sum + 0.125 * product(gq, w_query.T) + product(gk, w_key.T) + product(gv, w_value.T)
-    grad_tokens = reshard_out(grad_tokens.astype(BF), d, s)
+    gk_got, gv_got = flip(gk_peer, 1), flip(gv_peer, 1)
+    grad_tokens = token_grad(info, g1, gq, gk, gk_got, gv, gv_got, a1, b1, n)
+    grad_tokens = reshard_out(grad_tokens, d, s)
     return (output, grad_tokens, grad_source, grad_down, grad_up)
 
 

time: 1580 us -> 500 us (0.32)
  Pallas kernels: 1120 us -> 186 us
  matrix products: 119 us -> 0 us
  waiting for transfers between devices: 148 us -> 107 us
    pallas_call x4 -> x11, Pallas kernels: 1020 us -> 95.8 us  [the longest x8 53 us: fused(): pl.pallas_call(kernel, grid_spec=pltpu.PrefetchScalarGridSpec(num_scalar_...]
    dot_general x25 -> x0, matrix products: 119 us -> none  [product(): return jnp.dot(left, right, preferred_element_type=F32)]
    ppermute x97 -> x69, waiting for transfers between devices: 148 us -> 105 us  [move(): return lax.ppermute(value, ('dp', 'seq'), pairs)]
    ppermute x97 -> x69, starting transfers between devices: 133 us -> 119 us  [move(): return lax.ppermute(value, ('dp', 'seq'), pairs)]
  transfers between devices with their start and end apart: 97 -> 71, of which waited for: 33 -> 25; matrix products, arithmetic and copies ran while one was open for 7% -> 8% of each run, Pallas kernels for 70% -> 35%
where the time goes in v2:
time: 500 us; the launch traced here: 493 us
  Pallas kernels  186 us (37%)
  starting transfers between devices  120 us (24%)
  waiting for transfers between devices  107 us (21%)
  local copies, waits for them, and re-layouts  36 us (7%)
  other arithmetic  28.2 us (6%)
  between operations  16.4 us (3%)
    ppermute x69, starting transfers between devices, move(): return lax.ppermute(value, ('dp', 'seq'), pairs)  119 us
    ppermute x69, waiting for transfers between devices, move(): return lax.ppermute(value, ('dp', 'seq'), pairs)  105 us
    pallas_call x8, Pallas kernels, fused(): pl.pallas_call(kernel, grid_spec=pltpu.PrefetchScalarGridSpec(num_scalar_...  53 us
    pallas_call x2, Pallas kernels, attend_back(): pl.pallas_call(functools.partial(bwd_kernel, plans, C), grid_spec=pltpu.P...  46 us
    pallas_call x2, Pallas kernels, attend(): pl.pallas_call(functools.partial(fwd_kernel, plans, C), grid_spec=pltpu.P...  44.4 us
    unnamed x172, local copies, waits for them, and re-layouts  23.1 us
    pallas_call x1, Pallas kernels, ffn_back(): pl.pallas_call(ffn_back_kernel, grid=(F // block,), in_specs=[whole(g3),...  18.8 us
    pallas_call x1, Pallas kernels, contract(): pl.pallas_call(contract_kernel, grid=(F // block,), in_specs=[pl.BlockSpe...  14.3 us
  transfers between devices with their start and end apart: 71, of which 25 were waited for; matrix products, arithmetic and copies ran while one was open for 8% of the time, Pallas kernels for 35%

profile of v2, /device:TPU:1, one launch (start us, length us, event | category | flops | bytes accessed | tf_op | source)
XLA Modules:
  0.0 493.1 jit_solution(3611465470258992030)
XLA Ops:
  13.0 5.3 %collective-permute-start = (bf16[256,1024]{1,0:T(8,128)(2,1)S(1)}, bf16[256,1024]{1,0:T(8,128)(2,1)}, u32[]{:S(2)}, u32[]{:S(2)}) collective-permute-start(bf16[256,1024]{1,0:T(8,128)(2,1)S(1)} %get-tuple-element.111), channel_id=1, source_target_pairs={{0,0},{1,5},{2,4},{3,1},{4,2},{5,7},{6,6},{7,3},{8,8},{9,13},{10,1... | collective-permute-start | bytes 1572872 | tf_op jit(solution)/shard_map/ppermute | solution.py:470
  25.7 4.2 collective-permute-done
  30.0 5.7 %collective-permute-done.1 = bf16[256,1024]{1,0:T(8,128)(2,1)} collective-permute-done((bf16[256,1024]{1,0:T(8,128)(2,1)}, bf16[256,1024]{1,0:T(8,128)(2,1)}, u32[]{:S(2)}, u32[]{:S(2)}) %collective-permute-start.1) | collective-permute-done | bytes 524320 | tf_op jit(solution)/shard_map/ppermute | solution.py:470
  36.0 3.1 collective-permute-start.9
  49.5 3.8 collective-permute-start.19
  53.4 9.4 %collective-permute-done.20.refs_4_.refs_11_.refs_14_ = bf16[256,1024]{1,0:T(8,128)(2,1)S(1)} collective-permute-done((bf16[256,1024]{1,0:T(8,128)(2,1)S(1)}, bf16[256,1024]{1,0:T(8,128)(2,1)S(1)}, u32[]{:S(2)}, u32[]{:S(2)}) %collective-permute-start.20) | collective-permute-done | bytes 524320 | tf_op jit(solution)/shard_map/ppermute | solution.py:470
  62.8 11.9 %collective-permute-start.26 = (bf16[256,1024]{1,0:T(8,128)(2,1)S(1)}, bf16[256,1024]{1,0:T(8,128)(2,1)}, u32[]{:S(2)}, u32[]{:S(2)}) collective-permute-start(bf16[256,1024]{1,0:T(8,128)(2,1)S(1)} %constant_dynamic-update-slice_fusion.6.refs_10_.refs_2_.refs_0_), channel_id=1, source_target_pairs={{0,4},{1,5},{2,6},{3,7},{4,0},{5,1},{6,2},{7,3},{8,12},{9,13},{10,... | collective-permute-start | bytes 1572872 | tf_op jit(solution)/shard_map/ppermute | solution.py:470
  74.7 9.6 %collective-permute-start.33 = (bf16[256,1024]{1,0:T(8,128)(2,1)}, bf16[256,1024]{1,0:T(8,128)(2,1)}, u32[]{:S(2)}, u32[]{:S(2)}) collective-permute-start(bf16[256,1024]{1,0:T(8,128)(2,1)} %get-tuple-element.107), channel_id=1, source_target_pairs={{0,0},{1,5},{2,4},{3,1},{4,2},{5,7},{6,6},{7,3},{8,8},{9,13},{10,1... | collective-permute-start | bytes 1572872 | tf_op jit(solution)/shard_map/ppermute | solution.py:470
  84.3 4.3 collective-permute-done.22.refs_6_.refs_13_.refs_16_
  88.7 6.7 %collective-permute-start.34 = (bf16[256,1024]{1,0:T(8,128)(2,1)}, bf16[256,1024]{1,0:T(8,128)(2,1)}, u32[]{:S(2)}, u32[]{:S(2)}) collective-permute-start(bf16[256,1024]{1,0:T(8,128)(2,1)} %get-tuple-element.108), channel_id=1, source_target_pairs={{0,1},{1,4},{2,5},{3,0},{4,3},{5,6},{6,7},{7,2},{8,9},{9,12},{10,1... | collective-permute-start | bytes 1572872 | tf_op jit(solution)/shard_map/ppermute | solution.py:470
  95.4 7.5 %collective-permute-start.37 = (bf16[256,1024]{1,0:T(8,128)(2,1)}, bf16[256,1024]{1,0:T(8,128)(2,1)}, u32[]{:S(2)}, u32[]{:S(2)}) collective-permute-start(bf16[256,1024]{1,0:T(8,128)(2,1)} %get-tuple-element.103), channel_id=1, source_target_pairs={{0,0},{1,5},{2,4},{3,1},{4,2},{5,7},{6,6},{7,3},{8,8},{9,13},{10,1... | collective-permute-start | bytes 1572872 | tf_op jit(solution)/shard_map/ppermute | solution.py:470
  104.9 4.0 collective-permute-done.34
  108.9 11.1 %collective-permute-done.37 = bf16[256,1024]{1,0:T(8,128)(2,1)} collective-permute-done((bf16[256,1024]{1,0:T(8,128)(2,1)}, bf16[256,1024]{1,0:T(8,128)(2,1)}, u32[]{:S(2)}, u32[]{:S(2)}) %collective-permute-start.37) | collective-permute-done | bytes 524320 | tf_op jit(solution)/shard_map/ppermute | solution.py:470
  123.6 2.5 collective-permute-start.15
  133.1 6.9 %qkv.1 = (bf16[512,1024]{1,0:T(8,128)(2,1)}, bf16[512,1024]{1,0:T(8,128)(2,1)}, bf16[512,1024]{1,0:T(8,128)(2,1)}) custom-call(s32[2]{0:T(128)S(1)} %pad_add_fusion.2.info_ref.info, bf16[512,1024]{1,0:T(8,128)(2,1)} %pad_maximum_fusion.refs_0_, bf16[256,1024]{1,0:T(8,128)(2,1)S(1)} %copy-done.27, bf16[256,1024]{1,0:T(8,128)(2,1)S(1)} %copy-done.36, ...), custom_call_target="tpu_custom_call" | custom-call | flops 3221225472 | bytes 9437184 | tf_op jit(solution)/shard_map/qkv/pallas_call | solution.py:208
  140.0 4.6 collective-permute-done.24.refs_8_.refs_15_.refs_18_
  146.3 2.4 collective-permute-start.17
  153.2 5.5 %source_kv.1 = (bf16[512,1024]{1,0:T(8,128)(2,1)}, bf16[512,1024]{1,0:T(8,128)(2,1)}) custom-call(s32[2]{0:T(128)S(1)} %pad_add_fusion.2.info_ref.info, bf16[512,1024]{1,0:T(8,128)(2,1)} %pad_maximum_fusion.1.refs_0_, bf16[256,1024]{1,0:T(8,128)(2,1)S(1)} %copy-done.27, bf16[256,1024]{1,0:T(8,128)(2,1)S(1)} %copy-done.36, bf16[256,1024]{1,0:T(8,128)(2,1)S(1)} %copy-done.30, ...), custom_call_target="tpu_custom_call" | custom-call | flops 2147483648 | bytes 9437184 | tf_op jit(solution)/shard_map/source_kv/pallas_call | solution.py:208
  161.6 3.1 whole.1.co
  166.0 19.4 %attend.2 = (bf16[512,1024]{1,0:T(8,128)(2,1)}, bf16[8,2,5,256,256]{4,3,2,1,0:T(8,128)(2,1)}) custom-call(s32[2]{0:T(128)} %copy-done.46, bf16[512,1024]{1,0:T(8,128)(2,1)} %get-tuple-element.44.q_ref, bf16[512,1024]{1,0:T(8,128)(2,1)} %get-tuple-element.45.ko, bf16[512,1024]{1,0:T(8,128)(2,1)} %copy-done.79, bf16[512,1024]{1,0:T(8,128)(2,1)} %get-tuple-element.46.vo, ...), custom_call_target="tpu_custom_call" | custom-call | flops 5368709120 | bytes 10485760 | tf_op jit(solution)/shard_map/attend/pallas_call | solution.py:71
  185.4 6.3 %after_self.1 = (f32[512,1024]{1,0:T(8,128)}, f32[512,128]{1,0:T(8,128)S(1)}, bf16[512,1024]{1,0:T(8,128)(2,1)}) custom-call(s32[2]{0:T(128)S(1)} %copy-done.47, bf16[512,1024]{1,0:T(8,128)(2,1)} %pad_maximum_fusion.refs_0_, bf16[512,1024]{1,0:T(8,128)(2,1)} %get-tuple-element.47.refs_1_.o, ...), custom_call_target="tpu_custom_call" | custom-call | flops 2147483648 | bytes 10485760 | tf_op jit(solution)/shard_map/after_self/pallas_call | solution.py:208
  192.8 25.1 %attend.3 = (bf16[512,1024]{1,0:T(8,128)(2,1)}, bf16[8,2,8,256,256]{4,3,2,1,0:T(8,128)(2,1)}) custom-call(s32[2]{0:T(128)} %copy-done.46, bf16[512,1024]{1,0:T(8,128)(2,1)} %get-tuple-element.49.q_ref, bf16[512,1024]{1,0:T(8,128)(2,1)} %get-tuple-element.50.ko, bf16[512,1024]{1,0:T(8,128)(2,1)} %copy-done.82, bf16[512,1024]{1,0:T(8,128)(2,1)} %get-tuple-element.51.vo, ...), custom_call_target="tpu_custom_call" | custom-call | flops 8589934592 | bytes 16777216 | tf_op jit(solution)/shard_map/attend/pallas_call | solution.py:71
  218.0 7.9 %after_cross.1 = (f32[512,1024]{1,0:T(8,128)}, f32[512,128]{1,0:T(8,128)S(1)}, bf16[512,1024]{1,0:T(8,128)(2,1)}, bf16[512,512]{1,0:T(8,128)(2,1)S(1)}, bf16[512...) custom-call(s32[2]{0:T(128)S(1)} %copy-done.48, f32[512,1024]{1,0:T(8,128)} %get-tuple-element.48.refs_0_.refs_10_, ...), custom_call_target="tpu_custom_call" | custom-call | flops 2147483648 | bytes 9441280 | tf_op jit(solution)/shard_map/after_cross/pallas_call | solution.py:208
  229.4 9.7 %expand.1 = (bf16[512,4096]{1,0:T(8,128)(2,1)S(1)}, bf16[512,4096]{1,0:T(8,128)(2,1)S(1)}) custom-call(bf16[512,1024]{1,0:T(8,128)(2,1)S(1)} %copy-done.51, bf16[1024,4096]{1,0:T(8,128)(2,1)} %all-gather.3.cloned.1.call-done.e), custom_call_target="tpu_custom_call" | custom-call | flops 4294967296 | bytes 8388608 | tf_op jit(solution)/shard_map/expand/pallas_call | solution.py:328
  248.9 14.3 %contract.1 = (bf16[512,1024]{1,0:T(8,128)(2,1)S(1)}, f32[512,1024]{1,0:T(8,128)}, f32[512,1024]{1,0:T(8,128)}, f32[1024,512]{1,0:T(8,128)}, bf16[512,512]{1,0:T(8,128)(2,1)S(1)}) custom-call(bf16[512,4096]{1,0:T(8,128)(2,1)} %copy-done.59, bf16[4096,1024]{1,0:T(8,128)(2,1)} %all-gather.5.cloned.1.call-done.c, f32[512,1024]{1,0:T(8,128)} %get-tuple-element.55.base, ...), custom_call_target="tpu_custom_call" | custom-call | flops 6442450944 | bytes 8388608 | tf_op jit(solution)/shard_map/contract/pallas_call | solution.py:371
  263.2 2.5 select_convert_fusion
  266.8 2.4 select_convert_fusion.1
  269.2 18.8 %ffn_back.1 = (f32[512,1024]{1,0:T(8,128)}, bf16[512,1024]{1,0:T(8,128)(2,1)S(1)}) custom-call(f32[512,1024]{1,0:T(8,128)} %get-tuple-element.59.g3, bf16[4096,1024]{1,0:T(8,128)(2,1)} %all-gather.5.cloned.1.call-done.c, bf16[1024,4096]{1,0:T(8,128)(2,1)} %all-gather.3.cloned.1.call-done.e, bf16[512,4096]{1,0:T(8,128)(2,1)} %copy-done.60, ...), custom_call_target="tpu_custom_call" | custom-call | flops 9663676416 | bytes 16777216 | tf_op jit(solution)/shard_map/ffn_back/pallas_call | solution.py:410
  289.1 26.6 %attend_back.2 = (bf16[512,1024]{1,0:T(8,128)(2,1)}, f32[512,1024]{1,0:T(8,128)}, f32[512,1024]{1,0:T(8,128)}, bf16[512,1024]{1,0:T(8,128)(2,1)}, bf16[512,1024]{1,0:T(8,128)(2,1)}) custom-call(s32[2]{0:T(128)} %copy-done.46, bf16[512,1024]{1,0:T(8,128)(2,1)} %get-tuple-element.49.q_ref, bf16[512,1024]{1,0:T(8,128)(2,1)} %get-tuple-element.50.ko, ...), custom_call_target="tpu_custom_call" | custom-call | flops 17179869184 | bytes 16777216 | tf_op jit(solution)/shard_map/attend_back/pallas_call | solution.py:134
  317.4 12.5 %collective-permute-start.39 = (bf16[256,1024]{1,0:T(8,128)(2,1)}, bf16[256,1024]{1,0:T(8,128)(2,1)}, u32[]{:S(2)}, u32[]{:S(2)}) collective-permute-start(bf16[256,1024]{1,0:T(8,128)(2,1)} %get-tuple-element.99), channel_id=1, source_target_pairs={{0,0},{1,3},{2,4},{3,7},{4,2},{5,1},{6,6},{7,5},{8,8},{9,11},{10,1... | collective-permute-start | bytes 1572872 | tf_op jit(solution)/shard_map/ppermute | solution.py:470
  329.9 7.2 %before_self.1 = (f32[512,1024]{1,0:T(8,128)}, bf16[512,1024]{1,0:T(8,128)(2,1)}) custom-call(s32[2]{0:T(128)S(1)} %copy-done.49, f32[512,1024]{1,0:T(8,128)} %get-tuple-element.64.refs_0_, bf16[512,1024]{1,0:T(8,128)(2,1)} %get-tuple-element.67.refs_1_, bf16[256,1024]{1,0:T(8,128)(2,1)S(1)} %constant_dynamic-update-slice_fusion.6.refs_10_.refs_2_.refs_0_, ...), custom_call_target="tpu_custom_call" | custom-call | flops 2147483648 | bytes 13893632 | tf_op jit(solution)/shard_map/before_self/pallas_call | solution.py:208
  337.1 19.4 %attend_back.3 = (bf16[512,1024]{1,0:T(8,128)(2,1)}, f32[512,1024]{1,0:T(8,128)}, f32[512,1024]{1,0:T(8,128)}, bf16[512,1024]{1,0:T(8,128)(2,1)}, bf16[512,1024]{1,0:T(8,128)(2,1)}) custom-call(s32[2]{0:T(128)} %copy-done.46, bf16[512,1024]{1,0:T(8,128)(2,1)} %get-tuple-element.44.q_ref, bf16[512,1024]{1,0:T(8,128)(2,1)} %get-tuple-element.45.ko, ...), custom_call_target="tpu_custom_call" | custom-call | flops 10737418240 | bytes 10485760 | tf_op jit(solution)/shard_map/attend_back/pallas_call | solution.py:134
  360.2 12.0 %collective-permute-done.40 = bf16[256,1024]{1,0:T(8,128)(2,1)S(1)} collective-permute-done((bf16[256,1024]{1,0:T(8,128)(2,1)S(1)}, bf16[256,1024]{1,0:T(8,128)(2,1)S(1)}, u32[]{:S(2)}, u32[]{:S(2)}) %collective-permute-start.40) | collective-permute-done | bytes 524320 | tf_op jit(solution)/shard_map/ppermute | solution.py:470
  374.7 3.1 collective-permute-done.60
  377.9 6.5 %collective-permute-done.50 = bf16[256,512]{1,0:T(8,128)(2,1)S(1)} collective-permute-done((bf16[256,512]{1,0:T(8,128)(2,1)S(1)}, bf16[256,512]{1,0:T(8,128)(2,1)S(1)}, u32[]{:S(2)}, u32[]{:S(2)}) %collective-permute-start.50) | collective-permute-done | bytes 262176 | tf_op jit(solution)/shard_map/ppermute | solution.py:470
  384.7 3.8 collective-permute-done.61
  388.7 3.6 collective-permute-done.51
  392.3 3.4 collective-permute-start.62
  397.4 2.4 collective-permute-start.52
  416.8 7.6 %source_grad.1 = bf16[512,1024]{1,0:T(8,128)(2,1)} custom-call(s32[2]{0:T(128)S(1)} %copy-done.50, f32[512,1024]{1,0:T(8,128)} %get-tuple-element.77.refs_0_, bf16[512,1024]{1,0:T(8,128)(2,1)} %copy-done.64, bf16[256,1024]{1,0:T(8,128)(2,1)S(1)} %copy-done.28, bf16[256,1024]{1,0:T(8,128)(2,1)S(1)} %copy-done.37, bf16[256,1024]{1,0:T(8,128)(2,1)S(1)} %copy-done.31, ...), custom_call_target="tpu_custom_call" | custom-call | flops 2147483648 | bytes 14680064 | tf_op jit(solution)/shard_map/source_grad/pallas_call | solution.py:208
  425.7 12.4 %collective-permute-start.47 = (bf16[256,1024]{1,0:T(8,128)(2,1)S(1)}, bf16[256,1024]{1,0:T(8,128)(2,1)S(1)}, u32[]{:S(2)}, u32[]{:S(2)}) collective-permute-start(bf16[256,1024]{1,0:T(8,128)(2,1)S(1)} %get-tuple-element.91), channel_id=1, source_target_pairs={{0,0},{1,3},{2,4},{3,7},{4,2},{5,1},{6,6},{7,5},{8,8},{9,11},{10,1... | collective-permute-start | bytes 1572872 | tf_op jit(solution)/shard_map/ppermute | solution.py:470
  440.8 8.6 %token_grad.1 = bf16[512,1024]{1,0:T(8,128)(2,1)} custom-call(s32[2]{0:T(128)S(1)} %copy-done.50, f32[512,1024]{1,0:T(8,128)} %get-tuple-element.69.refs_0_, bf16[512,1024]{1,0:T(8,128)(2,1)} %get-tuple-element.72.refs_1_, bf16[256,1024]{1,0:T(8,128)(2,1)S(1)} %copy-done.28, bf16[256,1024]{1,0:T(8,128)(2,1)S(1)} %copy-done.37, ...), custom_call_target="tpu_custom_call" | custom-call | flops 3221225472 | bytes 17825792 | tf_op jit(solution)/shard_map/token_grad/pallas_call | solution.py:208
  452.6 2.5 collective-permute-start.44
  455.3 5.1 %collective-permute-done.66 = bf16[64,1024]{1,0:T(8,128)(2,1)S(1)} collective-permute-done((bf16[64,1024]{1,0:T(8,128)(2,1)S(1)}, bf16[64,1024]{1,0:T(8,128)(2,1)S(1)}, u32[]{:S(2)}, u32[]{:S(2)}) %collective-permute-start.66) | collective-permute-done | bytes 131104 | tf_op jit(solution)/shard_map/ppermute | solution.py:470
  460.6 4.1 collective-permute-done.56
  465.0 6.0 %collective-permute-done.67 = bf16[128,1024]{1,0:T(8,128)(2,1)S(1)} collective-permute-done((bf16[128,1024]{1,0:T(8,128)(2,1)S(1)}, bf16[128,1024]{1,0:T(8,128)(2,1)S(1)}, u32[]{:S(2)}, u32[]{:S(2)}) %collective-permute-start.67) | collective-permute-done | bytes 262176 | tf_op jit(solution)/shard_map/ppermute | solution.py:470
  471.1 5.0 %collective-permute-done.57 = bf16[256,512]{1,0:T(8,128)(2,1)S(1)} collective-permute-done((bf16[256,512]{1,0:T(8,128)(2,1)S(1)}, bf16[256,512]{1,0:T(8,128)(2,1)S(1)}, u32[]{:S(2)}, u32[]{:S(2)}) %collective-permute-start.57) | collective-permute-done | bytes 262176 | tf_op jit(solution)/shard_map/ppermute | solution.py:470
  476.2 3.7 collective-permute-start.68
  (369 shorter events, 103.4 us)
Async XLA Ops:
  7.2 221.0 %all-gather.3.cloned.1.call-start = ((), (), s32[]{:S(2)}) async-start(), calls=%async_computation | async-start | bytes 9437184 | tf_op jit(solution)/shard_map/all_gather | solution.py:580
  8.0 235.2 %all-gather.5.cloned.1.call-start = ((), (), s32[]{:S(2)}) async-start(), calls=%async_computation.1 | async-start | bytes 9437184 | tf_op jit(solution)/shard_map/all_gather | solution.py:581
  8.8 27.2 %collective-permute-start.3 = (bf16[256,1024]{1,0:T(8,128)(2,1)S(1)}, bf16[256,1024]{1,0:T(8,128)(2,1)S(1)}, u32[]{:S(2)}, u32[]{:S(2)}) collective-permute-start(bf16[256,1024]{1,0:T(8,128)(2,1)S(1)} %constant_dynamic-update-slice_fusion.refs_1_.refs_2_), channel_id=1, source_target_pairs={{0,8},{1,9},{2,10},{3,11},{4,12},{5,13},{6,14},{7,15},{8,0},{9,1},... | collective-permute-start | bytes 1572872 | tf_op jit(solution)/shard_map/ppermute | solution.py:470
  10.9 33.2 %collective-permute-start.5 = (bf16[256,1024]{1,0:T(8,128)(2,1)S(1)}, bf16[256,1024]{1,0:T(8,128)(2,1)S(1)}, u32[]{:S(2)}, u32[]{:S(2)}) collective-permute-start(bf16[256,1024]{1,0:T(8,128)(2,1)S(1)} %constant_dynamic-update-slice_fusion.refs_1_.refs_2_), channel_id=1, source_target_pairs={{0,16},{1,17},{2,18},{3,19},{4,20},{5,21},{6,22},{7,23},{8,24},{9,... | collective-permute-start | bytes 1572872 | tf_op jit(solution)/shard_map/ppermute | solution.py:470
  13.0 16.9 %collective-permute-start = (bf16[256,1024]{1,0:T(8,128)(2,1)S(1)}, bf16[256,1024]{1,0:T(8,128)(2,1)}, u32[]{:S(2)}, u32[]{:S(2)}) collective-permute-start(bf16[256,1024]{1,0:T(8,128)(2,1)S(1)} %get-tuple-element.111), channel_id=1, source_target_pairs={{0,0},{1,5},{2,4},{3,1},{4,2},{5,7},{6,6},{7,3},{8,8},{9,13},{10,1... | collective-permute-start | bytes 1572872 | tf_op jit(solution)/shard_map/ppermute | solution.py:470
  18.3 17.4 %collective-permute-start.1 = (bf16[256,1024]{1,0:T(8,128)(2,1)}, bf16[256,1024]{1,0:T(8,128)(2,1)}, u32[]{:S(2)}, u32[]{:S(2)}) collective-permute-start(bf16[256,1024]{1,0:T(8,128)(2,1)} %get-tuple-element.112), channel_id=1, source_target_pairs={{0,1},{1,4},{2,5},{3,0},{4,3},{5,6},{6,7},{7,2},{8,9},{9,12},{10,1... | collective-permute-start | bytes 1572872 | tf_op jit(solution)/shard_map/ppermute | solution.py:470
  25.3 21.8 %collective-permute-start.12 = (bf16[256,1024]{1,0:T(8,128)(2,1)}, bf16[256,1024]{1,0:T(8,128)(2,1)}, u32[]{:S(2)}, u32[]{:S(2)}) collective-permute-start(bf16[256,1024]{1,0:T(8,128)(2,1)} %constant_dynamic-update-slice_fusion.2.refs_9_.refs_12_), channel_id=1, source_target_pairs={{0,16},{1,17},{2,18},{3,19},{4,20},{5,21},{6,22},{7,23},{8,24},{9,... | collective-permute-start | bytes 1572872 | tf_op jit(solution)/shard_map/ppermute | solution.py:470
  30.0 18.2 %collective-permute-start.2 = (bf16[256,1024]{1,0:T(8,128)(2,1)S(1)}, bf16[256,1024]{1,0:T(8,128)(2,1)S(1)}, u32[]{:S(2)}, u32[]{:S(2)}) collective-permute-start(bf16[256,1024]{1,0:T(8,128)(2,1)S(1)} %constant_dynamic-update-slice_fusion.refs_1_.refs_2_), channel_id=1, source_target_pairs={{0,4},{1,5},{2,6},{3,7},{4,0},{5,1},{6,2},{7,3},{8,12},{9,13},{10,... | collective-permute-start | bytes 1572872 | tf_op jit(solution)/shard_map/ppermute | solution.py:470
  35.7 13.7 %collective-permute-start.10 = (bf16[256,1024]{1,0:T(8,128)(2,1)}, bf16[256,1024]{1,0:T(8,128)(2,1)}, u32[]{:S(2)}, u32[]{:S(2)}) collective-permute-start(bf16[256,1024]{1,0:T(8,128)(2,1)} %constant_dynamic-update-slice_fusion.2.refs_9_.refs_12_), channel_id=1, source_target_pairs={{0,8},{1,9},{2,10},{3,11},{4,12},{5,13},{6,14},{7,15},{8,0},{9,1},... | collective-permute-start | bytes 1572872 | tf_op jit(solution)/shard_map/ppermute | solution.py:470
  36.0 13.6 %collective-permute-start.9 = (bf16[256,1024]{1,0:T(8,128)(2,1)}, bf16[256,1024]{1,0:T(8,128)(2,1)}, u32[]{:S(2)}, u32[]{:S(2)}) collective-permute-start(bf16[256,1024]{1,0:T(8,128)(2,1)} %constant_dynamic-update-slice_fusion.2.refs_9_.refs_12_), channel_id=1, source_target_pairs={{0,4},{1,5},{2,6},{3,7},{4,0},{5,1},{6,2},{7,3},{8,12},{9,13},{10,... | collective-permute-start | bytes 1572872 | tf_op jit(solution)/shard_map/ppermute | solution.py:470
  44.1 18.7 %collective-permute-start.20 = (bf16[256,1024]{1,0:T(8,128)(2,1)S(1)}, bf16[256,1024]{1,0:T(8,128)(2,1)S(1)}, u32[]{:S(2)}, u32[]{:S(2)}) collective-permute-start(bf16[256,1024]{1,0:T(8,128)(2,1)S(1)} %constant_dynamic-update-slice_fusion.4.refs_2_.refs_9_.refs_12_), channel_id=1, source_target_pairs={{0,8},{1,9},{2,10},{3,11},{4,12},{5,13},{6,14},{7,15},{8,0},{9,1},... | collective-permute-start | bytes 1572872 | tf_op jit(solution)/shard_map/ppermute | solution.py:470
  47.1 27.6 %collective-permute-start.29 = (bf16[256,1024]{1,0:T(8,128)(2,1)S(1)}, bf16[256,1024]{1,0:T(8,128)(2,1)S(1)}, u32[]{:S(2)}, u32[]{:S(2)}) collective-permute-start(bf16[256,1024]{1,0:T(8,128)(2,1)S(1)} %constant_dynamic-update-slice_fusion.6.refs_10_.refs_2_.refs_0_), channel_id=1, source_target_pairs={{0,16},{1,17},{2,18},{3,19},{4,20},{5,21},{6,22},{7,23},{8,24},{9,... | collective-permute-start | bytes 1572872 | tf_op jit(solution)/shard_map/ppermute | solution.py:470
  49.0 39.7 %collective-permute-start.22 = (bf16[256,1024]{1,0:T(8,128)(2,1)S(1)}, bf16[256,1024]{1,0:T(8,128)(2,1)S(1)}, u32[]{:S(2)}, u32[]{:S(2)}) collective-permute-start(bf16[256,1024]{1,0:T(8,128)(2,1)S(1)} %constant_dynamic-update-slice_fusion.4.refs_2_.refs_9_.refs_12_), channel_id=1, source_target_pairs={{0,16},{1,17},{2,18},{3,19},{4,20},{5,21},{6,22},{7,23},{8,24},{9,... | collective-permute-start | bytes 1572872 | tf_op jit(solution)/shard_map/ppermute | solution.py:470
  49.4 45.9 %collective-permute-start.27 = (bf16[256,1024]{1,0:T(8,128)(2,1)S(1)}, bf16[256,1024]{1,0:T(8,128)(2,1)S(1)}, u32[]{:S(2)}, u32[]{:S(2)}) collective-permute-start(bf16[256,1024]{1,0:T(8,128)(2,1)S(1)} %constant_dynamic-update-slice_fusion.6.refs_10_.refs_2_.refs_0_), channel_id=1, source_target_pairs={{0,8},{1,9},{2,10},{3,11},{4,12},{5,13},{6,14},{7,15},{8,0},{9,1},... | collective-permute-start | bytes 1572872 | tf_op jit(solution)/shard_map/ppermute | solution.py:470
  49.5 53.4 %collective-permute-start.19 = (bf16[256,1024]{1,0:T(8,128)(2,1)S(1)}, bf16[256,1024]{1,0:T(8,128)(2,1)S(1)}, u32[]{:S(2)}, u32[]{:S(2)}) collective-permute-start(bf16[256,1024]{1,0:T(8,128)(2,1)S(1)} %constant_dynamic-update-slice_fusion.4.refs_2_.refs_9_.refs_12_), channel_id=1, source_target_pairs={{0,4},{1,5},{2,6},{3,7},{4,0},{5,1},{6,2},{7,3},{8,12},{9,13},{10,... | collective-permute-start | bytes 1572872 | tf_op jit(solution)/shard_map/ppermute | solution.py:470
  62.8 41.0 %collective-permute-start.26 = (bf16[256,1024]{1,0:T(8,128)(2,1)S(1)}, bf16[256,1024]{1,0:T(8,128)(2,1)}, u32[]{:S(2)}, u32[]{:S(2)}) collective-permute-start(bf16[256,1024]{1,0:T(8,128)(2,1)S(1)} %constant_dynamic-update-slice_fusion.6.refs_10_.refs_2_.refs_0_), channel_id=1, source_target_pairs={{0,4},{1,5},{2,6},{3,7},{4,0},{5,1},{6,2},{7,3},{8,12},{9,13},{10,... | collective-permute-start | bytes 1572872 | tf_op jit(solution)/shard_map/ppermute | solution.py:470
  74.7 29.1 %collective-permute-start.33 = (bf16[256,1024]{1,0:T(8,128)(2,1)}, bf16[256,1024]{1,0:T(8,128)(2,1)}, u32[]{:S(2)}, u32[]{:S(2)}) collective-permute-start(bf16[256,1024]{1,0:T(8,128)(2,1)} %get-tuple-element.107), channel_id=1, source_target_pairs={{0,0},{1,5},{2,4},{3,1},{4,2},{5,7},{6,6},{7,3},{8,8},{9,13},{10,1... | collective-permute-start | bytes 1572872 | tf_op jit(solution)/shard_map/ppermute | solution.py:470
  88.7 20.2 %collective-permute-start.34 = (bf16[256,1024]{1,0:T(8,128)(2,1)}, bf16[256,1024]{1,0:T(8,128)(2,1)}, u32[]{:S(2)}, u32[]{:S(2)}) collective-permute-start(bf16[256,1024]{1,0:T(8,128)(2,1)} %get-tuple-element.108), channel_id=1, source_target_pairs={{0,1},{1,4},{2,5},{3,0},{4,3},{5,6},{6,7},{7,2},{8,9},{9,12},{10,1... | collective-permute-start | bytes 1572872 | tf_op jit(solution)/shard_map/ppermute | solution.py:470
  95.4 24.7 %collective-permute-start.37 = (bf16[256,1024]{1,0:T(8,128)(2,1)}, bf16[256,1024]{1,0:T(8,128)(2,1)}, u32[]{:S(2)}, u32[]{:S(2)}) collective-permute-start(bf16[256,1024]{1,0:T(8,128)(2,1)} %get-tuple-element.103), channel_id=1, source_target_pairs={{0,0},{1,5},{2,4},{3,1},{4,2},{5,7},{6,6},{7,3},{8,8},{9,13},{10,1... | collective-permute-start | bytes 1572872 | tf_op jit(solution)/shard_map/ppermute | solution.py:470
  102.9 18.5 %collective-permute-start.7 = (bf16[256,1024]{1,0:T(8,128)(2,1)}, bf16[256,1024]{1,0:T(8,128)(2,1)}, u32[]{:S(2)}, u32[]{:S(2)}) collective-permute-start(bf16[256,1024]{1,0:T(8,128)(2,1)} %copy-done.29), channel_id=1, source_target_pairs={{0,16},{1,17},{2,18},{3,19},{4,20},{5,21},{6,22},{7,23},{8,24},{9,... | collective-permute-start | bytes 1572872 | tf_op jit(solution)/shard_map/ppermute | solution.py:470
  103.8 19.2 %collective-permute-start.4 = (bf16[256,1024]{1,0:T(8,128)(2,1)}, bf16[256,1024]{1,0:T(8,128)(2,1)S(1)}, u32[]{:S(2)}, u32[]{:S(2)}) collective-permute-start(bf16[256,1024]{1,0:T(8,128)(2,1)} %copy-done.29), channel_id=1, source_target_pairs={{0,4},{1,5},{2,6},{3,7},{4,0},{5,1},{6,2},{7,3},{8,12},{9,13},{10,... | collective-permute-start | bytes 1572872 | tf_op jit(solution)/shard_map/ppermute | solution.py:470
  103.9 19.7 %collective-permute-start.14 = (bf16[256,1024]{1,0:T(8,128)(2,1)}, bf16[256,1024]{1,0:T(8,128)(2,1)S(1)}, u32[]{:S(2)}, u32[]{:S(2)}) collective-permute-start(bf16[256,1024]{1,0:T(8,128)(2,1)} %collective-permute-done.12.refs_13_.refs_16_), channel_id=1, source_target_pairs={{0,8},{1,9},{2,10},{3,11},{4,12},{5,13},{6,14},{7,15},{8,0},{9,1},... | collective-permute-start | bytes 1572872 | tf_op jit(solution)/shard_map/ppermute | solution.py:470
  108.9 18.4 %collective-permute-start.13 = (bf16[256,1024]{1,0:T(8,128)(2,1)}, bf16[256,1024]{1,0:T(8,128)(2,1)S(1)}, u32[]{:S(2)}, u32[]{:S(2)}) collective-permute-start(bf16[256,1024]{1,0:T(8,128)(2,1)} %collective-permute-done.12.refs_13_.refs_16_), channel_id=1, source_target_pairs={{0,4},{1,5},{2,6},{3,7},{4,0},{5,1},{6,2},{7,3},{8,12},{9,13},{10,... | collective-permute-start | bytes 1572872 | tf_op jit(solution)/shard_map/ppermute | solution.py:470
  127.0 19.2 %collective-permute-start.38 = (bf16[256,1024]{1,0:T(8,128)(2,1)}, bf16[256,1024]{1,0:T(8,128)(2,1)S(1)}, u32[]{:S(2)}, u32[]{:S(2)}) collective-permute-start(bf16[256,1024]{1,0:T(8,128)(2,1)} %get-tuple-element.104), channel_id=1, source_target_pairs={{0,1},{1,4},{2,5},{3,0},{4,3},{5,6},{6,7},{7,2},{8,9},{9,12},{10,1... | collective-permute-start | bytes 1572872 | tf_op jit(solution)/shard_map/ppermute | solution.py:470
  127.3 17.3 %collective-permute-start.24 = (bf16[256,1024]{1,0:T(8,128)(2,1)S(1)}, bf16[256,1024]{1,0:T(8,128)(2,1)S(1)}, u32[]{:S(2)}, u32[]{:S(2)}) collective-permute-start(bf16[256,1024]{1,0:T(8,128)(2,1)S(1)} %collective-permute-done.20.refs_4_.refs_11_.refs_14_), channel_id=1, source_target_pairs={{0,16},{1,17},{2,18},{3,19},{4,20},{5,21},{6,22},{7,23},{8,24},{9,... | collective-permute-start | bytes 1572872 | tf_op jit(solution)/shard_map/ppermute | solution.py:470
  129.1 17.2 %collective-permute-start.31 = (bf16[256,1024]{1,0:T(8,128)(2,1)S(1)}, bf16[256,1024]{1,0:T(8,128)(2,1)S(1)}, u32[]{:S(2)}, u32[]{:S(2)}) collective-permute-start(bf16[256,1024]{1,0:T(8,128)(2,1)S(1)} %collective-permute-done.29.refs_14_.refs_6_.refs_4_), channel_id=1, source_target_pairs={{0,8},{1,9},{2,10},{3,11},{4,12},{5,13},{6,14},{7,15},{8,0},{9,1},... | collective-permute-start | bytes 1572872 | tf_op jit(solution)/shard_map/ppermute | solution.py:470
  131.6 17.9 %collective-permute-start.21 = (bf16[256,1024]{1,0:T(8,128)(2,1)S(1)}, bf16[256,1024]{1,0:T(8,128)(2,1)S(1)}, u32[]{:S(2)}, u32[]{:S(2)}) collective-permute-start(bf16[256,1024]{1,0:T(8,128)(2,1)S(1)} %collective-permute-done.20.refs_4_.refs_11_.refs_14_), channel_id=1, source_target_pairs={{0,4},{1,5},{2,6},{3,7},{4,0},{5,1},{6,2},{7,3},{8,12},{9,13},{10,... | collective-permute-start | bytes 1572872 | tf_op jit(solution)/shard_map/ppermute | solution.py:470
  132.3 17.3 %collective-permute-start.23 = (bf16[256,1024]{1,0:T(8,128)(2,1)S(1)}, bf16[256,1024]{1,0:T(8,128)(2,1)S(1)}, u32[]{:S(2)}, u32[]{:S(2)}) collective-permute-start(bf16[256,1024]{1,0:T(8,128)(2,1)S(1)} %collective-permute-done.22.refs_6_.refs_13_.refs_16_), channel_id=1, source_target_pairs={{0,4},{1,5},{2,6},{3,7},{4,0},{5,1},{6,2},{7,3},{8,12},{9,13},{10,... | collective-permute-start | bytes 1572872 | tf_op jit(solution)/shard_map/ppermute | solution.py:470
  146.2 18.5 %collective-permute-start.16 = (bf16[512,1024]{1,0:T(8,128)(2,1)}, bf16[512,1024]{1,0:T(8,128)(2,1)S(1)}, u32[]{:S(2)}, u32[]{:S(2)}) collective-permute-start(bf16[512,1024]{1,0:T(8,128)(2,1)} %get-tuple-element.45.ko), channel_id=1, source_target_pairs={{0,4},{1,5},{2,6},{3,7},{4,0},{5,1},{6,2},{7,3},{8,12},{9,13},{10,... | collective-permute-start | bytes 3145736 | tf_op jit(solution)/shard_map/ppermute | solution.py:470
  146.3 18.4 %collective-permute-start.17 = (bf16[512,1024]{1,0:T(8,128)(2,1)}, bf16[512,1024]{1,0:T(8,128)(2,1)S(1)}, u32[]{:S(2)}, u32[]{:S(2)}) collective-permute-start(bf16[512,1024]{1,0:T(8,128)(2,1)} %get-tuple-element.46.vo), channel_id=1, source_target_pairs={{0,4},{1,5},{2,6},{3,7},{4,0},{5,1},{6,2},{7,3},{8,12},{9,13},{10,... | collective-permute-start | bytes 3145736 | tf_op jit(solution)/shard_map/ppermute | solution.py:470
  149.5 9.2 %collective-permute-start.30 = (bf16[256,1024]{1,0:T(8,128)(2,1)S(1)}, bf16[256,1024]{1,0:T(8,128)(2,1)S(1)}, u32[]{:S(2)}, u32[]{:S(2)}) collective-permute-start(bf16[256,1024]{1,0:T(8,128)(2,1)S(1)} %collective-permute-done.29.refs_14_.refs_6_.refs_4_), channel_id=1, source_target_pairs={{0,4},{1,5},{2,6},{3,7},{4,0},{5,1},{6,2},{7,3},{8,12},{9,13},{10,... | collective-permute-start | bytes 1572872 | tf_op jit(solution)/shard_map/ppermute | solution.py:470
  149.6 9.3 %collective-permute-start.28 = (bf16[256,1024]{1,0:T(8,128)(2,1)S(1)}, bf16[256,1024]{1,0:T(8,128)(2,1)S(1)}, u32[]{:S(2)}, u32[]{:S(2)}) collective-permute-start(bf16[256,1024]{1,0:T(8,128)(2,1)S(1)} %copy-done.13), channel_id=1, source_target_pairs={{0,4},{1,5},{2,6},{3,7},{4,0},{5,1},{6,2},{7,3},{8,12},{9,13},{10,... | collective-permute-start | bytes 1572872 | tf_op jit(solution)/shard_map/ppermute | solution.py:470
  158.7 33.0 %collective-permute-start.35 = (bf16[512,1024]{1,0:T(8,128)(2,1)}, bf16[512,1024]{1,0:T(8,128)(2,1)S(1)}, u32[]{:S(2)}, u32[]{:S(2)}) collective-permute-start(bf16[512,1024]{1,0:T(8,128)(2,1)} %get-tuple-element.50.ko), channel_id=1, source_target_pairs={{0,4},{1,5},{2,6},{3,7},{4,0},{5,1},{6,2},{7,3},{8,12},{9,13},{10,... | collective-permute-start | bytes 3145736 | tf_op jit(solution)/shard_map/ppermute | solution.py:470
  158.9 32.9 %collective-permute-start.36 = (bf16[512,1024]{1,0:T(8,128)(2,1)}, bf16[512,1024]{1,0:T(8,128)(2,1)}, u32[]{:S(2)}, u32[]{:S(2)}) collective-permute-start(bf16[512,1024]{1,0:T(8,128)(2,1)} %get-tuple-element.51.vo), channel_id=1, source_target_pairs={{0,4},{1,5},{2,6},{3,7},{4,0},{5,1},{6,2},{7,3},{8,12},{9,13},{10,... | collective-permute-start | bytes 3145736 | tf_op jit(solution)/shard_map/ppermute | solution.py:470
  265.7 90.9 %collective-permute-start.59 = (bf16[256,1024]{1,0:T(8,128)(2,1)}, bf16[256,1024]{1,0:T(8,128)(2,1)}, u32[]{:S(2)}, u32[]{:S(2)}) collective-permute-start(bf16[256,1024]{1,0:T(8,128)(2,1)} %select_convert_fusion), channel_id=1, source_target_pairs={{0,4},{1,5},{2,6},{3,7},{4,0},{5,1},{6,2},{7,3},{8,12},{9,13},{10,... | collective-permute-start | bytes 1572872 | tf_op jit(solution)/shard_map/ppermute | solution.py:470
  269.2 89.0 %collective-permute-start.49 = (bf16[512,512]{1,0:T(8,128)(2,1)}, bf16[512,512]{1,0:T(8,128)(2,1)}, u32[]{:S(2)}, u32[]{:S(2)}) collective-permute-start(bf16[512,512]{1,0:T(8,128)(2,1)} %select_convert_fusion.1), channel_id=1, source_target_pairs={{0,4},{1,5},{2,6},{3,7},{4,0},{5,1},{6,2},{7,3},{8,12},{9,13},{10,... | collective-permute-start | bytes 1572872 | tf_op jit(solution)/shard_map/ppermute | solution.py:470
  315.7 100.1 %collective-permute-start.45 = (bf16[512,1024]{1,0:T(8,128)(2,1)}, bf16[512,1024]{1,0:T(8,128)(2,1)S(1)}, u32[]{:S(2)}, u32[]{:S(2)}) collective-permute-start(bf16[512,1024]{1,0:T(8,128)(2,1)} %get-tuple-element.78), channel_id=1, source_target_pairs={{0,4},{1,5},{2,6},{3,7},{4,0},{5,1},{6,2},{7,3},{8,12},{9,13},{10,... | collective-permute-start | bytes 3145736 | tf_op jit(solution)/shard_map/ppermute | solution.py:470
  316.3 99.7 %collective-permute-start.46 = (bf16[512,1024]{1,0:T(8,128)(2,1)}, bf16[512,1024]{1,0:T(8,128)(2,1)}, u32[]{:S(2)}, u32[]{:S(2)}) collective-permute-start(bf16[512,1024]{1,0:T(8,128)(2,1)} %get-tuple-element.80), channel_id=1, source_target_pairs={{0,4},{1,5},{2,6},{3,7},{4,0},{5,1},{6,2},{7,3},{8,12},{9,13},{10,... | collective-permute-start | bytes 3145736 | tf_op jit(solution)/shard_map/ppermute | solution.py:470
  317.4 42.6 %collective-permute-start.39 = (bf16[256,1024]{1,0:T(8,128)(2,1)}, bf16[256,1024]{1,0:T(8,128)(2,1)}, u32[]{:S(2)}, u32[]{:S(2)}) collective-permute-start(bf16[256,1024]{1,0:T(8,128)(2,1)} %get-tuple-element.99), channel_id=1, source_target_pairs={{0,0},{1,3},{2,4},{3,7},{4,2},{5,1},{6,6},{7,5},{8,8},{9,11},{10,1... | collective-permute-start | bytes 1572872 | tf_op jit(solution)/shard_map/ppermute | solution.py:470
  356.6 15.7 %collective-permute-start.40 = (bf16[256,1024]{1,0:T(8,128)(2,1)S(1)}, bf16[256,1024]{1,0:T(8,128)(2,1)S(1)}, u32[]{:S(2)}, u32[]{:S(2)}) collective-permute-start(bf16[256,1024]{1,0:T(8,128)(2,1)S(1)} %copy-done.73), channel_id=1, source_target_pairs={{0,3},{1,0},{2,7},{3,4},{4,1},{5,2},{6,5},{7,6},{8,11},{9,8},{10,1... | collective-permute-start | bytes 1572872 | tf_op jit(solution)/shard_map/ppermute | solution.py:470
  358.2 79.9 %collective-permute-start.41 = (bf16[512,1024]{1,0:T(8,128)(2,1)S(1)}, bf16[512,1024]{1,0:T(8,128)(2,1)S(1)}, u32[]{:S(2)}, u32[]{:S(2)}) collective-permute-start(bf16[512,1024]{1,0:T(8,128)(2,1)S(1)} %copy-done.80), channel_id=1, source_target_pairs={{0,4},{1,5},{2,6},{3,7},{4,0},{5,1},{6,2},{7,3},{8,12},{9,13},{10,... | collective-permute-start | bytes 3145736 | tf_op jit(solution)/shard_map/ppermute | solution.py:470
  360.0 79.8 %collective-permute-start.42 = (bf16[512,1024]{1,0:T(8,128)(2,1)S(1)}, bf16[512,1024]{1,0:T(8,128)(2,1)S(1)}, u32[]{:S(2)}, u32[]{:S(2)}) collective-permute-start(bf16[512,1024]{1,0:T(8,128)(2,1)S(1)} %copy-done.78), channel_id=1, source_target_pairs={{0,4},{1,5},{2,6},{3,7},{4,0},{5,1},{6,2},{7,3},{8,12},{9,13},{10,... | collective-permute-start | bytes 3145736 | tf_op jit(solution)/shard_map/ppermute | solution.py:470
  413.5 39.1 %collective-permute-start.65 = (bf16[32,1024]{1,0:T(8,128)(2,1)S(1)}, bf16[32,1024]{1,0:T(8,128)(2,1)S(1)}, u32[]{:S(2)}, u32[]{:S(2)}) collective-permute-start(bf16[32,1024]{1,0:T(8,128)(2,1)S(1)} %pad_maximum_fusion.13), channel_id=1, source_target_pairs={{0,2},{1,3},{2,0},{3,1},{4,6},{5,7},{6,4},{7,5},{8,10},{9,11},{10,... | collective-permute-start | bytes 196616 | tf_op jit(solution)/shard_map/ppermute | solution.py:470
  415.8 39.3 %collective-permute-start.55 = (bf16[64,512]{1,0:T(8,128)(2,1)S(1)}, bf16[64,512]{1,0:T(8,128)(2,1)S(1)}, u32[]{:S(2)}, u32[]{:S(2)}) collective-permute-start(bf16[64,512]{1,0:T(8,128)(2,1)S(1)} %pad_maximum_fusion.12), channel_id=1, source_target_pairs={{0,2},{1,3},{2,0},{3,1},{4,6},{5,7},{6,4},{7,5},{8,10},{9,11},{10,... | collective-permute-start | bytes 196616 | tf_op jit(solution)/shard_map/ppermute | solution.py:470
  425.7 54.3 %collective-permute-start.47 = (bf16[256,1024]{1,0:T(8,128)(2,1)S(1)}, bf16[256,1024]{1,0:T(8,128)(2,1)S(1)}, u32[]{:S(2)}, u32[]{:S(2)}) collective-permute-start(bf16[256,1024]{1,0:T(8,128)(2,1)S(1)} %get-tuple-element.91), channel_id=1, source_target_pairs={{0,0},{1,3},{2,4},{3,7},{4,2},{5,1},{6,6},{7,5},{8,8},{9,11},{10,1... | collective-permute-start | bytes 1572872 | tf_op jit(solution)/shard_map/ppermute | solution.py:470
  438.1 42.0 %collective-permute-start.48 = (bf16[256,1024]{1,0:T(8,128)(2,1)S(1)}, bf16[256,1024]{1,0:T(8,128)(2,1)S(1)}, u32[]{:S(2)}, u32[]{:S(2)}) collective-permute-start(bf16[256,1024]{1,0:T(8,128)(2,1)S(1)} %get-tuple-element.92), channel_id=1, source_target_pairs={{0,3},{1,0},{2,7},{3,4},{4,1},{5,2},{6,5},{7,6},{8,11},{9,8},{10,1... | collective-permute-start | bytes 1572872 | tf_op jit(solution)/shard_map/ppermute | solution.py:470
  450.6 30.5 %collective-permute-start.43 = (bf16[256,1024]{1,0:T(8,128)(2,1)S(1)}, bf16[256,1024]{1,0:T(8,128)(2,1)S(1)}, u32[]{:S(2)}, u32[]{:S(2)}) collective-permute-start(bf16[256,1024]{1,0:T(8,128)(2,1)S(1)} %get-tuple-element.95), channel_id=1, source_target_pairs={{0,0},{1,3},{2,4},{3,7},{4,2},{5,1},{6,6},{7,5},{8,8},{9,11},{10,1... | collective-permute-start | bytes 1572872 | tf_op jit(solution)/shard_map/ppermute | solution.py:470
  452.6 28.6 %collective-permute-start.44 = (bf16[256,1024]{1,0:T(8,128)(2,1)S(1)}, bf16[256,1024]{1,0:T(8,128)(2,1)S(1)}, u32[]{:S(2)}, u32[]{:S(2)}) collective-permute-start(bf16[256,1024]{1,0:T(8,128)(2,1)S(1)} %get-tuple-element.96), channel_id=1, source_target_pairs={{0,3},{1,0},{2,7},{3,4},{4,1},{5,2},{6,5},{7,6},{8,11},{9,8},{10,1... | collective-permute-start | bytes 1572872 | tf_op jit(solution)/shard_map/ppermute | solution.py:470
  (107 other events, 1291.3 us)
Sparse Core Ops, SparseCore 0:
  9.9 86.9 all-gather.2
  98.8 68.4 all-gather.4

commit v3 on v2

v3 whole, which is shorter than its diff:
```python
import functools
import jax
import jax.numpy as jnp
from jax.sharding import PartitionSpec as P
from jax import lax
from jax.experimental import pallas as pl
from jax.experimental.pallas import tpu as pltpu
BF=jnp.bfloat16; F32=jnp.float32
NEG=-1e30
LOG2E=1.4426950408889634

def cost(us):
    return pl.CostEstimate(flops=int(us * 1e9), bytes_accessed=1024, transcendentals=0)

VM=60*1024*1024

SELF_PLANS=(((((0,True),)), ((0,False),(2,False),(3,False),(1,True))),
            (((2,False),(0,True)), ((2,False),(0,False),(1,True))))
CROSS_PLANS=((((0,False),(1,False),(2,False),(3,False)),)*2,)

def nt(a,b): return lax.dot_general(a,b,(((1,),(1,)),((),())),preferred_element_type=F32)
def nn(a,b): return lax.dot_general(a,b,(((1,),(0,)),((),())),preferred_element_type=F32)

def half_mask(shape, h):
    l=lax.broadcasted_iota(jnp.int32, shape, 1)
    return (l<64) if h==0 else (l>=64)

def fwd_body(plan, C, q, ks, vs, qa, kas, o_ref, p_ref):
    n=0
    kaug=[[jnp.where(half_mask(k.shape,h),k,a) for k,a in zip(ks,kas)] for h in range(2)]
    vts=[v.T for v in vs]
    for slot,blocks in enumerate(plan):
        halves=[]
        for h in range(2):
            qs=q[slot*C:(slot+1)*C]; qas=qa[slot*C:(slot+1)*C]
            qh=jnp.where(half_mask(qs.shape,h),qs,qas)
            ss=[]
            for (kb,diag) in blocks:
                s=nt(kaug[h][kb],qh)
                if diag:
                    ki=lax.broadcasted_iota(jnp.int32,s.shape,0); qi=lax.broadcasted_iota(jnp.int32,s.shape,1)
                    s=jnp.where(ki<=qi,s,NEG)
                ss.append(s)
            m=functools.reduce(jnp.maximum,[jnp.max(s,axis=0,keepdims=True) for s in ss])
            ps=[jnp.exp2(s-m) for s in ss]
            l=functools.reduce(jnp.add,[jnp.sum(p,axis=0,keepdims=True) for p in ps])
            inv=1.0/l
            acc=None
            for i,((kb,_),p) in enumerate(zip(blocks,ps)):
                pb=(p*inv).astype(BF)
                p_ref[0,h,n+i]=pb
                t=nn(vts[kb][64*h:64*h+64],pb)
                acc=t if acc is None else acc+t
            halves.append(acc)
        n+=len(blocks)
        ot=jnp.concatenate(halves,axis=0)
        o_ref[slot*C:(slot+1)*C]=ot.T.astype(BF)

def fwd_kernel(plans, C, info, q_ref, ko, vo, kp, vp, qa, kao, kap, o_ref, p_ref):
    def run(plan):
        ks=[r[i*C:(i+1)*C] for r in (ko,kp) for i in range(2)]
        vs=[r[i*C:(i+1)*C] for r in (vo,vp) for i in range(2)]
        kas=[kao[0:C],kao[C:2*C],kap[0:C],kap[C:2*C]]
        fwd_body(plan,C,q_ref[...],ks,vs,qa[...],kas,o_ref,p_ref)
    if len(plans)==1: run(plans[0])
    else:
        for v,plan in enumerate(plans):
            pl.when(info[0]==v)(functools.partial(run,plan))

def attend(plans, info, q, own, peer, qa, kao, kap):
    T,D=q.shape; C=T//2; pairs=D//128
    nb=sum(len(b) for b in plans[0])
    col=pl.BlockSpec((T,128),lambda h,*_:(0,h))
    val=pl.BlockSpec((T,128),lambda h,*_:(0,pairs+h))
    fix=pl.BlockSpec((T,128),lambda h,*_:(0,0))
    return pl.pallas_call(
        functools.partial(fwd_kernel,plans,C),
        grid_spec=pltpu.PrefetchScalarGridSpec(num_scalar_prefetch=1,grid=(pairs,),
            in_specs=[col]+[col,val]*2+[fix]*3,
            out_specs=[col,pl.BlockSpec((1,2,nb,C,C),lambda h,*_:(h,0,0,0,0))]),
        out_shape=[jax.ShapeDtypeStruct((T,D),BF),jax.ShapeDtypeStruct((pairs,2,nb,C,C),BF)],
        compiler_params=pltpu.CompilerParams(vmem_limit_bytes=VM),
        cost_estimate=cost(20),
        name="attend")(info,q,own,own,peer,peer,qa,kao,kap)

def bwd_body(plan, C, q, ks, vs, do, o, p_ref, gq_ref, gown, gpeer):
    lane=lax.broadcasted_iota(jnp.int32,(C,128),1)
    l64=lax.rem(lane,64)
    ones=jnp.where(l64<2,1.0,0.0).astype(BF)
    vaug=[[jnp.where(half_mask(v.shape,h),v,ones) for v in vs] for h in range(2)]
    kts=[k.T for k in ks]
    gk=[None]*4; gv=[None]*4
    n=0
    zero=jnp.zeros((C,128),BF)
    for slot,blocks in enumerate(plan):
        halves=[]
        for h in range(2):
            hm=lane<64 if h==0 else lane>=64
            dos=do[slot*C:(slot+1)*C]; os=o[slot*C:(slot+1)*C]; qs=q[slot*C:(slot+1)*C]
            prod=jnp.where(hm,dos.astype(F32)*os.astype(F32),0.0)
            d=-jnp.sum(prod,axis=1,keepdims=True)
            hi=d.astype(BF); lo=(d-hi.astype(F32)).astype(BF)
            doa=jnp.where(hm,dos,jnp.where(l64==0,jnp.broadcast_to(hi,(C,128)),jnp.where(l64==1,jnp.broadcast_to(lo,(C,128)),zero)))
            dom=jnp.where(hm,dos,zero)
            qm=jnp.where(hm,qs,zero)
            acc=None
            for i,(kb,_) in enumerate(blocks):
                pb=p_ref[0,h,n+i]
                dp=nt(vaug[h][kb],doa)
                ds=(pb.astype(F32)*dp).astype(BF)
                a=nn(pb,dom); gv[kb]=a if gv[kb] is None else gv[kb]+a
                b=nn(ds,qm); gk[kb]=b if gk[kb] is None else gk[kb]+b
                t=nn(kts[kb][64*h:64*h+64],ds)
                acc=t if acc is None else acc+t
            halves.append(acc)
        n+=len(blocks)
        gq_ref[slot*C:(slot+1)*C]=jnp.concatenate(halves,axis=0).T.astype(BF)
    for kb in range(4):
        ref=gown if kb<2 else gpeer
        sl=slice((kb%2)*C,(kb%2)*C+C)
        z=jnp.zeros((C,128),F32)
        ref[sl,0:128]=((gk[kb] if gk[kb] is not None else z)*(1.0/LOG2E)).astype(ref.dtype)
        ref[sl,128:256]=(gv[kb] if gv[kb] is not None else z).astype(ref.dtype)

def bwd_kernel(plans, C, info, q_ref, ko, vo, kp, vp, do, o, p_ref, *refs):
    gq, gown, gpeer = refs[-3:]
    def run(plan):
        ks=[r[i*C:(i+1)*C] for r in (ko,kp) for i in range(2)]
        vs=[r[i*C:(i+1)*C] for r in (vo,vp) for i in range(2)]
        bwd_body(plan,C,q_ref[...],ks,vs,do[...],o[...],p_ref,gq,gown,gpeer)
    if len(plans)==1: run(plans[0])
    else:
        for v,plan in enumerate(plans):
            pl.when(info[0]==v)(functools.partial(run,plan))

def attend_back(plans, info, q, own, peer, do, o, p, deps=()):
    T,D=q.shape; C=T//2; pairs=D//128
    nb=p.shape[2]
    col=pl.BlockSpec((T,128),lambda h,*_:(0,h))
    wide=pl.BlockSpec((T,256),lambda h,*_:(0,h))
    val=pl.BlockSpec((T,128),lambda h,*_:(0,pairs+h))
    return pl.pallas_call(
        functools.partial(bwd_kernel,plans,C),
        grid_spec=pltpu.PrefetchScalarGridSpec(num_scalar_prefetch=1,grid=(pairs,),
            in_specs=[col]+[col,val]*2+[col]*2+[pl.BlockSpec((1,2,nb,C,C),lambda h,*_:(h,0,0,0,0))]+[pl.BlockSpec(memory_space=pl.ANY)]*len(deps),
            out_specs=[col]+[wide]*2),
        out_shape=[jax.ShapeDtypeStruct((T,D),BF),jax.ShapeDtypeStruct((T,2*D),F32),jax.ShapeDtypeStruct((T,2*D),BF)],
        compiler_params=pltpu.CompilerParams(vmem_limit_bytes=VM),
        cost_estimate=cost(22),
        name="attend_back")(info,q,own,own,peer,peer,do,o,p,*deps)


def vmem(mib):
    return pltpu.CompilerParams(vmem_limit_bytes=mib * 1024 * 1024)


class Piece:
    def __init__(self, parts, at, rows, stride=None, base=0):
        self.parts, self.at, self.rows, self.stride, self.base = parts, at, rows, stride or rows, base
        self.cols, self.dtype = parts[0][0].shape[1], parts[0][0].dtype


def shape_of(load):
    if not isinstance(load, list):
        return load.shape, load.dtype
    return (8 * load[0].stride, load[0].cols), load[0].dtype


def copies_of(load, refs, buf, owner, sem, first):
    if not isinstance(load, list):
        return [pltpu.make_async_copy(refs[0], buf, sem.at[first])]
    out = []
    for j, piece in enumerate(load):
        for m in range(8):
            to = pl.multiple_of((owner ^ m) * piece.stride + piece.base, 16)
            out.append(
                pltpu.make_async_copy(
                    refs[8 * j + m].at[pl.ds(piece.parts[m][1] + piece.at, piece.rows)],
                    buf.at[pl.ds(to, piece.rows)],
                    sem.at[first + 8 * j + m],
                )
            )
    return out


def arrays_of(load):
    return [a for piece in load for a, _ in piece.parts] if isinstance(load, list) else [load]


def gate(values, deps):
    def kernel(*refs):
        del refs

    n = len(values)
    anywhere = pl.BlockSpec(memory_space=pl.ANY)
    return pl.pallas_call(
        kernel,
        in_specs=[anywhere] * (n + len(deps)),
        out_specs=[anywhere] * n,
        out_shape=[jax.ShapeDtypeStruct(v.shape, v.dtype) for v in values],
        input_output_aliases={i: i for i in range(n)},
        cost_estimate=cost(0.1),
        name="gate",
    )(*values, *deps)


def barrier(*values):
    return gate(values, ())


def stage(expand_shard, contract_shard, deps):
    rows, cols = expand_shard.shape
    half = cols // 2

    def kernel(e_ref, c_ref, *refs):
        e1, e2, c = refs[-3:]
        e1[...] = e_ref[:, :half]
        e2[...] = e_ref[:, half:]
        c[...] = c_ref[...]

    full = pl.BlockSpec(memory_space=pltpu.VMEM)
    return pl.pallas_call(
        kernel,
        in_specs=[full, full] + [pl.BlockSpec(memory_space=pl.ANY)] * len(deps),
        out_specs=[full] * 3,
        out_shape=[jax.ShapeDtypeStruct((rows, half), BF)] * 2
        + [jax.ShapeDtypeStruct(contract_shard.shape, BF)],
        cost_estimate=cost(2),
        compiler_params=vmem(60),
        name="stage",
    )(expand_shard, contract_shard, *deps)


def fused(name, info, body, loads, outs, mib=60, deps=()):
    flat, places = [], []
    for load in loads:
        arrays = arrays_of(load)
        places.append((len(flat), len(arrays)))
        flat += arrays
    total, nout = len(flat), len(outs)

    def kernel(info_ref, *refs):
        out_refs = refs[total + len(deps) :][:nout]
        bufs, sem = refs[total + len(deps) + nout : -1], refs[-1]
        started = []
        for load, (first, count), buf in zip(loads, places, bufs):
            started.append(copies_of(load, refs[first : first + count], buf, info_ref[1], sem, first))
            for c in started[-1]:
                c.start()
        ready = set()

        def get(i):
            if i not in ready:
                for c in started[i]:
                    c.wait()
                ready.add(i)
            return bufs[i]

        body(info_ref, get, *out_refs)

    return pl.pallas_call(
        kernel,
        grid_spec=pltpu.PrefetchScalarGridSpec(
            num_scalar_prefetch=1,
            grid=(1,),
            in_specs=[pl.BlockSpec(memory_space=pl.ANY)] * (total + len(deps)),
            out_specs=[pl.BlockSpec(o.shape, lambda i, *_: (0, 0)) for o in outs],
            scratch_shapes=[pltpu.VMEM(*shape_of(load)) for load in loads] + [pltpu.SemaphoreType.DMA((total,))],
        ),
        out_shape=list(outs),
        compiler_params=vmem(mib),
        cost_estimate=cost(6),
        name=name,
    )(info, *flat, *deps)


def shape(rows, cols, dtype):
    return jax.ShapeDtypeStruct((rows, cols), dtype)


def norm_parts(v):
    mean = jnp.mean(v, axis=-1, keepdims=True)
    c = v - mean
    inv = lax.rsqrt(jnp.mean(c * c, axis=-1, keepdims=True) + 1e-05)
    return c * inv, inv


def norm_back(y, inv, g):
    return inv * (g - jnp.mean(g, axis=-1, keepdims=True) - y * jnp.mean(g * y, axis=-1, keepdims=True))


def gelu_pair(v):
    phi = 0.5 + 0.5 * lax.erf(v * 0.7071067811865476)
    pdf = jnp.exp(v * v * -0.5) * 0.3989422804014327
    return v * phi, phi + v * pdf


def tn(a, b):
    return lax.dot_general(a, b, (((0,), (0,)), ((), ())), preferred_element_type=F32)


def project_qkv(info, x, w_query, w_key, w_value, deps):
    T, D = x.shape

    def body(info_ref, get, q, kv):
        xv = get(0)[...]
        q[...] = (nn(xv, get(1)[...]) * (0.125 * LOG2E)).astype(BF)
        kv[:, :D] = nn(xv, get(2)[...]).astype(BF)
        kv[:, D:] = nn(xv, get(3)[...]).astype(BF)

    return fused("qkv", info, body, [x, w_query, w_key, w_value], [shape(T, D, BF), shape(T, 2 * D, BF)], deps=deps)


def project_source(info, x, w_key, w_value):
    T, D = x.shape

    def body(info_ref, get, kv):
        xv = get(0)[...]
        kv[:, :D] = nn(xv, get(1)[...]).astype(BF)
        kv[:, D:] = nn(xv, get(2)[...]).astype(BF)

    return fused("source_kv", info, body, [x, w_key, w_value], [shape(T, 2 * D, BF)])[0]


def after_self(info, x, att, w_out, c_query):
    T, D = x.shape

    def body(info_ref, get, y_ref, inv_ref, cq_ref):
        y, inv = norm_parts(get(0)[...].astype(F32) + nn(get(1)[...], get(2)[...]))
        y_ref[...] = y
        inv_ref[...] = jnp.broadcast_to(inv, inv_ref.shape)
        cq_ref[...] = (nn(y.astype(BF), get(3)[...]) * (0.125 * LOG2E)).astype(BF)

    return fused("after_self", info, body, [x, att, w_out, c_query],
                 [shape(T, D, F32), shape(T, 128, F32), shape(T, D, BF)])


def after_cross(info, y1, att, c_out, down, up, scale):
    T, D = y1.shape
    A = down.shape[1]

    def body(info_ref, get, y_ref, inv_ref, low_ref, sq_ref, gn_ref, base_ref):
        y, inv = norm_parts(get(0)[...] + nn(get(1)[...], get(2)[...]))
        y_ref[...] = y
        inv_ref[...] = jnp.broadcast_to(inv, inv_ref.shape)
        low = y.astype(BF)
        low_ref[...] = low
        h, g = gelu_pair(nn(low, get(3)[...]))
        hb = h.astype(BF)
        sq_ref[...] = hb
        gn_ref[...] = g.astype(BF)
        base_ref[...] = y + get(5)[0:1, 0:1] * nn(hb, get(4)[...])

    return fused("after_cross", info, body, [y1, att, c_out, down, up, scale],
                 [shape(T, D, F32), shape(T, 128, F32), shape(T, D, BF), shape(T, A, BF), shape(T, A, BF),
                  shape(T, D, F32)])


def expand(info, x, first, second, block=1024):
    T, D = x.shape
    width = first.cols
    F = 2 * width
    per = width // block

    def kernel(info_ref, x_ref, *refs):
        ins, (h_ref, g_ref, e, sem) = refs[:16], refs[16:]
        i = pl.program_id(0)
        copies = [copies_of([p], ins[8 * v : 8 * v + 8], e.at[v], info_ref[1], sem, 8 * v)
                  for v, p in enumerate((first, second))]

        @pl.when(i == 0)
        def _():
            for group in copies:
                for c in group:
                    c.start()

        for v in range(2):
            @pl.when(i == v * per)
            def _():
                for c in copies[v]:
                    c.wait()

        w = e[i // per, :, pl.ds(pl.multiple_of(lax.rem(i, per) * block, 128), block)]
        h, g = gelu_pair(nn(x_ref[...], w))
        h_ref[...] = h.astype(BF)
        g_ref[...] = g.astype(BF)

    out = pl.BlockSpec((T, block), lambda i, *_: (0, i))
    return pl.pallas_call(
        kernel,
        grid_spec=pltpu.PrefetchScalarGridSpec(
            num_scalar_prefetch=1,
            grid=(F // block,),
            in_specs=[pl.BlockSpec((T, D), lambda i, *_: (0, 0))] + [pl.BlockSpec(memory_space=pl.ANY)] * 16,
            out_specs=[out, out],
            scratch_shapes=[pltpu.VMEM((2, D, width), BF), pltpu.SemaphoreType.DMA((16,))],
        ),
        out_shape=[shape(T, F, BF)] * 2,
        compiler_params=vmem(60),
        cost_estimate=cost(12),
        name="expand",
    )(info, x, *[a for a, _ in first.parts], *[a for a, _ in second.parts])


def contract_kernel(h, c, base, low, sq, gn, up, g_out, scale, out_ref, g3_ref, gup_ref, gdown_ref, gnar_ref, acc):
    i = pl.program_id(0)

    @pl.when(i == 0)
    def _():
        acc[...] = base[...]

    acc[...] += nn(h[...], c[...])

    @pl.when(i == pl.num_programs(0) - 1)
    def _():
        y, inv = norm_parts(acc[...])
        out_ref[...] = y.astype(BF)
        g3 = norm_back(y, inv, g_out[...].astype(F32))
        g3_ref[...] = g3
        ga = (scale[0:1, 0:1] * g3).astype(BF)
        gup_ref[...] = tn(sq[...], ga).astype(BF)
        gnar = (gn[...].astype(F32) * nt(ga, up[...])).astype(BF)
        gnar_ref[...] = gnar
        gdown_ref[...] = tn(gnar, low[...]).astype(BF)


def contract(h, c, base, low, sq, gn, up, g_out, scale, block=1024):
    T, D = base.shape
    F = c.shape[0]
    A = sq.shape[1]

    def whole(a):
        return pl.BlockSpec(a.shape, lambda i: (0, 0), pipeline_mode=pl.Buffered(1))

    outs = [shape(T, D, BF), shape(T, D, F32), shape(A, D, BF), shape(A, D, BF), shape(T, A, BF)]
    return pl.pallas_call(
        contract_kernel,
        grid=(F // block,),
        in_specs=[pl.BlockSpec((T, block), lambda i: (0, i)), pl.BlockSpec((block, D), lambda i: (i, 0))]
        + [whole(a) for a in (base, low, sq, gn, up, g_out, scale)],
        out_specs=[pl.BlockSpec(o.shape, lambda i: (0, 0)) for o in outs],
        out_shape=outs,
        scratch_shapes=[pltpu.VMEM((T, D), F32)],
        compiler_params=vmem(60),
        cost_estimate=cost(14),
        name="contract",
    )(h, c, base, low, sq, gn, up, g_out, scale)


def ffn_back(info, g3, c, first, second, gp, gnar, down, y2, inv2, c_out, deps, block=1024):
    T, D = g3.shape
    F = c.shape[0]
    width = first.cols
    per = width // block
    loads = ([first], [second], c_out)
    extra = [a for load in loads for a in arrays_of(load)]
    count = len(extra)

    def kernel(info_ref, g3_ref, c_ref, gp_ref, gnar_ref, down_ref, y2_ref, inv2_ref, *refs):
        g2_ref, ga_ref, acc, ea, eb, co, sem = refs[-7:]
        i = pl.program_id(0)
        copies = [copies_of(load, refs[8 * v : count], buf, info_ref[1], sem, 8 * v)
                  for v, (load, buf) in enumerate(zip(loads, (ea, eb, co)))]

        @pl.when(i == 0)
        def _():
            for group in copies:
                for c in group:
                    c.start()
            acc[...] = g3_ref[...] + nt(gnar_ref[...], down_ref[...])

        gh = (nt(g3_ref[...].astype(BF), c_ref[...]) * gp_ref[...].astype(F32)).astype(BF)
        for v, e in enumerate((ea, eb)):
            @pl.when(i == v * per)
            def _():
                for c in copies[v]:
                    c.wait()

            @pl.when(i // per == v)
            def _():
                acc[...] += nt(gh, e[:, pl.ds(pl.multiple_of(lax.rem(i, per) * block, 128), block)])

        @pl.when(i == F // block - 1)
        def _():
            for c in copies[2]:
                c.wait()
            g2 = norm_back(y2_ref[...], inv2_ref[:, 0:1], acc[...])
            g2_ref[...] = g2
            ga_ref[...] = nt(g2.astype(BF), co[...]).astype(BF)

    def whole(a):
        return pl.BlockSpec(a.shape, lambda i, *_: (0, 0), pipeline_mode=pl.Buffered(1))

    outs = [shape(T, D, F32), shape(T, D, BF)]
    extra += list(deps)
    return pl.pallas_call(
        kernel,
        grid_spec=pltpu.PrefetchScalarGridSpec(
            num_scalar_prefetch=1,
            grid=(F // block,),
            in_specs=[whole(g3), pl.BlockSpec((block, D), lambda i, *_: (i, 0)),
                      pl.BlockSpec((T, block), lambda i, *_: (0, i))]
            + [whole(a) for a in (gnar, down, y2, inv2)] + [pl.BlockSpec(memory_space=pl.ANY)] * len(extra),
            out_specs=[pl.BlockSpec(o.shape, lambda i, *_: (0, 0)) for o in outs],
            scratch_shapes=[pltpu.VMEM((T, D), F32), pltpu.VMEM((D, width), BF), pltpu.VMEM((D, width), BF),
                            pltpu.VMEM(*shape_of(c_out)), pltpu.SemaphoreType.DMA((count,))],
        ),
        out_shape=outs,
        compiler_params=vmem(60),
        cost_estimate=cost(18),
        name="ffn_back",
    )(info, g3, c, gp, gnar, down, y2, inv2, *extra)


def before_self(info, g2, gq, y1, inv1, c_query, w_out, deps):
    T, D = g2.shape

    def body(info_ref, get, g1_ref, ga_ref):
        g = get(0)[...] + 0.125 * nt(get(1)[...], get(2)[...])
        g1 = norm_back(get(3)[...], get(4)[:, 0:1], g)
        g1_ref[...] = g1
        ga_ref[...] = nt(g1.astype(BF), get(5)[...]).astype(BF)

    return fused("before_self", info, body, [g2, gq, c_query, y1, inv1, w_out],
                 [shape(T, D, F32), shape(T, D, BF)], deps=deps)


def add_pairs(mine, got, buf):
    D = mine.shape[1] // 2
    for v in range(2):
        for h in range(D // 128):
            at = slice(256 * h + 128 * v, 256 * h + 128 * v + 128)
            buf[:, D * v + 128 * h : D * v + 128 * h + 128] = (mine[:, at] + got[:, at].astype(F32)).astype(BF)


def source_grad(info, gkv, got, w_key, w_value, deps):
    T, D = gkv.shape[0], gkv.shape[1] // 2

    def body(info_ref, get, out):
        buf = get(4)
        add_pairs(get(0), get(1), buf)
        out[...] = (nt(buf[:, :D], get(2)[...]) + nt(buf[:, D:], get(3)[...])).astype(BF)

    return fused("source_grad", info, body, [gkv, got, w_key, w_value, got], [shape(T, D, BF)], deps=deps)[0]


def token_grad(info, g1, gq, gkv, got, w_query, w_key, w_value, deps):
    T, D = g1.shape

    def body(info_ref, get, out):
        acc = get(0)[...] + 0.125 * nt(get(1)[...], get(2)[...])
        buf = get(7)
        add_pairs(get(3), get(4), buf)
        out[...] = (acc + nt(buf[:, :D], get(5)[...]) + nt(buf[:, D:], get(6)[...])).astype(BF)

    return fused("token_grad", info, body, [g1, gq, w_query, gkv, got, w_key, w_value, got],
                 [shape(T, D, BF)], deps=deps)[0]


def move(value, target):
    dp, seq = lax.axis_size("dp"), lax.axis_size("seq")
    pairs = []
    for d in range(dp):
        for s in range(seq):
            a, b = target(d, s)
            pairs.append((d * seq + s, a * seq + b))
    return lax.ppermute(value, ("dp", "seq"), pairs)


def flip(value, bit):
    return move(value, lambda d, s: (d ^ bit, s))


def core_of(chunk):
    return (0, 1, 1, 0)[chunk]


def pick(flag, first, second):
    return jnp.where(flag, first, second)


def take_pieces(value, s):
    return [lax.dynamic_index_in_dim(value, (s + k) % 2, 0, keepdims=False) for k in range(2)]


def send_pieces(pieces):
    return [
        move(piece, lambda a, q, k=k: (2 * (a // 2) + core_of(q), 2 * (a % 2) + (q + k) % 2))
        for k, piece in enumerate(pieces)
    ]


def join_pieces(got, d, s):
    even = (s + d) % 2 == 0
    return jnp.concatenate([pick(even, got[0], got[1]), pick(even, got[1], got[0])], axis=0)


def send_back(value, d, s):
    C = value.shape[0] // 2
    dp, seq = lax.axis_size("dp"), lax.axis_size("seq")
    got = []
    for k in range(2):
        slot = (s + k + d) % 2
        piece = lax.dynamic_slice_in_dim(value, slot * C, C, 0)
        back = {}
        for a in range(dp):
            for q in range(seq):
                back[(2 * (a // 2) + core_of(q), 2 * (a % 2) + (q + k) % 2)] = (a, q)
        got.append(move(piece, lambda a, b: back[(a, b)]))
    return got


def join_rows(got, s):
    even = s % 2 == 0
    return jnp.stack([pick(even, got[0], got[1]), pick(even, got[1], got[0])])


def first_hop(pair, low):
    return [flip(pair[0], 2 * low), flip(pair[1], 4 * low)]


def beside(pair, got):
    return [jnp.concatenate([own, other], axis=0) for own, other in zip(pair, got)]


def second_hop(near, low):
    return [flip(near[0], 4 * low), flip(near[1], 2 * low)]


def all_parts(near, far, low):
    out = []
    for v in range(2):
        half = near[v].shape[0] // 2
        b1, b2 = ((2, 4), (4, 2))[v]
        arrays = [near[v], far[v], flip(near[v], low), flip(far[v], low)]
        parts = {}
        for a, m in zip(arrays, (0, b2, 1, b2 ^ 1)):
            parts[m] = (a, 0)
            parts[m ^ b1] = (a, half)
        out.append([parts[m] for m in range(8)])
    return out


class Reduce:
    def __init__(self, value, d, s, low):
        self.d, self.s, self.low, self.value = d, s, low, value
        self.high = (d // low) % 2 == 1

    def plane(self, v, m):
        return flip(v, 2 * self.low * m)

    def line(self, v, m):
        return move(v, lambda a, b: (a, b ^ m))

    def send_pair(self):
        half = self.value.shape[0] // 2
        lo, hi = self.value[:half], self.value[half:]
        self.kept, self.got = pick(self.high, hi, lo), [flip(pick(self.high, lo, hi), self.low)]

    def send_parts(self, me, n, send):
        parts = self.value.reshape(n, -1, self.value.shape[1])
        take = [lax.dynamic_index_in_dim(parts, me ^ m, 0, keepdims=False) for m in range(n)]
        self.kept, self.got = take[0], [send(take[m], m) for m in range(1, n)]

    def add(self):
        total = self.kept.astype(F32)
        for got in self.got:
            total += got.astype(F32)
        self.value = total.astype(BF)

    def scatter_plane(self):
        self.send_parts(self.d // (2 * self.low), 4, self.plane)

    def scatter_line(self):
        self.send_parts(self.s, lax.axis_size("seq"), self.line)

    def low_bits(self):
        bit = 1
        while bit < self.low:
            got = flip(self.value, bit)
            self.value = (self.value.astype(F32) + got.astype(F32)).astype(BF)
            bit *= 2

    def spread(self, me, n, send):
        self.me, self.got = me, [self.value] + [send(self.value, m) for m in range(1, n)]

    def gather_line(self):
        self.spread(self.s, lax.axis_size("seq"), self.line)

    def gather_plane(self):
        self.spread(self.d // (2 * self.low), 4, self.plane)

    def gather_pair(self):
        self.spread((self.d // self.low) % 2, 2, lambda v, m: flip(v, self.low * m))

    def put(self):
        got = self.got
        n, rows = len(got), []
        for j in range(n):
            part = got[n - 1]
            for m in range(n - 1):
                part = pick((self.me ^ j) == m, got[m], part)
            rows.append(part)
        self.value = jnp.concatenate(rows, axis=0)


def local(tokens, source, target_lengths, source_lengths, step_index, self_query, self_key, self_value,
          self_out, cross_query, cross_key, cross_value, cross_out, ffn_expand, ffn_contract, adapter_down,
          adapter_up, grad_output):
    rows, C, D = tokens.shape
    dp, seq = lax.axis_size("dp"), lax.axis_size("seq")
    assert rows == 2 and seq == 4 and dp % 8 == 0
    low = dp // 8
    d, s = lax.axis_index("dp"), lax.axis_index("seq")
    core = d % 2
    info = jnp.stack([core, d // low]).astype(jnp.int32)

    x = join_pieces(send_pieces(take_pieces(tokens, s)), d, s)

    def widen(shard):
        if low == 1:
            return shard
        groups = [[g * low + i for i in range(low)] for g in range(8)]
        return lax.all_gather(shard, "dp", axis=0, tiled=True, axis_index_groups=groups)

    def two(a, b):
        return jnp.concatenate([a, b], axis=0)

    wide = [widen(w) for w in (self_query, self_key, self_value, self_out, cross_query, cross_key,
                               cross_value, cross_out, ffn_expand)]
    sq, sk, sv, so, cq_, ck_, cv_, co_, ex = wide
    n = sq.shape[0]
    def rows_of(*weights):
        return jnp.concatenate(weights, axis=0)

    h = n // 2
    pair = [rows_of(sk, sv[:h]), rows_of(sq, sv[h:])]
    hop = first_hop(pair, low)
    near = beside(pair, hop)
    a1, b1 = all_parts(near, second_hop(near, low), low)
    w_key, w_query = [Piece(a1, 0, n)], [Piece(b1, 0, n)]
    w_value = [Piece(a1, n, h, n, 0), Piece(b1, n, h, n, h)]
    pair2 = gate([rows_of(ck_, cv_, co_[:h]), rows_of(so, cq_, co_[h:])], hop)
    hop2 = first_hop(pair2, low)

    mine = jnp.concatenate([target_lengths, source_lengths[:, None]], axis=1)
    other = flip(mine, 1)
    table = jnp.concatenate([pick(core == 0, mine, other), pick(core == 0, other, mine)], axis=0)
    row = lax.dynamic_index_in_dim(table, s, 0, keepdims=False)
    lens, src_len = row[:-1], row[-1]
    docs = lens.shape[0]
    ends = jnp.cumsum(lens)[:-1]
    i = jnp.arange(2 * C, dtype=jnp.int32)
    slot = i // C

    def place(which):
        chunk = pick(which == 0, slot * 3, slot + 1)
        return chunk * C + i % C

    lanes = jnp.arange(128, dtype=jnp.int32) % 64

    def doc_hot(pos):
        doc = jnp.sum((pos[:, None] >= ends[None, :]).astype(jnp.int32), axis=-1)
        return doc[:, None] == lanes[None, :]

    own_pos, peer_pos = place(core), place(1 - core)
    k_aug = [doc_hot(own_pos).astype(BF), doc_hot(peer_pos).astype(BF)]
    q_aug = jnp.where(doc_hot(own_pos) | (lanes >= docs)[None, :], 0.0, NEG).astype(BF)
    ck_aug = [((pos[:, None] >= src_len) & (lanes == 0)[None, :]).astype(BF) for pos in (own_pos, peer_pos)]
    cq_aug = jnp.broadcast_to(jnp.where(lanes == 0, NEG, 0.0).astype(BF)[None, :], (2 * C, 128))

    scale = jnp.full((8, 128), (step_index[0] + 1).astype(F32) / 5.0, F32)
    e1, e2, c_shard = stage(ex, ffn_contract, hop)
    q, kv = project_qkv(info, x, w_query, w_key, w_value, (e1,))
    *hop2, q, kv = barrier(*hop2, q, kv)
    near2 = beside(pair2, hop2)
    kv_peer = flip(kv, 1)
    far2, got = second_hop(near2, low), send_pieces(gate(take_pieces(source, s), (q,)))
    attended, p_self = attend(SELF_PLANS, info, q, kv, kv_peer, q_aug, *k_aug)
    *far2, s0, s1, attended, e1, e2, c_shard = barrier(*far2, *got, attended, e1, e2, c_shard)
    w_contract = lax.all_gather(c_shard, "dp", axis=0, tiled=True)
    hop3 = first_hop([e1, e2], low)
    a2, b2 = all_parts(near2, far2, low)
    c_key, c_value = [Piece(a2, 0, n)], [Piece(a2, n, n)]
    w_out, c_query = [Piece(b2, 0, n)], [Piece(b2, n, n)]
    c_out = [Piece(a2, 2 * n, h, n, 0), Piece(b2, 2 * n, h, n, h)]
    src = join_pieces([s0, s1], d, s)
    skv = project_source(info, src, c_key, c_value)
    skv_peer = flip(skv, 1)
    y1, inv1, cq = after_self(info, x, attended, w_out, c_query)
    *hop3, skv_peer, cq = barrier(*hop3, skv_peer, cq)
    near3 = beside([e1, e2], hop3)
    far3, got = second_hop(near3, low), send_pieces(gate(take_pieces(grad_output, s), (cq,)))
    cross_attended, p_cross = attend(CROSS_PLANS, info, cq, skv, skv_peer, cq_aug, *ck_aug)
    *far3, s0, s1, cross_attended = barrier(*far3, *got, cross_attended)
    a3, b3 = all_parts(near3, far3, low)
    g_out = join_pieces([s0, s1], d, s)
    y2, inv2, second_low, squeezed, gn, base = after_cross(
        info, y1, cross_attended, c_out, adapter_down, adapter_up, scale
    )
    ea, eb = Piece(a3, 0, n), Piece(b3, 0, n)
    hidden, gp = expand(info, second_low, ea, eb)
    output, g3, grad_up, grad_down, gnar = contract(
        hidden, w_contract, base, second_low, squeezed, gn, adapter_up, g_out, scale
    )
    output = send_back(output, d, s)
    total = Reduce(two(grad_up, grad_down), d, s, low)
    total.send_pair()
    g2, grad_cross = ffn_back(info, g3, w_contract, ea, eb, gp, gnar, adapter_down, y2, inv2, c_out, ())
    *total.got, g2, grad_cross = barrier(*total.got, g2, grad_cross)
    total.add()
    total.scatter_plane()
    gq, gkv, gkv_peer = attend_back(
        CROSS_PLANS, info, cq, skv, skv_peer, grad_cross, cross_attended, p_cross, (total.kept,)
    )
    *total.got, o0, o1, gq, gkv_peer = barrier(*total.got, *output, gq, gkv_peer)
    output = [o0, o1]
    total.add()
    total.scatter_line()
    got = flip(gkv_peer, 1)
    g1, grad_self = before_self(info, g2, gq, y1, inv1, c_query, w_out, (total.kept,))
    *total.got, got, grad_self = barrier(*total.got, got, grad_self)
    total.add()
    total.low_bits()
    total.gather_line()
    grad_source = source_grad(info, gkv, got, c_key, c_value, (grad_self, total.value))
    *line, grad_source = barrier(*total.got[1:], grad_source)
    total.got[1:] = line
    total.put()
    total.gather_plane()
    pieces = send_back(grad_source, d, s)
    gq, gkv, gkv_peer = attend_back(
        SELF_PLANS, info, q, kv, kv_peer, grad_self, attended, p_self, (total.value,)
    )
    *total.got, o0, o1, gq, gkv_peer = barrier(*total.got, *pieces, gq, gkv_peer)
    got = flip(gkv_peer, 1)
    total.put()
    total.gather_pair()
    grad_tokens = token_grad(info, g1, gq, gkv, got, w_query, w_key, w_value, (total.value,))
    *total.got, grad_tokens = barrier(*total.got, grad_tokens)
    grad_tokens = send_back(grad_tokens, d, s)
    output, grad_source, grad_tokens = [join_rows(v, s) for v in (output, [o0, o1], grad_tokens)]
    total.put()
    grads = total.value.astype(F32)
    A = adapter_down.shape[1]
    grad_up, grad_down = grads[:A], grads[A:].T
    return (output, grad_tokens, grad_source, grad_down, grad_up)


def solution(mesh):
    rows = P("dp", "seq", None)
    weight = P("dp", None)
    return jax.shard_map(
        local,
        mesh=mesh,
        in_specs=(rows, rows, weight, P("dp"), P()) + (weight,) * 10 + (P(), P(), rows),
        out_specs=(rows, rows, rows, P(), P()),
        check_vma=False,
    )
```

time: 500 us -> 434 us (0.87)
  waiting for transfers between devices: 107 us -> 49.3 us
  starting transfers between devices: 120 us -> 80.6 us
  Pallas kernels: 186 us -> 203 us
  local copies, waits for them, and re-layouts: 36 us -> 49.6 us
    ppermute x69 -> x55, waiting for transfers between devices: 105 us -> 49.3 us  [move(): return lax.ppermute(value, ('dp', 'seq'), pairs)]
    ppermute x69 -> x55, starting transfers between devices: 119 us -> 80.5 us  [move(): return lax.ppermute(value, ('dp', 'seq'), pairs)]
    pallas_call x8 -> x7, Pallas kernels: 53 us -> 61 us  [fused(): pl.pallas_call(kernel, grid_spec=pltpu.PrefetchScalarGridSpec(num_scalar_...]
    pallas_call x2 -> x16, Pallas kernels: 28.5 us -> 35.9 us  [the longest x1 19.6 us: ffn_back(): pl.pallas_call(kernel, grid_spec=pltpu.PrefetchScalarGridSpec(num_scalar_...]
    unnamed x172 -> x125, local copies, waits for them, and re-layouts: 23.1 us -> 24.5 us
  transfers between devices with their start and end apart: 71 -> 56, of which waited for: 25 -> 12; matrix products, arithmetic and copies ran while one was open for 8% -> 13% of each run, Pallas kernels for 35% -> 44%
where the time goes in v3:
time: 434 us; the launch traced here: 427 us
  Pallas kernels  203 us (47%)
  starting transfers between devices  80.6 us (19%)
  local copies, waits for them, and re-layouts  49.6 us (11%)
  waiting for transfers between devices  49.3 us (11%)
  other arithmetic  29 us (7%)
  between operations  15.9 us (4%)
    ppermute x55, starting transfers between devices, move(): return lax.ppermute(value, ('dp', 'seq'), pairs)  80.5 us
    pallas_call x7, Pallas kernels, fused(): pl.pallas_call(kernel, grid_spec=pltpu.PrefetchScalarGridSpec(num_scalar_...  61 us
    ppermute x55, waiting for transfers between devices, move(): return lax.ppermute(value, ('dp', 'seq'), pairs)  49.3 us
    pallas_call x2, Pallas kernels, attend_back(): pl.pallas_call(functools.partial(bwd_kernel, plans, C), grid_spec=pltpu.P...  46.3 us
    pallas_call x2, Pallas kernels, attend(): pl.pallas_call(functools.partial(fwd_kernel, plans, C), grid_spec=pltpu.P...  44.5 us
    unnamed x125, local copies, waits for them, and re-layouts  24.5 us
    pallas_call x1, Pallas kernels, ffn_back(): pl.pallas_call(kernel, grid_spec=pltpu.PrefetchScalarGridSpec(num_scalar_...  19.6 us
    pallas_call x1, Pallas kernels, contract(): pl.pallas_call(contract_kernel, grid=(F // block,), in_specs=[pl.BlockSpe...  15.3 us
  transfers between devices with their start and end apart: 56, of which 12 were waited for; matrix products, arithmetic and copies ran while one was open for 13% of the time, Pallas kernels for 44%

profile of v3, /device:TPU:1, one launch (start us, length us, event | category | flops | bytes accessed | tf_op | source)
XLA Modules:
  0.0 427.4 jit_solution(1426324775690802809)
XLA Ops:
  9.3 2.1 collective-permute-start.2
  13.6 6.6 %collective-permute-done.2.refs_2_.refs_0_ = bf16[192,1024]{1,0:T(8,128)(2,1)S(1)} collective-permute-done((bf16[192,1024]{1,0:T(8,128)(2,1)S(1)}, bf16[192,1024]{1,0:T(8,128)(2,1)S(1)}, u32[]{:S(2)}, u32[]{:S(2)}) %collective-permute-start.2) | collective-permute-done | bytes 393248 | tf_op jit(solution)/shard_map/ppermute | solution.py:567
  23.7 2.2 dynamic-slice_bitcast_fusion.5
  25.9 6.2 %collective-permute-start = (bf16[256,1024]{1,0:T(8,128)(2,1)}, bf16[256,1024]{1,0:T(8,128)(2,1)}, u32[]{:S(2)}, u32[]{:S(2)}) collective-permute-start(bf16[256,1024]{1,0:T(8,128)(2,1)} %get-tuple-element.235), channel_id=1, source_target_pairs={{0,0},{1,5},{2,4},{3,1},{4,2},{5,7},{6,6},{7,3},{8,8},{9,13},{10,1... | collective-permute-start | bytes 1572872 | tf_op jit(solution)/shard_map/ppermute | solution.py:567
  33.7 2.3 dynamic-slice_bitcast_fusion.2
  37.1 6.6 %collective-permute-done = bf16[256,1024]{1,0:T(8,128)(2,1)} collective-permute-done((bf16[256,1024]{1,0:T(8,128)(2,1)}, bf16[256,1024]{1,0:T(8,128)(2,1)}, u32[]{:S(2)}, u32[]{:S(2)}) %collective-permute-start) | collective-permute-done | bytes 524320 | tf_op jit(solution)/shard_map/ppermute | solution.py:567
  45.0 2.3 pad_maximum_fusion.9
  47.4 2.9 stage.1
  55.2 2.5 collective-permute-start.17
  57.7 7.9 %qkv.1 = (bf16[512,1024]{1,0:T(8,128)(2,1)}, bf16[512,2048]{1,0:T(8,128)(2,1)}) custom-call(s32[2]{0:T(128)} %pad_add_fusion.2.info_ref.info, bf16[512,1024]{1,0:T(8,128)(2,1)} %pad_maximum_fusion.refs_0_, bf16[384,1024]{1,0:T(8,128)(2,1)} %copy-done.8, ...), custom_call_target="tpu_custom_call" | custom-call | flops 6000000000 | bytes 1024 | tf_op jit(solution)/shard_map/qkv/pallas_call | solution.py:261
  68.0 3.1 collective-permute-start.16
  73.2 2.0 constant_dynamic-update-slice_fusion.3
  77.1 8.1 %collective-permute-start.14 = (bf16[256,1024]{1,0:T(8,128)(2,1)}, bf16[256,1024]{1,0:T(8,128)(2,1)S(1)}, u32[]{:S(2)}, u32[]{:S(2)}) collective-permute-start(bf16[256,1024]{1,0:T(8,128)(2,1)} %get-tuple-element.105), channel_id=1, source_target_pairs={{0,0},{1,5},{2,4},{3,1},{4,2},{5,7},{6,6},{7,3},{8,8},{9,13},{10,1... | collective-permute-start | bytes 1572872 | tf_op jit(solution)/shard_map/ppermute | solution.py:567
  85.9 2.0 constant_dynamic-update-slice_fusion.refs_1_.refs_3_.refs_9_.refs_11_.refs_2_.refs_4_.refs_16_.refs_18_.refs_10_.refs_12_
  88.9 19.3 %attend.2 = (bf16[512,1024]{1,0:T(8,128)(2,1)}, bf16[8,2,5,256,256]{4,3,2,1,0:T(8,128)(2,1)}) custom-call(s32[2]{0:T(128)} %pad_add_fusion.2.info_ref.info, bf16[512,1024]{1,0:T(8,128)(2,1)} %get-tuple-element.104.refs_2_.q_ref, bf16[512,2048]{1,0:T(8,128)(2,1)} %get-tuple-element.107.ko.vo, bf16[512,2048]{1,0:T(8,128)(2,1)} %get-tuple-element.107.ko.vo, ...), custom_call_target="tpu_custom_call" | custom-call | flops 20000000000 | bytes 1024 | tf_op jit(solution)/shard_map/attend/pallas_call | solution.py:76
  108.3 8.9 %collective-permute-done.12.refs_0_ = bf16[640,1024]{1,0:T(8,128)(2,1)S(1)} collective-permute-done((bf16[640,1024]{1,0:T(8,128)(2,1)}, bf16[640,1024]{1,0:T(8,128)(2,1)S(1)}, u32[]{:S(2)}, u32[]{:S(2)}) %collective-permute-start.12) | collective-permute-done | bytes 1310752 | tf_op jit(solution)/shard_map/ppermute | solution.py:567
  121.5 1.9 collective-permute-done.23.refs_6_.refs_8_.refs_14_.refs_16_.refs_7_.refs_9_.refs_21_.refs_23_.refs_15_.refs_17_
  124.5 6.9 %source_kv.1.ko.vo = bf16[512,2048]{1,0:T(8,128)(2,1)} custom-call(s32[2]{0:T(128)} %pad_add_fusion.2.info_ref.info, bf16[512,1024]{1,0:T(8,128)(2,1)} %pad_maximum_fusion.1.refs_0_, bf16[640,1024]{1,0:T(8,128)(2,1)} %constant_dynamic-update-slice_fusion.refs_1_.refs_3_.refs_9_.refs_11_.refs_2_.refs_4_.refs_16_.refs_18_.refs_10_.refs_12_, ...), custom_call_target="tpu_custom_call" | custom-call | flops 6000000000 | bytes 1024 | tf_op jit(solution)/shard_map/source_kv/pallas_call | solution.py:261
  132.1 2.2 dynamic-slice_bitcast_fusion
  139.1 1.9 constant_dynamic-update-slice_fusion.7
  141.0 1.9 constant_dynamic-update-slice_fusion.5
  144.5 7.0 %after_self.1 = (f32[512,1024]{1,0:T(8,128)}, f32[512,128]{1,0:T(8,128)}, bf16[512,1024]{1,0:T(8,128)(2,1)}) custom-call(s32[2]{0:T(128)} %pad_add_fusion.2.info_ref.info, bf16[512,1024]{1,0:T(8,128)(2,1)} %pad_maximum_fusion.refs_0_, bf16[512,1024]{1,0:T(8,128)(2,1)} %get-tuple-element.111.refs_1_.o, ...), custom_call_target="tpu_custom_call" | custom-call | flops 6000000000 | bytes 1024 | tf_op jit(solution)/shard_map/after_self/pallas_call | solution.py:261
  152.2 1.9 constant_dynamic-update-slice_fusion.6.refs_8_.refs_12_
  154.1 2.1 collective-permute-start.26
  158.0 3.8 collective-permute-start.27
  163.5 1.9 constant_dynamic-update-slice_fusion.4.refs_0_.refs_2_
  167.0 25.2 %attend.3 = (bf16[512,1024]{1,0:T(8,128)(2,1)}, bf16[8,2,8,256,256]{4,3,2,1,0:T(8,128)(2,1)}) custom-call(s32[2]{0:T(128)} %pad_add_fusion.2.info_ref.info, bf16[512,1024]{1,0:T(8,128)(2,1)} %get-tuple-element.122.refs_2_.q_ref, bf16[512,2048]{1,0:T(8,128)(2,1)} %source_kv.1.ko.vo, bf16[512,2048]{1,0:T(8,128)(2,1)} %source_kv.1.ko.vo, ...), custom_call_target="tpu_custom_call" | custom-call | flops 20000000000 | bytes 1024 | tf_op jit(solution)/shard_map/attend/pallas_call | solution.py:76
  192.3 3.4 collective-permute-done.26.refs_1_
  202.0 9.0 %after_cross.1 = (f32[512,1024]{1,0:T(8,128)}, f32[512,128]{1,0:T(8,128)}, bf16[512,1024]{1,0:T(8,128)(2,1)}, bf16[512,512]{1,0:T(8,128)(2,1)}, bf16[512,512]{1,0:T(8,128)(2,1)}, /*index=5*/f32[512,1024]{1,0:T(8,128)}) custom-call(s32[2]{0:T(128)} %pad_add_fusion.2.info_ref.info, f32[512,1024]{1,0:T(8,128)} %get-tuple-element.113.refs_0_.refs_10_, ...), custom_call_target="tpu_custom_call" | custom-call | flops 6000000000 | bytes 1024 | tf_op jit(solution)/shard_map/after_cross/pallas_call | solution.py:261
  212.4 13.3 %expand.1 = (bf16[512,4096]{1,0:T(8,128)(2,1)}, bf16[512,4096]{1,0:T(8,128)(2,1)}) custom-call(s32[2]{0:T(128)} %pad_add_fusion.2.info_ref.info, bf16[512,1024]{1,0:T(8,128)(2,1)} %get-tuple-element.128.x_ref.low, bf16[256,2048]{1,0:T(8,128)(2,1)} %constant_dynamic-update-slice_fusion.4.refs_0_.refs_2_, ...), custom_call_target="tpu_custom_call" | custom-call | flops 12000000000 | bytes 1024 | tf_op jit(solution)/shard_map/expand/pallas_call | solution.py:389
  225.7 15.3 %contract.1 = (bf16[512,1024]{1,0:T(8,128)(2,1)}, f32[512,1024]{1,0:T(8,128)}, bf16[512,1024]{1,0:T(8,128)(2,1)}, bf16[512,1024]{1,0:T(8,128)(2,1)}, bf16[512,512]{1,0:T(8,128)(2,1)}) custom-call(bf16[512,4096]{1,0:T(8,128)(2,1)} %get-tuple-element.131.h, bf16[4096,1024]{1,0:T(8,128)(2,1)} %all-gather.2.cloned.1.call-done.c.c_ref, ...), custom_call_target="tpu_custom_call" | custom-call | flops 14000000000 | bytes 1024 | tf_op jit(solution)/shard_map/contract/pallas_call | solution.py:436
  244.1 4.1 collective-permute-start.37
  250.0 19.6 %ffn_back.1 = (f32[512,1024]{1,0:T(8,128)}, bf16[512,1024]{1,0:T(8,128)(2,1)}) custom-call(s32[2]{0:T(128)} %pad_add_fusion.2.info_ref.info, f32[512,1024]{1,0:T(8,128)} %get-tuple-element.140.g3_ref, bf16[4096,1024]{1,0:T(8,128)(2,1)} %all-gather.2.cloned.1.call-done.c.c_ref, bf16[512,4096]{1,0:T(8,128)(2,1)} %get-tuple-element.141.gp_ref, ...), custom_call_target="tpu_custom_call" | custom-call | flops 17999998976 | bytes 1024 | tf_op jit(solution)/shard_map/ffn_back/pallas_call | solution.py:496
  272.2 1.8 add_convert_fusion
  277.5 26.9 %attend_back.2 = (bf16[512,1024]{1,0:T(8,128)(2,1)}, f32[512,2048]{1,0:T(8,128)}, bf16[512,2048]{1,0:T(8,128)(2,1)}) custom-call(s32[2]{0:T(128)} %pad_add_fusion.2.info_ref.info, bf16[512,1024]{1,0:T(8,128)(2,1)} %get-tuple-element.122.refs_2_.q_ref, bf16[512,2048]{1,0:T(8,128)(2,1)} %source_kv.1.ko.vo, bf16[512,2048]{1,0:T(8,128)(2,1)} %source_kv.1.ko.vo, ...), custom_call_target="tpu_custom_call" | custom-call | flops 22000001024 | bytes 1024 | tf_op jit(solution)/shard_map/attend_back/pallas_call | solution.py:142
  309.5 2.1 collective-permute-start.40
  311.9 7.8 %before_self.1 = (f32[512,1024]{1,0:T(8,128)}, bf16[512,1024]{1,0:T(8,128)(2,1)}) custom-call(s32[2]{0:T(128)} %pad_add_fusion.2.info_ref.info, f32[512,1024]{1,0:T(8,128)} %get-tuple-element.159.refs_0_, bf16[512,1024]{1,0:T(8,128)(2,1)} %get-tuple-element.160.refs_1_, ...), custom_call_target="tpu_custom_call" | custom-call | flops 6000000000 | bytes 1024 | tf_op jit(solution)/shard_map/before_self/pallas_call | solution.py:261
  322.4 3.0 collective-permute-start.44
  325.7 10.4 %source_grad.1.refs_3_ = bf16[512,1024]{1,0:T(8,128)(2,1)} custom-call(s32[2]{0:T(128)} %pad_add_fusion.2.info_ref.info, f32[512,2048]{1,0:T(8,128)} %get-tuple-element.166.refs_0_, bf16[512,2048]{1,0:T(8,128)(2,1)} %get-tuple-element.167.refs_1_.refs_18_, ...), custom_call_target="tpu_custom_call" | custom-call | flops 6000000000 | bytes 1024 | tf_op jit(solution)/shard_map/source_grad/pallas_call | solution.py:261
  342.4 4.9 %collective-permute-start.49 = (bf16[256,1024]{1,0:T(8,128)(2,1)S(1)}, bf16[256,1024]{1,0:T(8,128)(2,1)S(1)}, u32[]{:S(2)}, u32[]{:S(2)}) collective-permute-start(bf16[256,1024]{1,0:T(8,128)(2,1)S(1)} %get-tuple-element.216), channel_id=1, source_target_pairs={{0,0},{1,3},{2,4},{3,7},{4,2},{5,1},{6,6},{7,5},{8,8},{9,11},{10,1... | collective-permute-start | bytes 1572872 | tf_op jit(solution)/shard_map/ppermute | solution.py:567
  347.3 2.9 collective-permute-start.50
  350.2 19.4 %attend_back.3 = (bf16[512,1024]{1,0:T(8,128)(2,1)}, f32[512,2048]{1,0:T(8,128)}, bf16[512,2048]{1,0:T(8,128)(2,1)}) custom-call(s32[2]{0:T(128)} %pad_add_fusion.2.info_ref.info, bf16[512,1024]{1,0:T(8,128)(2,1)} %get-tuple-element.104.refs_2_.q_ref, bf16[512,2048]{1,0:T(8,128)(2,1)} %get-tuple-element.107.ko.vo, ...), custom_call_target="tpu_custom_call" | custom-call | flops 22000001024 | bytes 1024 | tf_op jit(solution)/shard_map/attend_back/pallas_call | solution.py:142
  377.4 12.1 %token_grad.1.refs_2_ = bf16[512,1024]{1,0:T(8,128)(2,1)} custom-call(s32[2]{0:T(128)} %pad_add_fusion.2.info_ref.info, f32[512,1024]{1,0:T(8,128)} %get-tuple-element.180.refs_0_, bf16[512,1024]{1,0:T(8,128)(2,1)} %get-tuple-element.181.refs_1_, bf16[384,1024]{1,0:T(8,128)(2,1)} %copy-done.8, ...), custom_call_target="tpu_custom_call" | custom-call | flops 6000000000 | bytes 1024 | tf_op jit(solution)/shard_map/token_grad/pallas_call | solution.py:261
  389.5 2.3 constant_dynamic-slice_fusion.1
  391.8 2.9 collective-permute-start.53
  394.8 2.7 collective-permute-start.54
  401.0 1.8 copy.83
  402.8 16.4 %collective-permute-done.53 = bf16[256,1024]{1,0:T(8,128)(2,1)S(1)} collective-permute-done((bf16[256,1024]{1,0:T(8,128)(2,1)}, bf16[256,1024]{1,0:T(8,128)(2,1)S(1)}, u32[]{:S(2)}, u32[]{:S(2)}) %collective-permute-start.53) | collective-permute-done | bytes 524320 | tf_op jit(solution)/shard_map/ppermute | solution.py:567
  (282 shorter events, 87.5 us)
Async XLA Ops:
  7.2 218.6 %all-gather.2.cloned.1.call-start = ((), (), s32[]{:S(2)}) async-start(), calls=%async_computation | async-start | bytes 9437184 | tf_op jit(solution)/shard_map/all_gather | solution.py:781
  20.3 23.4 %collective-permute-start.10 = (bf16[384,1024]{1,0:T(8,128)(2,1)S(1)}, bf16[384,1024]{1,0:T(8,128)(2,1)S(1)}, u32[]{:S(2)}, u32[]{:S(2)}) collective-permute-start(bf16[384,1024]{1,0:T(8,128)(2,1)S(1)} %pad_maximum_fusion.8.refs_9_.refs_11_.refs_17_.refs_19_.refs_12_.refs_14_.refs_20_.refs_22_), channel_id=1, source_target_pairs={{0,16},{1,17},{2,18},{3,19},{4,20},{5,21},{6,22},{7,23},{8,24},{9,... | collective-permute-start | bytes 2359304 | tf_op jit(solution)/shard_map/ppermute | solution.py:567
  22.9 21.2 %collective-permute-start.7 = (bf16[384,1024]{1,0:T(8,128)(2,1)S(1)}, bf16[384,1024]{1,0:T(8,128)(2,1)S(1)}, u32[]{:S(2)}, u32[]{:S(2)}) collective-permute-start(bf16[384,1024]{1,0:T(8,128)(2,1)S(1)} %pad_maximum_fusion.7.refs_1_.refs_5_.refs_25_.refs_29_.refs_2_.refs_6_.refs_28_.refs_32_), channel_id=1, source_target_pairs={{0,8},{1,9},{2,10},{3,11},{4,12},{5,13},{6,14},{7,15},{8,0},{9,1},... | collective-permute-start | bytes 2359304 | tf_op jit(solution)/shard_map/ppermute | solution.py:567
  25.9 17.7 %collective-permute-start = (bf16[256,1024]{1,0:T(8,128)(2,1)}, bf16[256,1024]{1,0:T(8,128)(2,1)}, u32[]{:S(2)}, u32[]{:S(2)}) collective-permute-start(bf16[256,1024]{1,0:T(8,128)(2,1)} %get-tuple-element.235), channel_id=1, source_target_pairs={{0,0},{1,5},{2,4},{3,1},{4,2},{5,7},{6,6},{7,3},{8,8},{9,13},{10,1... | collective-permute-start | bytes 1572872 | tf_op jit(solution)/shard_map/ppermute | solution.py:567
  32.1 18.1 %collective-permute-start.1 = (bf16[256,1024]{1,0:T(8,128)(2,1)}, bf16[256,1024]{1,0:T(8,128)(2,1)}, u32[]{:S(2)}, u32[]{:S(2)}) collective-permute-start(bf16[256,1024]{1,0:T(8,128)(2,1)} %get-tuple-element.236), channel_id=1, source_target_pairs={{0,1},{1,4},{2,5},{3,0},{4,3},{5,6},{6,7},{7,2},{8,9},{9,12},{10,1... | collective-permute-start | bytes 1572872 | tf_op jit(solution)/shard_map/ppermute | solution.py:567
  37.0 15.9 %collective-permute-start.6 = (bf16[384,1024]{1,0:T(8,128)(2,1)S(1)}, bf16[384,1024]{1,0:T(8,128)(2,1)}, u32[]{:S(2)}, u32[]{:S(2)}) collective-permute-start(bf16[384,1024]{1,0:T(8,128)(2,1)S(1)} %pad_maximum_fusion.7.refs_1_.refs_5_.refs_25_.refs_29_.refs_2_.refs_6_.refs_28_.refs_32_), channel_id=1, source_target_pairs={{0,4},{1,5},{2,6},{3,7},{4,0},{5,1},{6,2},{7,3},{8,12},{9,13},{10,... | collective-permute-start | bytes 2359304 | tf_op jit(solution)/shard_map/ppermute | solution.py:567
  43.7 11.5 %collective-permute-start.9 = (bf16[384,1024]{1,0:T(8,128)(2,1)S(1)}, bf16[384,1024]{1,0:T(8,128)(2,1)}, u32[]{:S(2)}, u32[]{:S(2)}) collective-permute-start(bf16[384,1024]{1,0:T(8,128)(2,1)S(1)} %pad_maximum_fusion.8.refs_9_.refs_11_.refs_17_.refs_19_.refs_12_.refs_14_.refs_20_.refs_22_), channel_id=1, source_target_pairs={{0,4},{1,5},{2,6},{3,7},{4,0},{5,1},{6,2},{7,3},{8,12},{9,13},{10,... | collective-permute-start | bytes 2359304 | tf_op jit(solution)/shard_map/ppermute | solution.py:567
  43.7 14.0 %collective-permute-start.11 = (bf16[384,1024]{1,0:T(8,128)(2,1)S(1)}, bf16[384,1024]{1,0:T(8,128)(2,1)}, u32[]{:S(2)}, u32[]{:S(2)}) collective-permute-start(bf16[384,1024]{1,0:T(8,128)(2,1)S(1)} %collective-permute-done.10.refs_13_.refs_15_.refs_21_.refs_23_.refs_16_.refs_18_.refs_24_.refs_26_), channel_id=1, source_target_pairs={{0,4},{1,5},{2,6},{3,7},{4,0},{5,1},{6,2},{7,3},{8,12},{9,13},{10,... | collective-permute-start | bytes 2359304 | tf_op jit(solution)/shard_map/ppermute | solution.py:567
  44.2 13.5 %collective-permute-start.8 = (bf16[384,1024]{1,0:T(8,128)(2,1)S(1)}, bf16[384,1024]{1,0:T(8,128)(2,1)}, u32[]{:S(2)}, u32[]{:S(2)}) collective-permute-start(bf16[384,1024]{1,0:T(8,128)(2,1)S(1)} %collective-permute-done.7.refs_3_.refs_7_.refs_27_.refs_31_.refs_4_.refs_8_.refs_30_.refs_34_), channel_id=1, source_target_pairs={{0,4},{1,5},{2,6},{3,7},{4,0},{5,1},{6,2},{7,3},{8,12},{9,13},{10,... | collective-permute-start | bytes 2359304 | tf_op jit(solution)/shard_map/ppermute | solution.py:567
  50.3 15.4 %collective-permute-start.4 = (bf16[320,1024]{1,0:T(8,128)(2,1)}, bf16[320,1024]{1,0:T(8,128)(2,1)}, u32[]{:S(2)}, u32[]{:S(2)}) collective-permute-start(bf16[320,1024]{1,0:T(8,128)(2,1)} %get-tuple-element.97), channel_id=1, source_target_pairs={{0,8},{1,9},{2,10},{3,11},{4,12},{5,13},{6,14},{7,15},{8,0},{9,1},... | collective-permute-start | bytes 1966088 | tf_op jit(solution)/shard_map/ppermute | solution.py:567
  52.8 14.4 %collective-permute-start.5 = (bf16[320,1024]{1,0:T(8,128)(2,1)}, bf16[320,1024]{1,0:T(8,128)(2,1)S(1)}, u32[]{:S(2)}, u32[]{:S(2)}) collective-permute-start(bf16[320,1024]{1,0:T(8,128)(2,1)} %get-tuple-element.98), channel_id=1, source_target_pairs={{0,16},{1,17},{2,18},{3,19},{4,20},{5,21},{6,22},{7,23},{8,24},{9,... | collective-permute-start | bytes 1966088 | tf_op jit(solution)/shard_map/ppermute | solution.py:567
  55.2 15.9 %collective-permute-start.17 = (s32[2,5]{1,0:T(2,128)S(1)}, s32[2,5]{1,0:T(2,128)S(1)}, u32[]{:S(2)}, u32[]{:S(2)}) collective-permute-start(s32[2,5]{1,0:T(2,128)S(1)} %pad_add_fusion.1), channel_id=1, source_target_pairs={{0,4},{1,5},{2,6},{3,7},{4,0},{5,1},{6,2},{7,3},{8,12},{9,13},{10,... | collective-permute-start | bytes 128 | tf_op jit(solution)/shard_map/ppermute | solution.py:567
  68.0 20.9 %collective-permute-start.16 = (bf16[512,2048]{1,0:T(8,128)(2,1)}, bf16[512,2048]{1,0:T(8,128)(2,1)}, u32[]{:S(2)}, u32[]{:S(2)}) collective-permute-start(bf16[512,2048]{1,0:T(8,128)(2,1)} %get-tuple-element.107.ko.vo), channel_id=1, source_target_pairs={{0,4},{1,5},{2,6},{3,7},{4,0},{5,1},{6,2},{7,3},{8,12},{9,13},{10,... | collective-permute-start | bytes 6291464 | tf_op jit(solution)/shard_map/ppermute | solution.py:567
  77.0 31.3 %collective-permute-start.13 = (bf16[640,1024]{1,0:T(8,128)(2,1)}, bf16[640,1024]{1,0:T(8,128)(2,1)S(1)}, u32[]{:S(2)}, u32[]{:S(2)}) collective-permute-start(bf16[640,1024]{1,0:T(8,128)(2,1)} %constant_dynamic-update-slice_fusion.2.refs_2_.refs_6_.refs_10_.refs_14_.refs_24_.refs_28_.refs_12_.refs_16_), channel_id=1, source_target_pairs={{0,8},{1,9},{2,10},{3,11},{4,12},{5,13},{6,14},{7,15},{8,0},{9,1},... | collective-permute-start | bytes 3932168 | tf_op jit(solution)/shard_map/ppermute | solution.py:567
  77.1 31.1 %collective-permute-start.14 = (bf16[256,1024]{1,0:T(8,128)(2,1)}, bf16[256,1024]{1,0:T(8,128)(2,1)S(1)}, u32[]{:S(2)}, u32[]{:S(2)}) collective-permute-start(bf16[256,1024]{1,0:T(8,128)(2,1)} %get-tuple-element.105), channel_id=1, source_target_pairs={{0,0},{1,5},{2,4},{3,1},{4,2},{5,7},{6,6},{7,3},{8,8},{9,13},{10,1... | collective-permute-start | bytes 1572872 | tf_op jit(solution)/shard_map/ppermute | solution.py:567
  85.3 22.9 %collective-permute-start.15 = (bf16[256,1024]{1,0:T(8,128)(2,1)}, bf16[256,1024]{1,0:T(8,128)(2,1)S(1)}, u32[]{:S(2)}, u32[]{:S(2)}) collective-permute-start(bf16[256,1024]{1,0:T(8,128)(2,1)} %get-tuple-element.106), channel_id=1, source_target_pairs={{0,1},{1,4},{2,5},{3,0},{4,3},{5,6},{6,7},{7,2},{8,9},{9,12},{10,1... | collective-permute-start | bytes 1572872 | tf_op jit(solution)/shard_map/ppermute | solution.py:567
  87.9 29.2 %collective-permute-start.12 = (bf16[640,1024]{1,0:T(8,128)(2,1)}, bf16[640,1024]{1,0:T(8,128)(2,1)S(1)}, u32[]{:S(2)}, u32[]{:S(2)}) collective-permute-start(bf16[640,1024]{1,0:T(8,128)(2,1)} %constant_dynamic-update-slice_fusion.refs_1_.refs_3_.refs_9_.refs_11_.refs_2_.refs_4_.refs_16_.refs_18_.refs_10_.re, ...), channel_id=1, source_target_pairs={{0,16},{1,17},{2,18},{3,19},{4,20},{5,21},{6,22},{7,23},{8,24},{9,... | collective-permute-start | bytes 3932168 | tf_op jit(solution)/shard_map/ppermute | solution.py:567
  131.4 20.8 %collective-permute-start.24 = (bf16[512,2048]{1,0:T(8,128)(2,1)}, bf16[512,2048]{1,0:T(8,128)(2,1)}, u32[]{:S(2)}, u32[]{:S(2)}) collective-permute-start(bf16[512,2048]{1,0:T(8,128)(2,1)} %source_kv.1.ko.vo), channel_id=1, source_target_pairs={{0,4},{1,5},{2,6},{3,7},{4,0},{5,1},{6,2},{7,3},{8,12},{9,13},{10,... | collective-permute-start | bytes 6291464 | tf_op jit(solution)/shard_map/ppermute | solution.py:567
  131.6 11.3 %collective-permute-start.18 = (bf16[640,1024]{1,0:T(8,128)(2,1)}, bf16[640,1024]{1,0:T(8,128)(2,1)S(1)}, u32[]{:S(2)}, u32[]{:S(2)}) collective-permute-start(bf16[640,1024]{1,0:T(8,128)(2,1)} %constant_dynamic-update-slice_fusion.2.refs_2_.refs_6_.refs_10_.refs_14_.refs_24_.refs_28_.refs_12_.refs_16_), channel_id=1, source_target_pairs={{0,4},{1,5},{2,6},{3,7},{4,0},{5,1},{6,2},{7,3},{8,12},{9,13},{10,... | collective-permute-start | bytes 3932168 | tf_op jit(solution)/shard_map/ppermute | solution.py:567
  132.0 11.0 %collective-permute-start.19 = (bf16[640,1024]{1,0:T(8,128)(2,1)S(1)}, bf16[640,1024]{1,0:T(8,128)(2,1)S(1)}, u32[]{:S(2)}, u32[]{:S(2)}) collective-permute-start(bf16[640,1024]{1,0:T(8,128)(2,1)S(1)} %copy-done.1), channel_id=1, source_target_pairs={{0,4},{1,5},{2,6},{3,7},{4,0},{5,1},{6,2},{7,3},{8,12},{9,13},{10,... | collective-permute-start | bytes 3932168 | tf_op jit(solution)/shard_map/ppermute | solution.py:567
  136.5 15.6 %collective-permute-start.20 = (bf16[128,2048]{1,0:T(8,128)(2,1)}, bf16[128,2048]{1,0:T(8,128)(2,1)}, u32[]{:S(2)}, u32[]{:S(2)}) collective-permute-start(bf16[128,2048]{1,0:T(8,128)(2,1)} %get-tuple-element.114), channel_id=1, source_target_pairs={{0,8},{1,9},{2,10},{3,11},{4,12},{5,13},{6,14},{7,15},{8,0},{9,1},... | collective-permute-start | bytes 1572872 | tf_op jit(solution)/shard_map/ppermute | solution.py:567
  137.8 14.4 %collective-permute-start.21 = (bf16[128,2048]{1,0:T(8,128)(2,1)}, bf16[128,2048]{1,0:T(8,128)(2,1)}, u32[]{:S(2)}, u32[]{:S(2)}) collective-permute-start(bf16[128,2048]{1,0:T(8,128)(2,1)} %get-tuple-element.115), channel_id=1, source_target_pairs={{0,16},{1,17},{2,18},{3,19},{4,20},{5,21},{6,22},{7,23},{8,24},{9,... | collective-permute-start | bytes 1572872 | tf_op jit(solution)/shard_map/ppermute | solution.py:567
  154.1 41.6 %collective-permute-start.26 = (bf16[256,2048]{1,0:T(8,128)(2,1)}, bf16[256,2048]{1,0:T(8,128)(2,1)S(1)}, u32[]{:S(2)}, u32[]{:S(2)}) collective-permute-start(bf16[256,2048]{1,0:T(8,128)(2,1)} %constant_dynamic-update-slice_fusion.6.refs_8_.refs_12_), channel_id=1, source_target_pairs={{0,8},{1,9},{2,10},{3,11},{4,12},{5,13},{6,14},{7,15},{8,0},{9,1},... | collective-permute-start | bytes 3145736 | tf_op jit(solution)/shard_map/ppermute | solution.py:567
  156.2 54.8 %collective-permute-start.31 = (bf16[256,2048]{1,0:T(8,128)(2,1)}, bf16[256,2048]{1,0:T(8,128)(2,1)}, u32[]{:S(2)}, u32[]{:S(2)}) collective-permute-start(bf16[256,2048]{1,0:T(8,128)(2,1)} %constant_dynamic-update-slice_fusion.6.refs_8_.refs_12_), channel_id=1, source_target_pairs={{0,4},{1,5},{2,6},{3,7},{4,0},{5,1},{6,2},{7,3},{8,12},{9,13},{10,... | collective-permute-start | bytes 3145736 | tf_op jit(solution)/shard_map/ppermute | solution.py:567
  158.0 34.2 %collective-permute-start.27 = (bf16[256,1024]{1,0:T(8,128)(2,1)}, bf16[256,1024]{1,0:T(8,128)(2,1)S(1)}, u32[]{:S(2)}, u32[]{:S(2)}) collective-permute-start(bf16[256,1024]{1,0:T(8,128)(2,1)} %get-tuple-element.123), channel_id=1, source_target_pairs={{0,0},{1,5},{2,4},{3,1},{4,2},{5,7},{6,6},{7,3},{8,8},{9,13},{10,1... | collective-permute-start | bytes 1572872 | tf_op jit(solution)/shard_map/ppermute | solution.py:567
  161.8 30.4 %collective-permute-start.28 = (bf16[256,1024]{1,0:T(8,128)(2,1)}, bf16[256,1024]{1,0:T(8,128)(2,1)S(1)}, u32[]{:S(2)}, u32[]{:S(2)}) collective-permute-start(bf16[256,1024]{1,0:T(8,128)(2,1)} %get-tuple-element.124), channel_id=1, source_target_pairs={{0,1},{1,4},{2,5},{3,0},{4,3},{5,6},{6,7},{7,2},{8,9},{9,12},{10,1... | collective-permute-start | bytes 1572872 | tf_op jit(solution)/shard_map/ppermute | solution.py:567
  165.4 31.5 %collective-permute-start.25 = (bf16[256,2048]{1,0:T(8,128)(2,1)}, bf16[256,2048]{1,0:T(8,128)(2,1)S(1)}, u32[]{:S(2)}, u32[]{:S(2)}) collective-permute-start(bf16[256,2048]{1,0:T(8,128)(2,1)} %constant_dynamic-update-slice_fusion.4.refs_0_.refs_2_), channel_id=1, source_target_pairs={{0,16},{1,17},{2,18},{3,19},{4,20},{5,21},{6,22},{7,23},{8,24},{9,... | collective-permute-start | bytes 3145736 | tf_op jit(solution)/shard_map/ppermute | solution.py:567
  192.2 18.8 %collective-permute-start.29 = (bf16[256,2048]{1,0:T(8,128)(2,1)}, bf16[256,2048]{1,0:T(8,128)(2,1)}, u32[]{:S(2)}, u32[]{:S(2)}) collective-permute-start(bf16[256,2048]{1,0:T(8,128)(2,1)} %constant_dynamic-update-slice_fusion.4.refs_0_.refs_2_), channel_id=1, source_target_pairs={{0,4},{1,5},{2,6},{3,7},{4,0},{5,1},{6,2},{7,3},{8,12},{9,13},{10,... | collective-permute-start | bytes 3145736 | tf_op jit(solution)/shard_map/ppermute | solution.py:567
  197.9 13.1 %collective-permute-start.30 = (bf16[256,2048]{1,0:T(8,128)(2,1)}, bf16[256,2048]{1,0:T(8,128)(2,1)S(1)}, u32[]{:S(2)}, u32[]{:S(2)}) collective-permute-start(bf16[256,2048]{1,0:T(8,128)(2,1)} %get-tuple-element.129.refs_4_.refs_6_), channel_id=1, source_target_pairs={{0,4},{1,5},{2,6},{3,7},{4,0},{5,1},{6,2},{7,3},{8,12},{9,13},{10,... | collective-permute-start | bytes 3145736 | tf_op jit(solution)/shard_map/ppermute | solution.py:567
  198.3 12.7 %collective-permute-start.32 = (bf16[256,2048]{1,0:T(8,128)(2,1)}, bf16[256,2048]{1,0:T(8,128)(2,1)S(1)}, u32[]{:S(2)}, u32[]{:S(2)}) collective-permute-start(bf16[256,2048]{1,0:T(8,128)(2,1)} %get-tuple-element.130.refs_10_.refs_14_), channel_id=1, source_target_pairs={{0,4},{1,5},{2,6},{3,7},{4,0},{5,1},{6,2},{7,3},{8,12},{9,13},{10,... | collective-permute-start | bytes 3145736 | tf_op jit(solution)/shard_map/ppermute | solution.py:567
  242.5 27.2 %collective-permute-start.33 = (bf16[512,1024]{1,0:T(8,128)(2,1)S(1)}, bf16[512,1024]{1,0:T(8,128)(2,1)S(1)}, u32[]{:S(2)}, u32[]{:S(2)}) collective-permute-start(bf16[512,1024]{1,0:T(8,128)(2,1)S(1)} %broadcast_select_fusion.2), channel_id=1, source_target_pairs={{0,4},{1,5},{2,6},{3,7},{4,0},{5,1},{6,2},{7,3},{8,12},{9,13},{10,... | collective-permute-start | bytes 3145736 | tf_op jit(solution)/shard_map/ppermute | solution.py:567
  244.1 60.3 %collective-permute-start.37 = (bf16[256,1024]{1,0:T(8,128)(2,1)}, bf16[256,1024]{1,0:T(8,128)(2,1)}, u32[]{:S(2)}, u32[]{:S(2)}) collective-permute-start(bf16[256,1024]{1,0:T(8,128)(2,1)} %get-tuple-element.224), channel_id=1, source_target_pairs={{0,0},{1,3},{2,4},{3,7},{4,2},{5,1},{6,6},{7,5},{8,8},{9,11},{10,1... | collective-permute-start | bytes 1572872 | tf_op jit(solution)/shard_map/ppermute | solution.py:567
  248.2 56.2 %collective-permute-start.38 = (bf16[256,1024]{1,0:T(8,128)(2,1)}, bf16[256,1024]{1,0:T(8,128)(2,1)}, u32[]{:S(2)}, u32[]{:S(2)}) collective-permute-start(bf16[256,1024]{1,0:T(8,128)(2,1)} %get-tuple-element.223), channel_id=1, source_target_pairs={{0,3},{1,0},{2,7},{3,4},{4,1},{5,2},{6,5},{7,6},{8,11},{9,8},{10,1... | collective-permute-start | bytes 1572872 | tf_op jit(solution)/shard_map/ppermute | solution.py:567
  274.8 29.6 %collective-permute-start.34 = (bf16[128,1024]{1,0:T(8,128)(2,1)S(1)}, bf16[128,1024]{1,0:T(8,128)(2,1)S(1)}, u32[]{:S(2)}, u32[]{:S(2)}) collective-permute-start(bf16[128,1024]{1,0:T(8,128)(2,1)S(1)} %get-tuple-element.222), channel_id=1, source_target_pairs={{0,8},{1,9},{2,10},{3,11},{4,12},{5,13},{6,14},{7,15},{8,0},{9,1},... | collective-permute-start | bytes 786440 | tf_op jit(solution)/shard_map/ppermute | solution.py:567
  275.9 28.5 %collective-permute-start.35 = (bf16[128,1024]{1,0:T(8,128)(2,1)S(1)}, bf16[128,1024]{1,0:T(8,128)(2,1)S(1)}, u32[]{:S(2)}, u32[]{:S(2)}) collective-permute-start(bf16[128,1024]{1,0:T(8,128)(2,1)S(1)} %get-tuple-element.221), channel_id=1, source_target_pairs={{0,16},{1,17},{2,18},{3,19},{4,20},{5,21},{6,22},{7,23},{8,24},{9,... | collective-permute-start | bytes 786440 | tf_op jit(solution)/shard_map/ppermute | solution.py:567
  276.3 28.2 %collective-permute-start.36 = (bf16[128,1024]{1,0:T(8,128)(2,1)S(1)}, bf16[128,1024]{1,0:T(8,128)(2,1)S(1)}, u32[]{:S(2)}, u32[]{:S(2)}) collective-permute-start(bf16[128,1024]{1,0:T(8,128)(2,1)S(1)} %get-tuple-element.220), channel_id=1, source_target_pairs={{0,24},{1,25},{2,26},{3,27},{4,28},{5,29},{6,30},{7,31},{8,16},{9,... | collective-permute-start | bytes 786440 | tf_op jit(solution)/shard_map/ppermute | solution.py:567
  305.3 14.5 %collective-permute-start.42 = (bf16[512,2048]{1,0:T(8,128)(2,1)}, bf16[512,2048]{1,0:T(8,128)(2,1)S(1)}, u32[]{:S(2)}, u32[]{:S(2)}) collective-permute-start(bf16[512,2048]{1,0:T(8,128)(2,1)} %get-tuple-element.158), channel_id=1, source_target_pairs={{0,4},{1,5},{2,6},{3,7},{4,0},{5,1},{6,2},{7,3},{8,12},{9,13},{10,... | collective-permute-start | bytes 6291464 | tf_op jit(solution)/shard_map/ppermute | solution.py:567
  308.4 11.4 %collective-permute-start.39 = (bf16[32,1024]{1,0:T(8,128)(2,1)S(1)}, bf16[32,1024]{1,0:T(8,128)(2,1)S(1)}, u32[]{:S(2)}, u32[]{:S(2)}) collective-permute-start(bf16[32,1024]{1,0:T(8,128)(2,1)S(1)} %get-tuple-element.244), channel_id=1, source_target_pairs={{0,1},{1,0},{2,3},{3,2},{4,5},{5,4},{6,7},{7,6},{8,9},{9,8},{10,11... | collective-permute-start | bytes 196616 | tf_op jit(solution)/shard_map/ppermute | solution.py:567
  322.1 14.1 %collective-permute-start.43 = (bf16[32,1024]{1,0:T(8,128)(2,1)S(1)}, bf16[32,1024]{1,0:T(8,128)(2,1)S(1)}, u32[]{:S(2)}, u32[]{:S(2)}) collective-permute-start(bf16[32,1024]{1,0:T(8,128)(2,1)S(1)} %add_convert_fusion.2.refs_20_), channel_id=1, source_target_pairs={{0,1},{1,0},{2,3},{3,2},{4,5},{5,4},{6,7},{7,6},{8,9},{9,8},{10,11... | collective-permute-start | bytes 196616 | tf_op jit(solution)/shard_map/ppermute | solution.py:567
  322.4 13.8 %collective-permute-start.44 = (bf16[32,1024]{1,0:T(8,128)(2,1)S(1)}, bf16[32,1024]{1,0:T(8,128)(2,1)S(1)}, u32[]{:S(2)}, u32[]{:S(2)}) collective-permute-start(bf16[32,1024]{1,0:T(8,128)(2,1)S(1)} %add_convert_fusion.2.refs_20_), channel_id=1, source_target_pairs={{0,2},{1,3},{2,0},{3,1},{4,6},{5,7},{6,4},{7,5},{8,10},{9,11},{10,... | collective-permute-start | bytes 196616 | tf_op jit(solution)/shard_map/ppermute | solution.py:567
  338.4 31.1 %collective-permute-start.46 = (bf16[128,1024]{1,0:T(8,128)(2,1)S(1)}, bf16[128,1024]{1,0:T(8,128)(2,1)S(1)}, u32[]{:S(2)}, u32[]{:S(2)}) collective-permute-start(bf16[128,1024]{1,0:T(8,128)(2,1)S(1)} %pad_maximum_fusion.13.refs_0_), channel_id=1, source_target_pairs={{0,8},{1,9},{2,10},{3,11},{4,12},{5,13},{6,14},{7,15},{8,0},{9,1},... | collective-permute-start | bytes 786440 | tf_op jit(solution)/shard_map/ppermute | solution.py:567
  339.5 30.1 %collective-permute-start.47 = (bf16[128,1024]{1,0:T(8,128)(2,1)S(1)}, bf16[128,1024]{1,0:T(8,128)(2,1)S(1)}, u32[]{:S(2)}, u32[]{:S(2)}) collective-permute-start(bf16[128,1024]{1,0:T(8,128)(2,1)S(1)} %pad_maximum_fusion.13.refs_0_), channel_id=1, source_target_pairs={{0,16},{1,17},{2,18},{3,19},{4,20},{5,21},{6,22},{7,23},{8,24},{9,... | collective-permute-start | bytes 786440 | tf_op jit(solution)/shard_map/ppermute | solution.py:567
  339.9 29.7 %collective-permute-start.48 = (bf16[128,1024]{1,0:T(8,128)(2,1)S(1)}, bf16[128,1024]{1,0:T(8,128)(2,1)S(1)}, u32[]{:S(2)}, u32[]{:S(2)}) collective-permute-start(bf16[128,1024]{1,0:T(8,128)(2,1)S(1)} %pad_maximum_fusion.13.refs_0_), channel_id=1, source_target_pairs={{0,24},{1,25},{2,26},{3,27},{4,28},{5,29},{6,30},{7,31},{8,16},{9,... | collective-permute-start | bytes 786440 | tf_op jit(solution)/shard_map/ppermute | solution.py:567
  342.4 28.2 %collective-permute-start.49 = (bf16[256,1024]{1,0:T(8,128)(2,1)S(1)}, bf16[256,1024]{1,0:T(8,128)(2,1)S(1)}, u32[]{:S(2)}, u32[]{:S(2)}) collective-permute-start(bf16[256,1024]{1,0:T(8,128)(2,1)S(1)} %get-tuple-element.216), channel_id=1, source_target_pairs={{0,0},{1,3},{2,4},{3,7},{4,2},{5,1},{6,6},{7,5},{8,8},{9,11},{10,1... | collective-permute-start | bytes 1572872 | tf_op jit(solution)/shard_map/ppermute | solution.py:567
  347.3 23.3 %collective-permute-start.50 = (bf16[256,1024]{1,0:T(8,128)(2,1)S(1)}, bf16[256,1024]{1,0:T(8,128)(2,1)S(1)}, u32[]{:S(2)}, u32[]{:S(2)}) collective-permute-start(bf16[256,1024]{1,0:T(8,128)(2,1)S(1)} %get-tuple-element.215), channel_id=1, source_target_pairs={{0,3},{1,0},{2,7},{3,4},{4,1},{5,2},{6,5},{7,6},{8,11},{9,8},{10,1... | collective-permute-start | bytes 1572872 | tf_op jit(solution)/shard_map/ppermute | solution.py:567
  373.3 16.1 %collective-permute-start.51 = (bf16[512,1024]{1,0:T(8,128)(2,1)S(1)}, bf16[512,1024]{1,0:T(8,128)(2,1)}, u32[]{:S(2)}, u32[]{:S(2)}) collective-permute-start(bf16[512,1024]{1,0:T(8,128)(2,1)S(1)} %pad_maximum_fusion.4.refs_37_.refs_0_), channel_id=1, source_target_pairs={{0,4},{1,5},{2,6},{3,7},{4,0},{5,1},{6,2},{7,3},{8,12},{9,13},{10,... | collective-permute-start | bytes 3145736 | tf_op jit(solution)/shard_map/ppermute | solution.py:567
  391.8 27.4 %collective-permute-start.53 = (bf16[256,1024]{1,0:T(8,128)(2,1)}, bf16[256,1024]{1,0:T(8,128)(2,1)S(1)}, u32[]{:S(2)}, u32[]{:S(2)}) collective-permute-start(bf16[256,1024]{1,0:T(8,128)(2,1)} %get-tuple-element.209), channel_id=1, source_target_pairs={{0,0},{1,3},{2,4},{3,7},{4,2},{5,1},{6,6},{7,5},{8,8},{9,11},{10,1... | collective-permute-start | bytes 1572872 | tf_op jit(solution)/shard_map/ppermute | solution.py:567
  394.8 24.4 %collective-permute-start.54 = (bf16[256,1024]{1,0:T(8,128)(2,1)}, bf16[256,1024]{1,0:T(8,128)(2,1)S(1)}, u32[]{:S(2)}, u32[]{:S(2)}) collective-permute-start(bf16[256,1024]{1,0:T(8,128)(2,1)} %get-tuple-element.210), channel_id=1, source_target_pairs={{0,3},{1,0},{2,7},{3,4},{4,1},{5,2},{6,5},{7,6},{8,11},{9,8},{10,1... | collective-permute-start | bytes 1572872 | tf_op jit(solution)/shard_map/ppermute | solution.py:567
  (68 other events, 299.0 us)
Sparse Core Ops, SparseCore 0:
  118.3 73.1 all-gather.1

commit v4 on v3

v4 whole, which is shorter than its diff:
```python
import functools

import jax
import jax.numpy as jnp
from jax import lax
from jax.experimental import pallas as pl
from jax.experimental.pallas import tpu as pltpu
from jax.sharding import PartitionSpec as P

BF, F32 = jnp.bfloat16, jnp.float32
NEG = -1e30
LOG2E = 1.4426950408889634
PER = 2

SELF_PLANS = (
    (((0, True),), ((0, False), (2, False), (3, False), (1, True))),
    (((2, False), (0, True)), ((2, False), (0, False), (1, True))),
)
CROSS_PLANS = ((((0, False), (1, False), (2, False), (3, False)),) * 2,)


def nt(a, b):
    return lax.dot_general(a, b, (((1,), (1,)), ((), ())), preferred_element_type=F32)


def nn(a, b):
    return lax.dot_general(a, b, (((1,), (0,)), ((), ())), preferred_element_type=F32)


def tn(a, b):
    return lax.dot_general(a, b, (((0,), (0,)), ((), ())), preferred_element_type=F32)


def cost(us):
    return pl.CostEstimate(flops=int(us * 3e8), bytes_accessed=1024, transcendentals=0)


def params():
    return pltpu.CompilerParams(vmem_limit_bytes=64 * 1024 * 1024)


def shape(rows, cols, dtype):
    return jax.ShapeDtypeStruct((rows, cols), dtype)


class Whole:
    def __init__(self, array):
        self.arrays, self.shape, self.dtype, self.count = [array], array.shape, array.dtype, 1

    def copies(self, info, refs, buf, sem, first):
        return [pltpu.make_async_copy(refs[0], buf, sem.at[first])]


class Pieces:
    def __init__(self, stride, *pieces):
        self.stride, self.pieces = stride, pieces
        self.arrays = [a for parts, *_ in pieces for a, _ in parts]
        self.shape, self.dtype = (8 * stride, self.arrays[0].shape[1]), self.arrays[0].dtype
        self.count = len(self.arrays)

    def copies(self, info, refs, buf, sem, first):
        out = []
        for parts, at, rows, base in self.pieces:
            for m, (_, start) in enumerate(parts):
                to = pl.multiple_of((info[1] ^ m) * self.stride + base, 16)
                i = len(out)
                out.append(
                    pltpu.make_async_copy(
                        refs[i].at[pl.ds(start + at, rows)], buf.at[pl.ds(to, rows)], sem.at[first + i]
                    )
                )
        return out


class Shards:
    def __init__(self, array, owners, at, rows):
        self.arrays, self.count, self.at, self.rows = [array], owners, at, rows
        self.each = array.shape[0] // owners
        self.shape, self.dtype = (owners * rows, array.shape[1]), array.dtype

    def copies(self, info, refs, buf, sem, first):
        return [
            pltpu.make_async_copy(
                refs[0].at[pl.ds(j * self.each + self.at, self.rows)],
                buf.at[pl.ds(j * self.rows, self.rows)],
                sem.at[first + j],
            )
            for j in range(self.count)
        ]


class Slots:
    def __init__(self, arrays, at, rows):
        self.arrays, self.at, self.rows, self.count = list(arrays), at, rows, 2
        self.shape, self.dtype = (2 * rows, arrays[0].shape[1]), arrays[0].dtype

    def copies(self, info, refs, buf, sem, first):
        return [
            pltpu.make_async_copy(
                refs[k].at[pl.ds(self.at, self.rows)],
                buf.at[pl.ds(pl.multiple_of((info[2] ^ k) * self.rows, 16), self.rows)],
                sem.at[first + k],
            )
            for k in range(2)
        ]


class Chunk:
    def __init__(self, array, k):
        self.arrays, self.k, self.count = [array], k, 1
        self.shape, self.dtype = (array.shape[0] // 2, array.shape[1]), array.dtype

    def copies(self, info, refs, buf, sem, first):
        rows = self.shape[0]
        at = pl.multiple_of((info[2] ^ self.k) * rows, 16)
        return [pltpu.make_async_copy(refs[0].at[pl.ds(at, rows)], buf, sem.at[first])]


class Loads:
    def __init__(self, loads):
        self.loads = [v if hasattr(v, "copies") else Whole(v) for v in loads]
        self.arrays = [a for v in self.loads for a in v.arrays]
        self.specs = [pl.BlockSpec(memory_space=pl.ANY)] * len(self.arrays)
        self.scratch = [pltpu.VMEM(v.shape, v.dtype) for v in self.loads]
        self.scratch.append(pltpu.SemaphoreType.DMA((sum(v.count for v in self.loads),)))

    def bind(self, info, refs, scratch):
        bufs, sem = scratch[:-1], scratch[-1]
        at = first = 0
        out = []
        for v, buf in zip(self.loads, bufs):
            out.append((v.copies(info, refs[at : at + len(v.arrays)], buf, sem, first), buf))
            at += len(v.arrays)
            first += v.count
        return out


def start_all(bound):
    for copies, _ in bound:
        for c in copies:
            c.start()


def getter(bound):
    ready = set()

    def get(i):
        copies, buf = bound[i]
        if i not in ready:
            for c in copies:
                c.wait()
            ready.add(i)
        return buf

    return get


ANYWHERE = pl.BlockSpec(memory_space=pl.ANY)


def half_mask(shape, h):
    lane = lax.broadcasted_iota(jnp.int32, shape, 1)
    return (lane < 64) if h == 0 else (lane >= 64)


def top(parts):
    rows = 64
    pieces = [p[i : i + rows] for p in parts for i in range(0, p.shape[0], rows)]
    while len(pieces) > 1:
        pieces = [jnp.maximum(*pieces[i : i + 2]) if i + 1 < len(pieces) else pieces[i] for i in range(0, len(pieces), 2)]
    return jnp.max(pieces[0], axis=0, keepdims=True)


def forward_pair(plan, C, q, ks, vs, qa, kas, put, p_ref):
    kaug = [[jnp.where(half_mask(k.shape, h), k, a) for k, a in zip(ks, kas)] for h in range(2)]
    vts = [v.T for v in vs]
    ones = jnp.ones((16, C), BF)
    units, n = [], 0
    for slot, blocks in enumerate(plan):
        units += [(slot, h, n, blocks) for h in range(2)]
        n += len(blocks)

    def scores_of(unit):
        slot, h, _, blocks = unit
        rows = slice(slot * C, (slot + 1) * C)
        qh = jnp.where(half_mask((C, 128), h), q[rows], qa[rows])
        scores = []
        for kb, diagonal in blocks:
            s = nt(kaug[h][kb], qh)
            if diagonal:
                ki = lax.broadcasted_iota(jnp.int32, s.shape, 0)
                qi = lax.broadcasted_iota(jnp.int32, s.shape, 1)
                s = jnp.where(ki <= qi, s, NEG)
            scores.append(s)
        return scores, top(scores)

    def rest(unit, scores, m):
        _, h, n, blocks = unit
        ps = [jnp.exp2(s - m).astype(BF) for s in scores]
        for i, p in enumerate(ps):
            p_ref[h, n + i] = p
        values = [jnp.concatenate([vts[kb][64 * h : 64 * h + 64], ones], axis=0) for kb, _ in blocks]
        both = nn(jnp.concatenate(values, axis=1), jnp.concatenate(ps, axis=0))
        inv = 1.0 / both[64:65]
        return both[:64] * inv, jnp.broadcast_to(inv, (64, C))

    done = []
    AHEAD = 2
    pending = [scores_of(u) for u in units[:AHEAD]]
    for i, unit in enumerate(units):
        if i + AHEAD < len(units):
            pending.append(scores_of(units[i + AHEAD]))
        done.append(rest(unit, *pending[i]))
        if i % 2:
            halves, inverses = zip(*done[-2:])
            put(unit[0], jnp.concatenate(halves, axis=0).T.astype(BF), jnp.concatenate(inverses, axis=0).T)


def by_plan(plans, info, run):
    if len(plans) == 1:
        run(plans[0])
    else:
        for v, plan in enumerate(plans):
            pl.when(info[0] == v)(functools.partial(run, plan))


def attend(plans, info, q, own, peer, qa, kao, kap, loads, outs, finish, deps=()):
    T, D = q.shape
    C, pairs = T // 2, D // 128
    steps = pairs // PER
    nb = sum(len(b) for b in plans[0])
    held = Loads(loads)

    def kernel(info_ref, q_ref, ko, vo, kp, vp, qa_ref, kao_ref, kap_ref, *refs):
        ins = refs[: len(held.arrays)]
        o_ref, p_ref, r_ref, *out_refs = refs[len(held.arrays) + len(deps) :][: 3 + len(outs)]
        att, *scratch = refs[len(held.arrays) + len(deps) + 3 + len(outs) :]
        step = pl.program_id(0)
        bound = held.bind(info_ref, ins, scratch)
        pl.when(step == 0)(lambda: start_all(bound))

        def run(plan):
            for j in range(PER):
                at = slice(128 * j, 128 * j + 128)
                cols = pl.ds(pl.multiple_of((step * PER + j) * 128, 128), 128)

                def put(slot, value, inverse):
                    o_ref[slot * C : (slot + 1) * C, at] = value
                    r_ref[slot * C : (slot + 1) * C, at] = inverse
                    att[slot * C : (slot + 1) * C, cols] = value

                def chunks(*rs):
                    return [r[i * C : (i + 1) * C, at] for r in rs for i in range(2)]

                masks = [m[i * C : (i + 1) * C] for m in (kao_ref, kap_ref) for i in range(2)]
                forward_pair(plan, C, q_ref[:, at], chunks(ko, kp), chunks(vo, vp), qa_ref[...], masks, put, p_ref.at[j])

        by_plan(plans, info_ref, run)

        @pl.when(step == steps - 1)
        def _():
            finish(getter(bound), att, *out_refs)

    col = pl.BlockSpec((T, 128 * PER), lambda h, *_: (0, h))
    val = pl.BlockSpec((T, 128 * PER), lambda h, *_: (0, steps + h))
    fix = pl.BlockSpec((T, 128), lambda h, *_: (0, 0))
    return pl.pallas_call(
        kernel,
        grid_spec=pltpu.PrefetchScalarGridSpec(
            num_scalar_prefetch=1,
            grid=(steps,),
            in_specs=[col] + [col, val] * 2 + [fix] * 3 + held.specs + [ANYWHERE] * len(deps),
            out_specs=[col, pl.BlockSpec((PER, 2, nb, C, C), lambda h, *_: (h, 0, 0, 0, 0)), col]
            + [pl.BlockSpec(o.shape, lambda h, *_: (0, 0)) for o in outs],
            scratch_shapes=[pltpu.VMEM((T, D), BF)] + held.scratch,
        ),
        out_shape=[shape(T, D, BF), jax.ShapeDtypeStruct((pairs, 2, nb, C, C), BF), shape(T, D, F32)] + list(outs),
        compiler_params=params(),
        cost_estimate=cost(25),
        name="attend",
    )(info, q, own, own, peer, peer, qa, kao, kap, *held.arrays, *deps)


def backward_pair(plan, C, q, ks, vs, do, o, r, p_ref, put, gown, gpeer):
    lane = lax.broadcasted_iota(jnp.int32, (C, 128), 1)
    l64 = lax.rem(lane, 64)
    ones = jnp.where(l64 < 2, 1.0, 0.0).astype(BF)
    vaug = [[jnp.where(half_mask(v.shape, h), v, ones) for v in vs] for h in range(2)]
    kts = [k.T for k in ks]
    by_key = [[] for _ in range(4)]
    zero = jnp.zeros((C, 128), BF)
    units, n = [], 0
    for slot, blocks in enumerate(plan):
        units += [(slot, h, n, blocks) for h in range(2)]
        n += len(blocks)

    def probs_back(unit):
        slot, h, n, blocks = unit
        rows = slice(slot * C, (slot + 1) * C)
        scaled = do[rows].astype(F32) * r[rows]
        dos = scaled.astype(BF)
        hm = lane < 64 if h == 0 else lane >= 64
        d = -jnp.sum(jnp.where(hm, scaled * o[rows].astype(F32), 0.0), axis=1, keepdims=True)
        hi = d.astype(BF)
        lo = (d - hi.astype(F32)).astype(BF)
        tail = jnp.where(l64 == 0, jnp.broadcast_to(hi, (C, 128)), jnp.where(l64 == 1, jnp.broadcast_to(lo, (C, 128)), zero))
        doa = jnp.where(hm, dos, tail)
        return [nt(vaug[h][kb], doa) for kb, _ in blocks], jnp.where(hm, dos, zero), jnp.where(hm, q[rows], zero)

    def rest(unit, dps, dom, qm):
        slot, h, n, blocks = unit
        grads = []
        for i, ((kb, _), dp) in enumerate(zip(blocks, dps)):
            pb = p_ref[h, n + i]
            ds = (pb.astype(F32) * dp).astype(BF)
            grads.append(ds)
            by_key[kb].append((pb, ds, dom, qm))
        wide = jnp.concatenate([kts[kb][64 * h : 64 * h + 64] for kb, _ in blocks], axis=1)
        return nn(wide, jnp.concatenate(grads, axis=0))

    done = []
    BACK = 2
    pending = [probs_back(u) for u in units[:BACK]]
    for i, unit in enumerate(units):
        if i + BACK < len(units):
            pending.append(probs_back(units[i + BACK]))
        done.append(rest(unit, *pending[i]))
        if i % 2:
            put(unit[0], jnp.concatenate(done[-2:], axis=0).T.astype(BF))
    for kb in range(4):
        ref = gown if kb < 2 else gpeer
        rows = slice((kb % 2) * C, (kb % 2) * C + C)
        if by_key[kb]:
            pbs, dss, doms, qms = zip(*by_key[kb])
            gk = nn(jnp.concatenate(dss, axis=1), jnp.concatenate(qms, axis=0))
            gv = nn(jnp.concatenate(pbs, axis=1), jnp.concatenate(doms, axis=0))
        else:
            gk = gv = jnp.zeros((C, 128), F32)
        ref[rows, 0:128] = (gk * (1.0 / LOG2E)).astype(BF)
        ref[rows, 128:256] = gv.astype(BF)


def attend_back(plans, info, q, own, peer, do, o, r, p, loads, outs, finish, deps=()):
    T, D = q.shape
    C, pairs, nb = T // 2, D // 128, p.shape[2]
    steps = pairs // PER
    held = Loads(loads)

    def kernel(info_ref, q_ref, ko, vo, kp, vp, do_ref, o_ref, r_ref, p_ref, *refs):
        ins = refs[: len(held.arrays)]
        gown, gpeer, *out_refs = refs[len(held.arrays) + len(deps) :][: 2 + len(outs)]
        gq, *scratch = refs[len(held.arrays) + len(deps) + 2 + len(outs) :]
        step = pl.program_id(0)
        bound = held.bind(info_ref, ins, scratch)
        pl.when(step == 0)(lambda: start_all(bound))

        def run(plan):
            for j in range(PER):
                at = slice(128 * j, 128 * j + 128)
                wide = slice(256 * j, 256 * j + 256)
                cols = pl.ds(pl.multiple_of((step * PER + j) * 128, 128), 128)

                def put(slot, value):
                    gq[slot * C : (slot + 1) * C, cols] = value

                def chunks(*rs):
                    return [r[i * C : (i + 1) * C, at] for r in rs for i in range(2)]

                backward_pair(plan, C, q_ref[:, at], chunks(ko, kp), chunks(vo, vp), do_ref[:, at], o_ref[:, at],
                              r_ref[:, at], p_ref.at[j], put, gown.at[:, wide], gpeer.at[:, wide])

        by_plan(plans, info_ref, run)

        @pl.when(step == steps - 1)
        def _():
            finish(getter(bound), gq, *out_refs)

    col = pl.BlockSpec((T, 128 * PER), lambda h, *_: (0, h))
    val = pl.BlockSpec((T, 128 * PER), lambda h, *_: (0, steps + h))
    wide = pl.BlockSpec((T, 256 * PER), lambda h, *_: (0, h))
    return pl.pallas_call(
        kernel,
        grid_spec=pltpu.PrefetchScalarGridSpec(
            num_scalar_prefetch=1,
            grid=(steps,),
            in_specs=[col] + [col, val] * 2 + [col] * 3
            + [pl.BlockSpec((PER, 2, nb, C, C), lambda h, *_: (h, 0, 0, 0, 0))] + held.specs + [ANYWHERE] * len(deps),
            out_specs=[wide] * 2 + [pl.BlockSpec(v.shape, lambda h, *_: (0, 0)) for v in outs],
            scratch_shapes=[pltpu.VMEM((T, D), BF)] + held.scratch,
        ),
        out_shape=[shape(T, 2 * D, BF)] * 2 + list(outs),
        compiler_params=params(),
        cost_estimate=cost(25),
        name="attend_back",
    )(info, q, own, own, peer, peer, do, o, r, p, *held.arrays, *deps)


def gate(values, deps):
    def kernel(*refs):
        del refs

    n = len(values)
    return pl.pallas_call(
        kernel,
        in_specs=[ANYWHERE] * (n + len(deps)),
        out_specs=[ANYWHERE] * n,
        out_shape=[jax.ShapeDtypeStruct(v.shape, v.dtype) for v in values],
        input_output_aliases={i: i for i in range(n)},
        cost_estimate=cost(0.1),
        name="gate",
    )(*values, *deps)


def barrier(*values):
    return gate(values, ())


def beside(pair, got, deps=()):
    def kernel(a, b, c, d, *refs):
        ab, cd = refs[-2:]
        n, m = a.shape[0], c.shape[0]
        ab[:n] = a[...]
        ab[n:] = b[...]
        cd[:m] = c[...]
        cd[m:] = d[...]

    full = pl.BlockSpec(memory_space=pltpu.VMEM)
    return pl.pallas_call(
        kernel,
        in_specs=[full] * 4 + [ANYWHERE] * len(deps),
        out_specs=[full] * 2,
        out_shape=[shape(2 * v.shape[0], v.shape[1], BF) for v in pair],
        cost_estimate=cost(2),
        compiler_params=params(),
        name="beside",
    )(pair[0], got[0], pair[1], got[1], *deps)


def stage(expand_shard, contract_shard, others, deps):
    rows, cols = expand_shard.shape
    half = cols // 2
    n = len(others)

    def kernel(e_ref, c_ref, *refs):
        e1, e2, c, rest = refs[-4:]
        e1[...] = e_ref[:, :half]
        e2[...] = e_ref[:, half:]
        c[...] = c_ref[...]
        at = 0
        for r in refs[:n]:
            rest[at : at + r.shape[0]] = r[...]
            at += r.shape[0]

    full = pl.BlockSpec(memory_space=pltpu.VMEM)
    return pl.pallas_call(
        kernel,
        in_specs=[full] * (2 + n) + [ANYWHERE] * len(deps),
        out_specs=[full] * 4,
        out_shape=[shape(rows, half, BF)] * 2
        + [shape(*contract_shard.shape, BF), shape(sum(o.shape[0] for o in others), others[0].shape[1], BF)],
        cost_estimate=cost(3),
        compiler_params=params(),
        name="stage",
    )(expand_shard, contract_shard, *others, *deps)


def halves(array, deps):
    rows, half = array.shape[0], array.shape[1] // 2

    def kernel(a, *refs):
        refs[-2][...] = a[:, :half]
        refs[-1][...] = a[:, half:]

    full = pl.BlockSpec(memory_space=pltpu.VMEM)
    return pl.pallas_call(
        kernel,
        in_specs=[full] + [ANYWHERE] * len(deps),
        out_specs=[full] * 2,
        out_shape=[shape(rows, half, BF)] * 2,
        cost_estimate=cost(2),
        compiler_params=params(),
        name="halves",
    )(array, *deps)


def fused(name, info, body, loads, outs, deps=(), extra=()):
    held = Loads(loads)
    total, nout = len(held.arrays), len(outs)

    def kernel(info_ref, *refs):
        out_refs = refs[total + len(deps) :][:nout]
        scratch = refs[total + len(deps) + nout :]
        bound = held.bind(info_ref, refs[:total], scratch[len(extra) :])
        start_all(bound)
        body(info_ref, getter(bound), *out_refs, *scratch[: len(extra)])

    return pl.pallas_call(
        kernel,
        grid_spec=pltpu.PrefetchScalarGridSpec(
            num_scalar_prefetch=1,
            grid=(1,),
            in_specs=held.specs + [ANYWHERE] * len(deps),
            out_specs=[pl.BlockSpec(o.shape, lambda i, *_: (0, 0)) for o in outs],
            scratch_shapes=list(extra) + held.scratch,
        ),
        out_shape=list(outs),
        compiler_params=params(),
        cost_estimate=cost(6),
        name=name,
    )(info, *held.arrays, *deps)


def norm_parts(v):
    mean = jnp.mean(v, axis=-1, keepdims=True)
    c = v - mean
    inv = lax.rsqrt(jnp.mean(c * c, axis=-1, keepdims=True) + 1e-05)
    return c * inv, inv


def norm_back(y, inv, g):
    return inv * (g - jnp.mean(g, axis=-1, keepdims=True) - y * jnp.mean(g * y, axis=-1, keepdims=True))


def gelu_pair(v):
    phi = 0.5 + 0.5 * lax.erf(v * 0.7071067811865476)
    pdf = jnp.exp(v * v * -0.5) * 0.3989422804014327
    return v * phi, phi + v * pdf


def put_slots(info_ref, value, first, second):
    C = value.shape[0] // 2
    for k, ref in enumerate((first, second)):
        ref[...] = value[pl.ds(pl.multiple_of((info_ref[2] ^ k) * C, 16), C)].astype(BF)


def project_qkv(info, x, w_query, w_key, w_value, deps):
    T, D = x.shape

    def body(info_ref, get, q, kv):
        xv = get(0)[...]
        kv[:, :D] = nn(xv, get(1)[...]).astype(BF)
        kv[:, D:] = nn(xv, get(2)[...]).astype(BF)
        q[...] = (nn(xv, get(3)[...]) * (0.125 * LOG2E)).astype(BF)

    return fused("qkv", info, body, [x, w_key, w_value, w_query], [shape(T, D, BF), shape(T, 2 * D, BF)], deps=deps)


def project_source(info, x, w_key, w_value, deps):
    T, D = x.shape

    def body(info_ref, get, kv):
        xv = get(0)[...]
        kv[:, :D] = nn(xv, get(1)[...]).astype(BF)
        kv[:, D:] = nn(xv, get(2)[...]).astype(BF)

    return fused("source_kv", info, body, [x, w_key, w_value], [shape(T, 2 * D, BF)], deps=deps)[0]


def attend_self(info, q, kv, kv_peer, masks, deps):
    return attend(SELF_PLANS, info, q, kv, kv_peer, *masks, [], [], lambda get, att: None, deps)


def between(info, x, att, w_out, c_query, src, c_key, c_value, deps):
    T, D = x.shape

    def body(info_ref, get, kv, y_ref, low_ref, inv_ref, cq_ref):
        xv = get(0)[...]
        kv[:, :D] = nn(xv, get(1)[...]).astype(BF)
        kv[:, D:] = nn(xv, get(2)[...]).astype(BF)
        y, inv = norm_parts(get(5)[...].astype(F32) + nn(get(3)[...], get(4)[...]))
        low = y.astype(BF)
        y_ref[...] = y
        low_ref[...] = low
        inv_ref[...] = jnp.broadcast_to(inv, inv_ref.shape)
        cq_ref[...] = (nn(low, get(6)[...]) * (0.125 * LOG2E)).astype(BF)

    outs = [shape(T, 2 * D, BF), shape(T, D, F32), shape(T, D, BF), shape(T, 128, F32), shape(T, D, BF)]
    return fused("between", info, body, [src, c_key, c_value, att, w_out, x, c_query], outs, deps=deps)


def attend_cross(info, q, kv, kv_peer, masks, y1, c_out, down, up, scale):
    T, D = q.shape
    A = down.shape[1]

    def finish(get, att, low_ref, inv_ref, sq_ref, gn_ref, base_ref):
        y, inv = norm_parts(get(1)[...] + nn(att[...], get(0)[...]))
        inv_ref[...] = jnp.broadcast_to(inv, inv_ref.shape)
        low = y.astype(BF)
        low_ref[...] = low
        h, g = gelu_pair(nn(low, get(2)[...]))
        hb = h.astype(BF)
        sq_ref[...] = hb
        gn_ref[...] = g.astype(BF)
        base_ref[...] = y + get(4)[0:1, 0:1] * nn(hb, get(3)[...])

    outs = [shape(T, D, BF), shape(T, 128, F32), shape(T, A, BF), shape(T, A, BF), shape(T, D, F32)]
    return attend(CROSS_PLANS, info, q, kv, kv_peer, *masks, [c_out, y1, down, up, scale], outs, finish)


def expand(info, x, first, second, block=1024):
    T, D = x.shape
    width = first.shape[1]
    F = 2 * width
    per = width // block
    held = Loads([first, second])

    def kernel(info_ref, x_ref, *refs):
        ins, (h_ref, g_ref, *scratch) = refs[: len(held.arrays)], refs[len(held.arrays) :]
        i = pl.program_id(0)
        bound = held.bind(info_ref, ins, scratch)
        pl.when(i == 0)(lambda: start_all(bound))
        cols = pl.ds(pl.multiple_of(lax.rem(i, per) * block, 128), block)
        for v, (copies, buf) in enumerate(bound):
            @pl.when(i == v * per)
            def _():
                for c in copies:
                    c.wait()

            @pl.when(i // per == v)
            def _():
                h, g = gelu_pair(nn(x_ref[...], buf[:, cols]))
                h_ref[...] = h.astype(BF)
                g_ref[...] = g.astype(BF)

    out = pl.BlockSpec((T, block), lambda i, *_: (0, i))
    return pl.pallas_call(
        kernel,
        grid_spec=pltpu.PrefetchScalarGridSpec(
            num_scalar_prefetch=1,
            grid=(F // block,),
            in_specs=[pl.BlockSpec((T, D), lambda i, *_: (0, 0))] + held.specs,
            out_specs=[out, out],
            scratch_shapes=held.scratch,
        ),
        out_shape=[shape(T, F, BF)] * 2,
        compiler_params=params(),
        cost_estimate=cost(12),
        name="expand",
    )(info, x, *held.arrays)


def contract(info, h, c, base, low, sq, gn, up, g_out, scale, block=1024):
    T, D = base.shape
    F = c.shape[0]
    A = sq.shape[1]
    held = Loads([base, g_out, scale, sq, up, gn, low])

    def kernel(info_ref, h_ref, c_ref, *refs):
        ins = refs[: len(held.arrays)]
        out0, out1, g3_ref, kept_ref, sent_ref, gnar_ref, acc, *scratch = refs[len(held.arrays) :]
        i = pl.program_id(0)
        bound = held.bind(info_ref, ins, scratch)
        pl.when(i == 0)(lambda: start_all(bound))

        @pl.when(i == 0)
        def _():
            acc[...] = nn(h_ref[...], c_ref[...])

        @pl.when(i > 0)
        def _():
            acc[...] += nn(h_ref[...], c_ref[...])

        @pl.when(i == F // block - 1)
        def _():
            get = getter(bound)
            y, inv = norm_parts(acc[...] + get(0)[...])
            g3 = norm_back(y, inv, get(1)[...].astype(F32))
            g3_ref[...] = g3
            acc[...] = y
            put_slots(info_ref, acc, out0, out1)
            ga = (get(2)[0:1, 0:1] * g3).astype(BF)
            gup = tn(get(3)[...], ga).astype(BF)
            gnar = (get(5)[...].astype(F32) * nt(ga, get(4)[...])).astype(BF)
            gnar_ref[...] = gnar
            gdown = tn(gnar, get(6)[...]).astype(BF)
            for side, keep, send in ((0, gup, gdown), (1, gdown, gup)):
                @pl.when(info_ref[3] == side)
                def _():
                    kept_ref[...] = keep
                    sent_ref[...] = send

    outs = [shape(T // 2, D, BF)] * 2 + [shape(T, D, F32), shape(A, D, BF), shape(A, D, BF), shape(T, A, BF)]
    return pl.pallas_call(
        kernel,
        grid_spec=pltpu.PrefetchScalarGridSpec(
            num_scalar_prefetch=1,
            grid=(F // block,),
            in_specs=[pl.BlockSpec((T, block), lambda i, *_: (0, i)), pl.BlockSpec((block, D), lambda i, *_: (i, 0))]
            + held.specs,
            out_specs=[pl.BlockSpec(o.shape, lambda i, *_: (0, 0)) for o in outs],
            scratch_shapes=[pltpu.VMEM((T, D), F32)] + held.scratch,
        ),
        out_shape=outs,
        compiler_params=params(),
        cost_estimate=cost(14),
        name="contract",
    )(info, h, c, *held.arrays)


def ffn_back(info, g3, c, first, second, gp, gnar, down, low, inv, c_out, deps, block=1024):
    T, D = g3.shape
    F = c.shape[0]
    width = first.shape[1]
    per = width // block
    held = Loads([first, second, gnar, down, c_out, low, inv])

    def kernel(info_ref, g3_ref, c_ref, gp_ref, *refs):
        ins = refs[: len(held.arrays)]
        g2_ref, ga_ref, acc, *scratch = refs[len(held.arrays) + len(deps) :]
        i = pl.program_id(0)
        bound = held.bind(info_ref, ins, scratch)
        pl.when(i == 0)(lambda: start_all(bound))
        gh = (nt(g3_ref[...].astype(BF), c_ref[...]) * gp_ref[...].astype(F32)).astype(BF)

        @pl.when(i == 0)
        def _():
            acc[...] = g3_ref[...]

        for v in range(2):
            copies, e = bound[v]

            @pl.when(i == v * per)
            def _():
                for copy in copies:
                    copy.wait()

            @pl.when(i // per == v)
            def _():
                acc[...] += nt(gh, e[:, pl.ds(pl.multiple_of(lax.rem(i, per) * block, 128), block)])

        @pl.when(i == F // block - 1)
        def _():
            get = getter(bound)
            g2 = norm_back(get(5)[...].astype(F32), get(6)[:, 0:1], acc[...] + nt(get(2)[...], get(3)[...]))
            g2_ref[...] = g2
            ga_ref[...] = nt(g2.astype(BF), get(4)[...]).astype(BF)

    outs = [shape(T, D, F32), shape(T, D, BF)]
    return pl.pallas_call(
        kernel,
        grid_spec=pltpu.PrefetchScalarGridSpec(
            num_scalar_prefetch=1,
            grid=(F // block,),
            in_specs=[pl.BlockSpec((T, D), lambda i, *_: (0, 0)), pl.BlockSpec((block, D), lambda i, *_: (i, 0)),
                      pl.BlockSpec((T, block), lambda i, *_: (0, i))] + held.specs + [ANYWHERE] * len(deps),
            out_specs=[pl.BlockSpec(o.shape, lambda i, *_: (0, 0)) for o in outs],
            scratch_shapes=[pltpu.VMEM((T, D), F32)] + held.scratch,
        ),
        out_shape=outs,
        compiler_params=params(),
        cost_estimate=cost(18),
        name="ffn_back",
    )(info, g3, c, gp, *held.arrays, *deps)


def attend_cross_back(info, q, kv, kv_peer, do, o, r, p, g2, y1, inv1, c_query, w_out, deps):
    T, D = q.shape

    def finish(get, gq, g1_ref, ga_ref):
        g = get(1)[...] + 0.125 * nt(gq[...], get(0)[...])
        g1 = norm_back(get(2)[...].astype(F32), get(3)[:, 0:1], g)
        g1_ref[...] = g1
        ga_ref[...] = nt(g1.astype(BF), get(4)[...]).astype(BF)

    return attend_back(CROSS_PLANS, info, q, kv, kv_peer, do, o, r, p, [c_query, g2, y1, inv1, w_out],
                       [shape(T, D, F32), shape(T, D, BF)], finish, deps)


def attend_self_back(info, q, kv, kv_peer, do, o, r, p, g1, w_query, deps):
    T, D = q.shape

    def finish(get, gq, acc_ref):
        acc_ref[...] = get(1)[...] + 0.125 * nt(gq[...], get(0)[...])

    return attend_back(SELF_PLANS, info, q, kv, kv_peer, do, o, r, p, [w_query, g1], [shape(T, D, F32)], finish, deps)


def add_pairs(mine, got, part):
    D = mine.shape[1] // 2
    out = []
    for h in range(D // 128):
        at = slice(256 * h + 128 * part, 256 * h + 128 * part + 128)
        out.append((mine[:, at].astype(F32) + got[:, at].astype(F32)).astype(BF))
    return jnp.concatenate(out, axis=1)


def source_grad(info, gkv, got, w_key, w_value, deps):
    T, D = gkv.shape[0], gkv.shape[1] // 2

    def body(info_ref, get, out0, out1, total):
        mine, other = get(0), get(1)
        acc = nt(add_pairs(mine, other, 0), get(2)[...])
        total[...] = acc + nt(add_pairs(mine, other, 1), get(3)[...])
        put_slots(info_ref, total, out0, out1)

    return fused("source_grad", info, body, [gkv, got, w_key, w_value], [shape(T // 2, D, BF)] * 2, deps=deps,
                 extra=[pltpu.VMEM((T, D), F32)])


def token_grad(info, acc, gkv, got, w_key, w_value, deps):
    T, D = acc.shape

    def body(info_ref, get, out0, out1):
        mine, other = get(0), get(1)
        g = get(4)
        g[...] += nt(add_pairs(mine, other, 0), get(2)[...])
        g[...] += nt(add_pairs(mine, other, 1), get(3)[...])
        put_slots(info_ref, g, out0, out1)

    return fused("token_grad", info, body, [gkv, got, w_key, w_value, acc], [shape(T // 2, D, BF)] * 2, deps=deps)


def move(value, target):
    dp, seq = lax.axis_size("dp"), lax.axis_size("seq")
    pairs = []
    for d in range(dp):
        for s in range(seq):
            a, b = target(d, s)
            pairs.append((d * seq + s, a * seq + b))
    return lax.ppermute(value, ("dp", "seq"), pairs)


def flip(value, bit):
    return move(value, lambda d, s: (d ^ bit, s))


def core_of(chunk):
    return (0, 1, 1, 0)[chunk]


def pick(flag, first, second):
    return jnp.where(flag, first, second)


def send_pieces(pieces):
    return [
        move(piece, lambda a, q, k=k: (2 * (a // 2) + core_of(q), 2 * (a % 2) + (q + k) % 2))
        for k, piece in enumerate(pieces)
    ]


def take_pieces(value, s):
    return [lax.dynamic_index_in_dim(value, (s + k) % 2, 0, keepdims=False) for k in range(2)]


def send_back(pieces):
    dp, seq = lax.axis_size("dp"), lax.axis_size("seq")
    got = []
    for k, piece in enumerate(pieces):
        back = {}
        for a in range(dp):
            for q in range(seq):
                back[(2 * (a // 2) + core_of(q), 2 * (a % 2) + (q + k) % 2)] = (a, q)
        got.append(move(piece, lambda a, b: back[(a, b)]))
    return got


def join_rows(got, s):
    even = s % 2 == 0
    return jnp.stack([pick(even, got[0], got[1]), pick(even, got[1], got[0])])


def first_hop(pair, low):
    return [flip(pair[0], 2 * low), flip(pair[1], 4 * low)]


def second_hop(near, low):
    return [flip(near[0], 4 * low), flip(near[1], 2 * low)]


def all_parts(near, far, low):
    out = []
    for v in range(2):
        half = near[v].shape[0] // 2
        b1, b2 = ((2, 4), (4, 2))[v]
        arrays = [near[v], far[v], flip(near[v], low), flip(far[v], low)]
        parts = {}
        for a, m in zip(arrays, (0, b2, 1, b2 ^ 1)):
            parts[m] = (a, 0)
            parts[m ^ b1] = (a, half)
        out.append([parts[m] for m in range(8)])
    return out


class Reduce:
    def __init__(self, kept, sent, d, s, low):
        self.d, self.s, self.low = d, s, low
        self.kept, self.got = kept, [flip(sent, low)]

    def plane(self, v, m):
        return flip(v, 2 * self.low * m)

    def scatter_plane(self):
        me = self.d // (2 * self.low)
        parts = self.value.reshape(4, -1, self.value.shape[1])
        take = [lax.dynamic_index_in_dim(parts, me ^ m, 0, keepdims=False) for m in range(4)]
        self.kept, self.got = take[0], [self.plane(take[m], m) for m in range(1, 4)]

    def line(self, bit):
        self.kept, self.got = self.value, [move(self.value, lambda a, b: (a, b ^ bit))]

    def add(self):
        total = self.kept.astype(F32)
        for got in self.got:
            total += got.astype(F32)
        self.value = total.astype(BF)

    def low_bits(self):
        bit = 1
        while bit < self.low:
            got = flip(self.value, bit)
            self.value = (self.value.astype(F32) + got.astype(F32)).astype(BF)
            bit *= 2

    def gather_plane(self):
        self.me = self.d // (2 * self.low)
        self.got = [self.value] + [self.plane(self.value, m) for m in range(1, 4)]

    def put(self):
        got = self.got
        n, rows = len(got), []
        for j in range(n):
            part = got[n - 1]
            for m in range(n - 1):
                part = pick((self.me ^ j) == m, got[m], part)
            rows.append(part)
        self.value = jnp.concatenate(rows, axis=0)


def local(tokens, source, target_lengths, source_lengths, step_index, self_query, self_key, self_value,
          self_out, cross_query, cross_key, cross_value, cross_out, ffn_expand, ffn_contract, adapter_down,
          adapter_up, grad_output):
    rows, C, D = tokens.shape
    dp, seq = lax.axis_size("dp"), lax.axis_size("seq")
    assert rows == 2 and seq == 4 and dp % 8 == 0
    low = dp // 8
    d, s = lax.axis_index("dp"), lax.axis_index("seq")
    core = d % 2
    info = jnp.stack([core, d // low, (s + d) % 2, (d // low) % 2]).astype(jnp.int32)

    def widen(shard):
        if low == 1:
            return shard
        groups = [[g * low + i for i in range(low)] for g in range(8)]
        return lax.all_gather(shard, "dp", axis=0, tiled=True, axis_index_groups=groups)

    def rows_of(*weights):
        return jnp.concatenate(weights, axis=0)

    t = send_pieces(take_pieces(tokens, s))
    sq, sk, sv, ex = [widen(w) for w in (self_query, self_key, self_value, ffn_expand)]
    n = sq.shape[0]
    h = n // 2
    pair = [rows_of(sk, sv[:h]), rows_of(sq, sv[h:])]
    e1, e2, c_shard, rest = stage(ex, ffn_contract, [self_out, cross_key, cross_value, cross_query, cross_out], ())
    near = beside(pair, first_hop(pair, low), (t[0], rest))
    rest = lax.all_gather(rest, "dp", axis=0, tiled=True)
    each = self_out.shape[0]
    w_out, c_key, c_value, c_query, c_out = [Shards(rest, dp, j * each, each) for j in range(5)]

    mine = jnp.concatenate([target_lengths, source_lengths[:, None]], axis=1)
    other = flip(mine, 1)
    table = jnp.concatenate([pick(core == 0, mine, other), pick(core == 0, other, mine)], axis=0)
    row = lax.dynamic_index_in_dim(table, s, 0, keepdims=False)
    lens, src_len = row[:-1], row[-1]
    docs = lens.shape[0]
    ends = jnp.cumsum(lens)[:-1]
    i = jnp.arange(2 * C, dtype=jnp.int32)
    slot = i // C

    def place(which):
        chunk = pick(which == 0, slot * 3, slot + 1)
        return chunk * C + i % C

    lanes = jnp.arange(128, dtype=jnp.int32) % 64

    def doc_hot(pos):
        doc = jnp.sum((pos[:, None] >= ends[None, :]).astype(jnp.int32), axis=-1)
        return doc[:, None] == lanes[None, :]

    own_pos, peer_pos = place(core), place(1 - core)
    k_aug = [doc_hot(own_pos).astype(BF), doc_hot(peer_pos).astype(BF)]
    q_aug = jnp.where(doc_hot(own_pos) | (lanes >= docs)[None, :], 0.0, NEG).astype(BF)
    ck_aug = [((pos[:, None] >= src_len) & (lanes == 0)[None, :]).astype(BF) for pos in (own_pos, peer_pos)]
    cq_aug = jnp.broadcast_to(jnp.where(lanes == 0, NEG, 0.0).astype(BF)[None, :], (2 * C, 128))

    scale = jnp.full((8, 128), (step_index[0] + 1).astype(F32) / 5.0, F32)
    src = send_pieces(gate(take_pieces(source, s), t))
    *far, c_shard = gate(
        [*second_hop(near, low), c_shard], (*src, info, q_aug, *k_aug, cq_aug, *ck_aug, scale, e1, e2)
    )
    w_contract = lax.all_gather(c_shard, "dp", axis=0, tiled=True)
    a1, b1 = all_parts(near, far, low)
    w_key, w_query = Pieces(n, (a1, 0, n, 0)), Pieces(n, (b1, 0, n, 0))
    w_value = Pieces(n, (a1, n, h, 0), (b1, n, h, h))
    x = Slots(t, 0, C)
    q, kv = project_qkv(info, x, w_query, w_key, w_value, ())
    q, kv, e1, e2 = barrier(q, kv, e1, e2)
    kv_peer = flip(kv, 1)
    hop3 = first_hop([e1, e2], low)
    attended, p_self, r_self = attend_self(info, q, kv, kv_peer, (q_aug, *k_aug), ())
    *hop3, attended = barrier(*hop3, attended)
    near3 = beside([e1, e2], hop3)
    far3 = second_hop(near3, low)
    skv, y1, y1_low, inv1, cq = between(info, x, attended, w_out, c_query, Slots(src, 0, C), c_key, c_value, near3)
    skv, cq, *pieces = barrier(skv, cq, *take_pieces(grad_output, s))
    g_out = send_pieces(pieces)
    skv_peer = flip(skv, 1)
    cross_attended, p_cross, r_cross, second_low, inv2, squeezed, gn, base = attend_cross(
        info, cq, skv, skv_peer, (cq_aug, *ck_aug), y1, c_out, adapter_down, adapter_up, scale
    )
    *far3, g0, g1, second_low = barrier(*far3, *g_out, second_low)
    g_out = [g0, g1]
    a3, b3 = all_parts(near3, far3, low)
    ea, eb = Pieces(n, (a3, 0, n, 0)), Pieces(n, (b3, 0, n, 0))
    hidden, gp = expand(info, second_low, ea, eb)
    o0, o1, g3, kept, sent, gnar = contract(
        info, hidden, w_contract, base, second_low, squeezed, gn, adapter_up, Slots(g_out, 0, C), scale
    )
    output = send_back([o0, o1])
    total = Reduce(kept, sent, d, s, low)
    g2, grad_cross = ffn_back(info, g3, w_contract, ea, eb, gp, gnar, adapter_down, second_low, inv2, c_out, ())
    *total.got, g2, grad_cross = barrier(*total.got, g2, grad_cross)
    total.add()
    total.scatter_plane()
    gkv, gkv_peer, g1, grad_self = attend_cross_back(
        info, cq, skv, skv_peer, grad_cross, cross_attended, r_cross, p_cross, g2, y1_low, inv1, c_query, w_out, (total.kept,)
    )
    *total.got, o0, o1, grad_self, gkv_peer = barrier(*total.got, *output, grad_self, gkv_peer)
    output = [o0, o1]
    total.add()
    total.line(2)
    got = flip(gkv_peer, 1)
    pieces = source_grad(info, gkv, got, c_key, c_value, (grad_self, total.kept))
    pieces = send_back(pieces)
    gkv, gkv_peer, acc = attend_self_back(
        info, q, kv, kv_peer, grad_self, attended, r_self, p_self, g1, w_query, pieces[:0]
    )
    *total.got, s0, s1, gkv_peer = barrier(*total.got, *pieces, gkv_peer)
    got = flip(gkv_peer, 1)
    total.add()
    total.line(1)
    pieces = token_grad(info, acc, gkv, got, w_key, w_value, (total.kept,))
    *total.got, o0, o1, s0, s1, t0, t1 = barrier(*total.got, *output, s0, s1, *pieces)
    tokens_back = send_back([t0, t1])
    output = [o0, o1]
    total.add()
    total.low_bits()
    total.gather_plane()
    total.put()
    grads, other = total.value, flip(total.value, low)
    high = (d // low) % 2 == 1
    grad_up = pick(high, other, grads).astype(F32)
    grad_down = pick(high, grads, other).astype(F32).T
    output, grad_source, grad_tokens = [join_rows(v, s) for v in (output, [s0, s1], tokens_back)]
    return (output, grad_tokens, grad_source, grad_down, grad_up)


def solution(mesh):
    rows = P("dp", "seq", None)
    weight = P("dp", None)
    return jax.shard_map(
        local,
        mesh=mesh,
        in_specs=(rows, rows, weight, P("dp"), P()) + (weight,) * 10 + (P(), P(), rows),
        out_specs=(rows, rows, rows, P(), P()),
        check_vma=False,
    )
```

time: 434 us -> 372 us (0.86)
  local copies, waits for them, and re-layouts: 49.6 us -> 16.7 us
  Pallas kernels: 203 us -> 178 us
  waiting for transfers between devices: 49.3 us -> 64.4 us
  starting transfers between devices: 80.6 us -> 69.2 us
  other arithmetic: 29 us -> 22.1 us
    pallas_call x7 -> x4, Pallas kernels: 61 us -> 35.9 us  [fused(): pl.pallas_call(kernel, grid_spec=pltpu.PrefetchScalarGridSpec(num_scalar_...]
    ppermute x55 -> x43, waiting for transfers between devices: 49.3 us -> 64.4 us  [move(): return lax.ppermute(value, ('dp', 'seq'), pairs)]
    unnamed x125 -> x57, local copies, waits for them, and re-layouts: 24.5 us -> 10.7 us
    ppermute x55 -> x43, starting transfers between devices: 80.5 us -> 69.1 us  [move(): return lax.ppermute(value, ('dp', 'seq'), pairs)]
    select_n x8 -> x2, other arithmetic: 7.79 us -> 0.2 us  [pick(): return jnp.where(flag, first, second)]
    concatenate x4 -> x0, local copies, waits for them, and re-layouts: 6.61 us -> none  [beside(): jnp.concatenate([own, other], axis=0)]
    dynamic_slice x3 -> x0, local copies, waits for them, and re-layouts: 4.67 us -> none  [send_back(): piece = lax.dynamic_slice_in_dim(value, slot * C, C, 0)]
    pallas_call x19 -> x18, Pallas kernels: 109 us -> 109 us  [the longest x2 46.5 us: attend_back(): pl.pallas_call(kernel, grid_spec=pltpu.PrefetchScalarGridSpec(num_scalar_...]
  transfers between devices with their start and end apart: 56 -> 45, of which waited for: 12 -> 15; matrix products, arithmetic and copies ran while one was open for 13% -> 7% of each run, Pallas kernels for 44% -> 43%
where the time goes in v4:
time: 372 us; the launch traced here: 366 us
  Pallas kernels  178 us (48%)
  starting transfers between devices  69.2 us (19%)
  waiting for transfers between devices  64.4 us (17%)
  other arithmetic  22.1 us (6%)
  local copies, waits for them, and re-layouts  16.7 us (4%)
  between operations  15.5 us (4%)
    ppermute x43, starting transfers between devices, move(): return lax.ppermute(value, ('dp', 'seq'), pairs)  69.1 us
    ppermute x43, waiting for transfers between devices, move(): return lax.ppermute(value, ('dp', 'seq'), pairs)  64.4 us
    pallas_call x2, Pallas kernels, attend_back(): pl.pallas_call(kernel, grid_spec=pltpu.PrefetchScalarGridSpec(num_scalar_...  46.5 us
    pallas_call x2, Pallas kernels, attend(): pl.pallas_call(kernel, grid_spec=pltpu.PrefetchScalarGridSpec(num_scalar_...  36.8 us
    pallas_call x4, Pallas kernels, fused(): pl.pallas_call(kernel, grid_spec=pltpu.PrefetchScalarGridSpec(num_scalar_...  35.9 us
    pallas_call x1, Pallas kernels, ffn_back(): pl.pallas_call(kernel, grid_spec=pltpu.PrefetchScalarGridSpec(num_scalar_...  19.5 us
    pallas_call x1, Pallas kernels, contract(): pl.pallas_call(kernel, grid_spec=pltpu.PrefetchScalarGridSpec(num_scalar_...  16.4 us
    pallas_call x1, Pallas kernels, expand(): pl.pallas_call(kernel, grid_spec=pltpu.PrefetchScalarGridSpec(num_scalar_...  13.3 us
  transfers between devices with their start and end apart: 45, of which 15 were waited for; matrix products, arithmetic and copies ran while one was open for 7% of the time, Pallas kernels for 43%

profile of v4, /device:TPU:1, one launch (start us, length us, event | category | flops | bytes accessed | tf_op | source)
XLA Modules:
  0.0 365.5 jit_solution(13147802873180701109)
XLA Ops:
  7.2 3.7 %stage.1 = (bf16[128,2048]{1,0:T(8,128)(2,1)}, bf16[128,2048]{1,0:T(8,128)(2,1)}, bf16[512,1024]{1,0:T(8,128)(2,1)}, bf16[640,1024]{1,0:T(8,128)(2,1)}) custom-call(bf16[128,4096]{1,0:T(8,128)(2,1)} %e_ref.1, bf16[512,1024]{1,0:T(8,128)(2,1)} %c_ref.1, bf16[128,1024]{1,0:T(8,128)(2,1)} %refs_0_.1, bf16[128,1024]{1,0:T(8,128)(2,1)} %refs_1_.1, ...), custom_call_target="tpu_custom_call" | custom-call | flops 900000000 | bytes 1024 | tf_op jit(solution)/shard_map/stage/pallas_call | solution.py:455
  13.0 5.6 %collective-permute-start = (bf16[256,1024]{1,0:T(8,128)(2,1)S(1)}, bf16[256,1024]{1,0:T(8,128)(2,1)}, u32[]{:S(2)}, u32[]{:S(2)}) collective-permute-start(bf16[256,1024]{1,0:T(8,128)(2,1)S(1)} %get-tuple-element.216), channel_id=1, source_target_pairs={{0,0},{1,5},{2,4},{3,1},{4,2},{5,7},{6,6},{7,3},{8,8},{9,13},{10,1... | collective-permute-start | bytes 1572872 | tf_op jit(solution)/shard_map/ppermute | solution.py:820
  22.0 1.9 collective-permute-start.1
  30.2 4.8 %collective-permute-done.2.b = bf16[192,1024]{1,0:T(8,128)(2,1)S(1)} collective-permute-done((bf16[192,1024]{1,0:T(8,128)(2,1)S(1)}, bf16[192,1024]{1,0:T(8,128)(2,1)S(1)}, u32[]{:S(2)}, u32[]{:S(2)}) %collective-permute-start.2) | collective-permute-done | bytes 393248 | tf_op jit(solution)/shard_map/ppermute | solution.py:820
  34.9 2.4 collective-permute-done.3.d
  38.1 2.6 beside.2
  40.7 2.4 collective-permute-start.5
  44.5 1.9 collective-permute-start.7
  46.5 2.4 collective-permute-start.8
  51.3 11.8 %collective-permute-done.7.refs_3_.refs_0_ = bf16[256,1024]{1,0:T(8,128)(2,1)S(1)} collective-permute-done((bf16[256,1024]{1,0:T(8,128)(2,1)}, bf16[256,1024]{1,0:T(8,128)(2,1)S(1)}, u32[]{:S(2)}, u32[]{:S(2)}) %collective-permute-start.7) | collective-permute-done | bytes 524320 | tf_op jit(solution)/shard_map/ppermute | solution.py:820
  64.2 5.3 %collective-permute-done.5.refs_0_ = bf16[384,1024]{1,0:T(8,128)(2,1)S(1)} collective-permute-done((bf16[384,1024]{1,0:T(8,128)(2,1)}, bf16[384,1024]{1,0:T(8,128)(2,1)S(1)}, u32[]{:S(2)}, u32[]{:S(2)}) %collective-permute-start.5) | collective-permute-done | bytes 786464 | tf_op jit(solution)/shard_map/ppermute | solution.py:820
  74.2 3.4 collective-permute-done.4.refs_3_.refs_5_.refs_11_.refs_13_
  79.4 7.6 %qkv.1 = (bf16[512,1024]{1,0:T(8,128)(2,1)}, bf16[512,2048]{1,0:T(8,128)(2,1)}) custom-call(s32[4]{0:T(128)} %pad_add_fusion.2.refs_5_.info_ref, bf16[256,1024]{1,0:T(8,128)(2,1)} %collective-permute-done.refs_0_.refs_2_.refs_6_, bf16[256,1024]{1,0:T(8,128)(2,1)} %collective-permute-done.1.refs_3_.refs_1_.refs_7_, ...), custom_call_target="tpu_custom_call" | custom-call | flops 1800000000 | bytes 1024 | tf_op jit(solution)/shard_map/qkv/pallas_call | solution.py:497
  89.3 2.2 collective-permute-start.14
  91.6 12.8 %attend.2 = (bf16[512,1024]{1,0:T(8,128)(2,1)}, bf16[8,2,5,256,256]{4,3,2,1,0:T(8,128)(2,1)}, f32[512,1024]{1,0:T(8,128)}) custom-call(s32[4]{0:T(128)} %pad_add_fusion.2.refs_5_.info_ref, bf16[512,1024]{1,0:T(8,128)(2,1)} %get-tuple-element.108.q_ref, bf16[512,2048]{1,0:T(8,128)(2,1)} %get-tuple-element.109.ko.vo, ...), custom_call_target="tpu_custom_call" | custom-call | flops 7500000256 | bytes 1024 | tf_op jit(solution)/shard_map/attend/pallas_call | solution.py:267
  104.4 2.9 beside.3
  107.3 10.2 %between.1 = (bf16[512,2048]{1,0:T(8,128)(2,1)}, f32[512,1024]{1,0:T(8,128)}, bf16[512,1024]{1,0:T(8,128)(2,1)}, f32[512,128]{1,0:T(8,128)}, bf16[512,1024]{1,0:T(8,128)(2,1)}) custom-call(s32[4]{0:T(128)} %pad_add_fusion.2.refs_5_.info_ref, bf16[256,1024]{1,0:T(8,128)(2,1)} %copy-done.8, bf16[256,1024]{1,0:T(8,128)(2,1)} %copy-done.9, ...), custom_call_target="tpu_custom_call" | custom-call | flops 1800000000 | bytes 1024 | tf_op jit(solution)/shard_map/between/pallas_call | solution.py:497
  118.4 2.1 collective-permute-start.16
  121.5 5.3 %collective-permute-start.18 = (bf16[256,1024]{1,0:T(8,128)(2,1)}, bf16[256,1024]{1,0:T(8,128)(2,1)}, u32[]{:S(2)}, u32[]{:S(2)}) collective-permute-start(bf16[256,1024]{1,0:T(8,128)(2,1)} %get-tuple-element.118), channel_id=1, source_target_pairs={{0,0},{1,5},{2,4},{3,1},{4,2},{5,7},{6,6},{7,3},{8,8},{9,13},{10,1... | collective-permute-start | bytes 1572872 | tf_op jit(solution)/shard_map/ppermute | solution.py:820
  126.7 5.0 %collective-permute-start.19 = (bf16[256,1024]{1,0:T(8,128)(2,1)}, bf16[256,1024]{1,0:T(8,128)(2,1)}, u32[]{:S(2)}, u32[]{:S(2)}) collective-permute-start(bf16[256,1024]{1,0:T(8,128)(2,1)} %get-tuple-element.119), channel_id=1, source_target_pairs={{0,1},{1,4},{2,5},{3,0},{4,3},{5,6},{6,7},{7,2},{8,9},{9,12},{10,1... | collective-permute-start | bytes 1572872 | tf_op jit(solution)/shard_map/ppermute | solution.py:820
  131.7 24.0 %attend.3 = (bf16[512,1024]{1,0:T(8,128)(2,1)}, bf16[8,2,8,256,256]{4,3,2,1,0:T(8,128)(2,1)}, f32[512,1024]{1,0:T(8,128)}, bf16[512,1024]{1,0:T(8,128)(2,1)}, f3...) custom-call(s32[4]{0:T(128)} %pad_add_fusion.2.refs_5_.info_ref, ...), custom_call_target="tpu_custom_call" | custom-call | flops 7500000256 | bytes 1024 | tf_op jit(solution)/shard_map/attend/pallas_call | solution.py:267
  155.7 8.3 %collective-permute-done.16.refs_0_ = bf16[256,2048]{1,0:T(8,128)(2,1)} collective-permute-done((bf16[256,2048]{1,0:T(8,128)(2,1)}, bf16[256,2048]{1,0:T(8,128)(2,1)}, u32[]{:S(2)}, u32[]{:S(2)}) %collective-permute-start.16) | collective-permute-done | bytes 1048608 | tf_op jit(solution)/shard_map/ppermute | solution.py:820
  164.0 1.8 collective-permute-start.23
  165.8 2.5 collective-permute-start.22
  168.4 2.5 collective-permute-done.22.refs_5_.refs_7_
  170.9 1.7 collective-permute-done.24.refs_11_.refs_15_
  172.6 13.3 %expand.1 = (bf16[512,4096]{1,0:T(8,128)(2,1)}, bf16[512,4096]{1,0:T(8,128)(2,1)}) custom-call(s32[4]{0:T(128)} %pad_add_fusion.2.refs_5_.info_ref, bf16[512,1024]{1,0:T(8,128)(2,1)} %get-tuple-element.124.x_ref.refs_7_.refs_19_, bf16[256,2048]{1,0:T(8,128)(2,1)} %get-tuple-element.113.refs_9_.refs_0_.refs_2_, ...), custom_call_target="tpu_custom_call" | custom-call | flops 3600000000 | bytes 1024 | tf_op jit(solution)/shard_map/expand/pallas_call | solution.py:626
  186.0 16.4 %contract.1 = (bf16[256,1024]{1,0:T(8,128)(2,1)}, bf16[256,1024]{1,0:T(8,128)(2,1)}, f32[512,1024]{1,0:T(8,128)}, bf16[512,1024]{1,0:T(8,128)(2,1)}, bf16[512,10...) custom-call(s32[4]{0:T(128)} %pad_add_fusion.2.refs_5_.info_ref, bf16[512,4096]{1,0:T(8,128)(2,1)} %get-tuple-element.127.h_ref, ...), custom_call_target="tpu_custom_call" | custom-call | flops 4200000000 | bytes 1024 | tf_op jit(solution)/shard_map/contract/pallas_call | solution.py:683
  202.9 7.0 %collective-permute-start.29 = (bf16[256,1024]{1,0:T(8,128)(2,1)}, bf16[256,1024]{1,0:T(8,128)(2,1)}, u32[]{:S(2)}, u32[]{:S(2)}) collective-permute-start(bf16[256,1024]{1,0:T(8,128)(2,1)} %get-tuple-element.143), channel_id=1, source_target_pairs={{0,0},{1,3},{2,4},{3,7},{4,2},{5,1},{6,6},{7,5},{8,8},{9,11},{10,1... | collective-permute-start | bytes 1572872 | tf_op jit(solution)/shard_map/ppermute | solution.py:820
  209.9 19.5 %ffn_back.1 = (f32[512,1024]{1,0:T(8,128)}, bf16[512,1024]{1,0:T(8,128)(2,1)}) custom-call(s32[4]{0:T(128)} %pad_add_fusion.2.refs_5_.info_ref, f32[512,1024]{1,0:T(8,128)} %get-tuple-element.136.g3_ref, bf16[4096,1024]{1,0:T(8,128)(2,1)} %all-gather.5.cloned.1.call-done.c_ref, bf16[512,4096]{1,0:T(8,128)(2,1)} %get-tuple-element.137.gp_ref, ...), custom_call_target="tpu_custom_call" | custom-call | flops 5400000000 | bytes 1024 | tf_op jit(solution)/shard_map/ffn_back/pallas_call | solution.py:739
  234.3 1.6 collective-permute-start.28
  235.9 28.4 %attend_back.2 = (bf16[512,2048]{1,0:T(8,128)(2,1)}, bf16[512,2048]{1,0:T(8,128)(2,1)}, f32[512,1024]{1,0:T(8,128)}, bf16[512,1024]{1,0:T(8,128)(2,1)}) custom-call(s32[4]{0:T(128)} %pad_add_fusion.2.refs_5_.info_ref, bf16[512,1024]{1,0:T(8,128)(2,1)} %get-tuple-element.120.q_ref, bf16[512,2048]{1,0:T(8,128)(2,1)} %get-tuple-element.121.ko.vo, ...), custom_call_target="tpu_custom_call" | custom-call | flops 7500000256 | bytes 1024 | tf_op jit(solution)/shard_map/attend_back/pallas_call | solution.py:381
  265.4 2.0 add_convert_fusion.3.refs_5_
  267.4 3.4 collective-permute-start.31
  270.7 8.0 %source_grad.1 = (bf16[256,1024]{1,0:T(8,128)(2,1)}, bf16[256,1024]{1,0:T(8,128)(2,1)}) custom-call(s32[4]{0:T(128)} %pad_add_fusion.2.refs_5_.info_ref, bf16[512,2048]{1,0:T(8,128)(2,1)} %get-tuple-element.157.refs_0_, bf16[512,2048]{1,0:T(8,128)(2,1)} %collective-permute-done.32.refs_1_, ...), custom_call_target="tpu_custom_call" | custom-call | flops 1800000000 | bytes 1024 | tf_op jit(solution)/shard_map/source_grad/pallas_call | solution.py:497
  278.7 3.6 collective-permute-start.33
  282.3 1.8 collective-permute-start.34
  284.1 18.1 %attend_back.3 = (bf16[512,2048]{1,0:T(8,128)(2,1)}, bf16[512,2048]{1,0:T(8,128)(2,1)}, f32[512,1024]{1,0:T(8,128)}) custom-call(s32[4]{0:T(128)} %pad_add_fusion.2.refs_5_.info_ref, bf16[512,1024]{1,0:T(8,128)(2,1)} %get-tuple-element.108.q_ref, bf16[512,2048]{1,0:T(8,128)(2,1)} %get-tuple-element.109.ko.vo, bf16[512,2048]{1,0:T(8,128)(2,1)} %get-tuple-element.109.ko.vo, ...), custom_call_target="tpu_custom_call" | custom-call | flops 7500000256 | bytes 1024 | tf_op jit(solution)/shard_map/attend_back/pallas_call | solution.py:381
  302.2 4.3 %collective-permute-done.33.refs_1_ = bf16[256,1024]{1,0:T(8,128)(2,1)} collective-permute-done((bf16[256,1024]{1,0:T(8,128)(2,1)}, bf16[256,1024]{1,0:T(8,128)(2,1)}, u32[]{:S(2)}, u32[]{:S(2)}) %collective-permute-start.33) | collective-permute-done | bytes 524320 | tf_op jit(solution)/shard_map/ppermute | solution.py:820
  306.5 1.8 add_convert_fusion.2.refs_27_
  309.4 1.7 collective-permute-done.36.refs_1_
  311.0 10.1 %token_grad.1 = (bf16[256,1024]{1,0:T(8,128)(2,1)}, bf16[256,1024]{1,0:T(8,128)(2,1)}) custom-call(s32[4]{0:T(128)} %pad_add_fusion.2.refs_5_.info_ref, bf16[512,2048]{1,0:T(8,128)(2,1)} %get-tuple-element.171.refs_0_, bf16[512,2048]{1,0:T(8,128)(2,1)} %collective-permute-done.36.refs_1_, ...), custom_call_target="tpu_custom_call" | custom-call | flops 1800000000 | bytes 1024 | tf_op jit(solution)/shard_map/token_grad/pallas_call | solution.py:497
  323.2 1.8 collective-permute-start.41
  325.0 5.1 %collective-permute-start.37 = (bf16[256,1024]{1,0:T(8,128)(2,1)}, bf16[256,1024]{1,0:T(8,128)(2,1)S(1)}, u32[]{:S(2)}, u32[]{:S(2)}) collective-permute-start(bf16[256,1024]{1,0:T(8,128)(2,1)} %get-tuple-element.178), channel_id=1, source_target_pairs={{0,0},{1,3},{2,4},{3,7},{4,2},{5,1},{6,6},{7,5},{8,8},{9,11},{10,1... | collective-permute-start | bytes 1572872 | tf_op jit(solution)/shard_map/ppermute | solution.py:820
  331.7 4.9 %collective-permute-done.41 = bf16[128,1024]{1,0:T(8,128)(2,1)S(1)} collective-permute-done((bf16[128,1024]{1,0:T(8,128)(2,1)S(1)}, bf16[128,1024]{1,0:T(8,128)(2,1)S(1)}, u32[]{:S(2)}, u32[]{:S(2)}) %collective-permute-start.41) | collective-permute-done | bytes 262176 | tf_op jit(solution)/shard_map/ppermute | solution.py:820
  342.8 10.8 %collective-permute-done.37 = bf16[256,1024]{1,0:T(8,128)(2,1)S(1)} collective-permute-done((bf16[256,1024]{1,0:T(8,128)(2,1)}, bf16[256,1024]{1,0:T(8,128)(2,1)S(1)}, u32[]{:S(2)}, u32[]{:S(2)}) %collective-permute-start.37) | collective-permute-done | bytes 524320 | tf_op jit(solution)/shard_map/ppermute | solution.py:820
  354.8 1.9 select_convert_fusion
  356.7 1.8 copy.68
  (167 shorter events, 45.9 us)
Async XLA Ops:
  7.2 100.1 %all-gather.3.cloned.1.call-start = ((), (), s32[]{:S(2)}) async-start(), calls=%async_computation | async-start | bytes 11796480 | tf_op jit(solution)/shard_map/all_gather | solution.py:957
  11.0 175.0 %all-gather.5.cloned.1.call-start = ((), (), s32[]{:S(2)}) async-start(), calls=%async_computation.1 | async-start | bytes 9437184 | tf_op jit(solution)/shard_map/all_gather | solution.py:992
  12.1 15.4 %copy-start.14 = (bf16[2,256,1024]{2,1,0:T(8,128)(2,1)S(1)}, bf16[2,256,1024]{2,1,0:T(8,128)(2,1)}, u32[]{:S(2)}) copy-start(bf16[2,256,1024]{2,1,0:T(8,128)(2,1)} %param.19) | copy-start | bytes 3145732
  13.0 25.1 %collective-permute-start = (bf16[256,1024]{1,0:T(8,128)(2,1)S(1)}, bf16[256,1024]{1,0:T(8,128)(2,1)}, u32[]{:S(2)}, u32[]{:S(2)}) collective-permute-start(bf16[256,1024]{1,0:T(8,128)(2,1)S(1)} %get-tuple-element.216), channel_id=1, source_target_pairs={{0,0},{1,5},{2,4},{3,1},{4,2},{5,7},{6,6},{7,3},{8,8},{9,13},{10,1... | collective-permute-start | bytes 1572872 | tf_op jit(solution)/shard_map/ppermute | solution.py:820
  19.4 15.5 %collective-permute-start.2 = (bf16[192,1024]{1,0:T(8,128)(2,1)S(1)}, bf16[192,1024]{1,0:T(8,128)(2,1)S(1)}, u32[]{:S(2)}, u32[]{:S(2)}) collective-permute-start(bf16[192,1024]{1,0:T(8,128)(2,1)S(1)} %pad_maximum_fusion.4.a), channel_id=1, source_target_pairs={{0,8},{1,9},{2,10},{3,11},{4,12},{5,13},{6,14},{7,15},{8,0},{9,1},... | collective-permute-start | bytes 1179656 | tf_op jit(solution)/shard_map/ppermute | solution.py:820
  20.7 14.3 %copy-start.11 = (bf16[192,1024]{1,0:T(8,128)(2,1)}, bf16[192,1024]{1,0:T(8,128)(2,1)S(1)}, u32[]{:S(2)}) copy-start(bf16[192,1024]{1,0:T(8,128)(2,1)S(1)} %pad_maximum_fusion.5.c) | copy-start | bytes 1179652
  20.7 16.7 %collective-permute-start.3 = (bf16[192,1024]{1,0:T(8,128)(2,1)S(1)}, bf16[192,1024]{1,0:T(8,128)(2,1)S(1)}, u32[]{:S(2)}, u32[]{:S(2)}) collective-permute-start(bf16[192,1024]{1,0:T(8,128)(2,1)S(1)} %pad_maximum_fusion.5.c), channel_id=1, source_target_pairs={{0,16},{1,17},{2,18},{3,19},{4,20},{5,21},{6,22},{7,23},{8,24},{9,... | collective-permute-start | bytes 1179656 | tf_op jit(solution)/shard_map/ppermute | solution.py:820
  22.0 22.5 %collective-permute-start.1 = (bf16[256,1024]{1,0:T(8,128)(2,1)}, bf16[256,1024]{1,0:T(8,128)(2,1)}, u32[]{:S(2)}, u32[]{:S(2)}) collective-permute-start(bf16[256,1024]{1,0:T(8,128)(2,1)} %get-tuple-element.215), channel_id=1, source_target_pairs={{0,1},{1,4},{2,5},{3,0},{4,3},{5,6},{6,7},{7,2},{8,9},{9,12},{10,1... | collective-permute-start | bytes 1572872 | tf_op jit(solution)/shard_map/ppermute | solution.py:820
  24.1 4.5 %collective-permute-start.9 = (s32[2,5]{1,0:T(2,128)S(1)}, s32[2,5]{1,0:T(2,128)S(1)}, u32[]{:S(2)}, u32[]{:S(2)}) collective-permute-start(s32[2,5]{1,0:T(2,128)S(1)} %pad_add_fusion.1), channel_id=1, source_target_pairs={{0,4},{1,5},{2,6},{3,7},{4,0},{5,1},{6,2},{7,3},{8,12},{9,13},{10,... | collective-permute-start | bytes 128 | tf_op jit(solution)/shard_map/ppermute | solution.py:820
  40.7 29.4 %copy-start.25 = (bf16[128]{0:T(256)(128)(2,1)S(1)}, bf16[128]{0:T(256)(128)(2,1)}, u32[]{:S(2)}) copy-start(bf16[128]{0:T(256)(128)(2,1)} %select_convert_fusion.2) | copy-start | bytes 772
  40.7 28.8 %collective-permute-start.5 = (bf16[384,1024]{1,0:T(8,128)(2,1)}, bf16[384,1024]{1,0:T(8,128)(2,1)S(1)}, u32[]{:S(2)}, u32[]{:S(2)}) collective-permute-start(bf16[384,1024]{1,0:T(8,128)(2,1)} %get-tuple-element.95.refs_2_.refs_4_.refs_10_.refs_12_), channel_id=1, source_target_pairs={{0,16},{1,17},{2,18},{3,19},{4,20},{5,21},{6,22},{7,23},{8,24},{9,... | collective-permute-start | bytes 2359304 | tf_op jit(solution)/shard_map/ppermute | solution.py:820
  43.1 26.4 %collective-permute-start.6 = (bf16[384,1024]{1,0:T(8,128)(2,1)}, bf16[384,1024]{1,0:T(8,128)(2,1)S(1)}, u32[]{:S(2)}, u32[]{:S(2)}) collective-permute-start(bf16[384,1024]{1,0:T(8,128)(2,1)} %get-tuple-element.96.refs_18_.refs_22_.refs_26_.refs_30_.refs_0_.refs_4_), channel_id=1, source_target_pairs={{0,8},{1,9},{2,10},{3,11},{4,12},{5,13},{6,14},{7,15},{8,0},{9,1},... | collective-permute-start | bytes 2359304 | tf_op jit(solution)/shard_map/ppermute | solution.py:820
  44.5 18.5 %collective-permute-start.7 = (bf16[256,1024]{1,0:T(8,128)(2,1)}, bf16[256,1024]{1,0:T(8,128)(2,1)S(1)}, u32[]{:S(2)}, u32[]{:S(2)}) collective-permute-start(bf16[256,1024]{1,0:T(8,128)(2,1)} %get-tuple-element.98), channel_id=1, source_target_pairs={{0,0},{1,5},{2,4},{3,1},{4,2},{5,7},{6,6},{7,3},{8,8},{9,13},{10,1... | collective-permute-start | bytes 1572872 | tf_op jit(solution)/shard_map/ppermute | solution.py:820
  46.5 17.7 %collective-permute-start.8 = (bf16[256,1024]{1,0:T(8,128)(2,1)}, bf16[256,1024]{1,0:T(8,128)(2,1)S(1)}, u32[]{:S(2)}, u32[]{:S(2)}) collective-permute-start(bf16[256,1024]{1,0:T(8,128)(2,1)} %get-tuple-element.99), channel_id=1, source_target_pairs={{0,1},{1,4},{2,5},{3,0},{4,3},{5,6},{6,7},{7,2},{8,9},{9,12},{10,1... | collective-permute-start | bytes 1572872 | tf_op jit(solution)/shard_map/ppermute | solution.py:820
  71.9 2.3 collective-permute-start.11
  72.1 5.4 %collective-permute-start.4 = (bf16[384,1024]{1,0:T(8,128)(2,1)S(1)}, bf16[384,1024]{1,0:T(8,128)(2,1)S(1)}, u32[]{:S(2)}, u32[]{:S(2)}) collective-permute-start(bf16[384,1024]{1,0:T(8,128)(2,1)S(1)} %copy-done.2), channel_id=1, source_target_pairs={{0,4},{1,5},{2,6},{3,7},{4,0},{5,1},{6,2},{7,3},{8,12},{9,13},{10,... | collective-permute-start | bytes 2359304 | tf_op jit(solution)/shard_map/ppermute | solution.py:820
  72.4 6.1 %collective-permute-start.10 = (bf16[384,1024]{1,0:T(8,128)(2,1)}, bf16[384,1024]{1,0:T(8,128)(2,1)S(1)}, u32[]{:S(2)}, u32[]{:S(2)}) collective-permute-start(bf16[384,1024]{1,0:T(8,128)(2,1)} %get-tuple-element.102.refs_6_.refs_8_.refs_14_.refs_16_), channel_id=1, source_target_pairs={{0,4},{1,5},{2,6},{3,7},{4,0},{5,1},{6,2},{7,3},{8,12},{9,13},{10,... | collective-permute-start | bytes 2359304 | tf_op jit(solution)/shard_map/ppermute | solution.py:820
  72.7 6.8 %collective-permute-start.12 = (bf16[384,1024]{1,0:T(8,128)(2,1)}, bf16[384,1024]{1,0:T(8,128)(2,1)}, u32[]{:S(2)}, u32[]{:S(2)}) collective-permute-start(bf16[384,1024]{1,0:T(8,128)(2,1)} %get-tuple-element.103.refs_20_.refs_24_.refs_28_.refs_32_.refs_2_.refs_6_), channel_id=1, source_target_pairs={{0,4},{1,5},{2,6},{3,7},{4,0},{5,1},{6,2},{7,3},{8,12},{9,13},{10,... | collective-permute-start | bytes 2359304 | tf_op jit(solution)/shard_map/ppermute | solution.py:820
  87.0 4.6 %collective-permute-start.15 = (bf16[512,2048]{1,0:T(8,128)(2,1)}, bf16[512,2048]{1,0:T(8,128)(2,1)}, u32[]{:S(2)}, u32[]{:S(2)}) collective-permute-start(bf16[512,2048]{1,0:T(8,128)(2,1)} %get-tuple-element.109.ko.vo), channel_id=1, source_target_pairs={{0,4},{1,5},{2,6},{3,7},{4,0},{5,1},{6,2},{7,3},{8,12},{9,13},{10,... | collective-permute-start | bytes 6291464 | tf_op jit(solution)/shard_map/ppermute | solution.py:820
  89.3 15.1 %collective-permute-start.13 = (bf16[128,2048]{1,0:T(8,128)(2,1)}, bf16[128,2048]{1,0:T(8,128)(2,1)}, u32[]{:S(2)}, u32[]{:S(2)}) collective-permute-start(bf16[128,2048]{1,0:T(8,128)(2,1)} %get-tuple-element.106.a), channel_id=1, source_target_pairs={{0,8},{1,9},{2,10},{3,11},{4,12},{5,13},{6,14},{7,15},{8,0},{9,1},... | collective-permute-start | bytes 1572872 | tf_op jit(solution)/shard_map/ppermute | solution.py:820
  89.3 15.1 %collective-permute-start.14 = (bf16[128,2048]{1,0:T(8,128)(2,1)}, bf16[128,2048]{1,0:T(8,128)(2,1)}, u32[]{:S(2)}, u32[]{:S(2)}) collective-permute-start(bf16[128,2048]{1,0:T(8,128)(2,1)} %get-tuple-element.107.c), channel_id=1, source_target_pairs={{0,16},{1,17},{2,18},{3,19},{4,20},{5,21},{6,22},{7,23},{8,24},{9,... | collective-permute-start | bytes 1572872 | tf_op jit(solution)/shard_map/ppermute | solution.py:820
  117.5 9.2 %collective-permute-start.20 = (bf16[512,2048]{1,0:T(8,128)(2,1)}, bf16[512,2048]{1,0:T(8,128)(2,1)}, u32[]{:S(2)}, u32[]{:S(2)}) collective-permute-start(bf16[512,2048]{1,0:T(8,128)(2,1)} %get-tuple-element.121.ko.vo), channel_id=1, source_target_pairs={{0,4},{1,5},{2,6},{3,7},{4,0},{5,1},{6,2},{7,3},{8,12},{9,13},{10,... | collective-permute-start | bytes 6291464 | tf_op jit(solution)/shard_map/ppermute | solution.py:820
  118.4 45.6 %collective-permute-start.16 = (bf16[256,2048]{1,0:T(8,128)(2,1)}, bf16[256,2048]{1,0:T(8,128)(2,1)}, u32[]{:S(2)}, u32[]{:S(2)}) collective-permute-start(bf16[256,2048]{1,0:T(8,128)(2,1)} %get-tuple-element.113.refs_9_.refs_0_.refs_2_), channel_id=1, source_target_pairs={{0,16},{1,17},{2,18},{3,19},{4,20},{5,21},{6,22},{7,23},{8,24},{9,... | collective-permute-start | bytes 3145736 | tf_op jit(solution)/shard_map/ppermute | solution.py:820
  120.5 45.3 %collective-permute-start.17 = (bf16[256,2048]{1,0:T(8,128)(2,1)}, bf16[256,2048]{1,0:T(8,128)(2,1)}, u32[]{:S(2)}, u32[]{:S(2)}) collective-permute-start(bf16[256,2048]{1,0:T(8,128)(2,1)} %get-tuple-element.114.refs_10_.refs_8_.refs_12_), channel_id=1, source_target_pairs={{0,8},{1,9},{2,10},{3,11},{4,12},{5,13},{6,14},{7,15},{8,0},{9,1},... | collective-permute-start | bytes 3145736 | tf_op jit(solution)/shard_map/ppermute | solution.py:820
  120.8 47.5 %collective-permute-start.21 = (bf16[256,2048]{1,0:T(8,128)(2,1)}, bf16[256,2048]{1,0:T(8,128)(2,1)}, u32[]{:S(2)}, u32[]{:S(2)}) collective-permute-start(bf16[256,2048]{1,0:T(8,128)(2,1)} %get-tuple-element.113.refs_9_.refs_0_.refs_2_), channel_id=1, source_target_pairs={{0,4},{1,5},{2,6},{3,7},{4,0},{5,1},{6,2},{7,3},{8,12},{9,13},{10,... | collective-permute-start | bytes 3145736 | tf_op jit(solution)/shard_map/ppermute | solution.py:820
  121.5 44.3 %collective-permute-start.18 = (bf16[256,1024]{1,0:T(8,128)(2,1)}, bf16[256,1024]{1,0:T(8,128)(2,1)}, u32[]{:S(2)}, u32[]{:S(2)}) collective-permute-start(bf16[256,1024]{1,0:T(8,128)(2,1)} %get-tuple-element.118), channel_id=1, source_target_pairs={{0,0},{1,5},{2,4},{3,1},{4,2},{5,7},{6,6},{7,3},{8,8},{9,13},{10,1... | collective-permute-start | bytes 1572872 | tf_op jit(solution)/shard_map/ppermute | solution.py:820
  126.7 39.0 %collective-permute-start.19 = (bf16[256,1024]{1,0:T(8,128)(2,1)}, bf16[256,1024]{1,0:T(8,128)(2,1)}, u32[]{:S(2)}, u32[]{:S(2)}) collective-permute-start(bf16[256,1024]{1,0:T(8,128)(2,1)} %get-tuple-element.119), channel_id=1, source_target_pairs={{0,1},{1,4},{2,5},{3,0},{4,3},{5,6},{6,7},{7,2},{8,9},{9,12},{10,1... | collective-permute-start | bytes 1572872 | tf_op jit(solution)/shard_map/ppermute | solution.py:820
  164.0 4.4 %collective-permute-start.23 = (bf16[256,2048]{1,0:T(8,128)(2,1)}, bf16[256,2048]{1,0:T(8,128)(2,1)}, u32[]{:S(2)}, u32[]{:S(2)}) collective-permute-start(bf16[256,2048]{1,0:T(8,128)(2,1)} %get-tuple-element.114.refs_10_.refs_8_.refs_12_), channel_id=1, source_target_pairs={{0,4},{1,5},{2,6},{3,7},{4,0},{5,1},{6,2},{7,3},{8,12},{9,13},{10,... | collective-permute-start | bytes 3145736 | tf_op jit(solution)/shard_map/ppermute | solution.py:820
  165.8 5.2 %collective-permute-start.22 = (bf16[256,2048]{1,0:T(8,128)(2,1)}, bf16[256,2048]{1,0:T(8,128)(2,1)}, u32[]{:S(2)}, u32[]{:S(2)}) collective-permute-start(bf16[256,2048]{1,0:T(8,128)(2,1)} %get-tuple-element.125.refs_4_.refs_6_), channel_id=1, source_target_pairs={{0,4},{1,5},{2,6},{3,7},{4,0},{5,1},{6,2},{7,3},{8,12},{9,13},{10,... | collective-permute-start | bytes 3145736 | tf_op jit(solution)/shard_map/ppermute | solution.py:820
  168.3 4.3 %collective-permute-start.24 = (bf16[256,2048]{1,0:T(8,128)(2,1)}, bf16[256,2048]{1,0:T(8,128)(2,1)}, u32[]{:S(2)}, u32[]{:S(2)}) collective-permute-start(bf16[256,2048]{1,0:T(8,128)(2,1)} %get-tuple-element.126.refs_10_.refs_14_), channel_id=1, source_target_pairs={{0,4},{1,5},{2,6},{3,7},{4,0},{5,1},{6,2},{7,3},{8,12},{9,13},{10,... | collective-permute-start | bytes 3145736 | tf_op jit(solution)/shard_map/ppermute | solution.py:820
  202.5 26.9 %collective-permute-start.25 = (bf16[512,1024]{1,0:T(8,128)(2,1)}, bf16[512,1024]{1,0:T(8,128)(2,1)}, u32[]{:S(2)}, u32[]{:S(2)}) collective-permute-start(bf16[512,1024]{1,0:T(8,128)(2,1)} %get-tuple-element.135), channel_id=1, source_target_pairs={{0,4},{1,5},{2,6},{3,7},{4,0},{5,1},{6,2},{7,3},{8,12},{9,13},{10,... | collective-permute-start | bytes 3145736 | tf_op jit(solution)/shard_map/ppermute | solution.py:820
  202.9 61.5 %collective-permute-start.29 = (bf16[256,1024]{1,0:T(8,128)(2,1)}, bf16[256,1024]{1,0:T(8,128)(2,1)}, u32[]{:S(2)}, u32[]{:S(2)}) collective-permute-start(bf16[256,1024]{1,0:T(8,128)(2,1)} %get-tuple-element.143), channel_id=1, source_target_pairs={{0,0},{1,3},{2,4},{3,7},{4,2},{5,1},{6,6},{7,5},{8,8},{9,11},{10,1... | collective-permute-start | bytes 1572872 | tf_op jit(solution)/shard_map/ppermute | solution.py:820
  209.8 54.5 %collective-permute-start.30 = (bf16[256,1024]{1,0:T(8,128)(2,1)}, bf16[256,1024]{1,0:T(8,128)(2,1)}, u32[]{:S(2)}, u32[]{:S(2)}) collective-permute-start(bf16[256,1024]{1,0:T(8,128)(2,1)} %get-tuple-element.144), channel_id=1, source_target_pairs={{0,3},{1,0},{2,7},{3,4},{4,1},{5,2},{6,5},{7,6},{8,11},{9,8},{10,1... | collective-permute-start | bytes 1572872 | tf_op jit(solution)/shard_map/ppermute | solution.py:820
  233.3 31.1 %collective-permute-start.26 = (bf16[128,1024]{1,0:T(8,128)(2,1)}, bf16[128,1024]{1,0:T(8,128)(2,1)}, u32[]{:S(2)}, u32[]{:S(2)}) collective-permute-start(bf16[128,1024]{1,0:T(8,128)(2,1)} %get-tuple-element.210), channel_id=1, source_target_pairs={{0,8},{1,9},{2,10},{3,11},{4,12},{5,13},{6,14},{7,15},{8,0},{9,1},... | collective-permute-start | bytes 786440 | tf_op jit(solution)/shard_map/ppermute | solution.py:820
  233.8 30.6 %collective-permute-start.27 = (bf16[128,1024]{1,0:T(8,128)(2,1)}, bf16[128,1024]{1,0:T(8,128)(2,1)}, u32[]{:S(2)}, u32[]{:S(2)}) collective-permute-start(bf16[128,1024]{1,0:T(8,128)(2,1)} %get-tuple-element.209), channel_id=1, source_target_pairs={{0,16},{1,17},{2,18},{3,19},{4,20},{5,21},{6,22},{7,23},{8,24},{9,... | collective-permute-start | bytes 786440 | tf_op jit(solution)/shard_map/ppermute | solution.py:820
  234.3 30.1 %collective-permute-start.28 = (bf16[128,1024]{1,0:T(8,128)(2,1)}, bf16[128,1024]{1,0:T(8,128)(2,1)}, u32[]{:S(2)}, u32[]{:S(2)}) collective-permute-start(bf16[128,1024]{1,0:T(8,128)(2,1)} %get-tuple-element.208), channel_id=1, source_target_pairs={{0,24},{1,25},{2,26},{3,27},{4,28},{5,29},{6,30},{7,31},{8,16},{9,... | collective-permute-start | bytes 786440 | tf_op jit(solution)/shard_map/ppermute | solution.py:820
  264.4 6.3 %collective-permute-start.32 = (bf16[512,2048]{1,0:T(8,128)(2,1)}, bf16[512,2048]{1,0:T(8,128)(2,1)}, u32[]{:S(2)}, u32[]{:S(2)}) collective-permute-start(bf16[512,2048]{1,0:T(8,128)(2,1)} %get-tuple-element.158), channel_id=1, source_target_pairs={{0,4},{1,5},{2,6},{3,7},{4,0},{5,1},{6,2},{7,3},{8,12},{9,13},{10,... | collective-permute-start | bytes 6291464 | tf_op jit(solution)/shard_map/ppermute | solution.py:820
  267.4 34.8 %collective-permute-start.31 = (bf16[128,1024]{1,0:T(8,128)(2,1)}, bf16[128,1024]{1,0:T(8,128)(2,1)}, u32[]{:S(2)}, u32[]{:S(2)}) collective-permute-start(bf16[128,1024]{1,0:T(8,128)(2,1)} %add_convert_fusion.3.refs_5_), channel_id=1, source_target_pairs={{0,2},{1,3},{2,0},{3,1},{4,6},{5,7},{6,4},{7,5},{8,10},{9,11},{10,... | collective-permute-start | bytes 786440 | tf_op jit(solution)/shard_map/ppermute | solution.py:820
  278.7 27.8 %collective-permute-start.33 = (bf16[256,1024]{1,0:T(8,128)(2,1)}, bf16[256,1024]{1,0:T(8,128)(2,1)}, u32[]{:S(2)}, u32[]{:S(2)}) collective-permute-start(bf16[256,1024]{1,0:T(8,128)(2,1)} %get-tuple-element.160), channel_id=1, source_target_pairs={{0,0},{1,3},{2,4},{3,7},{4,2},{5,1},{6,6},{7,5},{8,8},{9,11},{10,1... | collective-permute-start | bytes 1572872 | tf_op jit(solution)/shard_map/ppermute | solution.py:820
  282.3 24.2 %collective-permute-start.34 = (bf16[256,1024]{1,0:T(8,128)(2,1)}, bf16[256,1024]{1,0:T(8,128)(2,1)}, u32[]{:S(2)}, u32[]{:S(2)}) collective-permute-start(bf16[256,1024]{1,0:T(8,128)(2,1)} %get-tuple-element.161), channel_id=1, source_target_pairs={{0,3},{1,0},{2,7},{3,4},{4,1},{5,2},{6,5},{7,6},{8,11},{9,8},{10,1... | collective-permute-start | bytes 1572872 | tf_op jit(solution)/shard_map/ppermute | solution.py:820
  306.5 4.5 %collective-permute-start.36 = (bf16[512,2048]{1,0:T(8,128)(2,1)}, bf16[512,2048]{1,0:T(8,128)(2,1)}, u32[]{:S(2)}, u32[]{:S(2)}) collective-permute-start(bf16[512,2048]{1,0:T(8,128)(2,1)} %get-tuple-element.172), channel_id=1, source_target_pairs={{0,4},{1,5},{2,6},{3,7},{4,0},{5,1},{6,2},{7,3},{8,12},{9,13},{10,... | collective-permute-start | bytes 6291464 | tf_op jit(solution)/shard_map/ppermute | solution.py:820
  308.3 12.9 %collective-permute-start.35 = (bf16[128,1024]{1,0:T(8,128)(2,1)}, bf16[128,1024]{1,0:T(8,128)(2,1)}, u32[]{:S(2)}, u32[]{:S(2)}) collective-permute-start(bf16[128,1024]{1,0:T(8,128)(2,1)} %add_convert_fusion.2.refs_27_), channel_id=1, source_target_pairs={{0,1},{1,0},{2,3},{3,2},{4,5},{5,4},{6,7},{7,6},{8,9},{9,8},{10,11... | collective-permute-start | bytes 786440 | tf_op jit(solution)/shard_map/ppermute | solution.py:820
  322.3 9.4 %collective-permute-start.39 = (bf16[128,1024]{1,0:T(8,128)(2,1)S(1)}, bf16[128,1024]{1,0:T(8,128)(2,1)S(1)}, u32[]{:S(2)}, u32[]{:S(2)}) collective-permute-start(bf16[128,1024]{1,0:T(8,128)(2,1)S(1)} %add_convert_fusion.1), channel_id=1, source_target_pairs={{0,16},{1,17},{2,18},{3,19},{4,20},{5,21},{6,22},{7,23},{8,24},{9,... | collective-permute-start | bytes 786440 | tf_op jit(solution)/shard_map/ppermute | solution.py:820
  323.1 8.6 %collective-permute-start.40 = (bf16[128,1024]{1,0:T(8,128)(2,1)S(1)}, bf16[128,1024]{1,0:T(8,128)(2,1)S(1)}, u32[]{:S(2)}, u32[]{:S(2)}) collective-permute-start(bf16[128,1024]{1,0:T(8,128)(2,1)S(1)} %add_convert_fusion.1), channel_id=1, source_target_pairs={{0,8},{1,9},{2,10},{3,11},{4,12},{5,13},{6,14},{7,15},{8,0},{9,1},... | collective-permute-start | bytes 786440 | tf_op jit(solution)/shard_map/ppermute | solution.py:820
  323.2 13.4 %collective-permute-start.41 = (bf16[128,1024]{1,0:T(8,128)(2,1)S(1)}, bf16[128,1024]{1,0:T(8,128)(2,1)S(1)}, u32[]{:S(2)}, u32[]{:S(2)}) collective-permute-start(bf16[128,1024]{1,0:T(8,128)(2,1)S(1)} %add_convert_fusion.1), channel_id=1, source_target_pairs={{0,24},{1,25},{2,26},{3,27},{4,28},{5,29},{6,30},{7,31},{8,16},{9,... | collective-permute-start | bytes 786440 | tf_op jit(solution)/shard_map/ppermute | solution.py:820
  325.0 28.6 %collective-permute-start.37 = (bf16[256,1024]{1,0:T(8,128)(2,1)}, bf16[256,1024]{1,0:T(8,128)(2,1)S(1)}, u32[]{:S(2)}, u32[]{:S(2)}) collective-permute-start(bf16[256,1024]{1,0:T(8,128)(2,1)} %get-tuple-element.178), channel_id=1, source_target_pairs={{0,0},{1,3},{2,4},{3,7},{4,2},{5,1},{6,6},{7,5},{8,8},{9,11},{10,1... | collective-permute-start | bytes 1572872 | tf_op jit(solution)/shard_map/ppermute | solution.py:820
  330.1 23.5 %collective-permute-start.38 = (bf16[256,1024]{1,0:T(8,128)(2,1)}, bf16[256,1024]{1,0:T(8,128)(2,1)S(1)}, u32[]{:S(2)}, u32[]{:S(2)}) collective-permute-start(bf16[256,1024]{1,0:T(8,128)(2,1)} %get-tuple-element.179), channel_id=1, source_target_pairs={{0,3},{1,0},{2,7},{3,4},{4,1},{5,2},{6,5},{7,6},{8,11},{9,8},{10,1... | collective-permute-start | bytes 1572872 | tf_op jit(solution)/shard_map/ppermute | solution.py:820
  336.8 18.0 %collective-permute-start.42 = (bf16[512,1024]{1,0:T(8,128)(2,1)S(1)}, bf16[512,1024]{1,0:T(8,128)(2,1)S(1)}, u32[]{:S(2)}, u32[]{:S(2)}) collective-permute-start(bf16[512,1024]{1,0:T(8,128)(2,1)S(1)} %pad_maximum_fusion.3), channel_id=1, source_target_pairs={{0,4},{1,5},{2,6},{3,7},{4,0},{5,1},{6,2},{7,3},{8,12},{9,13},{10,... | collective-permute-start | bytes 3145736 | tf_op jit(solution)/shard_map/ppermute | solution.py:820
  (25 other events, 119.3 us)
Sparse Core Ops, SparseCore 0:
  11.1 80.9 all-gather.2
  94.5 76.6 all-gather.4

commit v5 on v4

--- a/solution.py
+++ b/solution.py
@@ -436,51 +436,26 @@
     )(pair[0], got[0], pair[1], got[1], *deps)
 
 
-def stage(expand_shard, contract_shard, others, deps):
+def stage(expand_shard, contract_shard, deps):
     rows, cols = expand_shard.shape
     half = cols // 2
-    n = len(others)
 
     def kernel(e_ref, c_ref, *refs):
-        e1, e2, c, rest = refs[-4:]
+        e1, e2, c = refs[-3:]
         e1[...] = e_ref[:, :half]
         e2[...] = e_ref[:, half:]
         c[...] = c_ref[...]
-        at = 0
-        for r in refs[:n]:
-            rest[at : at + r.shape[0]] = r[...]
-            at += r.shape[0]
 
     full = pl.BlockSpec(memory_space=pltpu.VMEM)
     return pl.pallas_call(
         kernel,
-        in_specs=[full] * (2 + n) + [ANYWHERE] * len(deps),
-        out_specs=[full] * 4,
-        out_shape=[shape(rows, half, BF)] * 2
-        + [shape(*contract_shard.shape, BF), shape(sum(o.shape[0] for o in others), others[0].shape[1], BF)],
+        in_specs=[full, full] + [ANYWHERE] * len(deps),
+        out_specs=[full] * 3,
+        out_shape=[shape(rows, half, BF)] * 2 + [shape(*contract_shard.shape, BF)],
         cost_estimate=cost(3),
         compiler_params=params(),
         name="stage",
-    )(expand_shard, contract_shard, *others, *deps)
-
-
-def halves(array, deps):
-    rows, half = array.shape[0], array.shape[1] // 2
-
-    def kernel(a, *refs):
-        refs[-2][...] = a[:, :half]
-        refs[-1][...] = a[:, half:]
-
-    full = pl.BlockSpec(memory_space=pltpu.VMEM)
-    return pl.pallas_call(
-        kernel,
-        in_specs=[full] + [ANYWHERE] * len(deps),
-        out_specs=[full] * 2,
-        out_shape=[shape(rows, half, BF)] * 2,
-        cost_estimate=cost(2),
-        compiler_params=params(),
-        name="halves",
-    )(array, *deps)
+    )(expand_shard, contract_shard, *deps)
 
 
 def fused(name, info, body, loads, outs, deps=(), extra=()):
@@ -639,7 +614,7 @@
     )(info, x, *held.arrays)
 
 
-def contract(info, h, c, base, low, sq, gn, up, g_out, scale, block=1024):
+def contract(info, h, c, base, low, sq, gn, up, g_out, scale, block=2048):
     T, D = base.shape
     F = c.shape[0]
     A = sq.shape[1]
@@ -802,9 +777,10 @@
 
     def body(info_ref, get, out0, out1):
         mine, other = get(0), get(1)
+        total = nt(add_pairs(mine, other, 0), get(2)[...])
+        total += nt(add_pairs(mine, other, 1), get(3)[...])
         g = get(4)
-        g[...] += nt(add_pairs(mine, other, 0), get(2)[...])
-        g[...] += nt(add_pairs(mine, other, 1), get(3)[...])
+        g[...] += total
         put_slots(info_ref, g, out0, out1)
 
     return fused("token_grad", info, body, [gkv, got, w_key, w_value, acc], [shape(T // 2, D, BF)] * 2, deps=deps)
@@ -952,8 +928,9 @@
     n = sq.shape[0]
     h = n // 2
     pair = [rows_of(sk, sv[:h]), rows_of(sq, sv[h:])]
-    e1, e2, c_shard, rest = stage(ex, ffn_contract, [self_out, cross_key, cross_value, cross_query, cross_out], ())
-    near = beside(pair, first_hop(pair, low), (t[0], rest))
+    rest = rows_of(self_out, cross_key, cross_value, cross_query, cross_out)
+    near = beside(pair, first_hop(pair, low), (t[0],))
+    e1, e2, c_shard = stage(ex, ffn_contract, near)
     rest = lax.all_gather(rest, "dp", axis=0, tiled=True)
     each = self_out.shape[0]
     w_out, c_key, c_value, c_query, c_out = [Shards(rest, dp, j * each, each) for j in range(5)]
@@ -986,10 +963,9 @@
 
     scale = jnp.full((8, 128), (step_index[0] + 1).astype(F32) / 5.0, F32)
     src = send_pieces(gate(take_pieces(source, s), t))
-    *far, c_shard = gate(
-        [*second_hop(near, low), c_shard], (*src, info, q_aug, *k_aug, cq_aug, *ck_aug, scale, e1, e2)
+    far = gate(
+        second_hop(near, low), (*src, info, q_aug, *k_aug, cq_aug, *ck_aug, scale, e1, e2)
     )
-    w_contract = lax.all_gather(c_shard, "dp", axis=0, tiled=True)
     a1, b1 = all_parts(near, far, low)
     w_key, w_query = Pieces(n, (a1, 0, n, 0)), Pieces(n, (b1, 0, n, 0))
     w_value = Pieces(n, (a1, n, h, 0), (b1, n, h, h))
@@ -997,21 +973,29 @@
     q, kv = project_qkv(info, x, w_query, w_key, w_value, ())
     q, kv, e1, e2 = barrier(q, kv, e1, e2)
     kv_peer = flip(kv, 1)
-    hop3 = first_hop([e1, e2], low)
+    first3, second3 = first_hop([e1, e2], low), second_hop([e1, e2], low)
     attended, p_self, r_self = attend_self(info, q, kv, kv_peer, (q_aug, *k_aug), ())
-    *hop3, attended = barrier(*hop3, attended)
-    near3 = beside([e1, e2], hop3)
-    far3 = second_hop(near3, low)
-    skv, y1, y1_low, inv1, cq = between(info, x, attended, w_out, c_query, Slots(src, 0, C), c_key, c_value, near3)
-    skv, cq, *pieces = barrier(skv, cq, *take_pieces(grad_output, s))
+    *first3, attended, c_shard = barrier(*first3, attended, c_shard)
+    w_contract = lax.all_gather(c_shard, "dp", axis=0, tiled=True)
+    far3 = second_hop(first3, low)
+    flips = [flip(v, low) for v in (e1, e2, *first3)]
+    skv, y1, y1_low, inv1, cq = between(info, x, attended, w_out, c_query, Slots(src, 0, C), c_key, c_value, ())
+    *flips, skv, cq, h0, h1, g0, g1 = barrier(*flips, skv, cq, *second3, *take_pieces(grad_output, s))
+    second3, pieces = [h0, h1], [g0, g1]
     g_out = send_pieces(pieces)
     skv_peer = flip(skv, 1)
     cross_attended, p_cross, r_cross, second_low, inv2, squeezed, gn, base = attend_cross(
         info, cq, skv, skv_peer, (cq_aug, *ck_aug), y1, c_out, adapter_down, adapter_up, scale
     )
-    *far3, g0, g1, second_low = barrier(*far3, *g_out, second_low)
-    g_out = [g0, g1]
-    a3, b3 = all_parts(near3, far3, low)
+    f0, f1, h0, h1, g0, g1, second_low = barrier(*far3, *second3, *g_out, second_low)
+    far3, second3, g_out = [f0, f1], [h0, h1], [g0, g1]
+    a3, b3 = [
+        [(v, 0) for _, v in sorted(
+            {0: own, 1: flips[i], b1: first3[i], b1 ^ 1: flips[2 + i], b2: second3[i], b2 ^ 1: flip(second3[i], low),
+             6: far3[i], 7: flip(far3[i], low)}.items()
+        )]
+        for i, (own, b1, b2) in enumerate(((e1, 2, 4), (e2, 4, 2)))
+    ]
     ea, eb = Pieces(n, (a3, 0, n, 0)), Pieces(n, (b3, 0, n, 0))
     hidden, gp = expand(info, second_low, ea, eb)
     o0, o1, g3, kept, sent, gnar = contract(

time: 372 us -> 360 us (0.968)
  Pallas kernels: 178 us -> 172 us
  waiting for transfers between devices: 64.4 us -> 59.1 us
    ppermute x43 -> x49, waiting for transfers between devices: 64.4 us -> 59 us  [move(): return lax.ppermute(value, ('dp', 'seq'), pairs)]
    unnamed x57 -> x41, local copies, waits for them, and re-layouts: 10.7 us -> 8.84 us
    ppermute x43 -> x49, starting transfers between devices: 69.1 us -> 68.8 us  [move(): return lax.ppermute(value, ('dp', 'seq'), pairs)]
  transfers between devices with their start and end apart: 45 -> 51, of which waited for: 15 -> 20; matrix products, arithmetic and copies ran while one was open for 7% -> 8% of each run, Pallas kernels for 43% -> 44%
where the time goes in v5:
time: 360 us; the launch traced here: 354 us
  Pallas kernels  172 us (48%)
  starting transfers between devices  68.9 us (19%)
  waiting for transfers between devices  59.1 us (16%)
  other arithmetic  22 us (6%)
  local copies, waits for them, and re-layouts  16.4 us (5%)
  between operations  15.5 us (4%)
    ppermute x49, starting transfers between devices, move(): return lax.ppermute(value, ('dp', 'seq'), pairs)  68.8 us
    ppermute x49, waiting for transfers between devices, move(): return lax.ppermute(value, ('dp', 'seq'), pairs)  59 us
    pallas_call x2, Pallas kernels, attend_back(): pl.pallas_call(kernel, grid_spec=pltpu.PrefetchScalarGridSpec(num_scalar_...  46.6 us
    pallas_call x2, Pallas kernels, attend(): pl.pallas_call(kernel, grid_spec=pltpu.PrefetchScalarGridSpec(num_scalar_...  36.9 us
    pallas_call x4, Pallas kernels, fused(): pl.pallas_call(kernel, grid_spec=pltpu.PrefetchScalarGridSpec(num_scalar_...  34 us
    pallas_call x1, Pallas kernels, ffn_back(): pl.pallas_call(kernel, grid_spec=pltpu.PrefetchScalarGridSpec(num_scalar_...  19.8 us
    pallas_call x1, Pallas kernels, contract(): pl.pallas_call(kernel, grid_spec=pltpu.PrefetchScalarGridSpec(num_scalar_...  15.5 us
    pallas_call x1, Pallas kernels, expand(): pl.pallas_call(kernel, grid_spec=pltpu.PrefetchScalarGridSpec(num_scalar_...  13.4 us
  transfers between devices with their start and end apart: 51, of which 20 were waited for; matrix products, arithmetic and copies ran while one was open for 8% of the time, Pallas kernels for 44%

profile of v5, /device:TPU:1, one launch (start us, length us, event | category | flops | bytes accessed | tf_op | source)
XLA Modules:
  0.0 353.5 jit_solution(2403825961561308565)
XLA Ops:
  13.3 5.6 %collective-permute-start = (bf16[256,1024]{1,0:T(8,128)(2,1)S(1)}, bf16[256,1024]{1,0:T(8,128)(2,1)}, u32[]{:S(2)}, u32[]{:S(2)}) collective-permute-start(bf16[256,1024]{1,0:T(8,128)(2,1)S(1)} %get-tuple-element.226), channel_id=1, source_target_pairs={{0,0},{1,5},{2,4},{3,1},{4,2},{5,7},{6,6},{7,3},{8,8},{9,13},{10,1... | collective-permute-start | bytes 1572872 | tf_op jit(solution)/shard_map/ppermute | solution.py:796
  22.6 1.9 collective-permute-start.1
  30.7 3.9 %collective-permute-done.2.b = bf16[192,1024]{1,0:T(8,128)(2,1)} collective-permute-done((bf16[192,1024]{1,0:T(8,128)(2,1)S(1)}, bf16[192,1024]{1,0:T(8,128)(2,1)}, u32[]{:S(2)}, u32[]{:S(2)}) %collective-permute-start.2) | collective-permute-done | bytes 393248 | tf_op jit(solution)/shard_map/ppermute | solution.py:796
  34.6 2.6 collective-permute-done.3.d
  38.0 2.6 beside.1
  40.6 2.4 collective-permute-start.5
  43.6 1.5 and_convert_fusion
  45.1 1.9 collective-permute-start.7
  47.1 2.3 collective-permute-start.8
  51.0 2.9 stage.1
  53.9 9.9 %collective-permute-done.7.refs_2_.refs_0_ = bf16[256,1024]{1,0:T(8,128)(2,1)} collective-permute-done((bf16[256,1024]{1,0:T(8,128)(2,1)}, bf16[256,1024]{1,0:T(8,128)(2,1)}, u32[]{:S(2)}, u32[]{:S(2)}) %collective-permute-start.7) | collective-permute-done | bytes 524320 | tf_op jit(solution)/shard_map/ppermute | solution.py:796
  64.8 4.0 %collective-permute-done.5.refs_0_ = bf16[384,1024]{1,0:T(8,128)(2,1)} collective-permute-done((bf16[384,1024]{1,0:T(8,128)(2,1)}, bf16[384,1024]{1,0:T(8,128)(2,1)}, u32[]{:S(2)}, u32[]{:S(2)}) %collective-permute-start.5) | collective-permute-done | bytes 786464 | tf_op jit(solution)/shard_map/ppermute | solution.py:796
  71.1 2.1 collective-permute-done.10.refs_7_.refs_9_.refs_15_.refs_17_
  74.4 7.6 %qkv.1 = (bf16[512,1024]{1,0:T(8,128)(2,1)}, bf16[512,2048]{1,0:T(8,128)(2,1)}) custom-call(s32[4]{0:T(128)} %pad_add_fusion.2.refs_4_.info_ref, bf16[256,1024]{1,0:T(8,128)(2,1)} %collective-permute-done.refs_0_.refs_2_.refs_6_, bf16[256,1024]{1,0:T(8,128)(2,1)} %collective-permute-done.1.refs_3_.refs_1_.refs_7_, ...), custom_call_target="tpu_custom_call" | custom-call | flops 1800000000 | bytes 1024 | tf_op jit(solution)/shard_map/qkv/pallas_call | solution.py:472
  82.1 1.5 collective-permute-start.13
  84.7 1.9 collective-permute-done.15.kp.vp
  86.6 12.8 %attend.2 = (bf16[512,1024]{1,0:T(8,128)(2,1)}, bf16[8,2,5,256,256]{4,3,2,1,0:T(8,128)(2,1)}, f32[512,1024]{1,0:T(8,128)}) custom-call(s32[4]{0:T(128)} %pad_add_fusion.2.refs_4_.info_ref, bf16[512,1024]{1,0:T(8,128)(2,1)} %get-tuple-element.111.q_ref, bf16[512,2048]{1,0:T(8,128)(2,1)} %get-tuple-element.112.ko.vo, ...), custom_call_target="tpu_custom_call" | custom-call | flops 7500000256 | bytes 1024 | tf_op jit(solution)/shard_map/attend/pallas_call | solution.py:267
  105.0 10.1 %between.1 = (bf16[512,2048]{1,0:T(8,128)(2,1)}, f32[512,1024]{1,0:T(8,128)}, bf16[512,1024]{1,0:T(8,128)(2,1)}, f32[512,128]{1,0:T(8,128)}, bf16[512,1024]{1,0:T(8,128)(2,1)}) custom-call(s32[4]{0:T(128)} %pad_add_fusion.2.refs_4_.info_ref, bf16[256,1024]{1,0:T(8,128)(2,1)} %collective-permute-done.7.refs_2_.refs_0_, ...), custom_call_target="tpu_custom_call" | custom-call | flops 1800000000 | bytes 1024 | tf_op jit(solution)/shard_map/between/pallas_call | solution.py:472
  116.0 2.2 collective-permute-done.23.refs_7_
  118.2 4.0 %collective-permute-start.26 = (bf16[512,2048]{1,0:T(8,128)(2,1)}, bf16[512,2048]{1,0:T(8,128)(2,1)}, u32[]{:S(2)}, u32[]{:S(2)}) collective-permute-start(bf16[512,2048]{1,0:T(8,128)(2,1)} %get-tuple-element.125.ko.vo), channel_id=1, source_target_pairs={{0,4},{1,5},{2,6},{3,7},{4,0},{5,1},{6,2},{7,3},{8,12},{9,13},{10,... | collective-permute-start | bytes 6291464 | tf_op jit(solution)/shard_map/ppermute | solution.py:796
  122.3 9.6 %collective-permute-start.24 = (bf16[256,1024]{1,0:T(8,128)(2,1)}, bf16[256,1024]{1,0:T(8,128)(2,1)}, u32[]{:S(2)}, u32[]{:S(2)}) collective-permute-start(bf16[256,1024]{1,0:T(8,128)(2,1)} %get-tuple-element.122), channel_id=1, source_target_pairs={{0,0},{1,5},{2,4},{3,1},{4,2},{5,7},{6,6},{7,3},{8,8},{9,13},{10,1... | collective-permute-start | bytes 1572872 | tf_op jit(solution)/shard_map/ppermute | solution.py:796
  131.9 4.9 %collective-permute-start.25 = (bf16[256,1024]{1,0:T(8,128)(2,1)}, bf16[256,1024]{1,0:T(8,128)(2,1)}, u32[]{:S(2)}, u32[]{:S(2)}) collective-permute-start(bf16[256,1024]{1,0:T(8,128)(2,1)} %get-tuple-element.123), channel_id=1, source_target_pairs={{0,1},{1,4},{2,5},{3,0},{4,3},{5,6},{6,7},{7,2},{8,9},{9,12},{10,1... | collective-permute-start | bytes 1572872 | tf_op jit(solution)/shard_map/ppermute | solution.py:796
  136.8 24.1 %attend.3 = (bf16[512,1024]{1,0:T(8,128)(2,1)}, bf16[8,2,8,256,256]{4,3,2,1,0:T(8,128)(2,1)}, f32[512,1024]{1,0:T(8,128)}, bf16[512,1024]{1,0:T(8,128)(2,1)}, f3...) custom-call(s32[4]{0:T(128)} %pad_add_fusion.2.refs_4_.info_ref, ...), custom_call_target="tpu_custom_call" | custom-call | flops 7500000256 | bytes 1024 | tf_op jit(solution)/shard_map/attend/pallas_call | solution.py:267
  165.9 13.4 %expand.1 = (bf16[512,4096]{1,0:T(8,128)(2,1)}, bf16[512,4096]{1,0:T(8,128)(2,1)}) custom-call(s32[4]{0:T(128)} %pad_add_fusion.2.refs_4_.info_ref, bf16[512,1024]{1,0:T(8,128)(2,1)} %get-tuple-element.128.x_ref.refs_7_.refs_19_, bf16[128,2048]{1,0:T(8,128)(2,1)} %get-tuple-element.109.refs_0_, bf16[128,2048]{1,0:T(8,128)(2,1)} %get-tuple-element.129.refs_1_, ...), custom_call_target="tpu_custom_call" | custom-call | flops 3600000000 | bytes 1024 | tf_op jit(solution)/shard_map/expand/pallas_call | solution.py:601
  179.4 15.5 %contract.1 = (bf16[256,1024]{1,0:T(8,128)(2,1)}, bf16[256,1024]{1,0:T(8,128)(2,1)}, f32[512,1024]{1,0:T(8,128)}, bf16[512,1024]{1,0:T(8,128)(2,1)}, bf16[512,10...) custom-call(s32[4]{0:T(128)} %pad_add_fusion.2.refs_4_.info_ref, bf16[512,4096]{1,0:T(8,128)(2,1)} %get-tuple-element.137.h_ref, ...), custom_call_target="tpu_custom_call" | custom-call | flops 4200000000 | bytes 1024 | tf_op jit(solution)/shard_map/contract/pallas_call | solution.py:658
  195.1 1.9 collective-permute-start.35
  197.4 19.8 %ffn_back.1 = (f32[512,1024]{1,0:T(8,128)}, bf16[512,1024]{1,0:T(8,128)(2,1)}) custom-call(s32[4]{0:T(128)} %pad_add_fusion.2.refs_4_.info_ref, f32[512,1024]{1,0:T(8,128)} %get-tuple-element.146.g3_ref, bf16[4096,1024]{1,0:T(8,128)(2,1)} %all-gather.5.cloned.1.call-done.c_ref, bf16[512,4096]{1,0:T(8,128)(2,1)} %get-tuple-element.147.gp_ref, ...), custom_call_target="tpu_custom_call" | custom-call | flops 5400000000 | bytes 1024 | tf_op jit(solution)/shard_map/ffn_back/pallas_call | solution.py:714
  218.5 1.6 add_convert_fusion
  222.0 1.7 collective-permute-start.34
  223.7 28.4 %attend_back.2 = (bf16[512,2048]{1,0:T(8,128)(2,1)}, bf16[512,2048]{1,0:T(8,128)(2,1)}, f32[512,1024]{1,0:T(8,128)}, bf16[512,1024]{1,0:T(8,128)(2,1)}) custom-call(s32[4]{0:T(128)} %pad_add_fusion.2.refs_4_.info_ref, bf16[512,1024]{1,0:T(8,128)(2,1)} %get-tuple-element.124.q_ref, bf16[512,2048]{1,0:T(8,128)(2,1)} %get-tuple-element.125.ko.vo, ...), custom_call_target="tpu_custom_call" | custom-call | flops 7500000256 | bytes 1024 | tf_op jit(solution)/shard_map/attend_back/pallas_call | solution.py:381
  252.3 4.3 %collective-permute-start.38 = (bf16[512,2048]{1,0:T(8,128)(2,1)}, bf16[512,2048]{1,0:T(8,128)(2,1)}, u32[]{:S(2)}, u32[]{:S(2)}) collective-permute-start(bf16[512,2048]{1,0:T(8,128)(2,1)} %get-tuple-element.168), channel_id=1, source_target_pairs={{0,4},{1,5},{2,6},{3,7},{4,0},{5,1},{6,2},{7,3},{8,12},{9,13},{10,... | collective-permute-start | bytes 6291464 | tf_op jit(solution)/shard_map/ppermute | solution.py:796
  256.6 2.0 add_convert_fusion.3.refs_5_
  258.6 2.1 collective-permute-done.38.refs_1_
  260.7 8.0 %source_grad.1 = (bf16[256,1024]{1,0:T(8,128)(2,1)}, bf16[256,1024]{1,0:T(8,128)(2,1)}) custom-call(s32[4]{0:T(128)} %pad_add_fusion.2.refs_4_.info_ref, bf16[512,2048]{1,0:T(8,128)(2,1)} %get-tuple-element.167.refs_0_, bf16[512,2048]{1,0:T(8,128)(2,1)} %collective-permute-done.38.refs_1_, ...), custom_call_target="tpu_custom_call" | custom-call | flops 1800000000 | bytes 1024 | tf_op jit(solution)/shard_map/source_grad/pallas_call | solution.py:472
  268.7 3.1 collective-permute-start.39
  271.9 2.1 collective-permute-start.40
  273.9 18.1 %attend_back.3 = (bf16[512,2048]{1,0:T(8,128)(2,1)}, bf16[512,2048]{1,0:T(8,128)(2,1)}, f32[512,1024]{1,0:T(8,128)}) custom-call(s32[4]{0:T(128)} %pad_add_fusion.2.refs_4_.info_ref, bf16[512,1024]{1,0:T(8,128)(2,1)} %get-tuple-element.111.q_ref, bf16[512,2048]{1,0:T(8,128)(2,1)} %get-tuple-element.112.ko.vo, bf16[512,2048]{1,0:T(8,128)(2,1)} %get-tuple-element.112.ko.vo, ...), custom_call_target="tpu_custom_call" | custom-call | flops 7500000256 | bytes 1024 | tf_op jit(solution)/shard_map/attend_back/pallas_call | solution.py:381
  292.1 4.5 %collective-permute-done.39.refs_1_ = bf16[256,1024]{1,0:T(8,128)(2,1)} collective-permute-done((bf16[256,1024]{1,0:T(8,128)(2,1)}, bf16[256,1024]{1,0:T(8,128)(2,1)}, u32[]{:S(2)}, u32[]{:S(2)}) %collective-permute-start.39) | collective-permute-done | bytes 524320 | tf_op jit(solution)/shard_map/ppermute | solution.py:796
  296.6 1.8 add_convert_fusion.2.refs_27_
  299.4 1.7 collective-permute-done.42.refs_1_
  301.1 8.3 %token_grad.1 = (bf16[256,1024]{1,0:T(8,128)(2,1)}, bf16[256,1024]{1,0:T(8,128)(2,1)}) custom-call(s32[4]{0:T(128)} %pad_add_fusion.2.refs_4_.info_ref, bf16[512,2048]{1,0:T(8,128)(2,1)} %get-tuple-element.181.refs_0_, bf16[512,2048]{1,0:T(8,128)(2,1)} %collective-permute-done.42.refs_1_, ...), custom_call_target="tpu_custom_call" | custom-call | flops 1800000000 | bytes 1024 | tf_op jit(solution)/shard_map/token_grad/pallas_call | solution.py:472
  311.8 1.4 collective-permute-start.47
  313.3 4.6 %collective-permute-start.43 = (bf16[256,1024]{1,0:T(8,128)(2,1)}, bf16[256,1024]{1,0:T(8,128)(2,1)S(1)}, u32[]{:S(2)}, u32[]{:S(2)}) collective-permute-start(bf16[256,1024]{1,0:T(8,128)(2,1)} %get-tuple-element.188), channel_id=1, source_target_pairs={{0,0},{1,3},{2,4},{3,7},{4,2},{5,1},{6,6},{7,5},{8,8},{9,11},{10,1... | collective-permute-start | bytes 1572872 | tf_op jit(solution)/shard_map/ppermute | solution.py:796
  317.9 1.6 collective-permute-start.44
  319.5 5.4 %collective-permute-done.47 = bf16[128,1024]{1,0:T(8,128)(2,1)S(1)} collective-permute-done((bf16[128,1024]{1,0:T(8,128)(2,1)S(1)}, bf16[128,1024]{1,0:T(8,128)(2,1)S(1)}, u32[]{:S(2)}, u32[]{:S(2)}) %collective-permute-start.47) | collective-permute-done | bytes 262176 | tf_op jit(solution)/shard_map/ppermute | solution.py:796
  331.1 10.6 %collective-permute-done.43 = bf16[256,1024]{1,0:T(8,128)(2,1)S(1)} collective-permute-done((bf16[256,1024]{1,0:T(8,128)(2,1)}, bf16[256,1024]{1,0:T(8,128)(2,1)S(1)}, u32[]{:S(2)}, u32[]{:S(2)}) %collective-permute-start.43) | collective-permute-done | bytes 524320 | tf_op jit(solution)/shard_map/ppermute | solution.py:796
  342.8 1.9 select_convert_fusion
  344.7 1.8 copy.76
  (163 shorter events, 50.1 us)
Async XLA Ops:
  7.2 97.8 %all-gather.3.cloned.1.call-start = ((), (), s32[]{:S(2)}) async-start(), calls=%async_computation | async-start | bytes 11796480 | tf_op jit(solution)/shard_map/all_gather | solution.py:934
  12.3 167.0 %all-gather.5.cloned.1.call-start = ((), (), s32[]{:S(2)}) async-start(), calls=%async_computation.1 | async-start | bytes 9437184 | tf_op jit(solution)/shard_map/all_gather | solution.py:979
  13.3 24.7 %collective-permute-start = (bf16[256,1024]{1,0:T(8,128)(2,1)S(1)}, bf16[256,1024]{1,0:T(8,128)(2,1)}, u32[]{:S(2)}, u32[]{:S(2)}) collective-permute-start(bf16[256,1024]{1,0:T(8,128)(2,1)S(1)} %get-tuple-element.226), channel_id=1, source_target_pairs={{0,0},{1,5},{2,4},{3,1},{4,2},{5,7},{6,6},{7,3},{8,8},{9,13},{10,1... | collective-permute-start | bytes 1572872 | tf_op jit(solution)/shard_map/ppermute | solution.py:796
  20.0 14.7 %collective-permute-start.2 = (bf16[192,1024]{1,0:T(8,128)(2,1)S(1)}, bf16[192,1024]{1,0:T(8,128)(2,1)}, u32[]{:S(2)}, u32[]{:S(2)}) collective-permute-start(bf16[192,1024]{1,0:T(8,128)(2,1)S(1)} %pad_maximum_fusion.4.a), channel_id=1, source_target_pairs={{0,8},{1,9},{2,10},{3,11},{4,12},{5,13},{6,14},{7,15},{8,0},{9,1},... | collective-permute-start | bytes 1179656 | tf_op jit(solution)/shard_map/ppermute | solution.py:796
  21.3 16.0 %collective-permute-start.3 = (bf16[192,1024]{1,0:T(8,128)(2,1)S(1)}, bf16[192,1024]{1,0:T(8,128)(2,1)S(1)}, u32[]{:S(2)}, u32[]{:S(2)}) collective-permute-start(bf16[192,1024]{1,0:T(8,128)(2,1)S(1)} %pad_maximum_fusion.5.c), channel_id=1, source_target_pairs={{0,16},{1,17},{2,18},{3,19},{4,20},{5,21},{6,22},{7,23},{8,24},{9,... | collective-permute-start | bytes 1179656 | tf_op jit(solution)/shard_map/ppermute | solution.py:796
  22.6 22.5 %collective-permute-start.1 = (bf16[256,1024]{1,0:T(8,128)(2,1)}, bf16[256,1024]{1,0:T(8,128)(2,1)}, u32[]{:S(2)}, u32[]{:S(2)}) collective-permute-start(bf16[256,1024]{1,0:T(8,128)(2,1)} %get-tuple-element.225), channel_id=1, source_target_pairs={{0,1},{1,4},{2,5},{3,0},{4,3},{5,6},{6,7},{7,2},{8,9},{9,12},{10,1... | collective-permute-start | bytes 1572872 | tf_op jit(solution)/shard_map/ppermute | solution.py:796
  24.7 4.5 %collective-permute-start.9 = (s32[2,5]{1,0:T(2,128)S(1)}, s32[2,5]{1,0:T(2,128)S(1)}, u32[]{:S(2)}, u32[]{:S(2)}) collective-permute-start(s32[2,5]{1,0:T(2,128)S(1)} %pad_add_fusion.1), channel_id=1, source_target_pairs={{0,4},{1,5},{2,6},{3,7},{4,0},{5,1},{6,2},{7,3},{8,12},{9,13},{10,... | collective-permute-start | bytes 128 | tf_op jit(solution)/shard_map/ppermute | solution.py:796
  40.6 28.1 %collective-permute-start.5 = (bf16[384,1024]{1,0:T(8,128)(2,1)}, bf16[384,1024]{1,0:T(8,128)(2,1)}, u32[]{:S(2)}, u32[]{:S(2)}) collective-permute-start(bf16[384,1024]{1,0:T(8,128)(2,1)} %get-tuple-element.99.refs_0_.refs_2_.refs_4_.refs_10_.refs_12_), channel_id=1, source_target_pairs={{0,16},{1,17},{2,18},{3,19},{4,20},{5,21},{6,22},{7,23},{8,24},{9,... | collective-permute-start | bytes 2359304 | tf_op jit(solution)/shard_map/ppermute | solution.py:796
  43.0 25.8 %collective-permute-start.6 = (bf16[384,1024]{1,0:T(8,128)(2,1)}, bf16[384,1024]{1,0:T(8,128)(2,1)}, u32[]{:S(2)}, u32[]{:S(2)}) collective-permute-start(bf16[384,1024]{1,0:T(8,128)(2,1)} %get-tuple-element.100.refs_1_.refs_18_.refs_22_.refs_26_.refs_30_.refs_0_.refs_4_), channel_id=1, source_target_pairs={{0,8},{1,9},{2,10},{3,11},{4,12},{5,13},{6,14},{7,15},{8,0},{9,1},... | collective-permute-start | bytes 2359304 | tf_op jit(solution)/shard_map/ppermute | solution.py:796
  45.1 18.6 %collective-permute-start.7 = (bf16[256,1024]{1,0:T(8,128)(2,1)}, bf16[256,1024]{1,0:T(8,128)(2,1)}, u32[]{:S(2)}, u32[]{:S(2)}) collective-permute-start(bf16[256,1024]{1,0:T(8,128)(2,1)} %get-tuple-element.101), channel_id=1, source_target_pairs={{0,0},{1,5},{2,4},{3,1},{4,2},{5,7},{6,6},{7,3},{8,8},{9,13},{10,1... | collective-permute-start | bytes 1572872 | tf_op jit(solution)/shard_map/ppermute | solution.py:796
  47.1 17.7 %collective-permute-start.8 = (bf16[256,1024]{1,0:T(8,128)(2,1)}, bf16[256,1024]{1,0:T(8,128)(2,1)}, u32[]{:S(2)}, u32[]{:S(2)}) collective-permute-start(bf16[256,1024]{1,0:T(8,128)(2,1)} %get-tuple-element.102), channel_id=1, source_target_pairs={{0,1},{1,4},{2,5},{3,0},{4,3},{5,6},{6,7},{7,2},{8,9},{9,12},{10,1... | collective-permute-start | bytes 1572872 | tf_op jit(solution)/shard_map/ppermute | solution.py:796
  51.0 20.1 %collective-permute-start.11 = (bf16[384,1024]{1,0:T(8,128)(2,1)}, bf16[384,1024]{1,0:T(8,128)(2,1)}, u32[]{:S(2)}, u32[]{:S(2)}) collective-permute-start(bf16[384,1024]{1,0:T(8,128)(2,1)} %get-tuple-element.100.refs_1_.refs_18_.refs_22_.refs_26_.refs_30_.refs_0_.refs_4_), channel_id=1, source_target_pairs={{0,4},{1,5},{2,6},{3,7},{4,0},{5,1},{6,2},{7,3},{8,12},{9,13},{10,... | collective-permute-start | bytes 2359304 | tf_op jit(solution)/shard_map/ppermute | solution.py:796
  63.8 7.3 %collective-permute-start.4 = (bf16[384,1024]{1,0:T(8,128)(2,1)}, bf16[384,1024]{1,0:T(8,128)(2,1)}, u32[]{:S(2)}, u32[]{:S(2)}) collective-permute-start(bf16[384,1024]{1,0:T(8,128)(2,1)} %get-tuple-element.99.refs_0_.refs_2_.refs_4_.refs_10_.refs_12_), channel_id=1, source_target_pairs={{0,4},{1,5},{2,6},{3,7},{4,0},{5,1},{6,2},{7,3},{8,12},{9,13},{10,... | collective-permute-start | bytes 2359304 | tf_op jit(solution)/shard_map/ppermute | solution.py:796
  70.6 3.7 %collective-permute-start.12 = (bf16[384,1024]{1,0:T(8,128)(2,1)}, bf16[384,1024]{1,0:T(8,128)(2,1)}, u32[]{:S(2)}, u32[]{:S(2)}) collective-permute-start(bf16[384,1024]{1,0:T(8,128)(2,1)} %get-tuple-element.106.refs_20_.refs_24_.refs_28_.refs_32_.refs_2_.refs_6_), channel_id=1, source_target_pairs={{0,4},{1,5},{2,6},{3,7},{4,0},{5,1},{6,2},{7,3},{8,12},{9,13},{10,... | collective-permute-start | bytes 2359304 | tf_op jit(solution)/shard_map/ppermute | solution.py:796
  82.0 4.6 %collective-permute-start.15 = (bf16[512,2048]{1,0:T(8,128)(2,1)}, bf16[512,2048]{1,0:T(8,128)(2,1)}, u32[]{:S(2)}, u32[]{:S(2)}) collective-permute-start(bf16[512,2048]{1,0:T(8,128)(2,1)} %get-tuple-element.112.ko.vo), channel_id=1, source_target_pairs={{0,4},{1,5},{2,6},{3,7},{4,0},{5,1},{6,2},{7,3},{8,12},{9,13},{10,... | collective-permute-start | bytes 6291464 | tf_op jit(solution)/shard_map/ppermute | solution.py:796
  82.1 17.2 %collective-permute-start.13 = (bf16[128,2048]{1,0:T(8,128)(2,1)}, bf16[128,2048]{1,0:T(8,128)(2,1)}, u32[]{:S(2)}, u32[]{:S(2)}) collective-permute-start(bf16[128,2048]{1,0:T(8,128)(2,1)} %get-tuple-element.109.refs_0_), channel_id=1, source_target_pairs={{0,8},{1,9},{2,10},{3,11},{4,12},{5,13},{6,14},{7,15},{8,0},{9,1},... | collective-permute-start | bytes 1572872 | tf_op jit(solution)/shard_map/ppermute | solution.py:796
  83.6 17.0 %collective-permute-start.14 = (bf16[128,2048]{1,0:T(8,128)(2,1)}, bf16[128,2048]{1,0:T(8,128)(2,1)}, u32[]{:S(2)}, u32[]{:S(2)}) collective-permute-start(bf16[128,2048]{1,0:T(8,128)(2,1)} %get-tuple-element.110.refs_8_), channel_id=1, source_target_pairs={{0,16},{1,17},{2,18},{3,19},{4,20},{5,21},{6,22},{7,23},{8,24},{9,... | collective-permute-start | bytes 1572872 | tf_op jit(solution)/shard_map/ppermute | solution.py:796
  100.6 3.3 collective-permute-start.18
  101.4 13.7 %collective-permute-start.19 = (bf16[128,2048]{1,0:T(8,128)(2,1)}, bf16[128,2048]{1,0:T(8,128)(2,1)}, u32[]{:S(2)}, u32[]{:S(2)}) collective-permute-start(bf16[128,2048]{1,0:T(8,128)(2,1)} %get-tuple-element.110.refs_8_), channel_id=1, source_target_pairs={{0,4},{1,5},{2,6},{3,7},{4,0},{5,1},{6,2},{7,3},{8,12},{9,13},{10,... | collective-permute-start | bytes 1572872 | tf_op jit(solution)/shard_map/ppermute | solution.py:796
  101.5 14.6 %collective-permute-start.22 = (bf16[128,2048]{1,0:T(8,128)(2,1)}, bf16[128,2048]{1,0:T(8,128)(2,1)}, u32[]{:S(2)}, u32[]{:S(2)}) collective-permute-start(bf16[128,2048]{1,0:T(8,128)(2,1)} %get-tuple-element.109.refs_0_), channel_id=1, source_target_pairs={{0,16},{1,17},{2,18},{3,19},{4,20},{5,21},{6,22},{7,23},{8,24},{9,... | collective-permute-start | bytes 1572872 | tf_op jit(solution)/shard_map/ppermute | solution.py:796
  102.9 15.3 %collective-permute-start.23 = (bf16[128,2048]{1,0:T(8,128)(2,1)}, bf16[128,2048]{1,0:T(8,128)(2,1)}, u32[]{:S(2)}, u32[]{:S(2)}) collective-permute-start(bf16[128,2048]{1,0:T(8,128)(2,1)} %get-tuple-element.110.refs_8_), channel_id=1, source_target_pairs={{0,8},{1,9},{2,10},{3,11},{4,12},{5,13},{6,14},{7,15},{8,0},{9,1},... | collective-permute-start | bytes 1572872 | tf_op jit(solution)/shard_map/ppermute | solution.py:796
  103.0 15.2 %collective-permute-start.20 = (bf16[128,2048]{1,0:T(8,128)(2,1)}, bf16[128,2048]{1,0:T(8,128)(2,1)}, u32[]{:S(2)}, u32[]{:S(2)}) collective-permute-start(bf16[128,2048]{1,0:T(8,128)(2,1)} %get-tuple-element.115.refs_2_), channel_id=1, source_target_pairs={{0,4},{1,5},{2,6},{3,7},{4,0},{5,1},{6,2},{7,3},{8,12},{9,13},{10,... | collective-permute-start | bytes 1572872 | tf_op jit(solution)/shard_map/ppermute | solution.py:796
  104.0 14.2 %collective-permute-start.21 = (bf16[128,2048]{1,0:T(8,128)(2,1)}, bf16[128,2048]{1,0:T(8,128)(2,1)}, u32[]{:S(2)}, u32[]{:S(2)}) collective-permute-start(bf16[128,2048]{1,0:T(8,128)(2,1)} %get-tuple-element.116.refs_12_), channel_id=1, source_target_pairs={{0,4},{1,5},{2,6},{3,7},{4,0},{5,1},{6,2},{7,3},{8,12},{9,13},{10,... | collective-permute-start | bytes 1572872 | tf_op jit(solution)/shard_map/ppermute | solution.py:796
  118.2 18.6 %collective-permute-start.26 = (bf16[512,2048]{1,0:T(8,128)(2,1)}, bf16[512,2048]{1,0:T(8,128)(2,1)}, u32[]{:S(2)}, u32[]{:S(2)}) collective-permute-start(bf16[512,2048]{1,0:T(8,128)(2,1)} %get-tuple-element.125.ko.vo), channel_id=1, source_target_pairs={{0,4},{1,5},{2,6},{3,7},{4,0},{5,1},{6,2},{7,3},{8,12},{9,13},{10,... | collective-permute-start | bytes 6291464 | tf_op jit(solution)/shard_map/ppermute | solution.py:796
  122.2 38.7 %collective-permute-start.16 = (bf16[128,2048]{1,0:T(8,128)(2,1)}, bf16[128,2048]{1,0:T(8,128)(2,1)}, u32[]{:S(2)}, u32[]{:S(2)}) collective-permute-start(bf16[128,2048]{1,0:T(8,128)(2,1)} %get-tuple-element.115.refs_2_), channel_id=1, source_target_pairs={{0,16},{1,17},{2,18},{3,19},{4,20},{5,21},{6,22},{7,23},{8,24},{9,... | collective-permute-start | bytes 1572872 | tf_op jit(solution)/shard_map/ppermute | solution.py:796
  122.2 38.7 %collective-permute-start.17 = (bf16[128,2048]{1,0:T(8,128)(2,1)}, bf16[128,2048]{1,0:T(8,128)(2,1)}, u32[]{:S(2)}, u32[]{:S(2)}) collective-permute-start(bf16[128,2048]{1,0:T(8,128)(2,1)} %get-tuple-element.116.refs_12_), channel_id=1, source_target_pairs={{0,8},{1,9},{2,10},{3,11},{4,12},{5,13},{6,14},{7,15},{8,0},{9,1},... | collective-permute-start | bytes 1572872 | tf_op jit(solution)/shard_map/ppermute | solution.py:796
  122.3 38.6 %collective-permute-start.24 = (bf16[256,1024]{1,0:T(8,128)(2,1)}, bf16[256,1024]{1,0:T(8,128)(2,1)}, u32[]{:S(2)}, u32[]{:S(2)}) collective-permute-start(bf16[256,1024]{1,0:T(8,128)(2,1)} %get-tuple-element.122), channel_id=1, source_target_pairs={{0,0},{1,5},{2,4},{3,1},{4,2},{5,7},{6,6},{7,3},{8,8},{9,13},{10,1... | collective-permute-start | bytes 1572872 | tf_op jit(solution)/shard_map/ppermute | solution.py:796
  131.9 29.1 %collective-permute-start.25 = (bf16[256,1024]{1,0:T(8,128)(2,1)}, bf16[256,1024]{1,0:T(8,128)(2,1)}, u32[]{:S(2)}, u32[]{:S(2)}) collective-permute-start(bf16[256,1024]{1,0:T(8,128)(2,1)} %get-tuple-element.123), channel_id=1, source_target_pairs={{0,1},{1,4},{2,5},{3,0},{4,3},{5,6},{6,7},{7,2},{8,9},{9,12},{10,1... | collective-permute-start | bytes 1572872 | tf_op jit(solution)/shard_map/ppermute | solution.py:796
  161.6 3.6 %collective-permute-start.29 = (bf16[128,2048]{1,0:T(8,128)(2,1)}, bf16[128,2048]{1,0:T(8,128)(2,1)}, u32[]{:S(2)}, u32[]{:S(2)}) collective-permute-start(bf16[128,2048]{1,0:T(8,128)(2,1)} %get-tuple-element.134.refs_10_), channel_id=1, source_target_pairs={{0,4},{1,5},{2,6},{3,7},{4,0},{5,1},{6,2},{7,3},{8,12},{9,13},{10,... | collective-permute-start | bytes 1572872 | tf_op jit(solution)/shard_map/ppermute | solution.py:796
  161.7 4.3 %collective-permute-start.30 = (bf16[128,2048]{1,0:T(8,128)(2,1)}, bf16[128,2048]{1,0:T(8,128)(2,1)}, u32[]{:S(2)}, u32[]{:S(2)}) collective-permute-start(bf16[128,2048]{1,0:T(8,128)(2,1)} %get-tuple-element.136.refs_14_), channel_id=1, source_target_pairs={{0,4},{1,5},{2,6},{3,7},{4,0},{5,1},{6,2},{7,3},{8,12},{9,13},{10,... | collective-permute-start | bytes 1572872 | tf_op jit(solution)/shard_map/ppermute | solution.py:796
  194.9 22.4 %collective-permute-start.31 = (bf16[512,1024]{1,0:T(8,128)(2,1)}, bf16[512,1024]{1,0:T(8,128)(2,1)}, u32[]{:S(2)}, u32[]{:S(2)}) collective-permute-start(bf16[512,1024]{1,0:T(8,128)(2,1)} %get-tuple-element.145), channel_id=1, source_target_pairs={{0,4},{1,5},{2,6},{3,7},{4,0},{5,1},{6,2},{7,3},{8,12},{9,13},{10,... | collective-permute-start | bytes 3145736 | tf_op jit(solution)/shard_map/ppermute | solution.py:796
  195.1 57.1 %collective-permute-start.35 = (bf16[256,1024]{1,0:T(8,128)(2,1)}, bf16[256,1024]{1,0:T(8,128)(2,1)}, u32[]{:S(2)}, u32[]{:S(2)}) collective-permute-start(bf16[256,1024]{1,0:T(8,128)(2,1)} %get-tuple-element.153), channel_id=1, source_target_pairs={{0,0},{1,3},{2,4},{3,7},{4,2},{5,1},{6,6},{7,5},{8,8},{9,11},{10,1... | collective-permute-start | bytes 1572872 | tf_op jit(solution)/shard_map/ppermute | solution.py:796
  197.0 55.2 %collective-permute-start.36 = (bf16[256,1024]{1,0:T(8,128)(2,1)}, bf16[256,1024]{1,0:T(8,128)(2,1)}, u32[]{:S(2)}, u32[]{:S(2)}) collective-permute-start(bf16[256,1024]{1,0:T(8,128)(2,1)} %get-tuple-element.154), channel_id=1, source_target_pairs={{0,3},{1,0},{2,7},{3,4},{4,1},{5,2},{6,5},{7,6},{8,11},{9,8},{10,1... | collective-permute-start | bytes 1572872 | tf_op jit(solution)/shard_map/ppermute | solution.py:796
  221.1 31.1 %collective-permute-start.32 = (bf16[128,1024]{1,0:T(8,128)(2,1)}, bf16[128,1024]{1,0:T(8,128)(2,1)}, u32[]{:S(2)}, u32[]{:S(2)}) collective-permute-start(bf16[128,1024]{1,0:T(8,128)(2,1)} %get-tuple-element.220), channel_id=1, source_target_pairs={{0,8},{1,9},{2,10},{3,11},{4,12},{5,13},{6,14},{7,15},{8,0},{9,1},... | collective-permute-start | bytes 786440 | tf_op jit(solution)/shard_map/ppermute | solution.py:796
  221.5 30.7 %collective-permute-start.33 = (bf16[128,1024]{1,0:T(8,128)(2,1)}, bf16[128,1024]{1,0:T(8,128)(2,1)}, u32[]{:S(2)}, u32[]{:S(2)}) collective-permute-start(bf16[128,1024]{1,0:T(8,128)(2,1)} %get-tuple-element.219), channel_id=1, source_target_pairs={{0,16},{1,17},{2,18},{3,19},{4,20},{5,21},{6,22},{7,23},{8,24},{9,... | collective-permute-start | bytes 786440 | tf_op jit(solution)/shard_map/ppermute | solution.py:796
  222.0 30.2 %collective-permute-start.34 = (bf16[128,1024]{1,0:T(8,128)(2,1)}, bf16[128,1024]{1,0:T(8,128)(2,1)}, u32[]{:S(2)}, u32[]{:S(2)}) collective-permute-start(bf16[128,1024]{1,0:T(8,128)(2,1)} %get-tuple-element.218), channel_id=1, source_target_pairs={{0,24},{1,25},{2,26},{3,27},{4,28},{5,29},{6,30},{7,31},{8,16},{9,... | collective-permute-start | bytes 786440 | tf_op jit(solution)/shard_map/ppermute | solution.py:796
  252.3 8.5 %collective-permute-start.38 = (bf16[512,2048]{1,0:T(8,128)(2,1)}, bf16[512,2048]{1,0:T(8,128)(2,1)}, u32[]{:S(2)}, u32[]{:S(2)}) collective-permute-start(bf16[512,2048]{1,0:T(8,128)(2,1)} %get-tuple-element.168), channel_id=1, source_target_pairs={{0,4},{1,5},{2,6},{3,7},{4,0},{5,1},{6,2},{7,3},{8,12},{9,13},{10,... | collective-permute-start | bytes 6291464 | tf_op jit(solution)/shard_map/ppermute | solution.py:796
  258.6 33.5 %collective-permute-start.37 = (bf16[128,1024]{1,0:T(8,128)(2,1)}, bf16[128,1024]{1,0:T(8,128)(2,1)}, u32[]{:S(2)}, u32[]{:S(2)}) collective-permute-start(bf16[128,1024]{1,0:T(8,128)(2,1)} %add_convert_fusion.3.refs_5_), channel_id=1, source_target_pairs={{0,2},{1,3},{2,0},{3,1},{4,6},{5,7},{6,4},{7,5},{8,10},{9,11},{10,... | collective-permute-start | bytes 786440 | tf_op jit(solution)/shard_map/ppermute | solution.py:796
  268.7 27.9 %collective-permute-start.39 = (bf16[256,1024]{1,0:T(8,128)(2,1)}, bf16[256,1024]{1,0:T(8,128)(2,1)}, u32[]{:S(2)}, u32[]{:S(2)}) collective-permute-start(bf16[256,1024]{1,0:T(8,128)(2,1)} %get-tuple-element.170), channel_id=1, source_target_pairs={{0,0},{1,3},{2,4},{3,7},{4,2},{5,1},{6,6},{7,5},{8,8},{9,11},{10,1... | collective-permute-start | bytes 1572872 | tf_op jit(solution)/shard_map/ppermute | solution.py:796
  271.9 24.7 %collective-permute-start.40 = (bf16[256,1024]{1,0:T(8,128)(2,1)}, bf16[256,1024]{1,0:T(8,128)(2,1)}, u32[]{:S(2)}, u32[]{:S(2)}) collective-permute-start(bf16[256,1024]{1,0:T(8,128)(2,1)} %get-tuple-element.171), channel_id=1, source_target_pairs={{0,3},{1,0},{2,7},{3,4},{4,1},{5,2},{6,5},{7,6},{8,11},{9,8},{10,1... | collective-permute-start | bytes 1572872 | tf_op jit(solution)/shard_map/ppermute | solution.py:796
  296.6 4.5 %collective-permute-start.42 = (bf16[512,2048]{1,0:T(8,128)(2,1)}, bf16[512,2048]{1,0:T(8,128)(2,1)}, u32[]{:S(2)}, u32[]{:S(2)}) collective-permute-start(bf16[512,2048]{1,0:T(8,128)(2,1)} %get-tuple-element.182), channel_id=1, source_target_pairs={{0,4},{1,5},{2,6},{3,7},{4,0},{5,1},{6,2},{7,3},{8,12},{9,13},{10,... | collective-permute-start | bytes 6291464 | tf_op jit(solution)/shard_map/ppermute | solution.py:796
  298.4 11.0 %collective-permute-start.41 = (bf16[128,1024]{1,0:T(8,128)(2,1)}, bf16[128,1024]{1,0:T(8,128)(2,1)}, u32[]{:S(2)}, u32[]{:S(2)}) collective-permute-start(bf16[128,1024]{1,0:T(8,128)(2,1)} %add_convert_fusion.2.refs_27_), channel_id=1, source_target_pairs={{0,1},{1,0},{2,3},{3,2},{4,5},{5,4},{6,7},{7,6},{8,9},{9,8},{10,11... | collective-permute-start | bytes 786440 | tf_op jit(solution)/shard_map/ppermute | solution.py:796
  310.5 8.9 %collective-permute-start.45 = (bf16[128,1024]{1,0:T(8,128)(2,1)S(1)}, bf16[128,1024]{1,0:T(8,128)(2,1)S(1)}, u32[]{:S(2)}, u32[]{:S(2)}) collective-permute-start(bf16[128,1024]{1,0:T(8,128)(2,1)S(1)} %add_convert_fusion.1), channel_id=1, source_target_pairs={{0,16},{1,17},{2,18},{3,19},{4,20},{5,21},{6,22},{7,23},{8,24},{9,... | collective-permute-start | bytes 786440 | tf_op jit(solution)/shard_map/ppermute | solution.py:796
  311.8 7.7 %collective-permute-start.46 = (bf16[128,1024]{1,0:T(8,128)(2,1)S(1)}, bf16[128,1024]{1,0:T(8,128)(2,1)S(1)}, u32[]{:S(2)}, u32[]{:S(2)}) collective-permute-start(bf16[128,1024]{1,0:T(8,128)(2,1)S(1)} %add_convert_fusion.1), channel_id=1, source_target_pairs={{0,8},{1,9},{2,10},{3,11},{4,12},{5,13},{6,14},{7,15},{8,0},{9,1},... | collective-permute-start | bytes 786440 | tf_op jit(solution)/shard_map/ppermute | solution.py:796
  311.8 13.0 %collective-permute-start.47 = (bf16[128,1024]{1,0:T(8,128)(2,1)S(1)}, bf16[128,1024]{1,0:T(8,128)(2,1)S(1)}, u32[]{:S(2)}, u32[]{:S(2)}) collective-permute-start(bf16[128,1024]{1,0:T(8,128)(2,1)S(1)} %add_convert_fusion.1), channel_id=1, source_target_pairs={{0,24},{1,25},{2,26},{3,27},{4,28},{5,29},{6,30},{7,31},{8,16},{9,... | collective-permute-start | bytes 786440 | tf_op jit(solution)/shard_map/ppermute | solution.py:796
  313.3 28.4 %collective-permute-start.43 = (bf16[256,1024]{1,0:T(8,128)(2,1)}, bf16[256,1024]{1,0:T(8,128)(2,1)S(1)}, u32[]{:S(2)}, u32[]{:S(2)}) collective-permute-start(bf16[256,1024]{1,0:T(8,128)(2,1)} %get-tuple-element.188), channel_id=1, source_target_pairs={{0,0},{1,3},{2,4},{3,7},{4,2},{5,1},{6,6},{7,5},{8,8},{9,11},{10,1... | collective-permute-start | bytes 1572872 | tf_op jit(solution)/shard_map/ppermute | solution.py:796
  317.9 23.8 %collective-permute-start.44 = (bf16[256,1024]{1,0:T(8,128)(2,1)}, bf16[256,1024]{1,0:T(8,128)(2,1)S(1)}, u32[]{:S(2)}, u32[]{:S(2)}) collective-permute-start(bf16[256,1024]{1,0:T(8,128)(2,1)} %get-tuple-element.189), channel_id=1, source_target_pairs={{0,3},{1,0},{2,7},{3,4},{4,1},{5,2},{6,5},{7,6},{8,11},{9,8},{10,1... | collective-permute-start | bytes 1572872 | tf_op jit(solution)/shard_map/ppermute | solution.py:796
  325.1 17.8 %collective-permute-start.48 = (bf16[512,1024]{1,0:T(8,128)(2,1)S(1)}, bf16[512,1024]{1,0:T(8,128)(2,1)S(1)}, u32[]{:S(2)}, u32[]{:S(2)}) collective-permute-start(bf16[512,1024]{1,0:T(8,128)(2,1)S(1)} %pad_maximum_fusion.3), channel_id=1, source_target_pairs={{0,4},{1,5},{2,6},{3,7},{4,0},{5,1},{6,2},{7,3},{8,12},{9,13},{10,... | collective-permute-start | bytes 3145736 | tf_op jit(solution)/shard_map/ppermute | solution.py:796
  (21 other events, 145.1 us)
Sparse Core Ops, SparseCore 0:
  12.4 82.1 all-gather.2
  100.8 63.6 all-gather.4

commit v6 on v5

--- a/solution.py
+++ b/solution.py
@@ -436,6 +436,27 @@
     )(pair[0], got[0], pair[1], got[1], *deps)
 
 
+def join_up(arrays, deps):
+    rows = [a.shape[0] for a in arrays]
+
+    def kernel(*refs):
+        at = 0
+        for r, n in zip(refs, rows):
+            refs[-1][at : at + n] = r[...]
+            at += n
+
+    full = pl.BlockSpec(memory_space=pltpu.VMEM)
+    return pl.pallas_call(
+        kernel,
+        in_specs=[full] * len(arrays) + [ANYWHERE] * len(deps),
+        out_specs=full,
+        out_shape=shape(sum(rows), arrays[0].shape[1], BF),
+        cost_estimate=cost(2),
+        compiler_params=params(),
+        name="join_up",
+    )(*arrays, *deps)
+
+
 def stage(expand_shard, contract_shard, deps):
     rows, cols = expand_shard.shape
     half = cols // 2
@@ -572,82 +593,56 @@
     return attend(CROSS_PLANS, info, q, kv, kv_peer, *masks, [c_out, y1, down, up, scale], outs, finish)
 
 
-def expand(info, x, first, second, block=1024):
+def feed_forward(info, x, first, second, c, base, sq, gn, up, g_out, scale, block=1024):
     T, D = x.shape
     width = first.shape[1]
     F = 2 * width
     per = width // block
-    held = Loads([first, second])
-
-    def kernel(info_ref, x_ref, *refs):
-        ins, (h_ref, g_ref, *scratch) = refs[: len(held.arrays)], refs[len(held.arrays) :]
+    A = sq.shape[1]
+    held = Loads([first, second, base, g_out, scale, sq, up, gn])
+
+    def kernel(info_ref, x_ref, c_ref, *refs):
+        ins = refs[: len(held.arrays)]
+        gp_ref, out0, out1, g3_ref, kept_ref, sent_ref, gnar_ref, acc, *scratch = refs[len(held.arrays) :]
         i = pl.program_id(0)
         bound = held.bind(info_ref, ins, scratch)
         pl.when(i == 0)(lambda: start_all(bound))
         cols = pl.ds(pl.multiple_of(lax.rem(i, per) * block, 128), block)
-        for v, (copies, buf) in enumerate(bound):
+        for v in range(2):
+            copies, buf = bound[v]
+
             @pl.when(i == v * per)
             def _():
-                for c in copies:
-                    c.wait()
+                for copy in copies:
+                    copy.wait()
 
             @pl.when(i // per == v)
             def _():
                 h, g = gelu_pair(nn(x_ref[...], buf[:, cols]))
-                h_ref[...] = h.astype(BF)
-                g_ref[...] = g.astype(BF)
-
-    out = pl.BlockSpec((T, block), lambda i, *_: (0, i))
-    return pl.pallas_call(
-        kernel,
-        grid_spec=pltpu.PrefetchScalarGridSpec(
-            num_scalar_prefetch=1,
-            grid=(F // block,),
-            in_specs=[pl.BlockSpec((T, D), lambda i, *_: (0, 0))] + held.specs,
-            out_specs=[out, out],
-            scratch_shapes=held.scratch,
-        ),
-        out_shape=[shape(T, F, BF)] * 2,
-        compiler_params=params(),
-        cost_estimate=cost(12),
-        name="expand",
-    )(info, x, *held.arrays)
-
-
-def contract(info, h, c, base, low, sq, gn, up, g_out, scale, block=2048):
-    T, D = base.shape
-    F = c.shape[0]
-    A = sq.shape[1]
-    held = Loads([base, g_out, scale, sq, up, gn, low])
-
-    def kernel(info_ref, h_ref, c_ref, *refs):
-        ins = refs[: len(held.arrays)]
-        out0, out1, g3_ref, kept_ref, sent_ref, gnar_ref, acc, *scratch = refs[len(held.arrays) :]
-        i = pl.program_id(0)
-        bound = held.bind(info_ref, ins, scratch)
-        pl.when(i == 0)(lambda: start_all(bound))
-
-        @pl.when(i == 0)
-        def _():
-            acc[...] = nn(h_ref[...], c_ref[...])
-
-        @pl.when(i > 0)
-        def _():
-            acc[...] += nn(h_ref[...], c_ref[...])
+                gp_ref[...] = g.astype(BF)
+                part = nn(h.astype(BF), c_ref[...])
+
+                @pl.when(i == 0)
+                def _():
+                    acc[...] = part
+
+                @pl.when(i > 0)
+                def _():
+                    acc[...] += part
 
         @pl.when(i == F // block - 1)
         def _():
             get = getter(bound)
-            y, inv = norm_parts(acc[...] + get(0)[...])
-            g3 = norm_back(y, inv, get(1)[...].astype(F32))
+            y, inv = norm_parts(acc[...] + get(2)[...])
+            g3 = norm_back(y, inv, get(3)[...].astype(F32))
             g3_ref[...] = g3
             acc[...] = y
             put_slots(info_ref, acc, out0, out1)
-            ga = (get(2)[0:1, 0:1] * g3).astype(BF)
-            gup = tn(get(3)[...], ga).astype(BF)
-            gnar = (get(5)[...].astype(F32) * nt(ga, get(4)[...])).astype(BF)
+            ga = (get(4)[0:1, 0:1] * g3).astype(BF)
+            gup = tn(get(5)[...], ga).astype(BF)
+            gnar = (get(7)[...].astype(F32) * nt(ga, get(6)[...])).astype(BF)
             gnar_ref[...] = gnar
-            gdown = tn(gnar, get(6)[...]).astype(BF)
+            gdown = tn(gnar, x_ref[...]).astype(BF)
             for side, keep, send in ((0, gup, gdown), (1, gdown, gup)):
                 @pl.when(info_ref[3] == side)
                 def _():
@@ -660,16 +655,17 @@
         grid_spec=pltpu.PrefetchScalarGridSpec(
             num_scalar_prefetch=1,
             grid=(F // block,),
-            in_specs=[pl.BlockSpec((T, block), lambda i, *_: (0, i)), pl.BlockSpec((block, D), lambda i, *_: (i, 0))]
+            in_specs=[pl.BlockSpec((T, D), lambda i, *_: (0, 0)), pl.BlockSpec((block, D), lambda i, *_: (i, 0))]
             + held.specs,
-            out_specs=[pl.BlockSpec(o.shape, lambda i, *_: (0, 0)) for o in outs],
+            out_specs=[pl.BlockSpec((T, block), lambda i, *_: (0, i))]
+            + [pl.BlockSpec(o.shape, lambda i, *_: (0, 0)) for o in outs],
             scratch_shapes=[pltpu.VMEM((T, D), F32)] + held.scratch,
         ),
-        out_shape=outs,
+        out_shape=[shape(T, F, BF)] + outs,
         compiler_params=params(),
-        cost_estimate=cost(14),
-        name="contract",
-    )(info, h, c, *held.arrays)
+        cost_estimate=cost(26),
+        name="feed_forward",
+    )(info, x, c, *held.arrays)
 
 
 def ffn_back(info, g3, c, first, second, gp, gnar, down, low, inv, c_out, deps, block=1024):
@@ -928,7 +924,7 @@
     n = sq.shape[0]
     h = n // 2
     pair = [rows_of(sk, sv[:h]), rows_of(sq, sv[h:])]
-    rest = rows_of(self_out, cross_key, cross_value, cross_query, cross_out)
+    rest = join_up([self_out, cross_key, cross_value, cross_query, cross_out], ())
     near = beside(pair, first_hop(pair, low), (t[0],))
     e1, e2, c_shard = stage(ex, ffn_contract, near)
     rest = lax.all_gather(rest, "dp", axis=0, tiled=True)
@@ -997,9 +993,8 @@
         for i, (own, b1, b2) in enumerate(((e1, 2, 4), (e2, 4, 2)))
     ]
     ea, eb = Pieces(n, (a3, 0, n, 0)), Pieces(n, (b3, 0, n, 0))
-    hidden, gp = expand(info, second_low, ea, eb)
-    o0, o1, g3, kept, sent, gnar = contract(
-        info, hidden, w_contract, base, second_low, squeezed, gn, adapter_up, Slots(g_out, 0, C), scale
+    gp, o0, o1, g3, kept, sent, gnar = feed_forward(
+        info, second_low, ea, eb, w_contract, base, squeezed, gn, adapter_up, Slots(g_out, 0, C), scale
     )
     output = send_back([o0, o1])
     total = Reduce(kept, sent, d, s, low)

time: 360 us -> 353 us (0.981)
  local copies, waits for them, and re-layouts: 16.4 us -> 11.6 us
    ppermute x49, waiting for transfers between devices: 59 us -> 53.8 us  [move(): return lax.ppermute(value, ('dp', 'seq'), pairs)]
    unnamed x41 -> x35, local copies, waits for them, and re-layouts: 8.84 us -> 4.96 us
  transfers between devices with their start and end apart: 51 -> 51, of which waited for: 20 -> 19; matrix products, arithmetic and copies ran while one was open for 8% -> 7% of each run, Pallas kernels for 44% -> 41%
where the time goes in v6:
time: 353 us; the launch traced here: 346 us
  Pallas kernels  169 us (48%)
  starting transfers between devices  71.7 us (20%)
  waiting for transfers between devices  56.2 us (16%)
  other arithmetic  22 us (6%)
  between operations  15.7 us (4%)
  local copies, waits for them, and re-layouts  11.6 us (3%)
    ppermute x49, starting transfers between devices, move(): return lax.ppermute(value, ('dp', 'seq'), pairs)  71.7 us
    ppermute x49, waiting for transfers between devices, move(): return lax.ppermute(value, ('dp', 'seq'), pairs)  53.8 us
    pallas_call x2, Pallas kernels, attend_back(): pl.pallas_call(kernel, grid_spec=pltpu.PrefetchScalarGridSpec(num_scalar_...  46.4 us
    pallas_call x2, Pallas kernels, attend(): pl.pallas_call(kernel, grid_spec=pltpu.PrefetchScalarGridSpec(num_scalar_...  36.8 us
    pallas_call x4, Pallas kernels, fused(): pl.pallas_call(kernel, grid_spec=pltpu.PrefetchScalarGridSpec(num_scalar_...  34.2 us
    pallas_call x1, Pallas kernels, feed_forward(): pl.pallas_call(kernel, grid_spec=pltpu.PrefetchScalarGridSpec(num_scalar_...  23.7 us
    pallas_call x1, Pallas kernels, ffn_back(): pl.pallas_call(kernel, grid_spec=pltpu.PrefetchScalarGridSpec(num_scalar_...  20 us
  transfers between devices with their start and end apart: 51, of which 19 were waited for; matrix products, arithmetic and copies ran while one was open for 7% of the time, Pallas kernels for 41%

profile of v6, /device:TPU:1, one launch (start us, length us, event | category | flops | bytes accessed | tf_op | source)
XLA Modules:
  0.0 346.3 jit_solution(10022315031502783977)
XLA Ops:
  7.2 2.4 join_up.1
  11.7 5.6 %collective-permute-start = (bf16[256,1024]{1,0:T(8,128)(2,1)S(1)}, bf16[256,1024]{1,0:T(8,128)(2,1)}, u32[]{:S(2)}, u32[]{:S(2)}) collective-permute-start(bf16[256,1024]{1,0:T(8,128)(2,1)S(1)} %get-tuple-element.224), channel_id=1, source_target_pairs={{0,0},{1,5},{2,4},{3,1},{4,2},{5,7},{6,6},{7,3},{8,8},{9,13},{10,1... | collective-permute-start | bytes 1572872 | tf_op jit(solution)/shard_map/ppermute | solution.py:792
  20.0 1.9 collective-permute-start.1
  28.1 3.9 %collective-permute-done.2.b = bf16[192,1024]{1,0:T(8,128)(2,1)} collective-permute-done((bf16[192,1024]{1,0:T(8,128)(2,1)S(1)}, bf16[192,1024]{1,0:T(8,128)(2,1)}, u32[]{:S(2)}, u32[]{:S(2)}) %collective-permute-start.2) | collective-permute-done | bytes 393248 | tf_op jit(solution)/shard_map/ppermute | solution.py:792
  32.0 2.6 collective-permute-done.3.d
  35.4 2.6 beside.1
  38.0 2.4 collective-permute-start.5
  41.1 1.5 and_convert_fusion
  42.5 1.9 collective-permute-start.7
  44.5 2.3 collective-permute-start.8
  48.4 2.9 stage.1
  51.3 9.9 %collective-permute-done.7.refs_2_.refs_0_ = bf16[256,1024]{1,0:T(8,128)(2,1)} collective-permute-done((bf16[256,1024]{1,0:T(8,128)(2,1)}, bf16[256,1024]{1,0:T(8,128)(2,1)}, u32[]{:S(2)}, u32[]{:S(2)}) %collective-permute-start.7) | collective-permute-done | bytes 524320 | tf_op jit(solution)/shard_map/ppermute | solution.py:792
  62.2 4.0 %collective-permute-done.5.refs_0_ = bf16[384,1024]{1,0:T(8,128)(2,1)} collective-permute-done((bf16[384,1024]{1,0:T(8,128)(2,1)}, bf16[384,1024]{1,0:T(8,128)(2,1)}, u32[]{:S(2)}, u32[]{:S(2)}) %collective-permute-start.5) | collective-permute-done | bytes 786464 | tf_op jit(solution)/shard_map/ppermute | solution.py:792
  68.6 2.1 collective-permute-done.10.refs_7_.refs_9_.refs_15_.refs_17_
  71.9 7.7 %qkv.1 = (bf16[512,1024]{1,0:T(8,128)(2,1)}, bf16[512,2048]{1,0:T(8,128)(2,1)}) custom-call(s32[4]{0:T(128)} %pad_add_fusion.2.refs_4_.info_ref, bf16[256,1024]{1,0:T(8,128)(2,1)} %collective-permute-done.refs_0_.refs_2_.refs_6_, bf16[256,1024]{1,0:T(8,128)(2,1)} %collective-permute-done.1.refs_3_.refs_1_.refs_7_, ...), custom_call_target="tpu_custom_call" | custom-call | flops 1800000000 | bytes 1024 | tf_op jit(solution)/shard_map/qkv/pallas_call | solution.py:493
  79.7 1.4 collective-permute-start.13
  82.2 2.0 collective-permute-done.15.kp.vp
  84.2 12.5 %attend.2 = (bf16[512,1024]{1,0:T(8,128)(2,1)}, bf16[8,2,5,256,256]{4,3,2,1,0:T(8,128)(2,1)}, f32[512,1024]{1,0:T(8,128)}) custom-call(s32[4]{0:T(128)} %pad_add_fusion.2.refs_4_.info_ref, bf16[512,1024]{1,0:T(8,128)(2,1)} %get-tuple-element.110.q_ref, bf16[512,2048]{1,0:T(8,128)(2,1)} %get-tuple-element.111.ko.vo, ...), custom_call_target="tpu_custom_call" | custom-call | flops 7500000256 | bytes 1024 | tf_op jit(solution)/shard_map/attend/pallas_call | solution.py:267
  102.4 10.2 %between.1 = (bf16[512,2048]{1,0:T(8,128)(2,1)}, f32[512,1024]{1,0:T(8,128)}, bf16[512,1024]{1,0:T(8,128)(2,1)}, f32[512,128]{1,0:T(8,128)}, bf16[512,1024]{1,0:T(8,128)(2,1)}) custom-call(s32[4]{0:T(128)} %pad_add_fusion.2.refs_4_.info_ref, bf16[256,1024]{1,0:T(8,128)(2,1)} %collective-permute-done.7.refs_2_.refs_0_, ...), custom_call_target="tpu_custom_call" | custom-call | flops 1800000000 | bytes 1024 | tf_op jit(solution)/shard_map/between/pallas_call | solution.py:493
  113.3 2.1 collective-permute-done.23.refs_7_
  115.4 4.0 %collective-permute-start.26 = (bf16[512,2048]{1,0:T(8,128)(2,1)}, bf16[512,2048]{1,0:T(8,128)(2,1)}, u32[]{:S(2)}, u32[]{:S(2)}) collective-permute-start(bf16[512,2048]{1,0:T(8,128)(2,1)} %get-tuple-element.124.ko.vo), channel_id=1, source_target_pairs={{0,4},{1,5},{2,6},{3,7},{4,0},{5,1},{6,2},{7,3},{8,12},{9,13},{10,... | collective-permute-start | bytes 6291464 | tf_op jit(solution)/shard_map/ppermute | solution.py:792
  119.9 9.3 %collective-permute-start.24 = (bf16[256,1024]{1,0:T(8,128)(2,1)}, bf16[256,1024]{1,0:T(8,128)(2,1)}, u32[]{:S(2)}, u32[]{:S(2)}) collective-permute-start(bf16[256,1024]{1,0:T(8,128)(2,1)} %get-tuple-element.121), channel_id=1, source_target_pairs={{0,0},{1,5},{2,4},{3,1},{4,2},{5,7},{6,6},{7,3},{8,8},{9,13},{10,1... | collective-permute-start | bytes 1572872 | tf_op jit(solution)/shard_map/ppermute | solution.py:792
  129.2 4.9 %collective-permute-start.25 = (bf16[256,1024]{1,0:T(8,128)(2,1)}, bf16[256,1024]{1,0:T(8,128)(2,1)}, u32[]{:S(2)}, u32[]{:S(2)}) collective-permute-start(bf16[256,1024]{1,0:T(8,128)(2,1)} %get-tuple-element.122), channel_id=1, source_target_pairs={{0,1},{1,4},{2,5},{3,0},{4,3},{5,6},{6,7},{7,2},{8,9},{9,12},{10,1... | collective-permute-start | bytes 1572872 | tf_op jit(solution)/shard_map/ppermute | solution.py:792
  134.1 24.2 %attend.3 = (bf16[512,1024]{1,0:T(8,128)(2,1)}, bf16[8,2,8,256,256]{4,3,2,1,0:T(8,128)(2,1)}, f32[512,1024]{1,0:T(8,128)}, bf16[512,1024]{1,0:T(8,128)(2,1)}, f3...) custom-call(s32[4]{0:T(128)} %pad_add_fusion.2.refs_4_.info_ref, ...), custom_call_target="tpu_custom_call" | custom-call | flops 7500000256 | bytes 1024 | tf_op jit(solution)/shard_map/attend/pallas_call | solution.py:267
  159.5 2.4 all-gather.5.cloned.1.call-done.c_ref
  163.4 23.7 %feed_forward.1 = (bf16[512,4096]{1,0:T(8,128)(2,1)}, bf16[256,1024]{1,0:T(8,128)(2,1)}, bf16[256,1024]{1,0:T(8,128)(2,1)}, f32[512,1024]{1,0:T(8,128)}, bf16[51...) custom-call(s32[4]{0:T(128)} %pad_add_fusion.2.refs_4_.info_ref, ...), custom_call_target="tpu_custom_call" | custom-call | flops 7800000000 | bytes 1024 | tf_op jit(solution)/shard_map/feed_forward/pallas_call | solution.py:653
  187.3 2.6 collective-permute-start.35
  189.9 2.5 collective-permute-start.36
  192.4 20.0 %ffn_back.1 = (f32[512,1024]{1,0:T(8,128)}, bf16[512,1024]{1,0:T(8,128)(2,1)}) custom-call(s32[4]{0:T(128)} %pad_add_fusion.2.refs_4_.info_ref, f32[512,1024]{1,0:T(8,128)} %get-tuple-element.144.g3_ref, bf16[4096,1024]{1,0:T(8,128)(2,1)} %all-gather.5.cloned.1.call-done.c_ref, bf16[512,4096]{1,0:T(8,128)(2,1)} %get-tuple-element.145.gp_ref, ...), custom_call_target="tpu_custom_call" | custom-call | flops 5400000000 | bytes 1024 | tf_op jit(solution)/shard_map/ffn_back/pallas_call | solution.py:710
  213.7 1.6 add_convert_fusion
  216.4 1.5 collective-permute-start.32
  219.1 28.2 %attend_back.2 = (bf16[512,2048]{1,0:T(8,128)(2,1)}, bf16[512,2048]{1,0:T(8,128)(2,1)}, f32[512,1024]{1,0:T(8,128)}, bf16[512,1024]{1,0:T(8,128)(2,1)}) custom-call(s32[4]{0:T(128)} %pad_add_fusion.2.refs_4_.info_ref, bf16[512,1024]{1,0:T(8,128)(2,1)} %get-tuple-element.123.q_ref, bf16[512,2048]{1,0:T(8,128)(2,1)} %get-tuple-element.124.ko.vo, ...), custom_call_target="tpu_custom_call" | custom-call | flops 7500000256 | bytes 1024 | tf_op jit(solution)/shard_map/attend_back/pallas_call | solution.py:381
  247.3 1.5 collective-permute-start.38
  248.8 2.0 add_convert_fusion.3.refs_5_
  250.8 2.0 collective-permute-start.37
  252.9 8.0 %source_grad.1 = (bf16[256,1024]{1,0:T(8,128)(2,1)}, bf16[256,1024]{1,0:T(8,128)(2,1)}) custom-call(s32[4]{0:T(128)} %pad_add_fusion.2.refs_4_.info_ref, bf16[512,2048]{1,0:T(8,128)(2,1)} %get-tuple-element.165.refs_0_, bf16[512,2048]{1,0:T(8,128)(2,1)} %collective-permute-done.38.refs_1_, ...), custom_call_target="tpu_custom_call" | custom-call | flops 1800000000 | bytes 1024 | tf_op jit(solution)/shard_map/source_grad/pallas_call | solution.py:493
  260.9 4.2 %collective-permute-start.39 = (bf16[256,1024]{1,0:T(8,128)(2,1)}, bf16[256,1024]{1,0:T(8,128)(2,1)}, u32[]{:S(2)}, u32[]{:S(2)}) collective-permute-start(bf16[256,1024]{1,0:T(8,128)(2,1)} %get-tuple-element.168), channel_id=1, source_target_pairs={{0,0},{1,3},{2,4},{3,7},{4,2},{5,1},{6,6},{7,5},{8,8},{9,11},{10,1... | collective-permute-start | bytes 1572872 | tf_op jit(solution)/shard_map/ppermute | solution.py:792
  266.2 18.2 %attend_back.3 = (bf16[512,2048]{1,0:T(8,128)(2,1)}, bf16[512,2048]{1,0:T(8,128)(2,1)}, f32[512,1024]{1,0:T(8,128)}) custom-call(s32[4]{0:T(128)} %pad_add_fusion.2.refs_4_.info_ref, bf16[512,1024]{1,0:T(8,128)(2,1)} %get-tuple-element.110.q_ref, bf16[512,2048]{1,0:T(8,128)(2,1)} %get-tuple-element.111.ko.vo, bf16[512,2048]{1,0:T(8,128)(2,1)} %get-tuple-element.111.ko.vo, ...), custom_call_target="tpu_custom_call" | custom-call | flops 7500000256 | bytes 1024 | tf_op jit(solution)/shard_map/attend_back/pallas_call | solution.py:381
  284.4 4.1 %collective-permute-done.39.refs_1_ = bf16[256,1024]{1,0:T(8,128)(2,1)} collective-permute-done((bf16[256,1024]{1,0:T(8,128)(2,1)}, bf16[256,1024]{1,0:T(8,128)(2,1)}, u32[]{:S(2)}, u32[]{:S(2)}) %collective-permute-start.39) | collective-permute-done | bytes 524320 | tf_op jit(solution)/shard_map/ppermute | solution.py:792
  288.5 1.8 add_convert_fusion.2.refs_27_
  293.0 8.3 %token_grad.1 = (bf16[256,1024]{1,0:T(8,128)(2,1)}, bf16[256,1024]{1,0:T(8,128)(2,1)}) custom-call(s32[4]{0:T(128)} %pad_add_fusion.2.refs_4_.info_ref, bf16[512,2048]{1,0:T(8,128)(2,1)} %get-tuple-element.179.refs_0_, bf16[512,2048]{1,0:T(8,128)(2,1)} %collective-permute-done.42.refs_1_, ...), custom_call_target="tpu_custom_call" | custom-call | flops 1800000000 | bytes 1024 | tf_op jit(solution)/shard_map/token_grad/pallas_call | solution.py:493
  303.6 1.5 collective-permute-start.46
  305.8 4.4 %collective-permute-start.43 = (bf16[256,1024]{1,0:T(8,128)(2,1)}, bf16[256,1024]{1,0:T(8,128)(2,1)S(1)}, u32[]{:S(2)}, u32[]{:S(2)}) collective-permute-start(bf16[256,1024]{1,0:T(8,128)(2,1)} %get-tuple-element.186), channel_id=1, source_target_pairs={{0,0},{1,3},{2,4},{3,7},{4,2},{5,1},{6,6},{7,5},{8,8},{9,11},{10,1... | collective-permute-start | bytes 1572872 | tf_op jit(solution)/shard_map/ppermute | solution.py:792
  310.3 2.0 collective-permute-start.44
  312.3 5.5 %collective-permute-done.47 = bf16[128,1024]{1,0:T(8,128)(2,1)S(1)} collective-permute-done((bf16[128,1024]{1,0:T(8,128)(2,1)S(1)}, bf16[128,1024]{1,0:T(8,128)(2,1)S(1)}, u32[]{:S(2)}, u32[]{:S(2)}) %collective-permute-start.47) | collective-permute-done | bytes 262176 | tf_op jit(solution)/shard_map/ppermute | solution.py:792
  323.6 10.5 %collective-permute-done.43 = bf16[256,1024]{1,0:T(8,128)(2,1)S(1)} collective-permute-done((bf16[256,1024]{1,0:T(8,128)(2,1)}, bf16[256,1024]{1,0:T(8,128)(2,1)S(1)}, u32[]{:S(2)}, u32[]{:S(2)}) %collective-permute-start.43) | collective-permute-done | bytes 524320 | tf_op jit(solution)/shard_map/ppermute | solution.py:792
  335.3 1.9 select_convert_fusion
  337.2 1.8 copy.76
  (156 shorter events, 46.0 us)
Async XLA Ops:
  7.2 95.3 %all-gather.3.cloned.1.call-start = ((), (), s32[]{:S(2)}) async-start(), calls=%async_computation | async-start | bytes 11796480 | tf_op jit(solution)/shard_map/all_gather | solution.py:930
  9.6 152.2 %all-gather.5.cloned.1.call-start = ((), (), s32[]{:S(2)}) async-start(), calls=%async_computation.1 | async-start | bytes 9437184 | tf_op jit(solution)/shard_map/all_gather | solution.py:975
  11.7 23.7 %collective-permute-start = (bf16[256,1024]{1,0:T(8,128)(2,1)S(1)}, bf16[256,1024]{1,0:T(8,128)(2,1)}, u32[]{:S(2)}, u32[]{:S(2)}) collective-permute-start(bf16[256,1024]{1,0:T(8,128)(2,1)S(1)} %get-tuple-element.224), channel_id=1, source_target_pairs={{0,0},{1,5},{2,4},{3,1},{4,2},{5,7},{6,6},{7,3},{8,8},{9,13},{10,1... | collective-permute-start | bytes 1572872 | tf_op jit(solution)/shard_map/ppermute | solution.py:792
  17.4 14.6 %collective-permute-start.2 = (bf16[192,1024]{1,0:T(8,128)(2,1)S(1)}, bf16[192,1024]{1,0:T(8,128)(2,1)}, u32[]{:S(2)}, u32[]{:S(2)}) collective-permute-start(bf16[192,1024]{1,0:T(8,128)(2,1)S(1)} %pad_maximum_fusion.4.a), channel_id=1, source_target_pairs={{0,8},{1,9},{2,10},{3,11},{4,12},{5,13},{6,14},{7,15},{8,0},{9,1},... | collective-permute-start | bytes 1179656 | tf_op jit(solution)/shard_map/ppermute | solution.py:792
  18.7 15.9 %collective-permute-start.3 = (bf16[192,1024]{1,0:T(8,128)(2,1)S(1)}, bf16[192,1024]{1,0:T(8,128)(2,1)S(1)}, u32[]{:S(2)}, u32[]{:S(2)}) collective-permute-start(bf16[192,1024]{1,0:T(8,128)(2,1)S(1)} %pad_maximum_fusion.5.c), channel_id=1, source_target_pairs={{0,16},{1,17},{2,18},{3,19},{4,20},{5,21},{6,22},{7,23},{8,24},{9,... | collective-permute-start | bytes 1179656 | tf_op jit(solution)/shard_map/ppermute | solution.py:792
  20.0 22.5 %collective-permute-start.1 = (bf16[256,1024]{1,0:T(8,128)(2,1)}, bf16[256,1024]{1,0:T(8,128)(2,1)}, u32[]{:S(2)}, u32[]{:S(2)}) collective-permute-start(bf16[256,1024]{1,0:T(8,128)(2,1)} %get-tuple-element.223), channel_id=1, source_target_pairs={{0,1},{1,4},{2,5},{3,0},{4,3},{5,6},{6,7},{7,2},{8,9},{9,12},{10,1... | collective-permute-start | bytes 1572872 | tf_op jit(solution)/shard_map/ppermute | solution.py:792
  22.1 4.5 %collective-permute-start.9 = (s32[2,5]{1,0:T(2,128)S(1)}, s32[2,5]{1,0:T(2,128)S(1)}, u32[]{:S(2)}, u32[]{:S(2)}) collective-permute-start(s32[2,5]{1,0:T(2,128)S(1)} %pad_add_fusion.1), channel_id=1, source_target_pairs={{0,4},{1,5},{2,6},{3,7},{4,0},{5,1},{6,2},{7,3},{8,12},{9,13},{10,... | collective-permute-start | bytes 128 | tf_op jit(solution)/shard_map/ppermute | solution.py:792
  38.0 28.1 %collective-permute-start.5 = (bf16[384,1024]{1,0:T(8,128)(2,1)}, bf16[384,1024]{1,0:T(8,128)(2,1)}, u32[]{:S(2)}, u32[]{:S(2)}) collective-permute-start(bf16[384,1024]{1,0:T(8,128)(2,1)} %get-tuple-element.98.refs_0_.refs_2_.refs_4_.refs_10_.refs_12_), channel_id=1, source_target_pairs={{0,16},{1,17},{2,18},{3,19},{4,20},{5,21},{6,22},{7,23},{8,24},{9,... | collective-permute-start | bytes 2359304 | tf_op jit(solution)/shard_map/ppermute | solution.py:792
  40.4 25.8 %collective-permute-start.6 = (bf16[384,1024]{1,0:T(8,128)(2,1)}, bf16[384,1024]{1,0:T(8,128)(2,1)}, u32[]{:S(2)}, u32[]{:S(2)}) collective-permute-start(bf16[384,1024]{1,0:T(8,128)(2,1)} %get-tuple-element.99.refs_1_.refs_18_.refs_22_.refs_26_.refs_30_.refs_0_.refs_4_), channel_id=1, source_target_pairs={{0,8},{1,9},{2,10},{3,11},{4,12},{5,13},{6,14},{7,15},{8,0},{9,1},... | collective-permute-start | bytes 2359304 | tf_op jit(solution)/shard_map/ppermute | solution.py:792
  42.5 18.6 %collective-permute-start.7 = (bf16[256,1024]{1,0:T(8,128)(2,1)}, bf16[256,1024]{1,0:T(8,128)(2,1)}, u32[]{:S(2)}, u32[]{:S(2)}) collective-permute-start(bf16[256,1024]{1,0:T(8,128)(2,1)} %get-tuple-element.100), channel_id=1, source_target_pairs={{0,0},{1,5},{2,4},{3,1},{4,2},{5,7},{6,6},{7,3},{8,8},{9,13},{10,1... | collective-permute-start | bytes 1572872 | tf_op jit(solution)/shard_map/ppermute | solution.py:792
  44.5 17.7 %collective-permute-start.8 = (bf16[256,1024]{1,0:T(8,128)(2,1)}, bf16[256,1024]{1,0:T(8,128)(2,1)}, u32[]{:S(2)}, u32[]{:S(2)}) collective-permute-start(bf16[256,1024]{1,0:T(8,128)(2,1)} %get-tuple-element.101), channel_id=1, source_target_pairs={{0,1},{1,4},{2,5},{3,0},{4,3},{5,6},{6,7},{7,2},{8,9},{9,12},{10,1... | collective-permute-start | bytes 1572872 | tf_op jit(solution)/shard_map/ppermute | solution.py:792
  48.4 20.2 %collective-permute-start.11 = (bf16[384,1024]{1,0:T(8,128)(2,1)}, bf16[384,1024]{1,0:T(8,128)(2,1)}, u32[]{:S(2)}, u32[]{:S(2)}) collective-permute-start(bf16[384,1024]{1,0:T(8,128)(2,1)} %get-tuple-element.99.refs_1_.refs_18_.refs_22_.refs_26_.refs_30_.refs_0_.refs_4_), channel_id=1, source_target_pairs={{0,4},{1,5},{2,6},{3,7},{4,0},{5,1},{6,2},{7,3},{8,12},{9,13},{10,... | collective-permute-start | bytes 2359304 | tf_op jit(solution)/shard_map/ppermute | solution.py:792
  61.2 7.4 %collective-permute-start.4 = (bf16[384,1024]{1,0:T(8,128)(2,1)}, bf16[384,1024]{1,0:T(8,128)(2,1)}, u32[]{:S(2)}, u32[]{:S(2)}) collective-permute-start(bf16[384,1024]{1,0:T(8,128)(2,1)} %get-tuple-element.98.refs_0_.refs_2_.refs_4_.refs_10_.refs_12_), channel_id=1, source_target_pairs={{0,4},{1,5},{2,6},{3,7},{4,0},{5,1},{6,2},{7,3},{8,12},{9,13},{10,... | collective-permute-start | bytes 2359304 | tf_op jit(solution)/shard_map/ppermute | solution.py:792
  68.1 3.7 %collective-permute-start.12 = (bf16[384,1024]{1,0:T(8,128)(2,1)}, bf16[384,1024]{1,0:T(8,128)(2,1)}, u32[]{:S(2)}, u32[]{:S(2)}) collective-permute-start(bf16[384,1024]{1,0:T(8,128)(2,1)} %get-tuple-element.105.refs_20_.refs_24_.refs_28_.refs_32_.refs_2_.refs_6_), channel_id=1, source_target_pairs={{0,4},{1,5},{2,6},{3,7},{4,0},{5,1},{6,2},{7,3},{8,12},{9,13},{10,... | collective-permute-start | bytes 2359304 | tf_op jit(solution)/shard_map/ppermute | solution.py:792
  79.6 4.6 %collective-permute-start.15 = (bf16[512,2048]{1,0:T(8,128)(2,1)}, bf16[512,2048]{1,0:T(8,128)(2,1)}, u32[]{:S(2)}, u32[]{:S(2)}) collective-permute-start(bf16[512,2048]{1,0:T(8,128)(2,1)} %get-tuple-element.111.ko.vo), channel_id=1, source_target_pairs={{0,4},{1,5},{2,6},{3,7},{4,0},{5,1},{6,2},{7,3},{8,12},{9,13},{10,... | collective-permute-start | bytes 6291464 | tf_op jit(solution)/shard_map/ppermute | solution.py:792
  79.7 17.0 %collective-permute-start.13 = (bf16[128,2048]{1,0:T(8,128)(2,1)}, bf16[128,2048]{1,0:T(8,128)(2,1)}, u32[]{:S(2)}, u32[]{:S(2)}) collective-permute-start(bf16[128,2048]{1,0:T(8,128)(2,1)} %get-tuple-element.108.refs_0_), channel_id=1, source_target_pairs={{0,8},{1,9},{2,10},{3,11},{4,12},{5,13},{6,14},{7,15},{8,0},{9,1},... | collective-permute-start | bytes 1572872 | tf_op jit(solution)/shard_map/ppermute | solution.py:792
  81.1 16.9 %collective-permute-start.14 = (bf16[128,2048]{1,0:T(8,128)(2,1)}, bf16[128,2048]{1,0:T(8,128)(2,1)}, u32[]{:S(2)}, u32[]{:S(2)}) collective-permute-start(bf16[128,2048]{1,0:T(8,128)(2,1)} %get-tuple-element.109.refs_8_), channel_id=1, source_target_pairs={{0,16},{1,17},{2,18},{3,19},{4,20},{5,21},{6,22},{7,23},{8,24},{9,... | collective-permute-start | bytes 1572872 | tf_op jit(solution)/shard_map/ppermute | solution.py:792
  98.8 13.8 %collective-permute-start.19 = (bf16[128,2048]{1,0:T(8,128)(2,1)}, bf16[128,2048]{1,0:T(8,128)(2,1)}, u32[]{:S(2)}, u32[]{:S(2)}) collective-permute-start(bf16[128,2048]{1,0:T(8,128)(2,1)} %get-tuple-element.109.refs_8_), channel_id=1, source_target_pairs={{0,4},{1,5},{2,6},{3,7},{4,0},{5,1},{6,2},{7,3},{8,12},{9,13},{10,... | collective-permute-start | bytes 1572872 | tf_op jit(solution)/shard_map/ppermute | solution.py:792
  98.9 14.4 %collective-permute-start.22 = (bf16[128,2048]{1,0:T(8,128)(2,1)}, bf16[128,2048]{1,0:T(8,128)(2,1)}, u32[]{:S(2)}, u32[]{:S(2)}) collective-permute-start(bf16[128,2048]{1,0:T(8,128)(2,1)} %get-tuple-element.108.refs_0_), channel_id=1, source_target_pairs={{0,16},{1,17},{2,18},{3,19},{4,20},{5,21},{6,22},{7,23},{8,24},{9,... | collective-permute-start | bytes 1572872 | tf_op jit(solution)/shard_map/ppermute | solution.py:792
  100.1 15.3 %collective-permute-start.23 = (bf16[128,2048]{1,0:T(8,128)(2,1)}, bf16[128,2048]{1,0:T(8,128)(2,1)}, u32[]{:S(2)}, u32[]{:S(2)}) collective-permute-start(bf16[128,2048]{1,0:T(8,128)(2,1)} %get-tuple-element.109.refs_8_), channel_id=1, source_target_pairs={{0,8},{1,9},{2,10},{3,11},{4,12},{5,13},{6,14},{7,15},{8,0},{9,1},... | collective-permute-start | bytes 1572872 | tf_op jit(solution)/shard_map/ppermute | solution.py:792
  100.4 15.0 %collective-permute-start.20 = (bf16[128,2048]{1,0:T(8,128)(2,1)}, bf16[128,2048]{1,0:T(8,128)(2,1)}, u32[]{:S(2)}, u32[]{:S(2)}) collective-permute-start(bf16[128,2048]{1,0:T(8,128)(2,1)} %get-tuple-element.114.refs_2_), channel_id=1, source_target_pairs={{0,4},{1,5},{2,6},{3,7},{4,0},{5,1},{6,2},{7,3},{8,12},{9,13},{10,... | collective-permute-start | bytes 1572872 | tf_op jit(solution)/shard_map/ppermute | solution.py:792
  101.4 14.0 %collective-permute-start.21 = (bf16[128,2048]{1,0:T(8,128)(2,1)}, bf16[128,2048]{1,0:T(8,128)(2,1)}, u32[]{:S(2)}, u32[]{:S(2)}) collective-permute-start(bf16[128,2048]{1,0:T(8,128)(2,1)} %get-tuple-element.115.refs_12_), channel_id=1, source_target_pairs={{0,4},{1,5},{2,6},{3,7},{4,0},{5,1},{6,2},{7,3},{8,12},{9,13},{10,... | collective-permute-start | bytes 1572872 | tf_op jit(solution)/shard_map/ppermute | solution.py:792
  115.4 18.6 %collective-permute-start.26 = (bf16[512,2048]{1,0:T(8,128)(2,1)}, bf16[512,2048]{1,0:T(8,128)(2,1)}, u32[]{:S(2)}, u32[]{:S(2)}) collective-permute-start(bf16[512,2048]{1,0:T(8,128)(2,1)} %get-tuple-element.124.ko.vo), channel_id=1, source_target_pairs={{0,4},{1,5},{2,6},{3,7},{4,0},{5,1},{6,2},{7,3},{8,12},{9,13},{10,... | collective-permute-start | bytes 6291464 | tf_op jit(solution)/shard_map/ppermute | solution.py:792
  119.5 38.9 %collective-permute-start.16 = (bf16[128,2048]{1,0:T(8,128)(2,1)}, bf16[128,2048]{1,0:T(8,128)(2,1)}, u32[]{:S(2)}, u32[]{:S(2)}) collective-permute-start(bf16[128,2048]{1,0:T(8,128)(2,1)} %get-tuple-element.114.refs_2_), channel_id=1, source_target_pairs={{0,16},{1,17},{2,18},{3,19},{4,20},{5,21},{6,22},{7,23},{8,24},{9,... | collective-permute-start | bytes 1572872 | tf_op jit(solution)/shard_map/ppermute | solution.py:792
  119.5 38.9 %collective-permute-start.17 = (bf16[128,2048]{1,0:T(8,128)(2,1)}, bf16[128,2048]{1,0:T(8,128)(2,1)}, u32[]{:S(2)}, u32[]{:S(2)}) collective-permute-start(bf16[128,2048]{1,0:T(8,128)(2,1)} %get-tuple-element.115.refs_12_), channel_id=1, source_target_pairs={{0,8},{1,9},{2,10},{3,11},{4,12},{5,13},{6,14},{7,15},{8,0},{9,1},... | collective-permute-start | bytes 1572872 | tf_op jit(solution)/shard_map/ppermute | solution.py:792
  119.9 38.4 %collective-permute-start.24 = (bf16[256,1024]{1,0:T(8,128)(2,1)}, bf16[256,1024]{1,0:T(8,128)(2,1)}, u32[]{:S(2)}, u32[]{:S(2)}) collective-permute-start(bf16[256,1024]{1,0:T(8,128)(2,1)} %get-tuple-element.121), channel_id=1, source_target_pairs={{0,0},{1,5},{2,4},{3,1},{4,2},{5,7},{6,6},{7,3},{8,8},{9,13},{10,1... | collective-permute-start | bytes 1572872 | tf_op jit(solution)/shard_map/ppermute | solution.py:792
  129.2 29.2 %collective-permute-start.25 = (bf16[256,1024]{1,0:T(8,128)(2,1)}, bf16[256,1024]{1,0:T(8,128)(2,1)}, u32[]{:S(2)}, u32[]{:S(2)}) collective-permute-start(bf16[256,1024]{1,0:T(8,128)(2,1)} %get-tuple-element.122), channel_id=1, source_target_pairs={{0,1},{1,4},{2,5},{3,0},{4,3},{5,6},{6,7},{7,2},{8,9},{9,12},{10,1... | collective-permute-start | bytes 1572872 | tf_op jit(solution)/shard_map/ppermute | solution.py:792
  158.4 3.4 collective-permute-start.27
  159.0 3.6 %collective-permute-start.29 = (bf16[128,2048]{1,0:T(8,128)(2,1)}, bf16[128,2048]{1,0:T(8,128)(2,1)}, u32[]{:S(2)}, u32[]{:S(2)}) collective-permute-start(bf16[128,2048]{1,0:T(8,128)(2,1)} %get-tuple-element.134.refs_10_), channel_id=1, source_target_pairs={{0,4},{1,5},{2,6},{3,7},{4,0},{5,1},{6,2},{7,3},{8,12},{9,13},{10,... | collective-permute-start | bytes 1572872 | tf_op jit(solution)/shard_map/ppermute | solution.py:792
  159.0 4.3 %collective-permute-start.30 = (bf16[128,2048]{1,0:T(8,128)(2,1)}, bf16[128,2048]{1,0:T(8,128)(2,1)}, u32[]{:S(2)}, u32[]{:S(2)}) collective-permute-start(bf16[128,2048]{1,0:T(8,128)(2,1)} %get-tuple-element.136.refs_14_), channel_id=1, source_target_pairs={{0,4},{1,5},{2,6},{3,7},{4,0},{5,1},{6,2},{7,3},{8,12},{9,13},{10,... | collective-permute-start | bytes 1572872 | tf_op jit(solution)/shard_map/ppermute | solution.py:792
  187.1 25.4 %collective-permute-start.31 = (bf16[512,1024]{1,0:T(8,128)(2,1)}, bf16[512,1024]{1,0:T(8,128)(2,1)}, u32[]{:S(2)}, u32[]{:S(2)}) collective-permute-start(bf16[512,1024]{1,0:T(8,128)(2,1)} %get-tuple-element.143), channel_id=1, source_target_pairs={{0,4},{1,5},{2,6},{3,7},{4,0},{5,1},{6,2},{7,3},{8,12},{9,13},{10,... | collective-permute-start | bytes 3145736 | tf_op jit(solution)/shard_map/ppermute | solution.py:792
  187.3 59.9 %collective-permute-start.35 = (bf16[256,1024]{1,0:T(8,128)(2,1)}, bf16[256,1024]{1,0:T(8,128)(2,1)}, u32[]{:S(2)}, u32[]{:S(2)}) collective-permute-start(bf16[256,1024]{1,0:T(8,128)(2,1)} %get-tuple-element.151), channel_id=1, source_target_pairs={{0,0},{1,3},{2,4},{3,7},{4,2},{5,1},{6,6},{7,5},{8,8},{9,11},{10,1... | collective-permute-start | bytes 1572872 | tf_op jit(solution)/shard_map/ppermute | solution.py:792
  189.9 57.3 %collective-permute-start.36 = (bf16[256,1024]{1,0:T(8,128)(2,1)}, bf16[256,1024]{1,0:T(8,128)(2,1)}, u32[]{:S(2)}, u32[]{:S(2)}) collective-permute-start(bf16[256,1024]{1,0:T(8,128)(2,1)} %get-tuple-element.152), channel_id=1, source_target_pairs={{0,3},{1,0},{2,7},{3,4},{4,1},{5,2},{6,5},{7,6},{8,11},{9,8},{10,1... | collective-permute-start | bytes 1572872 | tf_op jit(solution)/shard_map/ppermute | solution.py:792
  216.4 30.9 %collective-permute-start.32 = (bf16[128,1024]{1,0:T(8,128)(2,1)}, bf16[128,1024]{1,0:T(8,128)(2,1)}, u32[]{:S(2)}, u32[]{:S(2)}) collective-permute-start(bf16[128,1024]{1,0:T(8,128)(2,1)} %get-tuple-element.218), channel_id=1, source_target_pairs={{0,8},{1,9},{2,10},{3,11},{4,12},{5,13},{6,14},{7,15},{8,0},{9,1},... | collective-permute-start | bytes 786440 | tf_op jit(solution)/shard_map/ppermute | solution.py:792
  217.9 29.4 %collective-permute-start.33 = (bf16[128,1024]{1,0:T(8,128)(2,1)}, bf16[128,1024]{1,0:T(8,128)(2,1)}, u32[]{:S(2)}, u32[]{:S(2)}) collective-permute-start(bf16[128,1024]{1,0:T(8,128)(2,1)} %get-tuple-element.217), channel_id=1, source_target_pairs={{0,16},{1,17},{2,18},{3,19},{4,20},{5,21},{6,22},{7,23},{8,24},{9,... | collective-permute-start | bytes 786440 | tf_op jit(solution)/shard_map/ppermute | solution.py:792
  218.2 29.0 %collective-permute-start.34 = (bf16[128,1024]{1,0:T(8,128)(2,1)}, bf16[128,1024]{1,0:T(8,128)(2,1)}, u32[]{:S(2)}, u32[]{:S(2)}) collective-permute-start(bf16[128,1024]{1,0:T(8,128)(2,1)} %get-tuple-element.216), channel_id=1, source_target_pairs={{0,24},{1,25},{2,26},{3,27},{4,28},{5,29},{6,30},{7,31},{8,16},{9,... | collective-permute-start | bytes 786440 | tf_op jit(solution)/shard_map/ppermute | solution.py:792
  247.3 5.6 %collective-permute-start.38 = (bf16[512,2048]{1,0:T(8,128)(2,1)}, bf16[512,2048]{1,0:T(8,128)(2,1)}, u32[]{:S(2)}, u32[]{:S(2)}) collective-permute-start(bf16[512,2048]{1,0:T(8,128)(2,1)} %get-tuple-element.166), channel_id=1, source_target_pairs={{0,4},{1,5},{2,6},{3,7},{4,0},{5,1},{6,2},{7,3},{8,12},{9,13},{10,... | collective-permute-start | bytes 6291464 | tf_op jit(solution)/shard_map/ppermute | solution.py:792
  250.8 33.6 %collective-permute-start.37 = (bf16[128,1024]{1,0:T(8,128)(2,1)}, bf16[128,1024]{1,0:T(8,128)(2,1)}, u32[]{:S(2)}, u32[]{:S(2)}) collective-permute-start(bf16[128,1024]{1,0:T(8,128)(2,1)} %add_convert_fusion.3.refs_5_), channel_id=1, source_target_pairs={{0,2},{1,3},{2,0},{3,1},{4,6},{5,7},{6,4},{7,5},{8,10},{9,11},{10,... | collective-permute-start | bytes 786440 | tf_op jit(solution)/shard_map/ppermute | solution.py:792
  260.9 27.5 %collective-permute-start.39 = (bf16[256,1024]{1,0:T(8,128)(2,1)}, bf16[256,1024]{1,0:T(8,128)(2,1)}, u32[]{:S(2)}, u32[]{:S(2)}) collective-permute-start(bf16[256,1024]{1,0:T(8,128)(2,1)} %get-tuple-element.168), channel_id=1, source_target_pairs={{0,0},{1,3},{2,4},{3,7},{4,2},{5,1},{6,6},{7,5},{8,8},{9,11},{10,1... | collective-permute-start | bytes 1572872 | tf_op jit(solution)/shard_map/ppermute | solution.py:792
  265.1 23.3 %collective-permute-start.40 = (bf16[256,1024]{1,0:T(8,128)(2,1)}, bf16[256,1024]{1,0:T(8,128)(2,1)}, u32[]{:S(2)}, u32[]{:S(2)}) collective-permute-start(bf16[256,1024]{1,0:T(8,128)(2,1)} %get-tuple-element.169), channel_id=1, source_target_pairs={{0,3},{1,0},{2,7},{3,4},{4,1},{5,2},{6,5},{7,6},{8,11},{9,8},{10,1... | collective-permute-start | bytes 1572872 | tf_op jit(solution)/shard_map/ppermute | solution.py:792
  288.5 4.5 %collective-permute-start.42 = (bf16[512,2048]{1,0:T(8,128)(2,1)}, bf16[512,2048]{1,0:T(8,128)(2,1)}, u32[]{:S(2)}, u32[]{:S(2)}) collective-permute-start(bf16[512,2048]{1,0:T(8,128)(2,1)} %get-tuple-element.180), channel_id=1, source_target_pairs={{0,4},{1,5},{2,6},{3,7},{4,0},{5,1},{6,2},{7,3},{8,12},{9,13},{10,... | collective-permute-start | bytes 6291464 | tf_op jit(solution)/shard_map/ppermute | solution.py:792
  290.3 11.0 %collective-permute-start.41 = (bf16[128,1024]{1,0:T(8,128)(2,1)}, bf16[128,1024]{1,0:T(8,128)(2,1)}, u32[]{:S(2)}, u32[]{:S(2)}) collective-permute-start(bf16[128,1024]{1,0:T(8,128)(2,1)} %add_convert_fusion.2.refs_27_), channel_id=1, source_target_pairs={{0,1},{1,0},{2,3},{3,2},{4,5},{5,4},{6,7},{7,6},{8,9},{9,8},{10,11... | collective-permute-start | bytes 786440 | tf_op jit(solution)/shard_map/ppermute | solution.py:792
  302.4 9.8 %collective-permute-start.45 = (bf16[128,1024]{1,0:T(8,128)(2,1)S(1)}, bf16[128,1024]{1,0:T(8,128)(2,1)S(1)}, u32[]{:S(2)}, u32[]{:S(2)}) collective-permute-start(bf16[128,1024]{1,0:T(8,128)(2,1)S(1)} %add_convert_fusion.1), channel_id=1, source_target_pairs={{0,16},{1,17},{2,18},{3,19},{4,20},{5,21},{6,22},{7,23},{8,24},{9,... | collective-permute-start | bytes 786440 | tf_op jit(solution)/shard_map/ppermute | solution.py:792
  303.6 8.7 %collective-permute-start.46 = (bf16[128,1024]{1,0:T(8,128)(2,1)S(1)}, bf16[128,1024]{1,0:T(8,128)(2,1)S(1)}, u32[]{:S(2)}, u32[]{:S(2)}) collective-permute-start(bf16[128,1024]{1,0:T(8,128)(2,1)S(1)} %add_convert_fusion.1), channel_id=1, source_target_pairs={{0,8},{1,9},{2,10},{3,11},{4,12},{5,13},{6,14},{7,15},{8,0},{9,1},... | collective-permute-start | bytes 786440 | tf_op jit(solution)/shard_map/ppermute | solution.py:792
  305.1 12.7 %collective-permute-start.47 = (bf16[128,1024]{1,0:T(8,128)(2,1)S(1)}, bf16[128,1024]{1,0:T(8,128)(2,1)S(1)}, u32[]{:S(2)}, u32[]{:S(2)}) collective-permute-start(bf16[128,1024]{1,0:T(8,128)(2,1)S(1)} %add_convert_fusion.1), channel_id=1, source_target_pairs={{0,24},{1,25},{2,26},{3,27},{4,28},{5,29},{6,30},{7,31},{8,16},{9,... | collective-permute-start | bytes 786440 | tf_op jit(solution)/shard_map/ppermute | solution.py:792
  305.8 28.3 %collective-permute-start.43 = (bf16[256,1024]{1,0:T(8,128)(2,1)}, bf16[256,1024]{1,0:T(8,128)(2,1)S(1)}, u32[]{:S(2)}, u32[]{:S(2)}) collective-permute-start(bf16[256,1024]{1,0:T(8,128)(2,1)} %get-tuple-element.186), channel_id=1, source_target_pairs={{0,0},{1,3},{2,4},{3,7},{4,2},{5,1},{6,6},{7,5},{8,8},{9,11},{10,1... | collective-permute-start | bytes 1572872 | tf_op jit(solution)/shard_map/ppermute | solution.py:792
  310.3 23.9 %collective-permute-start.44 = (bf16[256,1024]{1,0:T(8,128)(2,1)}, bf16[256,1024]{1,0:T(8,128)(2,1)S(1)}, u32[]{:S(2)}, u32[]{:S(2)}) collective-permute-start(bf16[256,1024]{1,0:T(8,128)(2,1)} %get-tuple-element.187), channel_id=1, source_target_pairs={{0,3},{1,0},{2,7},{3,4},{4,1},{5,2},{6,5},{7,6},{8,11},{9,8},{10,1... | collective-permute-start | bytes 1572872 | tf_op jit(solution)/shard_map/ppermute | solution.py:792
  317.9 17.4 %collective-permute-start.48 = (bf16[512,1024]{1,0:T(8,128)(2,1)S(1)}, bf16[512,1024]{1,0:T(8,128)(2,1)S(1)}, u32[]{:S(2)}, u32[]{:S(2)}) collective-permute-start(bf16[512,1024]{1,0:T(8,128)(2,1)S(1)} %pad_maximum_fusion.3), channel_id=1, source_target_pairs={{0,4},{1,5},{2,6},{3,7},{4,0},{5,1},{6,2},{7,3},{8,12},{9,13},{10,... | collective-permute-start | bytes 3145736 | tf_op jit(solution)/shard_map/ppermute | solution.py:792
  (20 other events, 137.1 us)
Sparse Core Ops, SparseCore 0:
  9.9 82.0 all-gather.2
  98.2 63.6 all-gather.4

commit v7 on v6

--- a/solution.py
+++ b/solution.py
@@ -574,42 +574,45 @@
     return fused("between", info, body, [src, c_key, c_value, att, w_out, x, c_query], outs, deps=deps)
 
 
-def attend_cross(info, q, kv, kv_peer, masks, y1, c_out, down, up, scale):
+def attend_cross(info, q, kv, kv_peer, masks, y1, c_out):
     T, D = q.shape
-    A = down.shape[1]
-
-    def finish(get, att, low_ref, inv_ref, sq_ref, gn_ref, base_ref):
+
+    def finish(get, att, low_ref, inv_ref, y_ref):
         y, inv = norm_parts(get(1)[...] + nn(att[...], get(0)[...]))
         inv_ref[...] = jnp.broadcast_to(inv, inv_ref.shape)
-        low = y.astype(BF)
-        low_ref[...] = low
-        h, g = gelu_pair(nn(low, get(2)[...]))
-        hb = h.astype(BF)
-        sq_ref[...] = hb
-        gn_ref[...] = g.astype(BF)
-        base_ref[...] = y + get(4)[0:1, 0:1] * nn(hb, get(3)[...])
-
-    outs = [shape(T, D, BF), shape(T, 128, F32), shape(T, A, BF), shape(T, A, BF), shape(T, D, F32)]
-    return attend(CROSS_PLANS, info, q, kv, kv_peer, *masks, [c_out, y1, down, up, scale], outs, finish)
-
-
-def feed_forward(info, x, first, second, c, base, sq, gn, up, g_out, scale, block=1024):
+        low_ref[...] = y.astype(BF)
+        y_ref[...] = y
+
+    outs = [shape(T, D, BF), shape(T, 128, F32), shape(T, D, F32)]
+    return attend(CROSS_PLANS, info, q, kv, kv_peer, *masks, [c_out, y1], outs, finish)
+
+
+def feed_forward(info, x, first, second, c, y2, down, up, g_out, scale, block=1024):
     T, D = x.shape
     width = first.shape[1]
     F = 2 * width
     per = width // block
-    A = sq.shape[1]
-    held = Loads([first, second, base, g_out, scale, sq, up, gn])
+    A = down.shape[1]
+    held = Loads([down, up, scale, first, second, y2, g_out])
 
     def kernel(info_ref, x_ref, c_ref, *refs):
         ins = refs[: len(held.arrays)]
-        gp_ref, out0, out1, g3_ref, kept_ref, sent_ref, gnar_ref, acc, *scratch = refs[len(held.arrays) :]
+        gp_ref, out0, out1, g3_ref, kept_ref, sent_ref, gnar_ref, acc, sq, gn, *scratch = refs[len(held.arrays) :]
         i = pl.program_id(0)
         bound = held.bind(info_ref, ins, scratch)
         pl.when(i == 0)(lambda: start_all(bound))
         cols = pl.ds(pl.multiple_of(lax.rem(i, per) * block, 128), block)
+
+        @pl.when(i == 0)
+        def _():
+            get = getter(bound)
+            h, g = gelu_pair(nn(x_ref[...], get(0)[...]))
+            sq[...] = h.astype(BF)
+            gn[...] = g.astype(BF)
+            acc[...] = get(2)[0:1, 0:1] * nn(sq[...], get(1)[...])
+
         for v in range(2):
-            copies, buf = bound[v]
+            copies, buf = bound[3 + v]
 
             @pl.when(i == v * per)
             def _():
@@ -620,29 +623,22 @@
             def _():
                 h, g = gelu_pair(nn(x_ref[...], buf[:, cols]))
                 gp_ref[...] = g.astype(BF)
-                part = nn(h.astype(BF), c_ref[...])
-
-                @pl.when(i == 0)
-                def _():
-                    acc[...] = part
-
-                @pl.when(i > 0)
-                def _():
-                    acc[...] += part
+                acc[...] += nn(h.astype(BF), c_ref[...])
 
         @pl.when(i == F // block - 1)
         def _():
-            get = getter(bound)
-            y, inv = norm_parts(acc[...] + get(2)[...])
-            g3 = norm_back(y, inv, get(3)[...].astype(F32))
+            get = getter(bound[5:])
+            y, inv = norm_parts(acc[...] + get(0)[...])
+            g3 = norm_back(y, inv, get(1)[...].astype(F32))
             g3_ref[...] = g3
             acc[...] = y
             put_slots(info_ref, acc, out0, out1)
-            ga = (get(4)[0:1, 0:1] * g3).astype(BF)
-            gup = tn(get(5)[...], ga).astype(BF)
-            gnar = (get(7)[...].astype(F32) * nt(ga, get(6)[...])).astype(BF)
+            ga = (bound[2][1][0:1, 0:1] * g3).astype(BF)
+            gup = tn(sq[...], ga).astype(BF)
+            gnar = (gn[...].astype(F32) * nt(ga, bound[1][1][...])).astype(BF)
             gnar_ref[...] = gnar
-            gdown = tn(gnar, x_ref[...]).astype(BF)
+            gdown = tn(x_ref[...], gnar).astype(BF)
+            gdown = jnp.concatenate([gdown[k : k + A] for k in range(0, D, A)], axis=1)
             for side, keep, send in ((0, gup, gdown), (1, gdown, gup)):
                 @pl.when(info_ref[3] == side)
                 def _():
@@ -659,7 +655,7 @@
             + held.specs,
             out_specs=[pl.BlockSpec((T, block), lambda i, *_: (0, i))]
             + [pl.BlockSpec(o.shape, lambda i, *_: (0, 0)) for o in outs],
-            scratch_shapes=[pltpu.VMEM((T, D), F32)] + held.scratch,
+            scratch_shapes=[pltpu.VMEM((T, D), F32)] + [pltpu.VMEM((T, A), BF)] * 2 + held.scratch,
         ),
         out_shape=[shape(T, F, BF)] + outs,
         compiler_params=params(),
@@ -980,8 +976,8 @@
     second3, pieces = [h0, h1], [g0, g1]
     g_out = send_pieces(pieces)
     skv_peer = flip(skv, 1)
-    cross_attended, p_cross, r_cross, second_low, inv2, squeezed, gn, base = attend_cross(
-        info, cq, skv, skv_peer, (cq_aug, *ck_aug), y1, c_out, adapter_down, adapter_up, scale
+    cross_attended, p_cross, r_cross, second_low, inv2, y2 = attend_cross(
+        info, cq, skv, skv_peer, (cq_aug, *ck_aug), y1, c_out
     )
     f0, f1, h0, h1, g0, g1, second_low = barrier(*far3, *second3, *g_out, second_low)
     far3, second3, g_out = [f0, f1], [h0, h1], [g0, g1]
@@ -994,7 +990,7 @@
     ]
     ea, eb = Pieces(n, (a3, 0, n, 0)), Pieces(n, (b3, 0, n, 0))
     gp, o0, o1, g3, kept, sent, gnar = feed_forward(
-        info, second_low, ea, eb, w_contract, base, squeezed, gn, adapter_up, Slots(g_out, 0, C), scale
+        info, second_low, ea, eb, w_contract, y2, adapter_down, adapter_up, Slots(g_out, 0, C), scale
     )
     output = send_back([o0, o1])
     total = Reduce(kept, sent, d, s, low)
@@ -1030,7 +1026,9 @@
     grads, other = total.value, flip(total.value, low)
     high = (d // low) % 2 == 1
     grad_up = pick(high, other, grads).astype(F32)
-    grad_down = pick(high, grads, other).astype(F32).T
+    A = adapter_down.shape[1]
+    grad_down = pick(high, grads, other).astype(F32)
+    grad_down = rows_of(*[grad_down[:, k : k + A] for k in range(0, D, A)])
     output, grad_source, grad_tokens = [join_rows(v, s) for v in (output, [s0, s1], tokens_back)]
     return (output, grad_tokens, grad_source, grad_down, grad_up)
 

time: 353 us -> 350 us (level)
  Pallas kernels: 169 us -> 165 us
  transfers between devices with their start and end apart: 51 -> 51, of which waited for: 19 -> 17; matrix products, arithmetic and copies ran while one was open for 7% -> 7% of each run, Pallas kernels for 41% -> 41%
where the time goes in v7:
time: 350 us; the launch traced here: 344 us
  Pallas kernels  165 us (47%)
  starting transfers between devices  70.3 us (20%)
  waiting for transfers between devices  58.1 us (17%)
  other arithmetic  23.5 us (7%)
  between operations  15.7 us (4%)
  local copies, waits for them, and re-layouts  10.8 us (3%)
    ppermute x49, starting transfers between devices, move(): return lax.ppermute(value, ('dp', 'seq'), pairs)  70.3 us
    ppermute x49, waiting for transfers between devices, move(): return lax.ppermute(value, ('dp', 'seq'), pairs)  53.8 us
    pallas_call x2, Pallas kernels, attend_back(): pl.pallas_call(kernel, grid_spec=pltpu.PrefetchScalarGridSpec(num_scalar_...  46.4 us
    pallas_call x4, Pallas kernels, fused(): pl.pallas_call(kernel, grid_spec=pltpu.PrefetchScalarGridSpec(num_scalar_...  34.2 us
    pallas_call x2, Pallas kernels, attend(): pl.pallas_call(kernel, grid_spec=pltpu.PrefetchScalarGridSpec(num_scalar_...  34.1 us
    pallas_call x1, Pallas kernels, feed_forward(): pl.pallas_call(kernel, grid_spec=pltpu.PrefetchScalarGridSpec(num_scalar_...  22.8 us
    pallas_call x1, Pallas kernels, ffn_back(): pl.pallas_call(kernel, grid_spec=pltpu.PrefetchScalarGridSpec(num_scalar_...  20 us
  transfers between devices with their start and end apart: 51, of which 17 were waited for; matrix products, arithmetic and copies ran while one was open for 7% of the time, Pallas kernels for 41%

profile of v7, /device:TPU:1, one launch (start us, length us, event | category | flops | bytes accessed | tf_op | source)
XLA Modules:
  0.0 343.7 jit_solution(7754220875584300804)
XLA Ops:
  7.2 2.4 join_up.1
  11.7 5.6 %collective-permute-start = (bf16[256,1024]{1,0:T(8,128)(2,1)S(1)}, bf16[256,1024]{1,0:T(8,128)(2,1)}, u32[]{:S(2)}, u32[]{:S(2)}) collective-permute-start(bf16[256,1024]{1,0:T(8,128)(2,1)S(1)} %get-tuple-element.212), channel_id=1, source_target_pairs={{0,0},{1,5},{2,4},{3,1},{4,2},{5,7},{6,6},{7,3},{8,8},{9,13},{10,1... | collective-permute-start | bytes 1572872 | tf_op jit(solution)/shard_map/ppermute | solution.py:788
  20.0 1.9 collective-permute-start.1
  28.2 3.8 %collective-permute-done.2.b = bf16[192,1024]{1,0:T(8,128)(2,1)} collective-permute-done((bf16[192,1024]{1,0:T(8,128)(2,1)S(1)}, bf16[192,1024]{1,0:T(8,128)(2,1)}, u32[]{:S(2)}, u32[]{:S(2)}) %collective-permute-start.2) | collective-permute-done | bytes 393248 | tf_op jit(solution)/shard_map/ppermute | solution.py:788
  32.0 2.6 collective-permute-done.3.d
  35.4 2.6 beside.1
  38.0 2.4 collective-permute-start.5
  41.0 1.5 and_convert_fusion
  42.6 1.9 collective-permute-start.7
  44.5 2.3 collective-permute-start.8
  48.5 2.9 stage.1
  51.4 9.8 %collective-permute-done.7.refs_2_.refs_0_ = bf16[256,1024]{1,0:T(8,128)(2,1)} collective-permute-done((bf16[256,1024]{1,0:T(8,128)(2,1)}, bf16[256,1024]{1,0:T(8,128)(2,1)}, u32[]{:S(2)}, u32[]{:S(2)}) %collective-permute-start.7) | collective-permute-done | bytes 524320 | tf_op jit(solution)/shard_map/ppermute | solution.py:788
  62.2 4.0 %collective-permute-done.5.refs_0_ = bf16[384,1024]{1,0:T(8,128)(2,1)} collective-permute-done((bf16[384,1024]{1,0:T(8,128)(2,1)}, bf16[384,1024]{1,0:T(8,128)(2,1)}, u32[]{:S(2)}, u32[]{:S(2)}) %collective-permute-start.5) | collective-permute-done | bytes 786464 | tf_op jit(solution)/shard_map/ppermute | solution.py:788
  68.6 2.1 collective-permute-done.10.refs_7_.refs_9_.refs_15_.refs_17_
  71.8 7.7 %qkv.1 = (bf16[512,1024]{1,0:T(8,128)(2,1)}, bf16[512,2048]{1,0:T(8,128)(2,1)}) custom-call(s32[4]{0:T(128)} %pad_add_fusion.2.refs_4_.info_ref, bf16[256,1024]{1,0:T(8,128)(2,1)} %collective-permute-done.refs_0_.refs_2_.refs_6_, bf16[256,1024]{1,0:T(8,128)(2,1)} %collective-permute-done.1.refs_3_.refs_1_.refs_7_, ...), custom_call_target="tpu_custom_call" | custom-call | flops 1800000000 | bytes 1024 | tf_op jit(solution)/shard_map/qkv/pallas_call | solution.py:493
  79.6 1.5 collective-permute-start.13
  82.2 1.9 collective-permute-done.15.kp.vp
  84.1 12.5 %attend.2 = (bf16[512,1024]{1,0:T(8,128)(2,1)}, bf16[8,2,5,256,256]{4,3,2,1,0:T(8,128)(2,1)}, f32[512,1024]{1,0:T(8,128)}) custom-call(s32[4]{0:T(128)} %pad_add_fusion.2.refs_4_.info_ref, bf16[512,1024]{1,0:T(8,128)(2,1)} %get-tuple-element.108.q_ref, bf16[512,2048]{1,0:T(8,128)(2,1)} %get-tuple-element.109.ko.vo, ...), custom_call_target="tpu_custom_call" | custom-call | flops 7500000256 | bytes 1024 | tf_op jit(solution)/shard_map/attend/pallas_call | solution.py:267
  96.6 1.4 collective-permute-done.14.refs_1_
  102.4 10.2 %between.1 = (bf16[512,2048]{1,0:T(8,128)(2,1)}, f32[512,1024]{1,0:T(8,128)}, bf16[512,1024]{1,0:T(8,128)(2,1)}, f32[512,128]{1,0:T(8,128)}, bf16[512,1024]{1,0:T(8,128)(2,1)}) custom-call(s32[4]{0:T(128)} %pad_add_fusion.2.refs_4_.info_ref, bf16[256,1024]{1,0:T(8,128)(2,1)} %collective-permute-done.7.refs_2_.refs_0_, ...), custom_call_target="tpu_custom_call" | custom-call | flops 1800000000 | bytes 1024 | tf_op jit(solution)/shard_map/between/pallas_call | solution.py:493
  113.3 2.1 collective-permute-done.23.refs_7_
  115.4 4.0 %collective-permute-start.26 = (bf16[512,2048]{1,0:T(8,128)(2,1)}, bf16[512,2048]{1,0:T(8,128)(2,1)}, u32[]{:S(2)}, u32[]{:S(2)}) collective-permute-start(bf16[512,2048]{1,0:T(8,128)(2,1)} %get-tuple-element.122.ko.vo), channel_id=1, source_target_pairs={{0,4},{1,5},{2,6},{3,7},{4,0},{5,1},{6,2},{7,3},{8,12},{9,13},{10,... | collective-permute-start | bytes 6291464 | tf_op jit(solution)/shard_map/ppermute | solution.py:788
  119.9 9.3 %collective-permute-start.24 = (bf16[256,1024]{1,0:T(8,128)(2,1)}, bf16[256,1024]{1,0:T(8,128)(2,1)}, u32[]{:S(2)}, u32[]{:S(2)}) collective-permute-start(bf16[256,1024]{1,0:T(8,128)(2,1)} %get-tuple-element.119), channel_id=1, source_target_pairs={{0,0},{1,5},{2,4},{3,1},{4,2},{5,7},{6,6},{7,3},{8,8},{9,13},{10,1... | collective-permute-start | bytes 1572872 | tf_op jit(solution)/shard_map/ppermute | solution.py:788
  129.2 4.9 %collective-permute-start.25 = (bf16[256,1024]{1,0:T(8,128)(2,1)}, bf16[256,1024]{1,0:T(8,128)(2,1)}, u32[]{:S(2)}, u32[]{:S(2)}) collective-permute-start(bf16[256,1024]{1,0:T(8,128)(2,1)} %get-tuple-element.120), channel_id=1, source_target_pairs={{0,1},{1,4},{2,5},{3,0},{4,3},{5,6},{6,7},{7,2},{8,9},{9,12},{10,1... | collective-permute-start | bytes 1572872 | tf_op jit(solution)/shard_map/ppermute | solution.py:788
  134.1 21.6 %attend.3 = (bf16[512,1024]{1,0:T(8,128)(2,1)}, bf16[8,2,8,256,256]{4,3,2,1,0:T(8,128)(2,1)}, f32[512,1024]{1,0:T(8,128)}, bf16[512,1024]{1,0:T(8,128)(2,1)}, f32[512,128]{1,0:T(8,128)}, /*index=5*/f32[512,1024]{1,0:T(8,128)}) custom-call(s32[4]{0:T(128)} %pad_add_fusion.2.refs_4_.info_ref, bf16[512,1024]{1,0:T(8,128)(2,1)} %get-tuple-element.121.q_ref, ...), custom_call_target="tpu_custom_call" | custom-call | flops 7500000256 | bytes 1024 | tf_op jit(solution)/shard_map/attend/pallas_call | solution.py:267
  156.8 4.2 %all-gather.5.cloned.1.call-done.c_ref = bf16[4096,1024]{1,0:T(8,128)(2,1)} async-done(((bf16[512,1024]{1,0:T(8,128)(2,1)}), bf16[4096,1024]{1,0:T(8,128)(2,1)}) %all-gather.5.cloned.1.call-update) | async-done | bytes 8388624 | tf_op jit(solution)/shard_map/all_gather | solution.py:971
  161.0 22.8 %feed_forward.1 = (bf16[512,4096]{1,0:T(8,128)(2,1)}, bf16[256,1024]{1,0:T(8,128)(2,1)}, bf16[256,1024]{1,0:T(8,128)(2,1)}, f32[512,1024]{1,0:T(8,128)}, bf16[51...) custom-call(s32[4]{0:T(128)} %pad_add_fusion.2.refs_4_.info_ref, ...), custom_call_target="tpu_custom_call" | custom-call | flops 7800000000 | bytes 1024 | tf_op jit(solution)/shard_map/feed_forward/pallas_call | solution.py:649
  184.1 4.8 %collective-permute-start.35 = (bf16[256,1024]{1,0:T(8,128)(2,1)}, bf16[256,1024]{1,0:T(8,128)(2,1)}, u32[]{:S(2)}, u32[]{:S(2)}) collective-permute-start(bf16[256,1024]{1,0:T(8,128)(2,1)} %get-tuple-element.147), channel_id=1, source_target_pairs={{0,0},{1,3},{2,4},{3,7},{4,2},{5,1},{6,6},{7,5},{8,8},{9,11},{10,1... | collective-permute-start | bytes 1572872 | tf_op jit(solution)/shard_map/ppermute | solution.py:788
  188.9 2.5 collective-permute-start.36
  191.4 20.0 %ffn_back.1 = (f32[512,1024]{1,0:T(8,128)}, bf16[512,1024]{1,0:T(8,128)(2,1)}) custom-call(s32[4]{0:T(128)} %pad_add_fusion.2.refs_4_.info_ref, f32[512,1024]{1,0:T(8,128)} %get-tuple-element.140.g3_ref, bf16[4096,1024]{1,0:T(8,128)(2,1)} %all-gather.5.cloned.1.call-done.c_ref, bf16[512,4096]{1,0:T(8,128)(2,1)} %get-tuple-element.141.gp_ref, ...), custom_call_target="tpu_custom_call" | custom-call | flops 5400000000 | bytes 1024 | tf_op jit(solution)/shard_map/ffn_back/pallas_call | solution.py:706
  212.7 1.6 add_convert_fusion
  215.4 1.4 collective-permute-start.32
  218.0 28.2 %attend_back.2 = (bf16[512,2048]{1,0:T(8,128)(2,1)}, bf16[512,2048]{1,0:T(8,128)(2,1)}, f32[512,1024]{1,0:T(8,128)}, bf16[512,1024]{1,0:T(8,128)(2,1)}) custom-call(s32[4]{0:T(128)} %pad_add_fusion.2.refs_4_.info_ref, bf16[512,1024]{1,0:T(8,128)(2,1)} %get-tuple-element.121.q_ref, bf16[512,2048]{1,0:T(8,128)(2,1)} %get-tuple-element.122.ko.vo, ...), custom_call_target="tpu_custom_call" | custom-call | flops 7500000256 | bytes 1024 | tf_op jit(solution)/shard_map/attend_back/pallas_call | solution.py:381
  247.2 2.0 add_convert_fusion.3.refs_5_
  249.2 2.6 collective-permute-start.37
  251.8 8.0 %source_grad.1 = (bf16[256,1024]{1,0:T(8,128)(2,1)}, bf16[256,1024]{1,0:T(8,128)(2,1)}) custom-call(s32[4]{0:T(128)} %pad_add_fusion.2.refs_4_.info_ref, bf16[512,2048]{1,0:T(8,128)(2,1)} %get-tuple-element.161.refs_0_, bf16[512,2048]{1,0:T(8,128)(2,1)} %collective-permute-done.38.refs_1_, ...), custom_call_target="tpu_custom_call" | custom-call | flops 1800000000 | bytes 1024 | tf_op jit(solution)/shard_map/source_grad/pallas_call | solution.py:493
  259.8 4.3 %collective-permute-start.39 = (bf16[256,1024]{1,0:T(8,128)(2,1)}, bf16[256,1024]{1,0:T(8,128)(2,1)}, u32[]{:S(2)}, u32[]{:S(2)}) collective-permute-start(bf16[256,1024]{1,0:T(8,128)(2,1)} %get-tuple-element.164), channel_id=1, source_target_pairs={{0,0},{1,3},{2,4},{3,7},{4,2},{5,1},{6,6},{7,5},{8,8},{9,11},{10,1... | collective-permute-start | bytes 1572872 | tf_op jit(solution)/shard_map/ppermute | solution.py:788
  264.2 18.2 %attend_back.3 = (bf16[512,2048]{1,0:T(8,128)(2,1)}, bf16[512,2048]{1,0:T(8,128)(2,1)}, f32[512,1024]{1,0:T(8,128)}) custom-call(s32[4]{0:T(128)} %pad_add_fusion.2.refs_4_.info_ref, bf16[512,1024]{1,0:T(8,128)(2,1)} %get-tuple-element.108.q_ref, bf16[512,2048]{1,0:T(8,128)(2,1)} %get-tuple-element.109.ko.vo, bf16[512,2048]{1,0:T(8,128)(2,1)} %get-tuple-element.109.ko.vo, ...), custom_call_target="tpu_custom_call" | custom-call | flops 7500000256 | bytes 1024 | tf_op jit(solution)/shard_map/attend_back/pallas_call | solution.py:381
  282.4 4.9 %collective-permute-done.39.refs_1_ = bf16[256,1024]{1,0:T(8,128)(2,1)} collective-permute-done((bf16[256,1024]{1,0:T(8,128)(2,1)}, bf16[256,1024]{1,0:T(8,128)(2,1)}, u32[]{:S(2)}, u32[]{:S(2)}) %collective-permute-start.39) | collective-permute-done | bytes 524320 | tf_op jit(solution)/shard_map/ppermute | solution.py:788
  287.2 1.8 add_convert_fusion.2.refs_27_
  289.4 2.3 collective-permute-done.42.refs_1_
  291.7 8.3 %token_grad.1 = (bf16[256,1024]{1,0:T(8,128)(2,1)}, bf16[256,1024]{1,0:T(8,128)(2,1)}) custom-call(s32[4]{0:T(128)} %pad_add_fusion.2.refs_4_.info_ref, bf16[512,2048]{1,0:T(8,128)(2,1)} %get-tuple-element.175.refs_0_, bf16[512,2048]{1,0:T(8,128)(2,1)} %collective-permute-done.42.refs_1_, ...), custom_call_target="tpu_custom_call" | custom-call | flops 1800000000 | bytes 1024 | tf_op jit(solution)/shard_map/token_grad/pallas_call | solution.py:493
  302.3 1.5 collective-permute-start.46
  303.9 4.8 %collective-permute-start.43 = (bf16[256,1024]{1,0:T(8,128)(2,1)}, bf16[256,1024]{1,0:T(8,128)(2,1)S(1)}, u32[]{:S(2)}, u32[]{:S(2)}) collective-permute-start(bf16[256,1024]{1,0:T(8,128)(2,1)} %get-tuple-element.182), channel_id=1, source_target_pairs={{0,0},{1,3},{2,4},{3,7},{4,2},{5,1},{6,6},{7,5},{8,8},{9,11},{10,1... | collective-permute-start | bytes 1572872 | tf_op jit(solution)/shard_map/ppermute | solution.py:788
  309.9 5.6 %collective-permute-done.47 = bf16[128,1024]{1,0:T(8,128)(2,1)S(1)} collective-permute-done((bf16[128,1024]{1,0:T(8,128)(2,1)S(1)}, bf16[128,1024]{1,0:T(8,128)(2,1)S(1)}, u32[]{:S(2)}, u32[]{:S(2)}) %collective-permute-start.47) | collective-permute-done | bytes 262176 | tf_op jit(solution)/shard_map/ppermute | solution.py:788
  321.7 10.1 %collective-permute-done.43 = bf16[256,1024]{1,0:T(8,128)(2,1)S(1)} collective-permute-done((bf16[256,1024]{1,0:T(8,128)(2,1)}, bf16[256,1024]{1,0:T(8,128)(2,1)S(1)}, u32[]{:S(2)}, u32[]{:S(2)}) %collective-permute-start.43) | collective-permute-done | bytes 524320 | tf_op jit(solution)/shard_map/ppermute | solution.py:788
  333.0 1.7 select_convert_fusion
  335.0 1.5 pad_maximum_fusion
  (157 shorter events, 41.9 us)
Async XLA Ops:
  7.2 95.3 %all-gather.3.cloned.1.call-start = ((), (), s32[]{:S(2)}) async-start(), calls=%async_computation | async-start | bytes 11796480 | tf_op jit(solution)/shard_map/all_gather | solution.py:926
  9.6 151.4 %all-gather.5.cloned.1.call-start = ((), (), s32[]{:S(2)}) async-start(), calls=%async_computation.1 | async-start | bytes 9437184 | tf_op jit(solution)/shard_map/all_gather | solution.py:971
  11.7 23.7 %collective-permute-start = (bf16[256,1024]{1,0:T(8,128)(2,1)S(1)}, bf16[256,1024]{1,0:T(8,128)(2,1)}, u32[]{:S(2)}, u32[]{:S(2)}) collective-permute-start(bf16[256,1024]{1,0:T(8,128)(2,1)S(1)} %get-tuple-element.212), channel_id=1, source_target_pairs={{0,0},{1,5},{2,4},{3,1},{4,2},{5,7},{6,6},{7,3},{8,8},{9,13},{10,1... | collective-permute-start | bytes 1572872 | tf_op jit(solution)/shard_map/ppermute | solution.py:788
  17.4 14.6 %collective-permute-start.2 = (bf16[192,1024]{1,0:T(8,128)(2,1)S(1)}, bf16[192,1024]{1,0:T(8,128)(2,1)}, u32[]{:S(2)}, u32[]{:S(2)}) collective-permute-start(bf16[192,1024]{1,0:T(8,128)(2,1)S(1)} %pad_maximum_fusion.5.a), channel_id=1, source_target_pairs={{0,8},{1,9},{2,10},{3,11},{4,12},{5,13},{6,14},{7,15},{8,0},{9,1},... | collective-permute-start | bytes 1179656 | tf_op jit(solution)/shard_map/ppermute | solution.py:788
  18.7 15.9 %collective-permute-start.3 = (bf16[192,1024]{1,0:T(8,128)(2,1)S(1)}, bf16[192,1024]{1,0:T(8,128)(2,1)S(1)}, u32[]{:S(2)}, u32[]{:S(2)}) collective-permute-start(bf16[192,1024]{1,0:T(8,128)(2,1)S(1)} %pad_maximum_fusion.6.c), channel_id=1, source_target_pairs={{0,16},{1,17},{2,18},{3,19},{4,20},{5,21},{6,22},{7,23},{8,24},{9,... | collective-permute-start | bytes 1179656 | tf_op jit(solution)/shard_map/ppermute | solution.py:788
  20.0 22.6 %collective-permute-start.1 = (bf16[256,1024]{1,0:T(8,128)(2,1)}, bf16[256,1024]{1,0:T(8,128)(2,1)}, u32[]{:S(2)}, u32[]{:S(2)}) collective-permute-start(bf16[256,1024]{1,0:T(8,128)(2,1)} %get-tuple-element.211), channel_id=1, source_target_pairs={{0,1},{1,4},{2,5},{3,0},{4,3},{5,6},{6,7},{7,2},{8,9},{9,12},{10,1... | collective-permute-start | bytes 1572872 | tf_op jit(solution)/shard_map/ppermute | solution.py:788
  22.1 4.5 %collective-permute-start.9 = (s32[2,5]{1,0:T(2,128)S(1)}, s32[2,5]{1,0:T(2,128)S(1)}, u32[]{:S(2)}, u32[]{:S(2)}) collective-permute-start(s32[2,5]{1,0:T(2,128)S(1)} %pad_add_fusion.1), channel_id=1, source_target_pairs={{0,4},{1,5},{2,6},{3,7},{4,0},{5,1},{6,2},{7,3},{8,12},{9,13},{10,... | collective-permute-start | bytes 128 | tf_op jit(solution)/shard_map/ppermute | solution.py:788
  38.0 28.1 %collective-permute-start.5 = (bf16[384,1024]{1,0:T(8,128)(2,1)}, bf16[384,1024]{1,0:T(8,128)(2,1)}, u32[]{:S(2)}, u32[]{:S(2)}) collective-permute-start(bf16[384,1024]{1,0:T(8,128)(2,1)} %get-tuple-element.96.refs_0_.refs_2_.refs_4_.refs_10_.refs_12_), channel_id=1, source_target_pairs={{0,16},{1,17},{2,18},{3,19},{4,20},{5,21},{6,22},{7,23},{8,24},{9,... | collective-permute-start | bytes 2359304 | tf_op jit(solution)/shard_map/ppermute | solution.py:788
  40.4 25.8 %collective-permute-start.6 = (bf16[384,1024]{1,0:T(8,128)(2,1)}, bf16[384,1024]{1,0:T(8,128)(2,1)}, u32[]{:S(2)}, u32[]{:S(2)}) collective-permute-start(bf16[384,1024]{1,0:T(8,128)(2,1)} %get-tuple-element.97.refs_1_.refs_18_.refs_22_.refs_26_.refs_30_.refs_0_.refs_4_), channel_id=1, source_target_pairs={{0,8},{1,9},{2,10},{3,11},{4,12},{5,13},{6,14},{7,15},{8,0},{9,1},... | collective-permute-start | bytes 2359304 | tf_op jit(solution)/shard_map/ppermute | solution.py:788
  42.6 18.6 %collective-permute-start.7 = (bf16[256,1024]{1,0:T(8,128)(2,1)}, bf16[256,1024]{1,0:T(8,128)(2,1)}, u32[]{:S(2)}, u32[]{:S(2)}) collective-permute-start(bf16[256,1024]{1,0:T(8,128)(2,1)} %get-tuple-element.98), channel_id=1, source_target_pairs={{0,0},{1,5},{2,4},{3,1},{4,2},{5,7},{6,6},{7,3},{8,8},{9,13},{10,1... | collective-permute-start | bytes 1572872 | tf_op jit(solution)/shard_map/ppermute | solution.py:788
  44.5 17.7 %collective-permute-start.8 = (bf16[256,1024]{1,0:T(8,128)(2,1)}, bf16[256,1024]{1,0:T(8,128)(2,1)}, u32[]{:S(2)}, u32[]{:S(2)}) collective-permute-start(bf16[256,1024]{1,0:T(8,128)(2,1)} %get-tuple-element.99), channel_id=1, source_target_pairs={{0,1},{1,4},{2,5},{3,0},{4,3},{5,6},{6,7},{7,2},{8,9},{9,12},{10,1... | collective-permute-start | bytes 1572872 | tf_op jit(solution)/shard_map/ppermute | solution.py:788
  48.5 20.1 %collective-permute-start.11 = (bf16[384,1024]{1,0:T(8,128)(2,1)}, bf16[384,1024]{1,0:T(8,128)(2,1)}, u32[]{:S(2)}, u32[]{:S(2)}) collective-permute-start(bf16[384,1024]{1,0:T(8,128)(2,1)} %get-tuple-element.97.refs_1_.refs_18_.refs_22_.refs_26_.refs_30_.refs_0_.refs_4_), channel_id=1, source_target_pairs={{0,4},{1,5},{2,6},{3,7},{4,0},{5,1},{6,2},{7,3},{8,12},{9,13},{10,... | collective-permute-start | bytes 2359304 | tf_op jit(solution)/shard_map/ppermute | solution.py:788
  61.2 7.4 %collective-permute-start.4 = (bf16[384,1024]{1,0:T(8,128)(2,1)}, bf16[384,1024]{1,0:T(8,128)(2,1)}, u32[]{:S(2)}, u32[]{:S(2)}) collective-permute-start(bf16[384,1024]{1,0:T(8,128)(2,1)} %get-tuple-element.96.refs_0_.refs_2_.refs_4_.refs_10_.refs_12_), channel_id=1, source_target_pairs={{0,4},{1,5},{2,6},{3,7},{4,0},{5,1},{6,2},{7,3},{8,12},{9,13},{10,... | collective-permute-start | bytes 2359304 | tf_op jit(solution)/shard_map/ppermute | solution.py:788
  79.5 4.6 %collective-permute-start.15 = (bf16[512,2048]{1,0:T(8,128)(2,1)}, bf16[512,2048]{1,0:T(8,128)(2,1)}, u32[]{:S(2)}, u32[]{:S(2)}) collective-permute-start(bf16[512,2048]{1,0:T(8,128)(2,1)} %get-tuple-element.109.ko.vo), channel_id=1, source_target_pairs={{0,4},{1,5},{2,6},{3,7},{4,0},{5,1},{6,2},{7,3},{8,12},{9,13},{10,... | collective-permute-start | bytes 6291464 | tf_op jit(solution)/shard_map/ppermute | solution.py:788
  79.6 17.0 %collective-permute-start.13 = (bf16[128,2048]{1,0:T(8,128)(2,1)}, bf16[128,2048]{1,0:T(8,128)(2,1)}, u32[]{:S(2)}, u32[]{:S(2)}) collective-permute-start(bf16[128,2048]{1,0:T(8,128)(2,1)} %get-tuple-element.106.refs_3_.refs_0_), channel_id=1, source_target_pairs={{0,8},{1,9},{2,10},{3,11},{4,12},{5,13},{6,14},{7,15},{8,0},{9,1},... | collective-permute-start | bytes 1572872 | tf_op jit(solution)/shard_map/ppermute | solution.py:788
  81.1 16.9 %collective-permute-start.14 = (bf16[128,2048]{1,0:T(8,128)(2,1)}, bf16[128,2048]{1,0:T(8,128)(2,1)}, u32[]{:S(2)}, u32[]{:S(2)}) collective-permute-start(bf16[128,2048]{1,0:T(8,128)(2,1)} %get-tuple-element.107.refs_11_.refs_8_), channel_id=1, source_target_pairs={{0,16},{1,17},{2,18},{3,19},{4,20},{5,21},{6,22},{7,23},{8,24},{9,... | collective-permute-start | bytes 1572872 | tf_op jit(solution)/shard_map/ppermute | solution.py:788
  98.8 13.8 %collective-permute-start.19 = (bf16[128,2048]{1,0:T(8,128)(2,1)}, bf16[128,2048]{1,0:T(8,128)(2,1)}, u32[]{:S(2)}, u32[]{:S(2)}) collective-permute-start(bf16[128,2048]{1,0:T(8,128)(2,1)} %get-tuple-element.107.refs_11_.refs_8_), channel_id=1, source_target_pairs={{0,4},{1,5},{2,6},{3,7},{4,0},{5,1},{6,2},{7,3},{8,12},{9,13},{10,... | collective-permute-start | bytes 1572872 | tf_op jit(solution)/shard_map/ppermute | solution.py:788
  98.9 14.4 %collective-permute-start.22 = (bf16[128,2048]{1,0:T(8,128)(2,1)}, bf16[128,2048]{1,0:T(8,128)(2,1)}, u32[]{:S(2)}, u32[]{:S(2)}) collective-permute-start(bf16[128,2048]{1,0:T(8,128)(2,1)} %get-tuple-element.106.refs_3_.refs_0_), channel_id=1, source_target_pairs={{0,16},{1,17},{2,18},{3,19},{4,20},{5,21},{6,22},{7,23},{8,24},{9,... | collective-permute-start | bytes 1572872 | tf_op jit(solution)/shard_map/ppermute | solution.py:788
  100.1 15.3 %collective-permute-start.23 = (bf16[128,2048]{1,0:T(8,128)(2,1)}, bf16[128,2048]{1,0:T(8,128)(2,1)}, u32[]{:S(2)}, u32[]{:S(2)}) collective-permute-start(bf16[128,2048]{1,0:T(8,128)(2,1)} %get-tuple-element.107.refs_11_.refs_8_), channel_id=1, source_target_pairs={{0,8},{1,9},{2,10},{3,11},{4,12},{5,13},{6,14},{7,15},{8,0},{9,1},... | collective-permute-start | bytes 1572872 | tf_op jit(solution)/shard_map/ppermute | solution.py:788
  100.4 15.0 %collective-permute-start.20 = (bf16[128,2048]{1,0:T(8,128)(2,1)}, bf16[128,2048]{1,0:T(8,128)(2,1)}, u32[]{:S(2)}, u32[]{:S(2)}) collective-permute-start(bf16[128,2048]{1,0:T(8,128)(2,1)} %get-tuple-element.112.refs_5_.refs_2_), channel_id=1, source_target_pairs={{0,4},{1,5},{2,6},{3,7},{4,0},{5,1},{6,2},{7,3},{8,12},{9,13},{10,... | collective-permute-start | bytes 1572872 | tf_op jit(solution)/shard_map/ppermute | solution.py:788
  101.4 14.0 %collective-permute-start.21 = (bf16[128,2048]{1,0:T(8,128)(2,1)}, bf16[128,2048]{1,0:T(8,128)(2,1)}, u32[]{:S(2)}, u32[]{:S(2)}) collective-permute-start(bf16[128,2048]{1,0:T(8,128)(2,1)} %get-tuple-element.113.refs_15_.refs_12_), channel_id=1, source_target_pairs={{0,4},{1,5},{2,6},{3,7},{4,0},{5,1},{6,2},{7,3},{8,12},{9,13},{10,... | collective-permute-start | bytes 1572872 | tf_op jit(solution)/shard_map/ppermute | solution.py:788
  115.4 18.7 %collective-permute-start.26 = (bf16[512,2048]{1,0:T(8,128)(2,1)}, bf16[512,2048]{1,0:T(8,128)(2,1)}, u32[]{:S(2)}, u32[]{:S(2)}) collective-permute-start(bf16[512,2048]{1,0:T(8,128)(2,1)} %get-tuple-element.122.ko.vo), channel_id=1, source_target_pairs={{0,4},{1,5},{2,6},{3,7},{4,0},{5,1},{6,2},{7,3},{8,12},{9,13},{10,... | collective-permute-start | bytes 6291464 | tf_op jit(solution)/shard_map/ppermute | solution.py:788
  119.4 36.2 %collective-permute-start.16 = (bf16[128,2048]{1,0:T(8,128)(2,1)}, bf16[128,2048]{1,0:T(8,128)(2,1)}, u32[]{:S(2)}, u32[]{:S(2)}) collective-permute-start(bf16[128,2048]{1,0:T(8,128)(2,1)} %get-tuple-element.112.refs_5_.refs_2_), channel_id=1, source_target_pairs={{0,16},{1,17},{2,18},{3,19},{4,20},{5,21},{6,22},{7,23},{8,24},{9,... | collective-permute-start | bytes 1572872 | tf_op jit(solution)/shard_map/ppermute | solution.py:788
  119.4 36.2 %collective-permute-start.17 = (bf16[128,2048]{1,0:T(8,128)(2,1)}, bf16[128,2048]{1,0:T(8,128)(2,1)}, u32[]{:S(2)}, u32[]{:S(2)}) collective-permute-start(bf16[128,2048]{1,0:T(8,128)(2,1)} %get-tuple-element.113.refs_15_.refs_12_), channel_id=1, source_target_pairs={{0,8},{1,9},{2,10},{3,11},{4,12},{5,13},{6,14},{7,15},{8,0},{9,1},... | collective-permute-start | bytes 1572872 | tf_op jit(solution)/shard_map/ppermute | solution.py:788
  119.9 35.7 %collective-permute-start.24 = (bf16[256,1024]{1,0:T(8,128)(2,1)}, bf16[256,1024]{1,0:T(8,128)(2,1)}, u32[]{:S(2)}, u32[]{:S(2)}) collective-permute-start(bf16[256,1024]{1,0:T(8,128)(2,1)} %get-tuple-element.119), channel_id=1, source_target_pairs={{0,0},{1,5},{2,4},{3,1},{4,2},{5,7},{6,6},{7,3},{8,8},{9,13},{10,1... | collective-permute-start | bytes 1572872 | tf_op jit(solution)/shard_map/ppermute | solution.py:788
  129.2 26.5 %collective-permute-start.25 = (bf16[256,1024]{1,0:T(8,128)(2,1)}, bf16[256,1024]{1,0:T(8,128)(2,1)}, u32[]{:S(2)}, u32[]{:S(2)}) collective-permute-start(bf16[256,1024]{1,0:T(8,128)(2,1)} %get-tuple-element.120), channel_id=1, source_target_pairs={{0,1},{1,4},{2,5},{3,0},{4,3},{5,6},{6,7},{7,2},{8,9},{9,12},{10,1... | collective-permute-start | bytes 1572872 | tf_op jit(solution)/shard_map/ppermute | solution.py:788
  155.7 5.3 %collective-permute-start.27 = (bf16[128,2048]{1,0:T(8,128)(2,1)}, bf16[128,2048]{1,0:T(8,128)(2,1)}, u32[]{:S(2)}, u32[]{:S(2)}) collective-permute-start(bf16[128,2048]{1,0:T(8,128)(2,1)} %get-tuple-element.129.refs_7_.refs_4_), channel_id=1, source_target_pairs={{0,4},{1,5},{2,6},{3,7},{4,0},{5,1},{6,2},{7,3},{8,12},{9,13},{10,... | collective-permute-start | bytes 1572872 | tf_op jit(solution)/shard_map/ppermute | solution.py:788
  155.8 5.2 %collective-permute-start.28 = (bf16[128,2048]{1,0:T(8,128)(2,1)}, bf16[128,2048]{1,0:T(8,128)(2,1)}, u32[]{:S(2)}, u32[]{:S(2)}) collective-permute-start(bf16[128,2048]{1,0:T(8,128)(2,1)} %get-tuple-element.130.refs_9_.refs_6_), channel_id=1, source_target_pairs={{0,4},{1,5},{2,6},{3,7},{4,0},{5,1},{6,2},{7,3},{8,12},{9,13},{10,... | collective-permute-start | bytes 1572872 | tf_op jit(solution)/shard_map/ppermute | solution.py:788
  156.3 4.7 %collective-permute-start.29 = (bf16[128,2048]{1,0:T(8,128)(2,1)}, bf16[128,2048]{1,0:T(8,128)(2,1)}, u32[]{:S(2)}, u32[]{:S(2)}) collective-permute-start(bf16[128,2048]{1,0:T(8,128)(2,1)} %get-tuple-element.132.refs_13_.refs_10_), channel_id=1, source_target_pairs={{0,4},{1,5},{2,6},{3,7},{4,0},{5,1},{6,2},{7,3},{8,12},{9,13},{10,... | collective-permute-start | bytes 1572872 | tf_op jit(solution)/shard_map/ppermute | solution.py:788
  156.4 4.7 %collective-permute-start.30 = (bf16[128,2048]{1,0:T(8,128)(2,1)}, bf16[128,2048]{1,0:T(8,128)(2,1)}, u32[]{:S(2)}, u32[]{:S(2)}) collective-permute-start(bf16[128,2048]{1,0:T(8,128)(2,1)} %get-tuple-element.134.refs_17_.refs_14_), channel_id=1, source_target_pairs={{0,4},{1,5},{2,6},{3,7},{4,0},{5,1},{6,2},{7,3},{8,12},{9,13},{10,... | collective-permute-start | bytes 1572872 | tf_op jit(solution)/shard_map/ppermute | solution.py:788
  183.8 27.7 %collective-permute-start.31 = (bf16[512,1024]{1,0:T(8,128)(2,1)}, bf16[512,1024]{1,0:T(8,128)(2,1)}, u32[]{:S(2)}, u32[]{:S(2)}) collective-permute-start(bf16[512,1024]{1,0:T(8,128)(2,1)} %get-tuple-element.139), channel_id=1, source_target_pairs={{0,4},{1,5},{2,6},{3,7},{4,0},{5,1},{6,2},{7,3},{8,12},{9,13},{10,... | collective-permute-start | bytes 3145736 | tf_op jit(solution)/shard_map/ppermute | solution.py:788
  184.1 62.1 %collective-permute-start.35 = (bf16[256,1024]{1,0:T(8,128)(2,1)}, bf16[256,1024]{1,0:T(8,128)(2,1)}, u32[]{:S(2)}, u32[]{:S(2)}) collective-permute-start(bf16[256,1024]{1,0:T(8,128)(2,1)} %get-tuple-element.147), channel_id=1, source_target_pairs={{0,0},{1,3},{2,4},{3,7},{4,2},{5,1},{6,6},{7,5},{8,8},{9,11},{10,1... | collective-permute-start | bytes 1572872 | tf_op jit(solution)/shard_map/ppermute | solution.py:788
  188.9 57.3 %collective-permute-start.36 = (bf16[256,1024]{1,0:T(8,128)(2,1)}, bf16[256,1024]{1,0:T(8,128)(2,1)}, u32[]{:S(2)}, u32[]{:S(2)}) collective-permute-start(bf16[256,1024]{1,0:T(8,128)(2,1)} %get-tuple-element.148), channel_id=1, source_target_pairs={{0,3},{1,0},{2,7},{3,4},{4,1},{5,2},{6,5},{7,6},{8,11},{9,8},{10,1... | collective-permute-start | bytes 1572872 | tf_op jit(solution)/shard_map/ppermute | solution.py:788
  215.4 30.9 %collective-permute-start.32 = (bf16[128,1024]{1,0:T(8,128)(2,1)}, bf16[128,1024]{1,0:T(8,128)(2,1)}, u32[]{:S(2)}, u32[]{:S(2)}) collective-permute-start(bf16[128,1024]{1,0:T(8,128)(2,1)} %get-tuple-element.206), channel_id=1, source_target_pairs={{0,8},{1,9},{2,10},{3,11},{4,12},{5,13},{6,14},{7,15},{8,0},{9,1},... | collective-permute-start | bytes 786440 | tf_op jit(solution)/shard_map/ppermute | solution.py:788
  216.8 29.4 %collective-permute-start.33 = (bf16[128,1024]{1,0:T(8,128)(2,1)}, bf16[128,1024]{1,0:T(8,128)(2,1)}, u32[]{:S(2)}, u32[]{:S(2)}) collective-permute-start(bf16[128,1024]{1,0:T(8,128)(2,1)} %get-tuple-element.205), channel_id=1, source_target_pairs={{0,16},{1,17},{2,18},{3,19},{4,20},{5,21},{6,22},{7,23},{8,24},{9,... | collective-permute-start | bytes 786440 | tf_op jit(solution)/shard_map/ppermute | solution.py:788
  217.2 29.1 %collective-permute-start.34 = (bf16[128,1024]{1,0:T(8,128)(2,1)}, bf16[128,1024]{1,0:T(8,128)(2,1)}, u32[]{:S(2)}, u32[]{:S(2)}) collective-permute-start(bf16[128,1024]{1,0:T(8,128)(2,1)} %get-tuple-element.204), channel_id=1, source_target_pairs={{0,24},{1,25},{2,26},{3,27},{4,28},{5,29},{6,30},{7,31},{8,16},{9,... | collective-permute-start | bytes 786440 | tf_op jit(solution)/shard_map/ppermute | solution.py:788
  246.3 5.5 %collective-permute-start.38 = (bf16[512,2048]{1,0:T(8,128)(2,1)}, bf16[512,2048]{1,0:T(8,128)(2,1)}, u32[]{:S(2)}, u32[]{:S(2)}) collective-permute-start(bf16[512,2048]{1,0:T(8,128)(2,1)} %get-tuple-element.162), channel_id=1, source_target_pairs={{0,4},{1,5},{2,6},{3,7},{4,0},{5,1},{6,2},{7,3},{8,12},{9,13},{10,... | collective-permute-start | bytes 6291464 | tf_op jit(solution)/shard_map/ppermute | solution.py:788
  249.2 33.1 %collective-permute-start.37 = (bf16[128,1024]{1,0:T(8,128)(2,1)}, bf16[128,1024]{1,0:T(8,128)(2,1)}, u32[]{:S(2)}, u32[]{:S(2)}) collective-permute-start(bf16[128,1024]{1,0:T(8,128)(2,1)} %add_convert_fusion.3.refs_5_), channel_id=1, source_target_pairs={{0,2},{1,3},{2,0},{3,1},{4,6},{5,7},{6,4},{7,5},{8,10},{9,11},{10,... | collective-permute-start | bytes 786440 | tf_op jit(solution)/shard_map/ppermute | solution.py:788
  259.8 27.5 %collective-permute-start.39 = (bf16[256,1024]{1,0:T(8,128)(2,1)}, bf16[256,1024]{1,0:T(8,128)(2,1)}, u32[]{:S(2)}, u32[]{:S(2)}) collective-permute-start(bf16[256,1024]{1,0:T(8,128)(2,1)} %get-tuple-element.164), channel_id=1, source_target_pairs={{0,0},{1,3},{2,4},{3,7},{4,2},{5,1},{6,6},{7,5},{8,8},{9,11},{10,1... | collective-permute-start | bytes 1572872 | tf_op jit(solution)/shard_map/ppermute | solution.py:788
  264.1 23.1 %collective-permute-start.40 = (bf16[256,1024]{1,0:T(8,128)(2,1)}, bf16[256,1024]{1,0:T(8,128)(2,1)}, u32[]{:S(2)}, u32[]{:S(2)}) collective-permute-start(bf16[256,1024]{1,0:T(8,128)(2,1)} %get-tuple-element.165), channel_id=1, source_target_pairs={{0,3},{1,0},{2,7},{3,4},{4,1},{5,2},{6,5},{7,6},{8,11},{9,8},{10,1... | collective-permute-start | bytes 1572872 | tf_op jit(solution)/shard_map/ppermute | solution.py:788
  287.2 4.5 %collective-permute-start.42 = (bf16[512,2048]{1,0:T(8,128)(2,1)}, bf16[512,2048]{1,0:T(8,128)(2,1)}, u32[]{:S(2)}, u32[]{:S(2)}) collective-permute-start(bf16[512,2048]{1,0:T(8,128)(2,1)} %get-tuple-element.176), channel_id=1, source_target_pairs={{0,4},{1,5},{2,6},{3,7},{4,0},{5,1},{6,2},{7,3},{8,12},{9,13},{10,... | collective-permute-start | bytes 6291464 | tf_op jit(solution)/shard_map/ppermute | solution.py:788
  289.0 11.0 %collective-permute-start.41 = (bf16[128,1024]{1,0:T(8,128)(2,1)}, bf16[128,1024]{1,0:T(8,128)(2,1)}, u32[]{:S(2)}, u32[]{:S(2)}) collective-permute-start(bf16[128,1024]{1,0:T(8,128)(2,1)} %add_convert_fusion.2.refs_27_), channel_id=1, source_target_pairs={{0,1},{1,0},{2,3},{3,2},{4,5},{5,4},{6,7},{7,6},{8,9},{9,8},{10,11... | collective-permute-start | bytes 786440 | tf_op jit(solution)/shard_map/ppermute | solution.py:788
  301.2 8.4 %collective-permute-start.45 = (bf16[128,1024]{1,0:T(8,128)(2,1)S(1)}, bf16[128,1024]{1,0:T(8,128)(2,1)S(1)}, u32[]{:S(2)}, u32[]{:S(2)}) collective-permute-start(bf16[128,1024]{1,0:T(8,128)(2,1)S(1)} %add_convert_fusion.1), channel_id=1, source_target_pairs={{0,16},{1,17},{2,18},{3,19},{4,20},{5,21},{6,22},{7,23},{8,24},{9,... | collective-permute-start | bytes 786440 | tf_op jit(solution)/shard_map/ppermute | solution.py:788
  302.3 7.6 %collective-permute-start.46 = (bf16[128,1024]{1,0:T(8,128)(2,1)S(1)}, bf16[128,1024]{1,0:T(8,128)(2,1)S(1)}, u32[]{:S(2)}, u32[]{:S(2)}) collective-permute-start(bf16[128,1024]{1,0:T(8,128)(2,1)S(1)} %add_convert_fusion.1), channel_id=1, source_target_pairs={{0,8},{1,9},{2,10},{3,11},{4,12},{5,13},{6,14},{7,15},{8,0},{9,1},... | collective-permute-start | bytes 786440 | tf_op jit(solution)/shard_map/ppermute | solution.py:788
  303.8 11.7 %collective-permute-start.47 = (bf16[128,1024]{1,0:T(8,128)(2,1)S(1)}, bf16[128,1024]{1,0:T(8,128)(2,1)S(1)}, u32[]{:S(2)}, u32[]{:S(2)}) collective-permute-start(bf16[128,1024]{1,0:T(8,128)(2,1)S(1)} %add_convert_fusion.1), channel_id=1, source_target_pairs={{0,24},{1,25},{2,26},{3,27},{4,28},{5,29},{6,30},{7,31},{8,16},{9,... | collective-permute-start | bytes 786440 | tf_op jit(solution)/shard_map/ppermute | solution.py:788
  303.9 28.0 %collective-permute-start.43 = (bf16[256,1024]{1,0:T(8,128)(2,1)}, bf16[256,1024]{1,0:T(8,128)(2,1)S(1)}, u32[]{:S(2)}, u32[]{:S(2)}) collective-permute-start(bf16[256,1024]{1,0:T(8,128)(2,1)} %get-tuple-element.182), channel_id=1, source_target_pairs={{0,0},{1,3},{2,4},{3,7},{4,2},{5,1},{6,6},{7,5},{8,8},{9,11},{10,1... | collective-permute-start | bytes 1572872 | tf_op jit(solution)/shard_map/ppermute | solution.py:788
  308.7 23.2 %collective-permute-start.44 = (bf16[256,1024]{1,0:T(8,128)(2,1)}, bf16[256,1024]{1,0:T(8,128)(2,1)S(1)}, u32[]{:S(2)}, u32[]{:S(2)}) collective-permute-start(bf16[256,1024]{1,0:T(8,128)(2,1)} %get-tuple-element.183), channel_id=1, source_target_pairs={{0,3},{1,0},{2,7},{3,4},{4,1},{5,2},{6,5},{7,6},{8,11},{9,8},{10,1... | collective-permute-start | bytes 1572872 | tf_op jit(solution)/shard_map/ppermute | solution.py:788
  315.7 17.3 %collective-permute-start.48 = (bf16[512,1024]{1,0:T(8,128)(2,1)S(1)}, bf16[512,1024]{1,0:T(8,128)(2,1)S(1)}, u32[]{:S(2)}, u32[]{:S(2)}) collective-permute-start(bf16[512,1024]{1,0:T(8,128)(2,1)S(1)} %pad_maximum_fusion.4), channel_id=1, source_target_pairs={{0,4},{1,5},{2,6},{3,7},{4,0},{5,1},{6,2},{7,3},{8,12},{9,13},{10,... | collective-permute-start | bytes 3145736 | tf_op jit(solution)/shard_map/ppermute | solution.py:788
  (20 other events, 137.2 us)
Sparse Core Ops, SparseCore 0:
  9.9 82.0 all-gather.2
  98.2 62.7 all-gather.4

commit v8 on v7

--- a/solution.py
+++ b/solution.py
@@ -669,7 +669,7 @@
     F = c.shape[0]
     width = first.shape[1]
     per = width // block
-    held = Loads([first, second, gnar, down, c_out, low, inv])
+    held = Loads([gnar, down, first, second, c_out, low, inv])
 
     def kernel(info_ref, g3_ref, c_ref, gp_ref, *refs):
         ins = refs[: len(held.arrays)]
@@ -681,10 +681,11 @@
 
         @pl.when(i == 0)
         def _():
-            acc[...] = g3_ref[...]
+            get = getter(bound[:2])
+            acc[...] = g3_ref[...] + nt(get(0)[...], get(1)[...])
 
         for v in range(2):
-            copies, e = bound[v]
+            copies, e = bound[2 + v]
 
             @pl.when(i == v * per)
             def _():
@@ -697,10 +698,10 @@
 
         @pl.when(i == F // block - 1)
         def _():
-            get = getter(bound)
-            g2 = norm_back(get(5)[...].astype(F32), get(6)[:, 0:1], acc[...] + nt(get(2)[...], get(3)[...]))
+            get = getter(bound[4:])
+            g2 = norm_back(get(1)[...].astype(F32), get(2)[:, 0:1], acc[...])
             g2_ref[...] = g2
-            ga_ref[...] = nt(g2.astype(BF), get(4)[...]).astype(BF)
+            ga_ref[...] = nt(g2.astype(BF), get(0)[...]).astype(BF)
 
     outs = [shape(T, D, F32), shape(T, D, BF)]
     return pl.pallas_call(

time: 350 us -> 350 us (level)
  no operation moved by 1% of the time
where the time goes in v8:
time: 350 us; the launch traced here: 344 us
  Pallas kernels  165 us (47%)
  starting transfers between devices  70.4 us (20%)
  waiting for transfers between devices  58 us (17%)
  other arithmetic  23.5 us (7%)
  between operations  15.7 us (4%)
  local copies, waits for them, and re-layouts  10.8 us (3%)
    ppermute x49, starting transfers between devices, move(): return lax.ppermute(value, ('dp', 'seq'), pairs)  70.3 us
    ppermute x49, waiting for transfers between devices, move(): return lax.ppermute(value, ('dp', 'seq'), pairs)  53.8 us
    pallas_call x2, Pallas kernels, attend_back(): pl.pallas_call(kernel, grid_spec=pltpu.PrefetchScalarGridSpec(num_scalar_...  46.3 us
    pallas_call x4, Pallas kernels, fused(): pl.pallas_call(kernel, grid_spec=pltpu.PrefetchScalarGridSpec(num_scalar_...  34.2 us
    pallas_call x2, Pallas kernels, attend(): pl.pallas_call(kernel, grid_spec=pltpu.PrefetchScalarGridSpec(num_scalar_...  34.1 us
    pallas_call x1, Pallas kernels, feed_forward(): pl.pallas_call(kernel, grid_spec=pltpu.PrefetchScalarGridSpec(num_scalar_...  22.8 us
    pallas_call x1, Pallas kernels, ffn_back(): pl.pallas_call(kernel, grid_spec=pltpu.PrefetchScalarGridSpec(num_scalar_...  19.9 us
  transfers between devices with their start and end apart: 51, of which 17 were waited for; matrix products, arithmetic and copies ran while one was open for 7% of the time, Pallas kernels for 41%

profile of v8, /device:TPU:1, one launch (start us, length us, event | category | flops | bytes accessed | tf_op | source)
XLA Modules:
  0.0 343.7 jit_solution(8222621579517104611)
XLA Ops:
  7.2 2.4 join_up.1
  11.7 5.6 %collective-permute-start = (bf16[256,1024]{1,0:T(8,128)(2,1)S(1)}, bf16[256,1024]{1,0:T(8,128)(2,1)}, u32[]{:S(2)}, u32[]{:S(2)}) collective-permute-start(bf16[256,1024]{1,0:T(8,128)(2,1)S(1)} %get-tuple-element.212), channel_id=1, source_target_pairs={{0,0},{1,5},{2,4},{3,1},{4,2},{5,7},{6,6},{7,3},{8,8},{9,13},{10,1... | collective-permute-start | bytes 1572872 | tf_op jit(solution)/shard_map/ppermute | solution.py:789
  20.0 1.9 collective-permute-start.1
  28.2 3.8 %collective-permute-done.2.b = bf16[192,1024]{1,0:T(8,128)(2,1)} collective-permute-done((bf16[192,1024]{1,0:T(8,128)(2,1)S(1)}, bf16[192,1024]{1,0:T(8,128)(2,1)}, u32[]{:S(2)}, u32[]{:S(2)}) %collective-permute-start.2) | collective-permute-done | bytes 393248 | tf_op jit(solution)/shard_map/ppermute | solution.py:789
  32.0 2.6 collective-permute-done.3.d
  35.4 2.6 beside.1
  38.0 2.4 collective-permute-start.5
  41.0 1.5 and_convert_fusion
  42.6 1.9 collective-permute-start.7
  44.5 2.3 collective-permute-start.8
  48.5 2.9 stage.1
  51.4 9.8 %collective-permute-done.7.refs_2_.refs_0_ = bf16[256,1024]{1,0:T(8,128)(2,1)} collective-permute-done((bf16[256,1024]{1,0:T(8,128)(2,1)}, bf16[256,1024]{1,0:T(8,128)(2,1)}, u32[]{:S(2)}, u32[]{:S(2)}) %collective-permute-start.7) | collective-permute-done | bytes 524320 | tf_op jit(solution)/shard_map/ppermute | solution.py:789
  62.2 4.0 %collective-permute-done.5.refs_0_ = bf16[384,1024]{1,0:T(8,128)(2,1)} collective-permute-done((bf16[384,1024]{1,0:T(8,128)(2,1)}, bf16[384,1024]{1,0:T(8,128)(2,1)}, u32[]{:S(2)}, u32[]{:S(2)}) %collective-permute-start.5) | collective-permute-done | bytes 786464 | tf_op jit(solution)/shard_map/ppermute | solution.py:789
  68.6 2.1 collective-permute-done.10.refs_7_.refs_9_.refs_15_.refs_17_
  71.8 7.7 %qkv.1 = (bf16[512,1024]{1,0:T(8,128)(2,1)}, bf16[512,2048]{1,0:T(8,128)(2,1)}) custom-call(s32[4]{0:T(128)} %pad_add_fusion.2.refs_4_.info_ref, bf16[256,1024]{1,0:T(8,128)(2,1)} %collective-permute-done.refs_0_.refs_2_.refs_6_, bf16[256,1024]{1,0:T(8,128)(2,1)} %collective-permute-done.1.refs_3_.refs_1_.refs_7_, ...), custom_call_target="tpu_custom_call" | custom-call | flops 1800000000 | bytes 1024 | tf_op jit(solution)/shard_map/qkv/pallas_call | solution.py:493
  79.6 1.5 collective-permute-start.13
  82.2 1.9 collective-permute-done.15.kp.vp
  84.1 12.5 %attend.2 = (bf16[512,1024]{1,0:T(8,128)(2,1)}, bf16[8,2,5,256,256]{4,3,2,1,0:T(8,128)(2,1)}, f32[512,1024]{1,0:T(8,128)}) custom-call(s32[4]{0:T(128)} %pad_add_fusion.2.refs_4_.info_ref, bf16[512,1024]{1,0:T(8,128)(2,1)} %get-tuple-element.108.q_ref, bf16[512,2048]{1,0:T(8,128)(2,1)} %get-tuple-element.109.ko.vo, ...), custom_call_target="tpu_custom_call" | custom-call | flops 7500000256 | bytes 1024 | tf_op jit(solution)/shard_map/attend/pallas_call | solution.py:267
  96.6 1.4 collective-permute-done.14.refs_1_
  102.4 10.2 %between.1 = (bf16[512,2048]{1,0:T(8,128)(2,1)}, f32[512,1024]{1,0:T(8,128)}, bf16[512,1024]{1,0:T(8,128)(2,1)}, f32[512,128]{1,0:T(8,128)}, bf16[512,1024]{1,0:T(8,128)(2,1)}) custom-call(s32[4]{0:T(128)} %pad_add_fusion.2.refs_4_.info_ref, bf16[256,1024]{1,0:T(8,128)(2,1)} %collective-permute-done.7.refs_2_.refs_0_, ...), custom_call_target="tpu_custom_call" | custom-call | flops 1800000000 | bytes 1024 | tf_op jit(solution)/shard_map/between/pallas_call | solution.py:493
  113.3 2.1 collective-permute-done.23.refs_7_
  115.4 4.0 %collective-permute-start.26 = (bf16[512,2048]{1,0:T(8,128)(2,1)}, bf16[512,2048]{1,0:T(8,128)(2,1)}, u32[]{:S(2)}, u32[]{:S(2)}) collective-permute-start(bf16[512,2048]{1,0:T(8,128)(2,1)} %get-tuple-element.122.ko.vo), channel_id=1, source_target_pairs={{0,4},{1,5},{2,6},{3,7},{4,0},{5,1},{6,2},{7,3},{8,12},{9,13},{10,... | collective-permute-start | bytes 6291464 | tf_op jit(solution)/shard_map/ppermute | solution.py:789
  119.9 9.3 %collective-permute-start.24 = (bf16[256,1024]{1,0:T(8,128)(2,1)}, bf16[256,1024]{1,0:T(8,128)(2,1)}, u32[]{:S(2)}, u32[]{:S(2)}) collective-permute-start(bf16[256,1024]{1,0:T(8,128)(2,1)} %get-tuple-element.119), channel_id=1, source_target_pairs={{0,0},{1,5},{2,4},{3,1},{4,2},{5,7},{6,6},{7,3},{8,8},{9,13},{10,1... | collective-permute-start | bytes 1572872 | tf_op jit(solution)/shard_map/ppermute | solution.py:789
  129.2 4.9 %collective-permute-start.25 = (bf16[256,1024]{1,0:T(8,128)(2,1)}, bf16[256,1024]{1,0:T(8,128)(2,1)}, u32[]{:S(2)}, u32[]{:S(2)}) collective-permute-start(bf16[256,1024]{1,0:T(8,128)(2,1)} %get-tuple-element.120), channel_id=1, source_target_pairs={{0,1},{1,4},{2,5},{3,0},{4,3},{5,6},{6,7},{7,2},{8,9},{9,12},{10,1... | collective-permute-start | bytes 1572872 | tf_op jit(solution)/shard_map/ppermute | solution.py:789
  134.1 21.6 %attend.3 = (bf16[512,1024]{1,0:T(8,128)(2,1)}, bf16[8,2,8,256,256]{4,3,2,1,0:T(8,128)(2,1)}, f32[512,1024]{1,0:T(8,128)}, bf16[512,1024]{1,0:T(8,128)(2,1)}, f32[512,128]{1,0:T(8,128)}, /*index=5*/f32[512,1024]{1,0:T(8,128)}) custom-call(s32[4]{0:T(128)} %pad_add_fusion.2.refs_4_.info_ref, bf16[512,1024]{1,0:T(8,128)(2,1)} %get-tuple-element.121.q_ref, ...), custom_call_target="tpu_custom_call" | custom-call | flops 7500000256 | bytes 1024 | tf_op jit(solution)/shard_map/attend/pallas_call | solution.py:267
  156.8 4.2 %all-gather.5.cloned.1.call-done.c_ref = bf16[4096,1024]{1,0:T(8,128)(2,1)} async-done(((bf16[512,1024]{1,0:T(8,128)(2,1)}), bf16[4096,1024]{1,0:T(8,128)(2,1)}) %all-gather.5.cloned.1.call-update) | async-done | bytes 8388624 | tf_op jit(solution)/shard_map/all_gather | solution.py:972
  161.0 22.8 %feed_forward.1 = (bf16[512,4096]{1,0:T(8,128)(2,1)}, bf16[256,1024]{1,0:T(8,128)(2,1)}, bf16[256,1024]{1,0:T(8,128)(2,1)}, f32[512,1024]{1,0:T(8,128)}, bf16[51...) custom-call(s32[4]{0:T(128)} %pad_add_fusion.2.refs_4_.info_ref, ...), custom_call_target="tpu_custom_call" | custom-call | flops 7800000000 | bytes 1024 | tf_op jit(solution)/shard_map/feed_forward/pallas_call | solution.py:649
  184.1 4.8 %collective-permute-start.35 = (bf16[256,1024]{1,0:T(8,128)(2,1)}, bf16[256,1024]{1,0:T(8,128)(2,1)}, u32[]{:S(2)}, u32[]{:S(2)}) collective-permute-start(bf16[256,1024]{1,0:T(8,128)(2,1)} %get-tuple-element.147), channel_id=1, source_target_pairs={{0,0},{1,3},{2,4},{3,7},{4,2},{5,1},{6,6},{7,5},{8,8},{9,11},{10,1... | collective-permute-start | bytes 1572872 | tf_op jit(solution)/shard_map/ppermute | solution.py:789
  188.9 2.5 collective-permute-start.36
  191.4 19.9 %ffn_back.1 = (f32[512,1024]{1,0:T(8,128)}, bf16[512,1024]{1,0:T(8,128)(2,1)}) custom-call(s32[4]{0:T(128)} %pad_add_fusion.2.refs_4_.info_ref, f32[512,1024]{1,0:T(8,128)} %get-tuple-element.140.g3_ref, bf16[4096,1024]{1,0:T(8,128)(2,1)} %all-gather.5.cloned.1.call-done.c_ref, bf16[512,4096]{1,0:T(8,128)(2,1)} %get-tuple-element.141.gp_ref, ...), custom_call_target="tpu_custom_call" | custom-call | flops 5400000000 | bytes 1024 | tf_op jit(solution)/shard_map/ffn_back/pallas_call | solution.py:707
  212.6 1.6 add_convert_fusion
  215.3 1.5 collective-permute-start.32
  217.9 28.2 %attend_back.2 = (bf16[512,2048]{1,0:T(8,128)(2,1)}, bf16[512,2048]{1,0:T(8,128)(2,1)}, f32[512,1024]{1,0:T(8,128)}, bf16[512,1024]{1,0:T(8,128)(2,1)}) custom-call(s32[4]{0:T(128)} %pad_add_fusion.2.refs_4_.info_ref, bf16[512,1024]{1,0:T(8,128)(2,1)} %get-tuple-element.121.q_ref, bf16[512,2048]{1,0:T(8,128)(2,1)} %get-tuple-element.122.ko.vo, ...), custom_call_target="tpu_custom_call" | custom-call | flops 7500000256 | bytes 1024 | tf_op jit(solution)/shard_map/attend_back/pallas_call | solution.py:381
  247.1 2.0 add_convert_fusion.3.refs_5_
  249.1 2.6 collective-permute-start.37
  251.7 8.0 %source_grad.1 = (bf16[256,1024]{1,0:T(8,128)(2,1)}, bf16[256,1024]{1,0:T(8,128)(2,1)}) custom-call(s32[4]{0:T(128)} %pad_add_fusion.2.refs_4_.info_ref, bf16[512,2048]{1,0:T(8,128)(2,1)} %get-tuple-element.161.refs_0_, bf16[512,2048]{1,0:T(8,128)(2,1)} %collective-permute-done.38.refs_1_, ...), custom_call_target="tpu_custom_call" | custom-call | flops 1800000000 | bytes 1024 | tf_op jit(solution)/shard_map/source_grad/pallas_call | solution.py:493
  259.7 4.3 %collective-permute-start.39 = (bf16[256,1024]{1,0:T(8,128)(2,1)}, bf16[256,1024]{1,0:T(8,128)(2,1)}, u32[]{:S(2)}, u32[]{:S(2)}) collective-permute-start(bf16[256,1024]{1,0:T(8,128)(2,1)} %get-tuple-element.164), channel_id=1, source_target_pairs={{0,0},{1,3},{2,4},{3,7},{4,2},{5,1},{6,6},{7,5},{8,8},{9,11},{10,1... | collective-permute-start | bytes 1572872 | tf_op jit(solution)/shard_map/ppermute | solution.py:789
  264.1 18.2 %attend_back.3 = (bf16[512,2048]{1,0:T(8,128)(2,1)}, bf16[512,2048]{1,0:T(8,128)(2,1)}, f32[512,1024]{1,0:T(8,128)}) custom-call(s32[4]{0:T(128)} %pad_add_fusion.2.refs_4_.info_ref, bf16[512,1024]{1,0:T(8,128)(2,1)} %get-tuple-element.108.q_ref, bf16[512,2048]{1,0:T(8,128)(2,1)} %get-tuple-element.109.ko.vo, bf16[512,2048]{1,0:T(8,128)(2,1)} %get-tuple-element.109.ko.vo, ...), custom_call_target="tpu_custom_call" | custom-call | flops 7500000256 | bytes 1024 | tf_op jit(solution)/shard_map/attend_back/pallas_call | solution.py:381
  282.3 4.9 %collective-permute-done.39.refs_1_ = bf16[256,1024]{1,0:T(8,128)(2,1)} collective-permute-done((bf16[256,1024]{1,0:T(8,128)(2,1)}, bf16[256,1024]{1,0:T(8,128)(2,1)}, u32[]{:S(2)}, u32[]{:S(2)}) %collective-permute-start.39) | collective-permute-done | bytes 524320 | tf_op jit(solution)/shard_map/ppermute | solution.py:789
  287.2 1.8 add_convert_fusion.2.refs_27_
  289.3 2.3 collective-permute-done.42.refs_1_
  291.7 8.3 %token_grad.1 = (bf16[256,1024]{1,0:T(8,128)(2,1)}, bf16[256,1024]{1,0:T(8,128)(2,1)}) custom-call(s32[4]{0:T(128)} %pad_add_fusion.2.refs_4_.info_ref, bf16[512,2048]{1,0:T(8,128)(2,1)} %get-tuple-element.175.refs_0_, bf16[512,2048]{1,0:T(8,128)(2,1)} %collective-permute-done.42.refs_1_, ...), custom_call_target="tpu_custom_call" | custom-call | flops 1800000000 | bytes 1024 | tf_op jit(solution)/shard_map/token_grad/pallas_call | solution.py:493
  302.2 1.5 collective-permute-start.46
  303.8 4.8 %collective-permute-start.43 = (bf16[256,1024]{1,0:T(8,128)(2,1)}, bf16[256,1024]{1,0:T(8,128)(2,1)S(1)}, u32[]{:S(2)}, u32[]{:S(2)}) collective-permute-start(bf16[256,1024]{1,0:T(8,128)(2,1)} %get-tuple-element.182), channel_id=1, source_target_pairs={{0,0},{1,3},{2,4},{3,7},{4,2},{5,1},{6,6},{7,5},{8,8},{9,11},{10,1... | collective-permute-start | bytes 1572872 | tf_op jit(solution)/shard_map/ppermute | solution.py:789
  309.8 5.6 %collective-permute-done.47 = bf16[128,1024]{1,0:T(8,128)(2,1)S(1)} collective-permute-done((bf16[128,1024]{1,0:T(8,128)(2,1)S(1)}, bf16[128,1024]{1,0:T(8,128)(2,1)S(1)}, u32[]{:S(2)}, u32[]{:S(2)}) %collective-permute-start.47) | collective-permute-done | bytes 262176 | tf_op jit(solution)/shard_map/ppermute | solution.py:789
  321.7 10.2 %collective-permute-done.43 = bf16[256,1024]{1,0:T(8,128)(2,1)S(1)} collective-permute-done((bf16[256,1024]{1,0:T(8,128)(2,1)}, bf16[256,1024]{1,0:T(8,128)(2,1)S(1)}, u32[]{:S(2)}, u32[]{:S(2)}) %collective-permute-start.43) | collective-permute-done | bytes 524320 | tf_op jit(solution)/shard_map/ppermute | solution.py:789
  333.0 1.7 select_convert_fusion
  334.9 1.5 pad_maximum_fusion
  (157 shorter events, 41.9 us)
Async XLA Ops:
  7.2 95.3 %all-gather.3.cloned.1.call-start = ((), (), s32[]{:S(2)}) async-start(), calls=%async_computation | async-start | bytes 11796480 | tf_op jit(solution)/shard_map/all_gather | solution.py:927
  9.6 151.4 %all-gather.5.cloned.1.call-start = ((), (), s32[]{:S(2)}) async-start(), calls=%async_computation.1 | async-start | bytes 9437184 | tf_op jit(solution)/shard_map/all_gather | solution.py:972
  11.7 23.7 %collective-permute-start = (bf16[256,1024]{1,0:T(8,128)(2,1)S(1)}, bf16[256,1024]{1,0:T(8,128)(2,1)}, u32[]{:S(2)}, u32[]{:S(2)}) collective-permute-start(bf16[256,1024]{1,0:T(8,128)(2,1)S(1)} %get-tuple-element.212), channel_id=1, source_target_pairs={{0,0},{1,5},{2,4},{3,1},{4,2},{5,7},{6,6},{7,3},{8,8},{9,13},{10,1... | collective-permute-start | bytes 1572872 | tf_op jit(solution)/shard_map/ppermute | solution.py:789
  17.4 14.6 %collective-permute-start.2 = (bf16[192,1024]{1,0:T(8,128)(2,1)S(1)}, bf16[192,1024]{1,0:T(8,128)(2,1)}, u32[]{:S(2)}, u32[]{:S(2)}) collective-permute-start(bf16[192,1024]{1,0:T(8,128)(2,1)S(1)} %pad_maximum_fusion.5.a), channel_id=1, source_target_pairs={{0,8},{1,9},{2,10},{3,11},{4,12},{5,13},{6,14},{7,15},{8,0},{9,1},... | collective-permute-start | bytes 1179656 | tf_op jit(solution)/shard_map/ppermute | solution.py:789
  18.7 15.9 %collective-permute-start.3 = (bf16[192,1024]{1,0:T(8,128)(2,1)S(1)}, bf16[192,1024]{1,0:T(8,128)(2,1)S(1)}, u32[]{:S(2)}, u32[]{:S(2)}) collective-permute-start(bf16[192,1024]{1,0:T(8,128)(2,1)S(1)} %pad_maximum_fusion.6.c), channel_id=1, source_target_pairs={{0,16},{1,17},{2,18},{3,19},{4,20},{5,21},{6,22},{7,23},{8,24},{9,... | collective-permute-start | bytes 1179656 | tf_op jit(solution)/shard_map/ppermute | solution.py:789
  20.0 22.6 %collective-permute-start.1 = (bf16[256,1024]{1,0:T(8,128)(2,1)}, bf16[256,1024]{1,0:T(8,128)(2,1)}, u32[]{:S(2)}, u32[]{:S(2)}) collective-permute-start(bf16[256,1024]{1,0:T(8,128)(2,1)} %get-tuple-element.211), channel_id=1, source_target_pairs={{0,1},{1,4},{2,5},{3,0},{4,3},{5,6},{6,7},{7,2},{8,9},{9,12},{10,1... | collective-permute-start | bytes 1572872 | tf_op jit(solution)/shard_map/ppermute | solution.py:789
  22.1 4.5 %collective-permute-start.9 = (s32[2,5]{1,0:T(2,128)S(1)}, s32[2,5]{1,0:T(2,128)S(1)}, u32[]{:S(2)}, u32[]{:S(2)}) collective-permute-start(s32[2,5]{1,0:T(2,128)S(1)} %pad_add_fusion.1), channel_id=1, source_target_pairs={{0,4},{1,5},{2,6},{3,7},{4,0},{5,1},{6,2},{7,3},{8,12},{9,13},{10,... | collective-permute-start | bytes 128 | tf_op jit(solution)/shard_map/ppermute | solution.py:789
  38.0 28.1 %collective-permute-start.5 = (bf16[384,1024]{1,0:T(8,128)(2,1)}, bf16[384,1024]{1,0:T(8,128)(2,1)}, u32[]{:S(2)}, u32[]{:S(2)}) collective-permute-start(bf16[384,1024]{1,0:T(8,128)(2,1)} %get-tuple-element.96.refs_0_.refs_2_.refs_4_.refs_10_.refs_12_), channel_id=1, source_target_pairs={{0,16},{1,17},{2,18},{3,19},{4,20},{5,21},{6,22},{7,23},{8,24},{9,... | collective-permute-start | bytes 2359304 | tf_op jit(solution)/shard_map/ppermute | solution.py:789
  40.4 25.8 %collective-permute-start.6 = (bf16[384,1024]{1,0:T(8,128)(2,1)}, bf16[384,1024]{1,0:T(8,128)(2,1)}, u32[]{:S(2)}, u32[]{:S(2)}) collective-permute-start(bf16[384,1024]{1,0:T(8,128)(2,1)} %get-tuple-element.97.refs_1_.refs_18_.refs_22_.refs_26_.refs_30_.refs_0_.refs_4_), channel_id=1, source_target_pairs={{0,8},{1,9},{2,10},{3,11},{4,12},{5,13},{6,14},{7,15},{8,0},{9,1},... | collective-permute-start | bytes 2359304 | tf_op jit(solution)/shard_map/ppermute | solution.py:789
  42.6 18.6 %collective-permute-start.7 = (bf16[256,1024]{1,0:T(8,128)(2,1)}, bf16[256,1024]{1,0:T(8,128)(2,1)}, u32[]{:S(2)}, u32[]{:S(2)}) collective-permute-start(bf16[256,1024]{1,0:T(8,128)(2,1)} %get-tuple-element.98), channel_id=1, source_target_pairs={{0,0},{1,5},{2,4},{3,1},{4,2},{5,7},{6,6},{7,3},{8,8},{9,13},{10,1... | collective-permute-start | bytes 1572872 | tf_op jit(solution)/shard_map/ppermute | solution.py:789
  44.5 17.7 %collective-permute-start.8 = (bf16[256,1024]{1,0:T(8,128)(2,1)}, bf16[256,1024]{1,0:T(8,128)(2,1)}, u32[]{:S(2)}, u32[]{:S(2)}) collective-permute-start(bf16[256,1024]{1,0:T(8,128)(2,1)} %get-tuple-element.99), channel_id=1, source_target_pairs={{0,1},{1,4},{2,5},{3,0},{4,3},{5,6},{6,7},{7,2},{8,9},{9,12},{10,1... | collective-permute-start | bytes 1572872 | tf_op jit(solution)/shard_map/ppermute | solution.py:789
  48.5 20.1 %collective-permute-start.11 = (bf16[384,1024]{1,0:T(8,128)(2,1)}, bf16[384,1024]{1,0:T(8,128)(2,1)}, u32[]{:S(2)}, u32[]{:S(2)}) collective-permute-start(bf16[384,1024]{1,0:T(8,128)(2,1)} %get-tuple-element.97.refs_1_.refs_18_.refs_22_.refs_26_.refs_30_.refs_0_.refs_4_), channel_id=1, source_target_pairs={{0,4},{1,5},{2,6},{3,7},{4,0},{5,1},{6,2},{7,3},{8,12},{9,13},{10,... | collective-permute-start | bytes 2359304 | tf_op jit(solution)/shard_map/ppermute | solution.py:789
  61.2 7.4 %collective-permute-start.4 = (bf16[384,1024]{1,0:T(8,128)(2,1)}, bf16[384,1024]{1,0:T(8,128)(2,1)}, u32[]{:S(2)}, u32[]{:S(2)}) collective-permute-start(bf16[384,1024]{1,0:T(8,128)(2,1)} %get-tuple-element.96.refs_0_.refs_2_.refs_4_.refs_10_.refs_12_), channel_id=1, source_target_pairs={{0,4},{1,5},{2,6},{3,7},{4,0},{5,1},{6,2},{7,3},{8,12},{9,13},{10,... | collective-permute-start | bytes 2359304 | tf_op jit(solution)/shard_map/ppermute | solution.py:789
  79.5 4.6 %collective-permute-start.15 = (bf16[512,2048]{1,0:T(8,128)(2,1)}, bf16[512,2048]{1,0:T(8,128)(2,1)}, u32[]{:S(2)}, u32[]{:S(2)}) collective-permute-start(bf16[512,2048]{1,0:T(8,128)(2,1)} %get-tuple-element.109.ko.vo), channel_id=1, source_target_pairs={{0,4},{1,5},{2,6},{3,7},{4,0},{5,1},{6,2},{7,3},{8,12},{9,13},{10,... | collective-permute-start | bytes 6291464 | tf_op jit(solution)/shard_map/ppermute | solution.py:789
  79.6 17.0 %collective-permute-start.13 = (bf16[128,2048]{1,0:T(8,128)(2,1)}, bf16[128,2048]{1,0:T(8,128)(2,1)}, u32[]{:S(2)}, u32[]{:S(2)}) collective-permute-start(bf16[128,2048]{1,0:T(8,128)(2,1)} %get-tuple-element.106.refs_3_.refs_2_), channel_id=1, source_target_pairs={{0,8},{1,9},{2,10},{3,11},{4,12},{5,13},{6,14},{7,15},{8,0},{9,1},... | collective-permute-start | bytes 1572872 | tf_op jit(solution)/shard_map/ppermute | solution.py:789
  81.1 16.9 %collective-permute-start.14 = (bf16[128,2048]{1,0:T(8,128)(2,1)}, bf16[128,2048]{1,0:T(8,128)(2,1)}, u32[]{:S(2)}, u32[]{:S(2)}) collective-permute-start(bf16[128,2048]{1,0:T(8,128)(2,1)} %get-tuple-element.107.refs_11_.refs_10_), channel_id=1, source_target_pairs={{0,16},{1,17},{2,18},{3,19},{4,20},{5,21},{6,22},{7,23},{8,24},{9,... | collective-permute-start | bytes 1572872 | tf_op jit(solution)/shard_map/ppermute | solution.py:789
  98.8 13.8 %collective-permute-start.19 = (bf16[128,2048]{1,0:T(8,128)(2,1)}, bf16[128,2048]{1,0:T(8,128)(2,1)}, u32[]{:S(2)}, u32[]{:S(2)}) collective-permute-start(bf16[128,2048]{1,0:T(8,128)(2,1)} %get-tuple-element.107.refs_11_.refs_10_), channel_id=1, source_target_pairs={{0,4},{1,5},{2,6},{3,7},{4,0},{5,1},{6,2},{7,3},{8,12},{9,13},{10,... | collective-permute-start | bytes 1572872 | tf_op jit(solution)/shard_map/ppermute | solution.py:789
  98.9 14.4 %collective-permute-start.22 = (bf16[128,2048]{1,0:T(8,128)(2,1)}, bf16[128,2048]{1,0:T(8,128)(2,1)}, u32[]{:S(2)}, u32[]{:S(2)}) collective-permute-start(bf16[128,2048]{1,0:T(8,128)(2,1)} %get-tuple-element.106.refs_3_.refs_2_), channel_id=1, source_target_pairs={{0,16},{1,17},{2,18},{3,19},{4,20},{5,21},{6,22},{7,23},{8,24},{9,... | collective-permute-start | bytes 1572872 | tf_op jit(solution)/shard_map/ppermute | solution.py:789
  100.1 15.3 %collective-permute-start.23 = (bf16[128,2048]{1,0:T(8,128)(2,1)}, bf16[128,2048]{1,0:T(8,128)(2,1)}, u32[]{:S(2)}, u32[]{:S(2)}) collective-permute-start(bf16[128,2048]{1,0:T(8,128)(2,1)} %get-tuple-element.107.refs_11_.refs_10_), channel_id=1, source_target_pairs={{0,8},{1,9},{2,10},{3,11},{4,12},{5,13},{6,14},{7,15},{8,0},{9,1},... | collective-permute-start | bytes 1572872 | tf_op jit(solution)/shard_map/ppermute | solution.py:789
  100.4 15.0 %collective-permute-start.20 = (bf16[128,2048]{1,0:T(8,128)(2,1)}, bf16[128,2048]{1,0:T(8,128)(2,1)}, u32[]{:S(2)}, u32[]{:S(2)}) collective-permute-start(bf16[128,2048]{1,0:T(8,128)(2,1)} %get-tuple-element.112.refs_5_.refs_4_), channel_id=1, source_target_pairs={{0,4},{1,5},{2,6},{3,7},{4,0},{5,1},{6,2},{7,3},{8,12},{9,13},{10,... | collective-permute-start | bytes 1572872 | tf_op jit(solution)/shard_map/ppermute | solution.py:789
  101.4 14.0 %collective-permute-start.21 = (bf16[128,2048]{1,0:T(8,128)(2,1)}, bf16[128,2048]{1,0:T(8,128)(2,1)}, u32[]{:S(2)}, u32[]{:S(2)}) collective-permute-start(bf16[128,2048]{1,0:T(8,128)(2,1)} %get-tuple-element.113.refs_15_.refs_14_), channel_id=1, source_target_pairs={{0,4},{1,5},{2,6},{3,7},{4,0},{5,1},{6,2},{7,3},{8,12},{9,13},{10,... | collective-permute-start | bytes 1572872 | tf_op jit(solution)/shard_map/ppermute | solution.py:789
  115.4 18.7 %collective-permute-start.26 = (bf16[512,2048]{1,0:T(8,128)(2,1)}, bf16[512,2048]{1,0:T(8,128)(2,1)}, u32[]{:S(2)}, u32[]{:S(2)}) collective-permute-start(bf16[512,2048]{1,0:T(8,128)(2,1)} %get-tuple-element.122.ko.vo), channel_id=1, source_target_pairs={{0,4},{1,5},{2,6},{3,7},{4,0},{5,1},{6,2},{7,3},{8,12},{9,13},{10,... | collective-permute-start | bytes 6291464 | tf_op jit(solution)/shard_map/ppermute | solution.py:789
  119.4 36.2 %collective-permute-start.16 = (bf16[128,2048]{1,0:T(8,128)(2,1)}, bf16[128,2048]{1,0:T(8,128)(2,1)}, u32[]{:S(2)}, u32[]{:S(2)}) collective-permute-start(bf16[128,2048]{1,0:T(8,128)(2,1)} %get-tuple-element.112.refs_5_.refs_4_), channel_id=1, source_target_pairs={{0,16},{1,17},{2,18},{3,19},{4,20},{5,21},{6,22},{7,23},{8,24},{9,... | collective-permute-start | bytes 1572872 | tf_op jit(solution)/shard_map/ppermute | solution.py:789
  119.4 36.2 %collective-permute-start.17 = (bf16[128,2048]{1,0:T(8,128)(2,1)}, bf16[128,2048]{1,0:T(8,128)(2,1)}, u32[]{:S(2)}, u32[]{:S(2)}) collective-permute-start(bf16[128,2048]{1,0:T(8,128)(2,1)} %get-tuple-element.113.refs_15_.refs_14_), channel_id=1, source_target_pairs={{0,8},{1,9},{2,10},{3,11},{4,12},{5,13},{6,14},{7,15},{8,0},{9,1},... | collective-permute-start | bytes 1572872 | tf_op jit(solution)/shard_map/ppermute | solution.py:789
  119.9 35.7 %collective-permute-start.24 = (bf16[256,1024]{1,0:T(8,128)(2,1)}, bf16[256,1024]{1,0:T(8,128)(2,1)}, u32[]{:S(2)}, u32[]{:S(2)}) collective-permute-start(bf16[256,1024]{1,0:T(8,128)(2,1)} %get-tuple-element.119), channel_id=1, source_target_pairs={{0,0},{1,5},{2,4},{3,1},{4,2},{5,7},{6,6},{7,3},{8,8},{9,13},{10,1... | collective-permute-start | bytes 1572872 | tf_op jit(solution)/shard_map/ppermute | solution.py:789
  129.2 26.5 %collective-permute-start.25 = (bf16[256,1024]{1,0:T(8,128)(2,1)}, bf16[256,1024]{1,0:T(8,128)(2,1)}, u32[]{:S(2)}, u32[]{:S(2)}) collective-permute-start(bf16[256,1024]{1,0:T(8,128)(2,1)} %get-tuple-element.120), channel_id=1, source_target_pairs={{0,1},{1,4},{2,5},{3,0},{4,3},{5,6},{6,7},{7,2},{8,9},{9,12},{10,1... | collective-permute-start | bytes 1572872 | tf_op jit(solution)/shard_map/ppermute | solution.py:789
  155.7 5.3 %collective-permute-start.27 = (bf16[128,2048]{1,0:T(8,128)(2,1)}, bf16[128,2048]{1,0:T(8,128)(2,1)}, u32[]{:S(2)}, u32[]{:S(2)}) collective-permute-start(bf16[128,2048]{1,0:T(8,128)(2,1)} %get-tuple-element.129.refs_7_.refs_6_), channel_id=1, source_target_pairs={{0,4},{1,5},{2,6},{3,7},{4,0},{5,1},{6,2},{7,3},{8,12},{9,13},{10,... | collective-permute-start | bytes 1572872 | tf_op jit(solution)/shard_map/ppermute | solution.py:789
  155.8 5.2 %collective-permute-start.28 = (bf16[128,2048]{1,0:T(8,128)(2,1)}, bf16[128,2048]{1,0:T(8,128)(2,1)}, u32[]{:S(2)}, u32[]{:S(2)}) collective-permute-start(bf16[128,2048]{1,0:T(8,128)(2,1)} %get-tuple-element.130.refs_9_.refs_8_), channel_id=1, source_target_pairs={{0,4},{1,5},{2,6},{3,7},{4,0},{5,1},{6,2},{7,3},{8,12},{9,13},{10,... | collective-permute-start | bytes 1572872 | tf_op jit(solution)/shard_map/ppermute | solution.py:789
  156.3 4.7 %collective-permute-start.29 = (bf16[128,2048]{1,0:T(8,128)(2,1)}, bf16[128,2048]{1,0:T(8,128)(2,1)}, u32[]{:S(2)}, u32[]{:S(2)}) collective-permute-start(bf16[128,2048]{1,0:T(8,128)(2,1)} %get-tuple-element.132.refs_13_.refs_12_), channel_id=1, source_target_pairs={{0,4},{1,5},{2,6},{3,7},{4,0},{5,1},{6,2},{7,3},{8,12},{9,13},{10,... | collective-permute-start | bytes 1572872 | tf_op jit(solution)/shard_map/ppermute | solution.py:789
  156.4 4.7 %collective-permute-start.30 = (bf16[128,2048]{1,0:T(8,128)(2,1)}, bf16[128,2048]{1,0:T(8,128)(2,1)}, u32[]{:S(2)}, u32[]{:S(2)}) collective-permute-start(bf16[128,2048]{1,0:T(8,128)(2,1)} %get-tuple-element.134.refs_17_.refs_16_), channel_id=1, source_target_pairs={{0,4},{1,5},{2,6},{3,7},{4,0},{5,1},{6,2},{7,3},{8,12},{9,13},{10,... | collective-permute-start | bytes 1572872 | tf_op jit(solution)/shard_map/ppermute | solution.py:789
  183.8 27.6 %collective-permute-start.31 = (bf16[512,1024]{1,0:T(8,128)(2,1)}, bf16[512,1024]{1,0:T(8,128)(2,1)}, u32[]{:S(2)}, u32[]{:S(2)}) collective-permute-start(bf16[512,1024]{1,0:T(8,128)(2,1)} %get-tuple-element.139), channel_id=1, source_target_pairs={{0,4},{1,5},{2,6},{3,7},{4,0},{5,1},{6,2},{7,3},{8,12},{9,13},{10,... | collective-permute-start | bytes 3145736 | tf_op jit(solution)/shard_map/ppermute | solution.py:789
  184.1 62.0 %collective-permute-start.35 = (bf16[256,1024]{1,0:T(8,128)(2,1)}, bf16[256,1024]{1,0:T(8,128)(2,1)}, u32[]{:S(2)}, u32[]{:S(2)}) collective-permute-start(bf16[256,1024]{1,0:T(8,128)(2,1)} %get-tuple-element.147), channel_id=1, source_target_pairs={{0,0},{1,3},{2,4},{3,7},{4,2},{5,1},{6,6},{7,5},{8,8},{9,11},{10,1... | collective-permute-start | bytes 1572872 | tf_op jit(solution)/shard_map/ppermute | solution.py:789
  188.9 57.2 %collective-permute-start.36 = (bf16[256,1024]{1,0:T(8,128)(2,1)}, bf16[256,1024]{1,0:T(8,128)(2,1)}, u32[]{:S(2)}, u32[]{:S(2)}) collective-permute-start(bf16[256,1024]{1,0:T(8,128)(2,1)} %get-tuple-element.148), channel_id=1, source_target_pairs={{0,3},{1,0},{2,7},{3,4},{4,1},{5,2},{6,5},{7,6},{8,11},{9,8},{10,1... | collective-permute-start | bytes 1572872 | tf_op jit(solution)/shard_map/ppermute | solution.py:789
  215.3 30.8 %collective-permute-start.32 = (bf16[128,1024]{1,0:T(8,128)(2,1)}, bf16[128,1024]{1,0:T(8,128)(2,1)}, u32[]{:S(2)}, u32[]{:S(2)}) collective-permute-start(bf16[128,1024]{1,0:T(8,128)(2,1)} %get-tuple-element.206), channel_id=1, source_target_pairs={{0,8},{1,9},{2,10},{3,11},{4,12},{5,13},{6,14},{7,15},{8,0},{9,1},... | collective-permute-start | bytes 786440 | tf_op jit(solution)/shard_map/ppermute | solution.py:789
  216.7 29.4 %collective-permute-start.33 = (bf16[128,1024]{1,0:T(8,128)(2,1)}, bf16[128,1024]{1,0:T(8,128)(2,1)}, u32[]{:S(2)}, u32[]{:S(2)}) collective-permute-start(bf16[128,1024]{1,0:T(8,128)(2,1)} %get-tuple-element.205), channel_id=1, source_target_pairs={{0,16},{1,17},{2,18},{3,19},{4,20},{5,21},{6,22},{7,23},{8,24},{9,... | collective-permute-start | bytes 786440 | tf_op jit(solution)/shard_map/ppermute | solution.py:789
  217.1 29.0 %collective-permute-start.34 = (bf16[128,1024]{1,0:T(8,128)(2,1)}, bf16[128,1024]{1,0:T(8,128)(2,1)}, u32[]{:S(2)}, u32[]{:S(2)}) collective-permute-start(bf16[128,1024]{1,0:T(8,128)(2,1)} %get-tuple-element.204), channel_id=1, source_target_pairs={{0,24},{1,25},{2,26},{3,27},{4,28},{5,29},{6,30},{7,31},{8,16},{9,... | collective-permute-start | bytes 786440 | tf_op jit(solution)/shard_map/ppermute | solution.py:789
  246.2 5.5 %collective-permute-start.38 = (bf16[512,2048]{1,0:T(8,128)(2,1)}, bf16[512,2048]{1,0:T(8,128)(2,1)}, u32[]{:S(2)}, u32[]{:S(2)}) collective-permute-start(bf16[512,2048]{1,0:T(8,128)(2,1)} %get-tuple-element.162), channel_id=1, source_target_pairs={{0,4},{1,5},{2,6},{3,7},{4,0},{5,1},{6,2},{7,3},{8,12},{9,13},{10,... | collective-permute-start | bytes 6291464 | tf_op jit(solution)/shard_map/ppermute | solution.py:789
  249.1 33.2 %collective-permute-start.37 = (bf16[128,1024]{1,0:T(8,128)(2,1)}, bf16[128,1024]{1,0:T(8,128)(2,1)}, u32[]{:S(2)}, u32[]{:S(2)}) collective-permute-start(bf16[128,1024]{1,0:T(8,128)(2,1)} %add_convert_fusion.3.refs_5_), channel_id=1, source_target_pairs={{0,2},{1,3},{2,0},{3,1},{4,6},{5,7},{6,4},{7,5},{8,10},{9,11},{10,... | collective-permute-start | bytes 786440 | tf_op jit(solution)/shard_map/ppermute | solution.py:789
  259.7 27.5 %collective-permute-start.39 = (bf16[256,1024]{1,0:T(8,128)(2,1)}, bf16[256,1024]{1,0:T(8,128)(2,1)}, u32[]{:S(2)}, u32[]{:S(2)}) collective-permute-start(bf16[256,1024]{1,0:T(8,128)(2,1)} %get-tuple-element.164), channel_id=1, source_target_pairs={{0,0},{1,3},{2,4},{3,7},{4,2},{5,1},{6,6},{7,5},{8,8},{9,11},{10,1... | collective-permute-start | bytes 1572872 | tf_op jit(solution)/shard_map/ppermute | solution.py:789
  264.0 23.2 %collective-permute-start.40 = (bf16[256,1024]{1,0:T(8,128)(2,1)}, bf16[256,1024]{1,0:T(8,128)(2,1)}, u32[]{:S(2)}, u32[]{:S(2)}) collective-permute-start(bf16[256,1024]{1,0:T(8,128)(2,1)} %get-tuple-element.165), channel_id=1, source_target_pairs={{0,3},{1,0},{2,7},{3,4},{4,1},{5,2},{6,5},{7,6},{8,11},{9,8},{10,1... | collective-permute-start | bytes 1572872 | tf_op jit(solution)/shard_map/ppermute | solution.py:789
  287.2 4.5 %collective-permute-start.42 = (bf16[512,2048]{1,0:T(8,128)(2,1)}, bf16[512,2048]{1,0:T(8,128)(2,1)}, u32[]{:S(2)}, u32[]{:S(2)}) collective-permute-start(bf16[512,2048]{1,0:T(8,128)(2,1)} %get-tuple-element.176), channel_id=1, source_target_pairs={{0,4},{1,5},{2,6},{3,7},{4,0},{5,1},{6,2},{7,3},{8,12},{9,13},{10,... | collective-permute-start | bytes 6291464 | tf_op jit(solution)/shard_map/ppermute | solution.py:789
  289.0 11.0 %collective-permute-start.41 = (bf16[128,1024]{1,0:T(8,128)(2,1)}, bf16[128,1024]{1,0:T(8,128)(2,1)}, u32[]{:S(2)}, u32[]{:S(2)}) collective-permute-start(bf16[128,1024]{1,0:T(8,128)(2,1)} %add_convert_fusion.2.refs_27_), channel_id=1, source_target_pairs={{0,1},{1,0},{2,3},{3,2},{4,5},{5,4},{6,7},{7,6},{8,9},{9,8},{10,11... | collective-permute-start | bytes 786440 | tf_op jit(solution)/shard_map/ppermute | solution.py:789
  301.1 8.5 %collective-permute-start.45 = (bf16[128,1024]{1,0:T(8,128)(2,1)S(1)}, bf16[128,1024]{1,0:T(8,128)(2,1)S(1)}, u32[]{:S(2)}, u32[]{:S(2)}) collective-permute-start(bf16[128,1024]{1,0:T(8,128)(2,1)S(1)} %add_convert_fusion.1), channel_id=1, source_target_pairs={{0,16},{1,17},{2,18},{3,19},{4,20},{5,21},{6,22},{7,23},{8,24},{9,... | collective-permute-start | bytes 786440 | tf_op jit(solution)/shard_map/ppermute | solution.py:789
  302.2 7.6 %collective-permute-start.46 = (bf16[128,1024]{1,0:T(8,128)(2,1)S(1)}, bf16[128,1024]{1,0:T(8,128)(2,1)S(1)}, u32[]{:S(2)}, u32[]{:S(2)}) collective-permute-start(bf16[128,1024]{1,0:T(8,128)(2,1)S(1)} %add_convert_fusion.1), channel_id=1, source_target_pairs={{0,8},{1,9},{2,10},{3,11},{4,12},{5,13},{6,14},{7,15},{8,0},{9,1},... | collective-permute-start | bytes 786440 | tf_op jit(solution)/shard_map/ppermute | solution.py:789
  303.8 11.7 %collective-permute-start.47 = (bf16[128,1024]{1,0:T(8,128)(2,1)S(1)}, bf16[128,1024]{1,0:T(8,128)(2,1)S(1)}, u32[]{:S(2)}, u32[]{:S(2)}) collective-permute-start(bf16[128,1024]{1,0:T(8,128)(2,1)S(1)} %add_convert_fusion.1), channel_id=1, source_target_pairs={{0,24},{1,25},{2,26},{3,27},{4,28},{5,29},{6,30},{7,31},{8,16},{9,... | collective-permute-start | bytes 786440 | tf_op jit(solution)/shard_map/ppermute | solution.py:789
  303.8 28.0 %collective-permute-start.43 = (bf16[256,1024]{1,0:T(8,128)(2,1)}, bf16[256,1024]{1,0:T(8,128)(2,1)S(1)}, u32[]{:S(2)}, u32[]{:S(2)}) collective-permute-start(bf16[256,1024]{1,0:T(8,128)(2,1)} %get-tuple-element.182), channel_id=1, source_target_pairs={{0,0},{1,3},{2,4},{3,7},{4,2},{5,1},{6,6},{7,5},{8,8},{9,11},{10,1... | collective-permute-start | bytes 1572872 | tf_op jit(solution)/shard_map/ppermute | solution.py:789
  308.6 23.2 %collective-permute-start.44 = (bf16[256,1024]{1,0:T(8,128)(2,1)}, bf16[256,1024]{1,0:T(8,128)(2,1)S(1)}, u32[]{:S(2)}, u32[]{:S(2)}) collective-permute-start(bf16[256,1024]{1,0:T(8,128)(2,1)} %get-tuple-element.183), channel_id=1, source_target_pairs={{0,3},{1,0},{2,7},{3,4},{4,1},{5,2},{6,5},{7,6},{8,11},{9,8},{10,1... | collective-permute-start | bytes 1572872 | tf_op jit(solution)/shard_map/ppermute | solution.py:789
  315.6 17.3 %collective-permute-start.48 = (bf16[512,1024]{1,0:T(8,128)(2,1)S(1)}, bf16[512,1024]{1,0:T(8,128)(2,1)S(1)}, u32[]{:S(2)}, u32[]{:S(2)}) collective-permute-start(bf16[512,1024]{1,0:T(8,128)(2,1)S(1)} %pad_maximum_fusion.4), channel_id=1, source_target_pairs={{0,4},{1,5},{2,6},{3,7},{4,0},{5,1},{6,2},{7,3},{8,12},{9,13},{10,... | collective-permute-start | bytes 3145736 | tf_op jit(solution)/shard_map/ppermute | solution.py:789
  (20 other events, 137.2 us)
Sparse Core Ops, SparseCore 0:
  9.9 82.0 all-gather.2
  98.2 62.7 all-gather.4
